TPU v7x, 32 devices: a whole 2x2x4 slice. The times are simulated.
32 devices in a mesh: segment: 4 (over y, x), space: 8 (over z, core).
Axes of the slice: x: 2, y: 2, z: 4, core: 2. Of those that a mesh axis runs over, the one named last changes fastest.
Arguments:
- node_states: bfloat16 [2, 64, 29, 128], P(None, 'space'), may hold values from -6 to 6
- species: int32 [2, 64], P(None, 'space'), may hold values from 0 to 99
- species_table: bfloat16 [100, 128], replicated, may hold values from -6 to 6
- places: float32 [2, 3, 64], P(None, None, 'space'), may hold values from 0 to 2
- sources: int32 [2, 64, 8], P(None, 'space'), may hold values from 0 to 63, as said below
- radial_rate: float32 [4, 128], P('segment'), may hold values from 0.2 to 1.5
- zero_weight: bfloat16 [4, 896, 896], P('segment'), may hold values from -0.1875 to 0.1875
- one_weight: bfloat16 [4, 2, 768, 768], P('segment'), may hold values from -0.21875 to 0.21875
- two_weight: bfloat16 [4, 2, 640, 640], P('segment'), may hold values from -0.25 to 0.25
- read_weight: float32 [128], replicated, may hold values from -0.5 to 0.5
- energy_grad: float32 [2, 64], P(None, 'space'), may hold values from -6 to 6
Outputs:
- energies: float32 [2, 64], P(None, 'space')
- place_grads: float32 [2, 3, 64], P(None, None, 'space')
Inputs may be any that keep to these rules, and one draw needn't show every extreme that they name: Each atom's 8 sources are distinct, differ from the atom, and lie in the atom's slab (index // 8) or in one of the two slabs beside it, the slabs forming a closed chain.
All inputs are finite; a program needn't handle non-finite values.
Results may differ from a plain program's by a relative error of at most 0.012.
The roundings to bfloat16 on the way count: a program that leaves them out, or rounds other values in their place, can miss the bound.
Values may be sent and summed in bfloat16 or wider, within the bound.
No kernel may reach another device: no remote copies, remote signals or barrier semaphores. Data moves between devices by JAX's collectives and lax.ppermute only.
A program may use at most 128 MiB of HBM per device.

v0:
```python
import functools

import jax
import jax.numpy as jnp
from jax import lax
from jax.experimental import pallas as pl
from jax.experimental.pallas import tpu as pltpu
from jax.sharding import PartitionSpec as P

SLAB_DEPTH = 2.0
F32 = jnp.float32
BF16 = jnp.bfloat16
LINK = F32
VMEM_LIMIT = 40 * 1024 * 1024


def split(value):
    high = value.astype(BF16)
    low = (value - high.astype(F32)).astype(BF16)
    return high, low


def dot(a, b):
    return lax.dot_general(a, b, (((1,), (0,)), ((), ())), preferred_element_type=F32)


def dot_t(a, b):
    return lax.dot_general(a, b, (((1,), (1,)), ((), ())), preferred_element_type=F32)


def fine_dot(value, weights, product):
    rows = value.shape[0]
    stacked = jnp.concatenate(split(value), axis=0)
    outs = []
    for weight in weights:
        out = product(stacked, weight)
        outs.append(out[:rows] + out[rows:])
    return outs


def silu_parts(value):
    gate = 1.0 / (1.0 + jnp.exp(-value))
    return gate, value * gate


class Sizes:
    def __init__(self, zero_shape, one_shape, two_shape, channels):
        self.c = channels
        self.zero = zero_shape[-1] // channels
        self.one = one_shape[-1] // channels
        self.two = two_shape[-1] // channels
        self.coefs = self.zero + 2 * (self.one + self.two)
        self.starts = (self.zero, self.zero + 2 * self.one)
        self.counts = (self.one, self.two)

    def cols(self, first, count=1):
        return slice(first * self.c, (first + count) * self.c)


def picked_group(refs, hot, sz, first, count):
    cols = sz.cols(first, count)
    window = jnp.concatenate([ref[:, cols] for ref in refs], axis=0)
    return dot(hot, window)


def pool(value, rows):
    total = value[:rows]
    for start in range(rows, value.shape[0], rows):
        total = total + value[start : start + rows]
    return total


def geo_at(geo_ref, which, edges):
    return geo_ref[which * edges : (which + 1) * edges, :]


def forward(refs, hot_ref, geo_ref, zero_ref, one_ref, two_ref, sz, rows, last):
    hot = hot_ref[...]
    edges = hot.shape[0]
    factor = (edges // rows) ** (-0.5)
    radial = geo_at(geo_ref, 0, edges)

    def scaled(block):
        return (block * radial).astype(BF16).astype(F32)

    pooled = [None] * sz.coefs
    group = picked_group(refs, hot, sz, 0, sz.zero)
    zin = jnp.concatenate(
        [pool(scaled(group[:, sz.cols(k)]), rows) for k in range(sz.zero)], axis=1
    )
    kept = 1 if last else sz.zero
    (zout,) = fine_dot(zin, [zero_ref[:, sz.cols(0, kept)]], dot)
    for k in range(kept):
        pooled[k] = zout[:, sz.cols(k)] * factor
    for order in range(2):
        first, count = sz.starts[order], sz.counts[order]
        weight_ref = (one_ref, two_ref)[order]
        cos = geo_at(geo_ref, 1 + 2 * order, edges)
        sin = geo_at(geo_ref, 2 + 2 * order, edges)
        group = picked_group(refs, hot, sz, first, 2 * count)
        res, ims = [], []
        for k in range(count):
            re = scaled(group[:, sz.cols(k)])
            im = scaled(group[:, sz.cols(count + k)])
            res.append(pool(cos * re - sin * im, rows))
            ims.append(pool(sin * re + cos * im, rows))
        both = jnp.concatenate(
            [jnp.concatenate(res, axis=1), jnp.concatenate(ims, axis=1)], axis=0
        )
        a, b = fine_dot(both, [weight_ref[0], weight_ref[1]], dot)
        out_re = (a[:rows] - b[rows:]) * factor
        out_im = (b[:rows] + a[rows:]) * factor
        for k in range(count):
            pooled[first + k] = out_re[:, sz.cols(k)]
            pooled[first + count + k] = out_im[:, sz.cols(k)]
    return pooled


def signal_of(pooled, sz):
    total = pooled[0]
    for k in range(sz.zero, sz.coefs):
        total = total + pooled[k] * pooled[k]
    return total


def backward(
    upstream, pooled, refs, hot_ref, hot_t_ref, geo_ref, zero_ref, one_ref, two_ref, sz, rows, last, outs, places_ref
):
    hot = hot_ref[...]
    edges = hot.shape[0]
    factor = (edges // rows) ** (-0.5)
    signal = signal_of(pooled, sz)
    gate, _ = silu_parts(signal)
    slope = gate * (1.0 - gate)
    d_signal = upstream[0] * (gate + signal * slope)
    if not last:
        inner = upstream[1] * pooled[1]
        for k in range(2, sz.coefs):
            inner = inner + upstream[k] * pooled[k]
        d_signal = d_signal + inner * slope
    d_pooled = [d_signal * factor]
    for k in range(1, sz.coefs):
        if last:
            d_pooled.append(2.0 * factor * d_signal * pooled[k] if k >= sz.zero else None)
        else:
            term = gate * upstream[k]
            if k >= sz.zero:
                term = term + 2.0 * d_signal * pooled[k]
            d_pooled.append(term * factor)

    radial = geo_at(geo_ref, 0, edges)
    kept = 1 if last else sz.zero
    (dz,) = fine_dot(jnp.concatenate(d_pooled[:kept], axis=1), [zero_ref[:, sz.cols(0, kept)]], dot_t)

    def spread(block):
        return jnp.concatenate([block] * (edges // rows), axis=0)

    hot_t = None if outs is None else hot_t_ref[...]

    def scatter(first, blocks):
        if outs is None:
            return
        value = jnp.concatenate(blocks, axis=1)
        high, low = split(value)
        back = dot(hot_t, high) + dot(hot_t, low)
        cols = sz.cols(first, len(blocks))
        for place in range(3):
            part = back[place * rows : (place + 1) * rows]
            if place == 1 and not last:
                part = part + jnp.concatenate(upstream[first : first + len(blocks)], axis=1)
            elif place == 1 and first == 0:
                part = jnp.concatenate([part[:, : sz.c] + upstream[0], part[:, sz.c :]], axis=1)
            outs[place][:, cols] = part.astype(outs[place].dtype)

    q_len = jnp.zeros((edges, sz.c), F32)
    group = picked_group(refs, hot, sz, 0, sz.zero)
    blocks = []
    for k in range(sz.zero):
        grad = spread(dz[:, sz.cols(k)])
        q_len = q_len + grad * group[:, sz.cols(k)]
        blocks.append(grad * radial)
    q_len = q_len * radial
    scatter(0, blocks)
    q_turn = []
    for order in range(2):
        first, count = sz.starts[order], sz.counts[order]
        weight_ref = (one_ref, two_ref)[order]
        cos = geo_at(geo_ref, 1 + 2 * order, edges)
        sin = geo_at(geo_ref, 2 + 2 * order, edges)
        both = jnp.concatenate(
            [
                jnp.concatenate(d_pooled[first : first + count], axis=1),
                jnp.concatenate(d_pooled[first + count : first + 2 * count], axis=1),
            ],
            axis=0,
        )
        a, b = fine_dot(both, [weight_ref[0], weight_ref[1]], dot_t)
        d_re = a[:rows] + b[rows:]
        d_im = a[rows:] - b[:rows]
        group = picked_group(refs, hot, sz, first, 2 * count)
        q_cos = jnp.zeros((edges, sz.c), F32)
        q_sin = jnp.zeros((edges, sz.c), F32)
        cos_r = cos * radial
        sin_r = sin * radial
        blocks_re, blocks_im = [], []
        for k in range(count):
            re = group[:, sz.cols(k)]
            im = group[:, sz.cols(count + k)]
            g_re = spread(d_re[:, sz.cols(k)])
            g_im = spread(d_im[:, sz.cols(k)])
            q_cos = q_cos + (re * g_re + im * g_im)
            q_sin = q_sin + (re * g_im - im * g_re)
            if outs is not None:
                blocks_re.append(cos_r * g_re + sin_r * g_im)
                blocks_im.append(cos_r * g_im - sin_r * g_re)
        scatter(first, blocks_re + blocks_im)
        q_cos = q_cos * radial
        q_sin = q_sin * radial
        q_len = q_len + cos * q_cos + sin * q_sin
        q_turn.append((q_cos, q_sin))

    rate = geo_at(geo_ref, 11, edges)

    def total(value):
        return jnp.sum(value, axis=1, keepdims=True)

    d_len = -total(q_len * rate)
    (dc1, ds1), (dc2, ds2) = [(total(a), total(b)) for a, b in q_turn]
    c1, s1 = geo_at(geo_ref, 1, edges), geo_at(geo_ref, 2, edges)
    ux, uy, uz = (geo_at(geo_ref, 5 + n, edges) for n in range(3))
    inv_planar = geo_at(geo_ref, 8, edges)
    dc1 = dc1 + 2.0 * (c1 * dc2 + s1 * ds2)
    ds1 = ds1 + 2.0 * (c1 * ds2 - s1 * dc2)
    along = c1 * dc1 + s1 * ds1
    dx = (dc1 - along * c1) * inv_planar + d_len * ux
    dy = (ds1 - along * s1) * inv_planar + d_len * uy
    dz_ = d_len * uz
    lane = lax.broadcasted_iota(jnp.int32, (edges, sz.c), 1)
    change = jnp.where(lane == 0, dx, jnp.where(lane == 1, dy, jnp.where(lane == 2, dz_, 0.0)))
    high, rest = change.astype(BF16), None
    rest = change - high.astype(F32)
    mid = rest.astype(BF16)
    low = (rest - mid.astype(F32)).astype(BF16)
    hot_t = hot_t_ref[...]
    moved = dot(hot_t, high) + dot(hot_t, mid) + dot(hot_t, low)
    places_ref[:rows, :] = moved[:rows]
    places_ref[rows : 2 * rows, :] = moved[rows : 2 * rows] - pool(change, rows)
    places_ref[2 * rows :, :] = moved[2 * rows :]


def geometry_kernel(index_ref, places_ref, rate_ref, hot_ref, geo_ref):
    edges = index_ref.shape[0]
    window = places_ref.shape[0]
    rows = window // 3
    c = rate_ref.shape[1]
    hot = (index_ref[...] == lax.broadcasted_iota(jnp.int32, (edges, window), 1)).astype(BF16)
    hot_ref[...] = hot
    repeats = edges // rows
    offset = []
    for n in range(3):
        column = jnp.broadcast_to(places_ref[:, n : n + 1], (window, c))
        high = column.astype(BF16)
        rest = column - high.astype(F32)
        mid = rest.astype(BF16)
        low = (rest - mid.astype(F32)).astype(BF16)
        there = dot(hot, high) + dot(hot, mid) + dot(hot, low)
        offset.append(there - jnp.concatenate([column[rows : 2 * rows]] * repeats, axis=0))
    flat = offset[0] * offset[0] + offset[1] * offset[1] + 1.0
    length = jnp.sqrt(flat + offset[2] * offset[2])
    planar = jnp.sqrt(flat)
    c1, s1 = offset[0] / planar, offset[1] / planar
    rate = jnp.broadcast_to(rate_ref[...], (edges, c))
    parts = [
        jnp.exp(-rate * length),
        c1,
        s1,
        c1 * c1 - s1 * s1,
        2.0 * c1 * s1,
        offset[0] / length,
        offset[1] / length,
        offset[2] / length,
        1.0 / planar,
        offset[0],
        offset[1],
        rate,
    ]
    for n, part in enumerate(parts):
        geo_ref[n * edges : (n + 1) * edges, :] = part


def forward_kernel(
    tick, sz, flag_ref, left_ref, own_ref, right_ref, hot_ref, geo_ref, zero_ref, one_ref, two_ref, out_ref, pooled_ref
):
    @pl.when(flag_ref[0] == tick)
    def _():
        rows = own_ref.shape[0]
        refs = (left_ref, own_ref, right_ref)
        pooled = forward(refs, hot_ref, geo_ref, zero_ref, one_ref, two_ref, sz, rows, False)
        for k in range(sz.coefs):
            pooled_ref[:, sz.cols(k)] = pooled[k]
        signal = signal_of(pooled, sz)
        gate, lifted = silu_parts(signal)
        for k in range(sz.coefs):
            added = lifted if k == 0 else gate * pooled[k]
            out_ref[:, sz.cols(k)] = (own_ref[:, sz.cols(k)].astype(F32) + added).astype(BF16)


def turn_kernel(
    tick, sz, flag_ref, left_ref, own_ref, right_ref, hot_ref, hot_t_ref, geo_ref, zero_ref, one_ref, two_ref,
    read_ref, seed_ref, *out_refs
):
    energy_ref, places_ref = out_refs[:2]
    outs = out_refs[2:] or None

    @pl.when(flag_ref[0] == tick)
    def _():
        rows = own_ref.shape[0]
        refs = (left_ref, own_ref, right_ref)
        pooled = forward(refs, hot_ref, geo_ref, zero_ref, one_ref, two_ref, sz, rows, True)
        signal = signal_of(pooled, sz)
        _, lifted = silu_parts(signal)
        updated = own_ref[:, sz.cols(0)].astype(F32) + lifted
        gate, active = silu_parts(updated)
        read = read_ref[...]
        energy_ref[...] = jnp.sum(read * active, axis=1, keepdims=True)
        upstream = [seed_ref[...] * read * (gate + updated * gate * (1.0 - gate))]
        backward(
            upstream, pooled, refs, hot_ref, hot_t_ref, geo_ref, zero_ref, one_ref, two_ref, sz, rows, True, outs, places_ref
        )


def backward_kernel(
    tick, sz, flag_ref, upstream_ref, pooled_ref, left_ref, own_ref, right_ref, hot_ref, hot_t_ref, geo_ref,
    zero_ref, one_ref, two_ref, *out_refs
):
    places_ref = out_refs[0]
    outs = out_refs[1:] or None

    @pl.when(flag_ref[0] == tick)
    def _():
        rows = own_ref.shape[0]
        refs = (left_ref, own_ref, right_ref)
        upstream = [upstream_ref[:, sz.cols(k)].astype(F32) for k in range(sz.coefs)]
        pooled = [pooled_ref[:, sz.cols(k)] for k in range(sz.coefs)]
        backward(
            upstream, pooled, refs, hot_ref, hot_t_ref, geo_ref, zero_ref, one_ref, two_ref, sz, rows, False, outs, places_ref
        )


def on_vmem(value):
    return pltpu.with_memory_space_constraint(value, pltpu.VMEM)


def call(body, operands, shapes, flagged, name):
    in_specs = [pl.BlockSpec(memory_space=pltpu.VMEM) for _ in operands]
    if flagged:
        in_specs[0] = pl.BlockSpec(memory_space=pltpu.SMEM)
    return pl.pallas_call(
        body,
        out_shape=shapes,
        in_specs=in_specs,
        out_specs=jax.tree.map(lambda _: pl.BlockSpec(memory_space=pltpu.VMEM), shapes),
        compiler_params=pltpu.CompilerParams(vmem_limit_bytes=VMEM_LIMIT),
        name=name,
    )(*operands)


def on_device(
    node_states,
    species,
    species_table,
    places,
    sources,
    radial_rate,
    zero_weight,
    one_weight,
    two_weight,
    read_weight,
    energy_grad,
):
    segments = lax.axis_size("segment")
    slabs = lax.axis_size("space")
    segment_now = lax.axis_index("segment")
    slab_now = lax.axis_index("space")
    batches, per_slab = species.shape
    coefs, channels = node_states.shape[2:]
    neighbours = sources.shape[2]
    rows = batches * per_slab
    edges = rows * neighbours
    width = coefs * channels
    sz = Sizes(zero_weight.shape, one_weight.shape, two_weight.shape, channels)
    axes = ("segment", "space")

    def to_right(value):
        return lax.ppermute(value, "space", [(i, (i + 1) % slabs) for i in range(slabs)])

    def to_left(value):
        return lax.ppermute(value, "space", [((i + 1) % slabs, i) for i in range(slabs)])

    def in_segment(value, segment, by):
        pairs = [(segment * slabs + i, segment * slabs + (i + by) % slabs) for i in range(slabs)]
        return lax.ppermute(value, axes, pairs)

    def hop(value, start, stop):
        return lax.ppermute(value, axes, [(start * slabs + i, stop * slabs + i) for i in range(slabs)])

    onehot = (species[..., None] == jnp.arange(species_table.shape[0], dtype=jnp.int32)).astype(BF16)
    embed = jnp.einsum("bak,kc->bac", onehot, species_table, preferred_element_type=F32)
    start = jnp.concatenate(
        [(node_states[:, :, 0].astype(F32) + embed).astype(BF16)[:, :, None], node_states[:, :, 1:]], axis=2
    ).reshape(rows, width)

    own_places = places.transpose(0, 2, 1).reshape(rows, 3)
    lift = jnp.array([0.0, 0.0, SLAB_DEPTH], F32)
    window_places = jnp.concatenate(
        [to_right(own_places) - lift, own_places, to_left(own_places) + lift], axis=0
    )
    window = jnp.mod(sources // per_slab - slab_now + 1, slabs)
    batch = jnp.arange(batches, dtype=jnp.int32)[:, None, None]
    index = window * rows + batch * per_slab + sources % per_slab
    index = index.transpose(2, 0, 1).reshape(1, edges)
    hot_t = (index == jnp.arange(3 * rows, dtype=jnp.int32)[:, None]).astype(BF16)
    hot, geo = call(
        geometry_kernel,
        [index.reshape(edges, 1), window_places, radial_rate],
        [jax.ShapeDtypeStruct((edges, 3 * rows), BF16), jax.ShapeDtypeStruct((12 * edges, channels), F32)],
        False,
        "geometry",
    )
    flag = jnp.reshape(segment_now, (1,)).astype(jnp.int32)
    weights = [on_vmem(zero_weight[0]), on_vmem(one_weight[0]), on_vmem(two_weight[0])]
    states = jax.ShapeDtypeStruct((rows, width), BF16)
    wide = jax.ShapeDtypeStruct((rows, width), F32)
    link = jax.ShapeDtypeStruct((rows, width), LINK)
    place_shape = jax.ShapeDtypeStruct((3 * rows, channels), F32)

    around = [(to_right(start), start, to_left(start))]
    pooled = []
    for tick in range(segments - 1):
        out, kept = call(
            functools.partial(forward_kernel, tick, sz),
            [flag, *around[tick], hot, geo, *weights],
            [states, wide],
            True,
            "forward",
        )
        pooled.append(kept)
        own = hop(out, tick, tick + 1)
        around.append((in_segment(own, tick + 1, 1), own, in_segment(own, tick + 1, -1)))
    final = segments - 1
    seeds = jnp.broadcast_to(energy_grad.reshape(rows, 1), (rows, channels))
    more = [link, wide, link]
    energy, moved, *parts = call(
        functools.partial(turn_kernel, final, sz),
        [flag, *around[final], hot, hot_t, geo, *weights, read_weight.reshape(1, channels), seeds],
        [jax.ShapeDtypeStruct((rows, 1), F32), place_shape] + (more if final else []),
        True,
        "turn",
    )
    moves = [moved]
    for tick in reversed(range(segments - 1)):
        low, own, high = parts
        back_low = in_segment(low, tick + 1, -1)
        back_high = in_segment(high, tick + 1, 1)
        total = (own + back_low.astype(F32) + back_high.astype(F32)).astype(BF16)
        upstream = hop(total, tick + 1, tick)
        moved, *parts = call(
            functools.partial(backward_kernel, tick, sz),
            [flag, upstream, pooled[tick], *around[tick], hot, hot_t, geo, *weights],
            [place_shape] + (more if tick else []),
            True,
            "backward",
        )
        moves.insert(0, moved)

    here = jnp.zeros((3 * rows, 3), F32)
    for tick in range(segments):
        here = jnp.where(segment_now == tick, moves[tick][:, :3], here)
    shares = here[rows : 2 * rows] + to_left(here[:rows]) + to_right(here[2 * rows :])
    energies = jnp.where(segment_now == final, energy, 0.0)
    whole = lax.psum(jnp.concatenate([shares, energies], axis=1), "segment")
    whole = whole.reshape(batches, per_slab, 4)
    return whole[..., 3], whole[..., :3].transpose(0, 2, 1)


def solution(mesh):
    in_specs = (
        P(None, "space", None, None),
        P(None, "space"),
        P(),
        P(None, None, "space"),
        P(None, "space", None),
        P("segment", None),
        P("segment", None, None),
        P("segment", None, None, None),
        P("segment", None, None, None),
        P(),
        P(None, "space"),
    )
    out_specs = (P(None, "space"), P(None, None, "space"))
    return jax.shard_map(
        on_device, mesh=mesh, in_specs=in_specs, out_specs=out_specs, check_vma=False
    )
```

profile of v0, /device:TPU:0, one launch (start us, length us, event | category | flops | bytes accessed | tf_op | source)
XLA Modules:
  0.0 165.6 jit_solution(13590265701382936456)
XLA Ops:
  0.6 0.8 reshape.34
  1.9 4.0 %collective-permute-start.3 = (f32[16,3]{0,1:T(4,128)S(1)}, f32[16,3]{0,1:T(4,128)S(1)}, u32[]{:S(2)}, u32[]{:S(2)}) collective-permute-start(f32[16,3]{0,1:T(4,128)S(1)} %reshape.34), channel_id=1, source_target_pairs={{1,0},{2,1},{3,2},{4,3},{5,4},{6,5},{7,6},{0,7},{9,8},{10,9},{11,1... | collective-permute-start | bytes 584 | tf_op jit(solution)/shard_map/ppermute | solution.py:398
  5.9 0.9 slice.34
  6.8 0.9 fusion.1
  7.8 3.5 %collective-permute-start.1 = (bf16[16,3712]{1,0:T(8,128)(2,1)S(1)}, bf16[16,3712]{1,0:T(8,128)(2,1)S(1)}, u32[]{:S(2)}, u32[]{:S(2)}) collective-permute-start(bf16[16,3712]{1,0:T(8,128)(2,1)S(1)} %maximum_bitcast_fusion.own_ref), channel_id=1, source_target_pairs={{1,0},{2,1},{3,2},{4,3},{5,4},{6,5},{7,6},{0,7},{9,8},{10,9},{11,1... | collective-permute-start | bytes 356360 | tf_op jit(solution)/shard_map/ppermute | solution.py:398
  11.3 0.8 fusion.13
  12.3 0.7 broadcast_add_fusion
  13.0 0.7 broadcast_add_fusion.1
  15.0 0.7 copy-done.22
  15.7 1.7 %copy-done.1 = bf16[1,2,768,768]{3,2,1,0:T(8,128)(2,1)S(1)} copy-done((bf16[1,2,768,768]{3,2,1,0:T(8,128)(2,1)S(1)}, bf16[1,2,768,768]{3,2,1,0:T(8,128)(2,1)}, u32[]{:S(2)}) %copy-start.1) | copy-done | bytes 2359320
  17.3 1.4 copy-done.3
  18.8 1.4 copy-done.7
  20.2 0.9 copy-done.23
  21.1 1.7 %forward.3 = (bf16[16,3712]{1,0:T(8,128)(2,1)S(1)}, f32[16,3712]{1,0:T(8,128)S(1)}) custom-call(s32[1]{0:T(128)} %bitcast.flag_ref, bf16[16,3712]{1,0:T(8,128)(2,1)S(1)} %collective-permute-done.left_ref, bf16[16,3712]{1,0:T(8,128)(2,1)S(1)} %maximum_bitcast_fusion.own_ref, bf16[16,3712]{1,0:T(8,128)(2,1)S(1)} %copy-done.23, ...), custom_call_target="tpu_custom_call" | custom-call | tf_op jit(solution)/shard_map/forward/pallas_call | solution.py:358
  22.8 0.7 copy-done.29
  23.5 2.3 %collective-permute-start.4 = (bf16[16,3712]{1,0:T(8,128)(2,1)S(1)}, bf16[16,3712]{1,0:T(8,128)(2,1)S(1)}, u32[]{:S(2)}, u32[]{:S(2)}) collective-permute-start(bf16[16,3712]{1,0:T(8,128)(2,1)S(1)} %get-tuple-element.25), channel_id=1, source_target_pairs={{0,8},{1,9},{2,10},{3,11},{4,12},{5,13},{6,14},{7,15}} | collective-permute-start | bytes 356360 | tf_op jit(solution)/shard_map/ppermute | solution.py:405
  25.8 2.4 %collective-permute-done.4.own_ref = bf16[16,3712]{1,0:T(8,128)(2,1)S(1)} collective-permute-done((bf16[16,3712]{1,0:T(8,128)(2,1)S(1)}, bf16[16,3712]{1,0:T(8,128)(2,1)S(1)}, u32[]{:S(2)}, u32[]{:S(2)}) %collective-permute-start.4) | collective-permute-done | bytes 118816 | tf_op jit(solution)/shard_map/ppermute | solution.py:405
  28.9 0.7 collective-permute-start.6
  30.3 0.7 copy-done.25
  31.0 0.8 collective-permute-start.7
  31.8 0.7 collective-permute-start.8
  32.5 0.7 collective-permute-start.9
  33.2 0.7 forward.5
  33.9 0.7 copy-done.27
  34.6 1.3 collective-permute-start.10
  36.8 0.7 collective-permute-start.12
  37.6 1.4 copy-done.5
  39.0 1.4 copy-done.8
  40.4 1.0 turn.1
  42.1 0.7 collective-permute-start.14
  42.8 0.7 collective-permute-start.15
  43.6 0.8 collective-permute-start.16
  44.4 0.7 collective-permute-start.17
  45.2 0.7 collective-permute-start.18
  46.1 0.7 collective-permute-start.19
  46.8 0.7 collective-permute-start.20
  47.5 0.7 add_convert_fusion
  48.2 1.3 collective-permute-start.21
  49.5 94.4 %collective-permute-done.21.upstream_ref = bf16[16,3712]{1,0:T(8,128)(2,1)S(1)} collective-permute-done((bf16[16,3712]{1,0:T(8,128)(2,1)}, bf16[16,3712]{1,0:T(8,128)(2,1)S(1)}, u32[]{:S(2)}, u32[]{:S(2)}) %collective-permute-start.21) | collective-permute-done | bytes 118816 | tf_op jit(solution)/shard_map/ppermute | solution.py:405
  143.9 1.4 copy-done.6
  145.3 1.4 copy-done.9
  146.7 0.9 copy-done.21
  147.6 0.9 copy-done.24
  148.5 0.9 copy-done.30
  149.4 2.3 %backward.5 = f32[48,128]{1,0:T(8,128)S(1)} custom-call(s32[1]{0:T(128)} %bitcast.flag_ref, bf16[16,3712]{1,0:T(8,128)(2,1)S(1)} %collective-permute-done.21.upstream_ref, f32[16,3712]{1,0:T(8,128)S(1)} %copy-done.30, bf16[16,3712]{1,0:T(8,128)(2,1)S(1)} %copy-done.21, bf16[16,3712]{1,0:T(8,128)(2,1)S(1)} %maximum_bitcast_fusion.own_ref, ...), custom_call_target="tpu_custom_call" | custom-call | tf_op jit(solution)/shard_map/backward/pallas_call | solution.py:358
  152.5 0.8 collective-permute-done.22
  153.2 3.6 %collective-permute-done.23 = f32[16,3]{1,0:T(8,128)S(1)} collective-permute-done((f32[16,3]{1,0:T(8,128)S(1)}, f32[16,3]{1,0:T(8,128)S(1)}, u32[]{:S(2)}, u32[]{:S(2)}) %collective-permute-start.23) | collective-permute-done | bytes 224 | tf_op jit(solution)/shard_map/ppermute | solution.py:395
  157.0 7.4 %psum.7 = f32[2,8,4]{1,0,2:T(2,128)S(1)} all-reduce(f32[2,8,4]{1,0,2:T(2,128)S(1)} %reshape.36), channel_id=1, replica_groups=mesh['segment'=4,'space'=8] {'segment'}, use_global_device_ids=true, to_apply=%region_0.1 | all-reduce | flops 64 | bytes 512 | tf_op jit(solution)/shard_map/psum | solution.py:481
  (106 shorter events, 7.2 us)
Async XLA Ops:
  0.6 6.2 %copy-start = (bf16[100,128]{1,0:T(8,128)(2,1)S(1)}, bf16[100,128]{1,0:T(8,128)(2,1)}, u32[]{:S(2)}) copy-start(bf16[100,128]{1,0:T(8,128)(2,1)} %param.14) | copy-start | bytes 76804
  1.4 10.9 %collective-permute-start.2 = (f32[16,3]{0,1:T(4,128)S(1)}, f32[16,3]{0,1:T(4,128)S(1)}, u32[]{:S(2)}, u32[]{:S(2)}) collective-permute-start(f32[16,3]{0,1:T(4,128)S(1)} %reshape.34), channel_id=1, source_target_pairs={{0,1},{1,2},{2,3},{3,4},{4,5},{5,6},{6,7},{7,0},{8,9},{9,10},{10,1... | collective-permute-start | bytes 584 | tf_op jit(solution)/shard_map/ppermute | solution.py:395
  1.9 11.2 %collective-permute-start.3 = (f32[16,3]{0,1:T(4,128)S(1)}, f32[16,3]{0,1:T(4,128)S(1)}, u32[]{:S(2)}, u32[]{:S(2)}) collective-permute-start(f32[16,3]{0,1:T(4,128)S(1)} %reshape.34), channel_id=1, source_target_pairs={{1,0},{2,1},{3,2},{4,3},{5,4},{6,5},{7,6},{0,7},{9,8},{10,9},{11,1... | collective-permute-start | bytes 584 | tf_op jit(solution)/shard_map/ppermute | solution.py:398
  7.7 7.2 %collective-permute-start = (bf16[16,3712]{1,0:T(8,128)(2,1)S(1)}, bf16[16,3712]{1,0:T(8,128)(2,1)S(1)}, u32[]{:S(2)}, u32[]{:S(2)}) collective-permute-start(bf16[16,3712]{1,0:T(8,128)(2,1)S(1)} %maximum_bitcast_fusion.own_ref), channel_id=1, source_target_pairs={{0,1},{1,2},{2,3},{3,4},{4,5},{5,6},{6,7},{7,0},{8,9},{9,10},{10,1... | collective-permute-start | bytes 356360 | tf_op jit(solution)/shard_map/ppermute | solution.py:395
  7.8 7.2 %collective-permute-start.1 = (bf16[16,3712]{1,0:T(8,128)(2,1)S(1)}, bf16[16,3712]{1,0:T(8,128)(2,1)S(1)}, u32[]{:S(2)}, u32[]{:S(2)}) collective-permute-start(bf16[16,3712]{1,0:T(8,128)(2,1)S(1)} %maximum_bitcast_fusion.own_ref), channel_id=1, source_target_pairs={{1,0},{2,1},{3,2},{4,3},{5,4},{6,5},{7,6},{0,7},{9,8},{10,9},{11,1... | collective-permute-start | bytes 356360 | tf_op jit(solution)/shard_map/ppermute | solution.py:398
  15.0 7.8 %copy-start.20 = (bf16[16,3712]{1,0:T(8,128)(2,1)}, bf16[16,3712]{1,0:T(8,128)(2,1)S(1)}, u32[]{:S(2)}) copy-start(bf16[16,3712]{1,0:T(8,128)(2,1)S(1)} %collective-permute-done.left_ref) | copy-start | bytes 356356
  15.7 1.7 %copy-start.1 = (bf16[1,2,768,768]{3,2,1,0:T(8,128)(2,1)S(1)}, bf16[1,2,768,768]{3,2,1,0:T(8,128)(2,1)}, u32[]{:S(2)}) copy-start(bf16[1,2,768,768]{3,2,1,0:T(8,128)(2,1)} %param.19) | copy-start | bytes 7077892
  17.3 1.4 copy-start.3
  18.8 1.4 copy-start.7
  20.2 0.9 copy-start.23
  21.1 8.5 %copy-start.2 = (bf16[1,2,768,768]{3,2,1,0:T(8,128)(2,1)S(1)}, bf16[1,2,768,768]{3,2,1,0:T(8,128)(2,1)}, u32[]{:S(2)}) copy-start(bf16[1,2,768,768]{3,2,1,0:T(8,128)(2,1)} %param.19) | copy-start | bytes 7077892
  21.1 8.5 %copy-start.4 = (bf16[1,2,640,640]{3,2,1,0:T(8,128)(2,1)S(1)}, bf16[1,2,640,640]{3,2,1,0:T(8,128)(2,1)}, u32[]{:S(2)}) copy-start(bf16[1,2,640,640]{3,2,1,0:T(8,128)(2,1)} %param.20) | copy-start | bytes 4915204
  23.5 4.7 %collective-permute-start.4 = (bf16[16,3712]{1,0:T(8,128)(2,1)S(1)}, bf16[16,3712]{1,0:T(8,128)(2,1)S(1)}, u32[]{:S(2)}, u32[]{:S(2)}) collective-permute-start(bf16[16,3712]{1,0:T(8,128)(2,1)S(1)} %get-tuple-element.25), channel_id=1, source_target_pairs={{0,8},{1,9},{2,10},{3,11},{4,12},{5,13},{6,14},{7,15}} | collective-permute-start | bytes 356360 | tf_op jit(solution)/shard_map/ppermute | solution.py:405
  28.2 1.3 collective-permute-start.5
  28.9 0.7 collective-permute-start.6
  31.0 5.0 %copy-start.33 = (f32[2,8]{1,0:T(2,128)S(1)}, f32[2,8]{1,0:T(2,128)}, u32[]{:S(2)}) copy-start(f32[2,8]{1,0:T(2,128)} %param.22) | copy-start | bytes 196
  31.0 6.6 %copy-start.32 = (f32[128]{0:T(128)S(1)}, f32[128]{0:T(128)}, u32[]{:S(2)}) copy-start(f32[128]{0:T(128)} %param.21) | copy-start | bytes 1540
  31.0 0.8 collective-permute-start.7
  31.8 2.1 %copy-start.14 = (bf16[16,3712]{1,0:T(8,128)(2,1)}, bf16[16,3712]{1,0:T(8,128)(2,1)S(1)}, u32[]{:S(2)}) copy-start(bf16[16,3712]{1,0:T(8,128)(2,1)S(1)} %collective-permute-done.7.own_ref) | copy-start | bytes 356356
  31.8 1.4 collective-permute-start.8
  32.5 0.7 collective-permute-start.9
  34.6 1.5 collective-permute-start.10
  36.1 1.4 collective-permute-start.11
  36.8 0.7 collective-permute-start.12
  37.6 1.4 copy-start.5
  39.0 1.4 copy-start.8
  40.4 3.1 %copy-start.15 = (bf16[16,3712]{1,0:T(8,128)(2,1)S(1)}, bf16[16,3712]{1,0:T(8,128)(2,1)}, u32[]{:S(2)}) copy-start(bf16[16,3712]{1,0:T(8,128)(2,1)} %copy-done.14) | copy-start | bytes 356356
  40.4 3.1 %copy-start.17 = (bf16[16,3712]{1,0:T(8,128)(2,1)S(1)}, bf16[16,3712]{1,0:T(8,128)(2,1)}, u32[]{:S(2)}) copy-start(bf16[16,3712]{1,0:T(8,128)(2,1)} %copy-done.16) | copy-start | bytes 356356
  40.4 3.1 %copy-start.19 = (bf16[16,3712]{1,0:T(8,128)(2,1)S(1)}, bf16[16,3712]{1,0:T(8,128)(2,1)}, u32[]{:S(2)}) copy-start(bf16[16,3712]{1,0:T(8,128)(2,1)} %copy-done.18) | copy-start | bytes 356356
  40.4 3.1 %copy-start.28 = (f32[16,3712]{1,0:T(8,128)S(1)}, f32[16,3712]{1,0:T(8,128)}, u32[]{:S(2)}) copy-start(f32[16,3712]{1,0:T(8,128)} %copy-done.27) | copy-start | bytes 712708
  41.4 1.4 collective-permute-start.13
  42.1 0.7 collective-permute-start.14
  42.8 0.7 collective-permute-start.15
  43.5 2.3 %copy-start.11 = (bf16[16,3712]{1,0:T(8,128)(2,1)S(1)}, bf16[16,3712]{1,0:T(8,128)(2,1)}, u32[]{:S(2)}) copy-start(bf16[16,3712]{1,0:T(8,128)(2,1)} %copy-done.10) | copy-start | bytes 356356
  43.5 2.3 %copy-start.13 = (bf16[16,3712]{1,0:T(8,128)(2,1)S(1)}, bf16[16,3712]{1,0:T(8,128)(2,1)}, u32[]{:S(2)}) copy-start(bf16[16,3712]{1,0:T(8,128)(2,1)} %copy-done.12) | copy-start | bytes 356356
  43.6 2.3 %copy-start.26 = (f32[16,3712]{1,0:T(8,128)S(1)}, f32[16,3712]{1,0:T(8,128)}, u32[]{:S(2)}) copy-start(f32[16,3712]{1,0:T(8,128)} %copy-done.25) | copy-start | bytes 712708
  43.6 1.5 collective-permute-start.16
  44.4 0.7 collective-permute-start.17
  45.2 0.7 collective-permute-start.18
  46.1 1.4 collective-permute-start.19
  46.8 0.7 collective-permute-start.20
  48.2 95.7 %collective-permute-start.21 = (bf16[16,3712]{1,0:T(8,128)(2,1)}, bf16[16,3712]{1,0:T(8,128)(2,1)S(1)}, u32[]{:S(2)}, u32[]{:S(2)}) collective-permute-start(bf16[16,3712]{1,0:T(8,128)(2,1)} %add_convert_fusion), channel_id=1, source_target_pairs={{8,0},{9,1},{10,2},{11,3},{12,4},{13,5},{14,6},{15,7}} | collective-permute-start | bytes 356360 | tf_op jit(solution)/shard_map/ppermute | solution.py:405
  143.9 1.4 copy-start.6
  145.3 1.4 copy-start.9
  146.7 0.9 copy-start.21
  148.5 0.9 copy-start.30
  151.8 1.4 collective-permute-start.22
  151.9 4.9 %collective-permute-start.23 = (f32[16,3]{1,0:T(8,128)S(1)}, f32[16,3]{1,0:T(8,128)S(1)}, u32[]{:S(2)}, u32[]{:S(2)}) collective-permute-start(f32[16,3]{1,0:T(8,128)S(1)} %get-tuple-element.45), channel_id=1, source_target_pairs={{0,1},{1,2},{2,3},{3,4},{4,5},{5,6},{6,7},{7,0},{8,9},{9,10},{10,1... | collective-permute-start | bytes 584 | tf_op jit(solution)/shard_map/ppermute | solution.py:395
  (10 other events, 7.2 us)
where the time goes:
time: 166 us
  waiting for transfers between devices  101 us (61%)
  starting transfers between devices  23.8 us (14%)
  local copies, waits for them, and re-layouts  21.6 us (13%)
  blocking collectives  7.44 us (4%)
  Pallas kernels  6.25 us (4%)
  other arithmetic  3.17 us (2%)
    ppermute x6, waiting for transfers between devices, hop(): lax.ppermute(value, axes, [(start * slabs + i, stop * slabs + i) for i in...  96.8 us
    unnamed x68, local copies, waits for them, and re-layouts  18 us
    ppermute x12, starting transfers between devices, in_segment(): return lax.ppermute(value, axes, pairs)  8.16 us
    ppermute x3, starting transfers between devices, to_left(): lax.ppermute(value, 'space', [((i + 1) % slabs, i) for i in range(slabs)])  7.63 us
    psum x1, blocking collectives, on_device(): whole = lax.psum(jnp.concatenate([shares, energies], axis=1), 'segment')  7.44 us
    ppermute x6, starting transfers between devices, hop(): lax.ppermute(value, axes, [(start * slabs + i, stop * slabs + i) for i in...  7.02 us
    pallas_call x8, Pallas kernels, call(): pl.pallas_call(body, out_shape=shapes, in_specs=in_specs, out_specs=jax.t...  6.25 us
    ppermute x3, waiting for transfers between devices, to_right(): lax.ppermute(value, 'space', [(i, (i + 1) % slabs) for i in range(slabs)])  3.57 us
  transfers between devices with their start and end apart: 24, of which 4 were waited for; matrix products, arithmetic and copies ran while one was open for 3% of the time, Pallas kernels for 0%

commit v1 on v0

v1 whole, which is shorter than its diff:
```python
import functools

import jax
import jax.numpy as jnp
from jax import lax
from jax.experimental import pallas as pl
from jax.experimental.pallas import tpu as pltpu
from jax.sharding import PartitionSpec as P

SLAB_DEPTH = 2.0
F32 = jnp.float32
BF16 = jnp.bfloat16
VMEM_LIMIT = 16 * 1024 * 1024

MID, LOW, SOURCES = 32, 64, 96
BASE = 256


def split(value):
    high = value.astype(BF16)
    low = (value - high.astype(F32)).astype(BF16)
    return high, low


def split3(value):
    high = value.astype(BF16)
    rest = value - high.astype(F32)
    mid = rest.astype(BF16)
    return high, mid, (rest - mid.astype(F32)).astype(BF16)


def encode(value):
    high, mid, low = split3(value)
    return high.astype(F32) + pltpu.roll(mid.astype(F32), MID, 1) + pltpu.roll(low.astype(F32), LOW, 1)


def decode(value):
    lanes = value.shape[1]
    whole = value + pltpu.roll(value, lanes - MID, 1) + pltpu.roll(value, lanes - LOW, 1)
    lane = lax.broadcasted_iota(jnp.int32, value.shape, 1)
    return jnp.where(lane < 4, whole, 0.0)


def dot(a, b):
    return lax.dot_general(a, b, (((1,), (0,)), ((), ())), preferred_element_type=F32)


def dot_t(a, b):
    return lax.dot_general(a, b, (((1,), (1,)), ((), ())), preferred_element_type=F32)


def fine_dot(value, weights, product):
    rows = value.shape[0]
    stacked = jnp.concatenate(split(value), axis=0)
    outs = []
    for weight in weights:
        out = product(stacked, weight)
        outs.append(out[:rows] + out[rows:])
    return outs


def silu_parts(value):
    gate = 1.0 / (1.0 + jnp.exp(-value))
    return gate, value * gate


class Sizes:
    def __init__(self, zero_shape, one_shape, two_shape, channels):
        self.c = channels
        self.zero = zero_shape[-1] // channels
        self.one = one_shape[-1] // channels
        self.two = two_shape[-1] // channels
        self.coefs = self.zero + 2 * (self.one + self.two)
        self.starts = (self.zero, self.zero + 2 * self.one)
        self.counts = (self.one, self.two)

    def cols(self, first, count=1):
        return slice(first * self.c, (first + count) * self.c)


def picked_group(refs, hot, first, count):
    blocks = []
    for k in range(first, first + count):
        blocks.append(jnp.concatenate([ref[k].astype(F32) for ref in refs], axis=0).astype(BF16))
    return dot(hot, jnp.concatenate(blocks, axis=1))


def pool(value, rows):
    total = value[:rows]
    for start in range(rows, value.shape[0], rows):
        total = total + value[start : start + rows]
    return total


def geo_at(geo_ref, which, edges):
    return geo_ref[which * edges : (which + 1) * edges, :]


def forward(refs, hot_ref, geo_ref, zero_ref, one_ref, two_ref, sz, rows, last):
    hot = hot_ref[...]
    edges = hot.shape[0]
    factor = (edges // rows) ** (-0.5)
    radial = geo_at(geo_ref, 0, edges)

    def scaled(block):
        return (block * radial).astype(BF16).astype(F32)

    pooled = [None] * sz.coefs
    group = picked_group(refs, hot, 0, sz.zero)
    zin = jnp.concatenate(
        [pool(scaled(group[:, sz.cols(k)]), rows) for k in range(sz.zero)], axis=1
    )
    kept = 1 if last else sz.zero
    (zout,) = fine_dot(zin, [zero_ref[:, sz.cols(0, kept)]], dot)
    for k in range(kept):
        pooled[k] = zout[:, sz.cols(k)] * factor
    for order in range(2):
        first, count = sz.starts[order], sz.counts[order]
        weight_ref = (one_ref, two_ref)[order]
        cos = geo_at(geo_ref, 1 + 2 * order, edges)
        sin = geo_at(geo_ref, 2 + 2 * order, edges)
        group = picked_group(refs, hot, first, 2 * count)
        res, ims = [], []
        for k in range(count):
            re = scaled(group[:, sz.cols(k)])
            im = scaled(group[:, sz.cols(count + k)])
            res.append(pool(cos * re - sin * im, rows))
            ims.append(pool(sin * re + cos * im, rows))
        both = jnp.concatenate(
            [jnp.concatenate(res, axis=1), jnp.concatenate(ims, axis=1)], axis=0
        )
        a, b = fine_dot(both, [weight_ref[0], weight_ref[1]], dot)
        out_re = (a[:rows] - b[rows:]) * factor
        out_im = (b[:rows] + a[rows:]) * factor
        for k in range(count):
            pooled[first + k] = out_re[:, sz.cols(k)]
            pooled[first + count + k] = out_im[:, sz.cols(k)]
    return pooled


def signal_of(pooled, sz):
    total = pooled[0]
    for k in range(sz.zero, sz.coefs):
        total = total + pooled[k] * pooled[k]
    return total


def backward(
    upstream, carried, pooled, refs, hot_ref, hot_t_ref, geo_ref, zero_ref, one_ref, two_ref, sz, rows, last, outs
):
    hot = hot_ref[...]
    hot_t = hot_t_ref[...]
    edges = hot.shape[0]
    slab = rows // 2
    factor = (edges // rows) ** (-0.5)
    signal = signal_of(pooled, sz)
    gate, _ = silu_parts(signal)
    slope = gate * (1.0 - gate)
    d_signal = upstream[0] * (gate + signal * slope)
    if not last:
        inner = upstream[1] * pooled[1]
        for k in range(2, sz.coefs):
            inner = inner + upstream[k] * pooled[k]
        d_signal = d_signal + inner * slope
    d_pooled = [d_signal * factor]
    for k in range(1, sz.coefs):
        if last:
            d_pooled.append(2.0 * factor * d_signal * pooled[k] if k >= sz.zero else None)
        else:
            term = gate * upstream[k]
            if k >= sz.zero:
                term = term + 2.0 * d_signal * pooled[k]
            d_pooled.append(term * factor)

    radial = geo_at(geo_ref, 0, edges)
    kept = 1 if last else sz.zero
    (dz,) = fine_dot(jnp.concatenate(d_pooled[:kept], axis=1), [zero_ref[:, sz.cols(0, kept)]], dot_t)

    def spread(block):
        return jnp.concatenate([block] * (edges // rows), axis=0)

    def scatter(first, blocks):
        if outs is None:
            return
        high, low = split(jnp.concatenate(blocks, axis=1))
        back = dot(hot_t, high) + dot(hot_t, low)
        for n in range(len(blocks)):
            k = first + n
            part = back[:, sz.cols(n)]
            middle = part[slab : slab + rows]
            if not last or k == 0:
                middle = middle + upstream[k]
            outs[0][k] = part[:slab].astype(BF16)
            outs[1][k] = middle.astype(BF16)
            outs[2][k] = part[slab + rows :].astype(BF16)

    q_len = jnp.zeros((edges, sz.c), F32)
    group = picked_group(refs, hot, 0, sz.zero)
    blocks = []
    for k in range(sz.zero):
        grad = spread(dz[:, sz.cols(k)])
        q_len = q_len + grad * group[:, sz.cols(k)]
        blocks.append(grad * radial)
    q_len = q_len * radial
    scatter(0, blocks)
    q_turn = []
    for order in range(2):
        first, count = sz.starts[order], sz.counts[order]
        weight_ref = (one_ref, two_ref)[order]
        cos = geo_at(geo_ref, 1 + 2 * order, edges)
        sin = geo_at(geo_ref, 2 + 2 * order, edges)
        both = jnp.concatenate(
            [
                jnp.concatenate(d_pooled[first : first + count], axis=1),
                jnp.concatenate(d_pooled[first + count : first + 2 * count], axis=1),
            ],
            axis=0,
        )
        a, b = fine_dot(both, [weight_ref[0], weight_ref[1]], dot_t)
        d_re = a[:rows] + b[rows:]
        d_im = a[rows:] - b[:rows]
        group = picked_group(refs, hot, first, 2 * count)
        q_cos = jnp.zeros((edges, sz.c), F32)
        q_sin = jnp.zeros((edges, sz.c), F32)
        cos_r = cos * radial
        sin_r = sin * radial
        blocks_re, blocks_im = [], []
        for k in range(count):
            re = group[:, sz.cols(k)]
            im = group[:, sz.cols(count + k)]
            g_re = spread(d_re[:, sz.cols(k)])
            g_im = spread(d_im[:, sz.cols(k)])
            q_cos = q_cos + (re * g_re + im * g_im)
            q_sin = q_sin + (re * g_im - im * g_re)
            if outs is not None:
                blocks_re.append(cos_r * g_re + sin_r * g_im)
                blocks_im.append(cos_r * g_im - sin_r * g_re)
        scatter(first, blocks_re + blocks_im)
        q_cos = q_cos * radial
        q_sin = q_sin * radial
        q_len = q_len + cos * q_cos + sin * q_sin
        q_turn.append((q_cos, q_sin))

    rate = geo_at(geo_ref, 9, edges)

    def total(value):
        return jnp.sum(value, axis=1, keepdims=True)

    d_len = -total(q_len * rate)
    (dc1, ds1), (dc2, ds2) = [(total(a), total(b)) for a, b in q_turn]
    c1, s1 = geo_at(geo_ref, 1, edges), geo_at(geo_ref, 2, edges)
    ux, uy, uz = (geo_at(geo_ref, 5 + n, edges) for n in range(3))
    inv_planar = geo_at(geo_ref, 8, edges)
    dc1 = dc1 + 2.0 * (c1 * dc2 + s1 * ds2)
    ds1 = ds1 + 2.0 * (c1 * ds2 - s1 * dc2)
    along = c1 * dc1 + s1 * ds1
    dx = (dc1 - along * c1) * inv_planar + d_len * ux
    dy = (ds1 - along * s1) * inv_planar + d_len * uy
    dz_ = d_len * uz
    lane = lax.broadcasted_iota(jnp.int32, (edges, sz.c), 1)
    change = jnp.where(lane == 0, dx, jnp.where(lane == 1, dy, jnp.where(lane == 2, dz_, 0.0)))
    moved = sum(dot(hot_t, part) for part in split3(change))
    own = moved[slab : slab + rows] - pool(change, rows) + carried
    return moved[:slab], own, moved[slab + rows :]


def send_back(moved, outs, sz):
    for ref, value in zip(outs, moved):
        ref[sz.coefs] = encode(value).astype(BF16)


def pack_kernel(
    node_hbm, places_hbm, species_hbm, sources_hbm, grad_hbm, table_hbm, mine_ref, other_ref,
    states, places, species, sources, grads, table, sems
):
    slab_now = lax.axis_index("space")
    batch = lax.rem(slab_now, 2)
    copies = []
    pairs = (
        (node_hbm, states), (places_hbm, places), (species_hbm, species), (sources_hbm, sources),
        (grad_hbm, grads), (table_hbm, table),
    )
    for n, (source, target) in enumerate(pairs):
        copies.append(pltpu.make_async_copy(source, target, sems.at[n]))
        copies[-1].start()
    for copy in copies:
        copy.wait()
    coefs, per_slab, c = states.shape[1:]
    lane = lax.broadcasted_iota(jnp.int32, (per_slab, c), 1)
    eye = (
        lax.broadcasted_iota(jnp.int32, (per_slab, per_slab), 0)
        == lax.broadcasted_iota(jnp.int32, (per_slab, per_slab), 1)
    )

    def column(row):
        return jnp.sum(jnp.where(eye, jnp.broadcast_to(row, (per_slab, per_slab)), 0.0), axis=1, keepdims=True)

    both = []
    for b in range(2):
        names = column(species[b : b + 1, :].astype(F32)).astype(jnp.int32)
        kinds = table.shape[0]
        hot = (names == lax.broadcasted_iota(jnp.int32, (per_slab, kinds), 1)).astype(BF16)
        first = (states[b, 0].astype(F32) + dot(hot, table[...])).astype(BF16)
        extra = jnp.zeros((per_slab, c), F32)
        for n in range(3):
            extra = jnp.where(lane == n, column(places[n, b : b + 1, :]), extra)
        extra = encode(jnp.where(lane == 3, column(grads[b : b + 1, :]), extra))
        for j in range(sources.shape[2]):
            index = sources[b, :, j : j + 1]
            extra = jnp.where(lane == SOURCES + j, (index // BASE).astype(F32), extra)
            extra = jnp.where(lane == SOURCES + 8 + j, (index % BASE).astype(F32), extra)
        both.append((first, extra.astype(BF16)))
    for ref, chosen in ((mine_ref, batch), (other_ref, 1 - batch)):
        ref[pl.ds(0, coefs)] = states[chosen]
        ref[0] = jnp.where(chosen == 0, both[0][0].astype(F32), both[1][0].astype(F32)).astype(BF16)
        ref[coefs] = jnp.where(chosen == 0, both[0][1].astype(F32), both[1][1].astype(F32)).astype(BF16)


def open_kernel(
    slabs, neighbours, mine_ref, partner_ref, straight_ref, cross_ref, rate_ref,
    left_ref, own_ref, right_ref, hot_ref, hot_t_ref, geo_ref, seed_ref
):
    slab_now = lax.axis_index("space")
    batch = lax.rem(slab_now, 2)
    even = batch == 0
    coefs = own_ref.shape[0]
    rows, c = own_ref.shape[1:]
    per_slab = rows // 2
    window = 2 * rows
    edges = rows * neighbours

    def choose(a, b):
        return jnp.where(even, a, b)

    def parts(k):
        mine, partner = mine_ref[k].astype(F32), partner_ref[k].astype(F32)
        straight, cross = straight_ref[k].astype(F32), cross_ref[k].astype(F32)
        own = jnp.concatenate([choose(mine, partner), choose(partner, mine)], axis=0)
        return choose(cross, straight), own, choose(straight, cross)

    @pl.when(lax.axis_index("segment") == 0)
    def _():
        for k in range(coefs):
            left, own, right = parts(k)
            left_ref[k] = left.astype(BF16)
            own_ref[k] = own.astype(BF16)
            right_ref[k] = right.astype(BF16)

    extra = jnp.concatenate(parts(coefs), axis=0)
    numbers = decode(extra)
    seed_ref[...] = jnp.broadcast_to(numbers[per_slab : per_slab + rows, 3:4], (rows, c))
    own_extra = extra[per_slab : per_slab + rows]
    low = pltpu.roll(own_extra, c - 8, 1)
    index = own_extra.astype(jnp.int32) * BASE + low.astype(jnp.int32)
    first_slab = slab_now - batch
    place = lax.rem(index // per_slab - first_slab + (1 + slabs), slabs) * per_slab + index % per_slab
    columns = lax.broadcasted_iota(jnp.int32, (rows, c), 1)
    hot = jnp.concatenate(
        [
            (place[:, SOURCES + j : SOURCES + j + 1] == columns).astype(F32)
            for j in range(neighbours)
        ],
        axis=0,
    )
    hot_ref[...] = hot.astype(BF16)[:, :window]
    hot_t_ref[...] = jnp.transpose(hot).astype(BF16)[:window]
    hot = hot.astype(BF16)[:, :window]
    level = lax.broadcasted_iota(jnp.int32, (window, c), 0) // per_slab - 1
    offset = []
    for n in range(3):
        column = jnp.broadcast_to(numbers[:, n : n + 1], (window, c))
        if n == 2:
            column = column + SLAB_DEPTH * level.astype(F32)
        there = sum(dot(hot, part) for part in split3(column))
        offset.append(there - jnp.concatenate([column[per_slab : per_slab + rows]] * neighbours, axis=0))
    flat = offset[0] * offset[0] + offset[1] * offset[1] + 1.0
    length = jnp.sqrt(flat + offset[2] * offset[2])
    planar = jnp.sqrt(flat)
    c1, s1 = offset[0] / planar, offset[1] / planar
    rate = jnp.broadcast_to(rate_ref[...], (edges, c))
    values = [
        jnp.exp(-rate * length),
        c1,
        s1,
        c1 * c1 - s1 * s1,
        2.0 * c1 * s1,
        offset[0] / length,
        offset[1] / length,
        offset[2] / length,
        1.0 / planar,
        rate,
    ]
    for n, value in enumerate(values):
        geo_ref[n * edges : (n + 1) * edges, :] = value


def stage_kernel(zero_hbm, one_hbm, two_hbm, zero_ref, one_ref, two_ref, sems):
    copies = [
        pltpu.make_async_copy(source, target, sems.at[n])
        for n, (source, target) in enumerate(((zero_hbm, zero_ref), (one_hbm, one_ref), (two_hbm, two_ref)))
    ]
    for copy in copies:
        copy.start()
    for copy in copies:
        copy.wait()


def forward_kernel(
    tick, sz, left_ref, own_ref, right_ref, hot_ref, geo_ref, zero_ref, one_ref, two_ref,
    out_ref, low_ref, high_ref, pooled_ref
):
    @pl.when(lax.axis_index("segment") == tick)
    def _():
        rows = own_ref.shape[1]
        slab = rows // 2
        refs = (left_ref, own_ref, right_ref)
        pooled = forward(refs, hot_ref, geo_ref, zero_ref, one_ref, two_ref, sz, rows, False)
        signal = signal_of(pooled, sz)
        gate, lifted = silu_parts(signal)
        for k in range(sz.coefs):
            pooled_ref[k] = pooled[k]
            added = lifted if k == 0 else gate * pooled[k]
            updated = own_ref[k].astype(F32) + added
            out_ref[k] = updated.astype(BF16)
            low_ref[k] = updated[:slab].astype(BF16)
            high_ref[k] = updated[slab:].astype(BF16)


def turn_kernel(
    tick, sz, left_ref, own_ref, right_ref, hot_ref, hot_t_ref, geo_ref, zero_ref, one_ref, two_ref,
    read_ref, seed_ref, *outs
):
    @pl.when(lax.axis_index("segment") == tick)
    def _():
        rows = own_ref.shape[1]
        refs = (left_ref, own_ref, right_ref)
        pooled = forward(refs, hot_ref, geo_ref, zero_ref, one_ref, two_ref, sz, rows, True)
        signal = signal_of(pooled, sz)
        _, lifted = silu_parts(signal)
        updated = own_ref[0].astype(F32) + lifted
        gate, active = silu_parts(updated)
        read = read_ref[...]
        energy = jnp.sum(read * active, axis=1, keepdims=True)
        lane = lax.broadcasted_iota(jnp.int32, (rows, sz.c), 1)
        carried = jnp.where(lane == 3, energy, 0.0)
        upstream = [seed_ref[...] * read * (gate + updated * gate * (1.0 - gate))]
        moved = backward(
            upstream, carried, pooled, refs, hot_ref, hot_t_ref, geo_ref, zero_ref, one_ref, two_ref, sz, rows, True, outs
        )
        send_back(moved, outs, sz)


def backward_kernel(
    tick, sz, up_own_ref, up_low_ref, up_high_ref, pooled_ref, left_ref, own_ref, right_ref, hot_ref, hot_t_ref, geo_ref,
    zero_ref, one_ref, two_ref, *outs
):
    @pl.when(lax.axis_index("segment") == tick)
    def _():
        rows = own_ref.shape[1]
        refs = (left_ref, own_ref, right_ref)

        def arrived(k):
            halves = jnp.concatenate([up_low_ref[k].astype(F32), up_high_ref[k].astype(F32)], axis=0)
            return up_own_ref[k].astype(F32) + halves

        upstream = [arrived(k) for k in range(sz.coefs)]
        halves = jnp.concatenate(
            [decode(up_low_ref[sz.coefs].astype(F32)), decode(up_high_ref[sz.coefs].astype(F32))], axis=0
        )
        carried = decode(up_own_ref[sz.coefs].astype(F32)) + halves
        pooled = [pooled_ref[k] for k in range(sz.coefs)]
        moved = backward(
            upstream, carried, pooled, refs, hot_ref, hot_t_ref, geo_ref, zero_ref, one_ref, two_ref, sz, rows, False,
            outs if tick else None,
        )
        if tick:
            send_back(moved, outs, sz)
        else:
            share(moved, outs)


def share(moved, outs):
    left, own, right = moved
    slab = left.shape[0]
    even = lax.rem(lax.axis_index("space"), 2) == 0
    low, high = own[:slab], own[slab:]
    outs[0][...] = jnp.where(even, low, high)
    outs[1][...] = jnp.where(even, high, low)
    outs[2][...] = jnp.where(even, right, left)
    outs[3][...] = jnp.where(even, left, right)


def call(body, operands, shapes, name, spaces=None, scratch=()):
    spaces = spaces or [pltpu.VMEM] * len(operands)
    return pl.pallas_call(
        body,
        out_shape=shapes,
        in_specs=[pl.BlockSpec(memory_space=space) for space in spaces],
        out_specs=[pl.BlockSpec(memory_space=pltpu.VMEM) for _ in shapes],
        scratch_shapes=list(scratch),
        compiler_params=pltpu.CompilerParams(vmem_limit_bytes=VMEM_LIMIT),
        name=name,
    )(*operands)


def on_device(
    node_states,
    species,
    species_table,
    places,
    sources,
    radial_rate,
    zero_weight,
    one_weight,
    two_weight,
    read_weight,
    energy_grad,
):
    segments = lax.axis_size("segment")
    slabs = lax.axis_size("space")
    segment_now = lax.axis_index("segment")
    even = lax.rem(lax.axis_index("space"), 2) == 0
    batches, per_slab = species.shape
    coefs, channels = node_states.shape[2:]
    neighbours = sources.shape[2]
    rows = batches * per_slab
    edges = rows * neighbours
    sz = Sizes(zero_weight.shape, one_weight.shape, two_weight.shape, channels)
    axes = ("segment", "space")
    shape = jax.ShapeDtypeStruct

    def to_partner(i):
        return i + 1 - 2 * (i % 2)

    def outward(i):
        return (i + (2 if i % 2 else -2)) % slabs

    def inward(i):
        return (i + (-2 if i % 2 else 2)) % slabs

    def across(i):
        return (i + (1 if i % 2 else -1)) % slabs

    def within(value, target, only=None):
        chosen = range(segments) if only is None else [only]
        return lax.ppermute(value, axes, [(s * slabs + i, s * slabs + target(i)) for s in chosen for i in range(slabs)])

    def hop(value, start, stop, by):
        pairs = [(start * slabs + i, stop * slabs + (i + by) % slabs) for i in range(slabs)]
        return lax.ppermute(value, axes, pairs)

    raw = [
        node_states.transpose(0, 2, 1, 3), places.transpose(1, 0, 2), species, sources, energy_grad, species_table,
    ]
    packed = shape((coefs + 1, per_slab, channels), BF16)
    mine, other = call(
        pack_kernel, raw, [packed, packed], "pack", [pltpu.HBM] * len(raw),
        [pltpu.VMEM(v.shape, v.dtype) for v in raw] + [pltpu.SemaphoreType.DMA((len(raw),))],
    )
    partner = within(other, to_partner)
    straight = within(mine, outward)
    cross = within(other, across)
    weights = [zero_weight[0], one_weight[0], two_weight[0]]
    weights = call(
        stage_kernel, weights, [pltpu.VMEM(w.shape, w.dtype) for w in weights], "stage", [pltpu.HBM] * 3,
        [pltpu.SemaphoreType.DMA((3,))],
    )
    whole = shape((coefs, rows, channels), BF16)
    half = shape((coefs, per_slab, channels), BF16)
    left, own, right, hot, hot_t, geo, seeds = call(
        functools.partial(open_kernel, slabs, neighbours),
        [mine, partner, straight, cross, radial_rate],
        [
            half, whole, half, shape((edges, 2 * rows), BF16), shape((2 * rows, edges), BF16),
            shape((10 * edges, channels), F32), shape((rows, channels), F32),
        ],
        "open",
    )
    around = [(left, own, right)]
    kept = []
    for tick in range(segments - 1):
        out, low, high, pooled = call(
            functools.partial(forward_kernel, tick, sz),
            [*around[tick], hot, geo, *weights],
            [whole, half, half, shape((coefs, rows, channels), F32)],
            "forward",
        )
        kept.append(pooled)
        own = hop(out, tick, tick + 1, 0)
        right = hop(low, tick, tick + 1, -2)
        left = hop(high, tick, tick + 1, 2)
        around.append((left, own, right))
    final = segments - 1
    whole_more = shape((coefs + 1, rows, channels), BF16)
    last_shape = [shape((per_slab, channels), F32)] * 4
    parts = call(
        functools.partial(turn_kernel, final, sz),
        [*around[final], hot, hot_t, geo, *weights, read_weight.reshape(1, channels), seeds],
        [packed, whole_more, packed],
        "turn",
    )
    for tick in reversed(range(segments - 1)):
        left, own, right = parts
        up_own = hop(own, tick + 1, tick, 0)
        up_low = hop(right, tick + 1, tick, 2)
        up_high = hop(left, tick + 1, tick, -2)
        parts = call(
            functools.partial(backward_kernel, tick, sz),
            [up_own, up_low, up_high, kept[tick], *around[tick], hot, hot_t, geo, *weights],
            [packed, whole_more, packed] if tick else last_shape,
            "backward",
        )
    here, theirs, straight, cross = (value[:, :4] for value in parts)
    here = here + within(straight, inward, 0)
    there = within(theirs, to_partner, 0) + within(cross, across, 0)
    both = jnp.where(even, jnp.stack([here, there]), jnp.stack([there, here]))
    total = jnp.where(segment_now == 0, both, 0.0)
    for stop in range(1, segments):
        total = total + hop(both, 0, stop, 0)
    return total[..., 3], total[..., :3].transpose(0, 2, 1)


def solution(mesh):
    in_specs = (
        P(None, "space", None, None),
        P(None, "space"),
        P(),
        P(None, None, "space"),
        P(None, "space", None),
        P("segment", None),
        P("segment", None, None),
        P("segment", None, None, None),
        P("segment", None, None, None),
        P(),
        P(None, "space"),
    )
    out_specs = (P(None, "space"), P(None, None, "space"))
    return jax.shard_map(
        on_device, mesh=mesh, in_specs=in_specs, out_specs=out_specs, check_vma=False
    )
```

time: 166 us -> 111 us (0.67)
  waiting for transfers between devices: 101 us -> 52.8 us
  starting transfers between devices: 23.8 us -> 35.8 us
  local copies, waits for them, and re-layouts: 21.6 us -> 13.1 us
  blocking collectives: 7.44 us -> 0 us
  other arithmetic: 3.17 us -> 0.02 us
    ppermute x24 -> x27, waiting for transfers between devices: 101 us -> 52.8 us  [the longest x21 50.7 us: hop(): return lax.ppermute(value, axes, pairs)]
    ppermute x24 -> x27, starting transfers between devices: 23.8 us -> 35.8 us  [the longest x21 20.9 us: hop(): return lax.ppermute(value, axes, pairs)]
    psum x1 -> x0, blocking collectives: 7.44 us -> none  [on_device(): whole = lax.psum(jnp.concatenate([shares, energies], axis=1), 'segment')]
    unnamed x68 -> x31, local copies, waits for them, and re-layouts: 18 us -> 12.3 us
    pallas_call x8 -> x10, Pallas kernels: 6.25 us -> 7.46 us  [call(): pl.pallas_call(body, out_shape=shapes, in_specs=[pl.BlockSpec(memory_spac...]
  transfers between devices with their start and end apart: 24 -> 27, of which waited for: 4 -> 5; matrix products, arithmetic and copies ran while one was open for 3% -> 0% of each run, Pallas kernels for 0% -> 0%
where the time goes in v1:
time: 111 us; the launch traced here: 110 us
  waiting for transfers between devices  52.8 us (48%)
  starting transfers between devices  35.8 us (32%)
  local copies, waits for them, and re-layouts  13.1 us (12%)
  Pallas kernels  7.46 us (7%)
  between operations  1.12 us (1%)
    ppermute x21, waiting for transfers between devices, hop(): return lax.ppermute(value, axes, pairs)  50.7 us
    ppermute x21, starting transfers between devices, hop(): return lax.ppermute(value, axes, pairs)  20.9 us
    ppermute x6, starting transfers between devices, within(): lax.ppermute(value, axes, [(s * slabs + i, s * slabs + target(i)) for s i...  14.9 us
    unnamed x31, local copies, waits for them, and re-layouts  12.3 us
    pallas_call x10, Pallas kernels, call(): pl.pallas_call(body, out_shape=shapes, in_specs=[pl.BlockSpec(memory_spac...  7.46 us
  transfers between devices with their start and end apart: 27, of which 5 were waited for; matrix products, arithmetic and copies ran while one was open for 0% of the time, Pallas kernels for 0%

profile of v1, /device:TPU:0, one launch (start us, length us, event | category | flops | bytes accessed | tf_op | source)
XLA Modules:
  0.0 110.2 jit_solution(15104453030946989424)
XLA Ops:
  0.6 0.9 copy-done.7
  1.5 0.7 copy-done.8
  2.3 0.7 copy-done.9
  3.0 0.7 copy-done.10
  3.7 0.7 copy-done.11
  4.3 0.7 copy-done.12
  5.5 0.5 collective-permute-start
  6.0 4.7 %collective-permute-start.1 = (bf16[30,8,128]{2,1,0:T(8,128)(2,1)S(1)}, bf16[30,8,128]{2,1,0:T(8,128)(2,1)S(1)}, u32[]{:S(2)}, u32[]{:S(2)}) collective-permute-start(bf16[30,8,128]{2,1,0:T(8,128)(2,1)S(1)} %get-tuple-element.39.mine_ref), channel_id=1, source_target_pairs={{0,6},{1,3},{2,0},{3,5},{4,2},{5,7},{6,4},{7,1},{8,14},{9,11},{10,... | collective-permute-start | bytes 184328 | tf_op jit(solution)/shard_map/ppermute | solution.py:546
  10.7 1.7 %copy-done.4 = bf16[1,2,768,768]{3,2,1,0:T(8,128)(2,1)S(1)} copy-done((bf16[1,2,768,768]{3,2,1,0:T(8,128)(2,1)S(1)}, bf16[1,2,768,768]{3,2,1,0:T(8,128)(2,1)}, u32[]{:S(2)}) %copy-start.4) | copy-done | bytes 2359320
  12.4 1.4 %copy-done.5 = bf16[1,2,640,640]{3,2,1,0:T(8,128)(2,1)S(1)} copy-done((bf16[1,2,640,640]{3,2,1,0:T(8,128)(2,1)S(1)}, bf16[1,2,640,640]{3,2,1,0:T(8,128)(2,1)}, u32[]{:S(2)}) %copy-start.5) | copy-done | bytes 1638424
  13.8 1.4 %copy-done.6 = bf16[1,896,896]{2,1,0:T(8,128)(2,1)S(1)} copy-done((bf16[1,896,896]{2,1,0:T(8,128)(2,1)S(1)}, bf16[1,896,896]{2,1,0:T(8,128)(2,1)}, u32[]{:S(2)}) %copy-start.6) | copy-done | bytes 1605656
  15.2 0.5 stage.1
  16.1 0.5 open.1
  16.6 1.7 %forward.3 = (bf16[29,16,128]{2,1,0:T(8,128)(2,1)S(1)}, bf16[29,8,128]{2,1,0:T(8,128)(2,1)S(1)}, bf16[29,8,128]{2,1,0:T(8,128)(2,1)S(1)}, f32[29,16,128]{2,1,0:T(8,128)S(1)}) custom-call(bf16[29,8,128]{2,1,0:T(8,128)(2,1)S(1)} %get-tuple-element.41.left_ref, bf16[29,16,128]{2,1,0:T(8,128)(2,1)S(1)} %get-tuple-element.42.own_ref, ...), custom_call_target="tpu_custom_call" | custom-call | tf_op jit(solution)/shard_map/forward/pallas_call | solution.py:495
  18.3 1.7 %collective-permute-start.4 = (bf16[29,16,128]{2,1,0:T(8,128)(2,1)S(1)}, bf16[29,16,128]{2,1,0:T(8,128)(2,1)S(1)}, u32[]{:S(2)}, u32[]{:S(2)}) collective-permute-start(bf16[29,16,128]{2,1,0:T(8,128)(2,1)S(1)} %get-tuple-element.50), channel_id=1, source_target_pairs={{0,8},{1,9},{2,10},{3,11},{4,12},{5,13},{6,14},{7,15}} | collective-permute-start | bytes 356360 | tf_op jit(solution)/shard_map/ppermute | solution.py:550
  20.0 1.3 %collective-permute-start.3 = (bf16[29,8,128]{2,1,0:T(8,128)(2,1)S(1)}, bf16[29,8,128]{2,1,0:T(8,128)(2,1)S(1)}, u32[]{:S(2)}, u32[]{:S(2)}) collective-permute-start(bf16[29,8,128]{2,1,0:T(8,128)(2,1)S(1)} %get-tuple-element.49), channel_id=1, source_target_pairs={{0,10},{1,11},{2,12},{3,13},{4,14},{5,15},{6,8},{7,9}} | collective-permute-start | bytes 178184 | tf_op jit(solution)/shard_map/ppermute | solution.py:550
  21.3 2.2 %collective-permute-start.5 = (bf16[29,8,128]{2,1,0:T(8,128)(2,1)S(1)}, bf16[29,8,128]{2,1,0:T(8,128)(2,1)S(1)}, u32[]{:S(2)}, u32[]{:S(2)}) collective-permute-start(bf16[29,8,128]{2,1,0:T(8,128)(2,1)S(1)} %get-tuple-element.51), channel_id=1, source_target_pairs={{0,14},{1,15},{2,8},{3,9},{4,10},{5,11},{6,12},{7,13}} | collective-permute-start | bytes 178184 | tf_op jit(solution)/shard_map/ppermute | solution.py:550
  23.6 1.8 %collective-permute-done.5.right_ref = bf16[29,8,128]{2,1,0:T(8,128)(2,1)S(1)} collective-permute-done((bf16[29,8,128]{2,1,0:T(8,128)(2,1)S(1)}, bf16[29,8,128]{2,1,0:T(8,128)(2,1)S(1)}, u32[]{:S(2)}, u32[]{:S(2)}) %collective-permute-start.5) | collective-permute-done | bytes 59424 | tf_op jit(solution)/shard_map/ppermute | solution.py:550
  25.4 0.7 collective-permute-start.7
  26.1 0.7 collective-permute-start.6
  26.8 0.7 collective-permute-start.8
  27.5 0.7 collective-permute-start.10
  28.2 0.7 collective-permute-start.11
  28.8 0.7 collective-permute-start.9
  29.6 0.7 collective-permute-start.12
  30.3 0.7 collective-permute-start.13
  30.9 0.7 collective-permute-start.14
  31.7 0.7 collective-permute-start.15
  32.3 0.7 collective-permute-start.16
  33.0 0.7 collective-permute-start.17
  33.7 0.9 backward.4
  34.6 1.3 %collective-permute-start.18 = (bf16[30,16,128]{2,1,0:T(8,128)(2,1)}, bf16[30,16,128]{2,1,0:T(8,128)(2,1)}, u32[]{:S(2)}, u32[]{:S(2)}) collective-permute-start(bf16[30,16,128]{2,1,0:T(8,128)(2,1)} %get-tuple-element.68), channel_id=1, source_target_pairs={{8,0},{9,1},{10,2},{11,3},{12,4},{13,5},{14,6},{15,7}} | collective-permute-start | bytes 368648 | tf_op jit(solution)/shard_map/ppermute | solution.py:550
  35.9 1.3 %collective-permute-start.19 = (bf16[30,8,128]{2,1,0:T(8,128)(2,1)}, bf16[30,8,128]{2,1,0:T(8,128)(2,1)}, u32[]{:S(2)}, u32[]{:S(2)}) collective-permute-start(bf16[30,8,128]{2,1,0:T(8,128)(2,1)} %get-tuple-element.69), channel_id=1, source_target_pairs={{8,2},{9,3},{10,4},{11,5},{12,6},{13,7},{14,0},{15,1}} | collective-permute-start | bytes 184328 | tf_op jit(solution)/shard_map/ppermute | solution.py:550
  37.2 1.3 %collective-permute-start.20 = (bf16[30,8,128]{2,1,0:T(8,128)(2,1)}, bf16[30,8,128]{2,1,0:T(8,128)(2,1)}, u32[]{:S(2)}, u32[]{:S(2)}) collective-permute-start(bf16[30,8,128]{2,1,0:T(8,128)(2,1)} %get-tuple-element.70), channel_id=1, source_target_pairs={{8,6},{9,7},{10,0},{11,1},{12,2},{13,3},{14,4},{15,5}} | collective-permute-start | bytes 184328 | tf_op jit(solution)/shard_map/ppermute | solution.py:550
  38.5 47.5 %collective-permute-done.19.up_low_ref = bf16[30,8,128]{2,1,0:T(8,128)(2,1)} collective-permute-done((bf16[30,8,128]{2,1,0:T(8,128)(2,1)}, bf16[30,8,128]{2,1,0:T(8,128)(2,1)}, u32[]{:S(2)}, u32[]{:S(2)}) %collective-permute-start.19) | collective-permute-done | bytes 61472 | tf_op jit(solution)/shard_map/ppermute | solution.py:550
  86.1 1.4 %copy-done.1 = bf16[2,640,640]{2,1,0:T(8,128)(2,1)S(1)} copy-done((bf16[2,640,640]{2,1,0:T(8,128)(2,1)S(1)}, bf16[2,640,640]{2,1,0:T(8,128)(2,1)}, u32[]{:S(2)}) %copy-start.1) | copy-done | bytes 1638424
  87.5 1.4 %copy-done.3 = bf16[896,896]{1,0:T(8,128)(2,1)S(1)} copy-done((bf16[896,896]{1,0:T(8,128)(2,1)S(1)}, bf16[896,896]{1,0:T(8,128)(2,1)}, u32[]{:S(2)}) %copy-start.3) | copy-done | bytes 1605656
  88.9 3.3 %backward.5 = (f32[8,128]{1,0:T(8,128)S(1)}, f32[8,128]{1,0:T(8,128)S(1)}, f32[8,128]{1,0:T(8,128)S(1)}, f32[8,128]{1,0:T(8,128)S(1)}) custom-call(bf16[30,16,128]{2,1,0:T(8,128)(2,1)} %collective-permute-done.18.up_own_ref, bf16[30,8,128]{2,1,0:T(8,128)(2,1)} %collective-permute-done.19.up_low_ref, bf16[30,8,128]{2,1,0:T(8,128)(2,1)} %collective-permute-done.20.up_high_ref, ...), custom_call_target="tpu_custom_call" | custom-call | tf_op jit(solution)/shard_map/backward/pallas_call | solution.py:495
  92.2 2.9 %collective-permute-start.21 = (f32[8,4]{1,0:T(8,128)S(1)}, f32[8,4]{1,0:T(8,128)S(1)}, u32[]{:S(2)}, u32[]{:S(2)}) collective-permute-start(f32[8,4]{1,0:T(8,128)S(1)} %bitcast.22), channel_id=1, source_target_pairs={{0,2},{1,7},{2,4},{3,1},{4,6},{5,3},{6,0},{7,5}} | collective-permute-start | bytes 392 | tf_op jit(solution)/shard_map/ppermute | solution.py:546
  95.1 1.9 %collective-permute-start.22 = (f32[8,4]{1,0:T(8,128)S(1)}, f32[8,4]{1,0:T(8,128)S(1)}, u32[]{:S(2)}, u32[]{:S(2)}) collective-permute-start(f32[8,4]{1,0:T(8,128)S(1)} %bitcast.21), channel_id=1, source_target_pairs={{0,1},{1,0},{2,3},{3,2},{4,5},{5,4},{6,7},{7,6}} | collective-permute-start | bytes 392 | tf_op jit(solution)/shard_map/ppermute | solution.py:546
  97.1 4.8 %collective-permute-start.23 = (f32[8,4]{1,0:T(8,128)S(1)}, f32[8,4]{1,0:T(8,128)S(1)}, u32[]{:S(2)}, u32[]{:S(2)}) collective-permute-start(f32[8,4]{1,0:T(8,128)S(1)} %bitcast.20), channel_id=1, source_target_pairs={{0,7},{1,2},{2,1},{3,4},{4,3},{5,6},{6,5},{7,0}} | collective-permute-start | bytes 392 | tf_op jit(solution)/shard_map/ppermute | solution.py:546
  102.0 1.8 %collective-permute-done.23 = f32[8,4]{1,0:T(8,128)S(1)} collective-permute-done((f32[8,4]{1,0:T(8,128)S(1)}, f32[8,4]{1,0:T(8,128)S(1)}, u32[]{:S(2)}, u32[]{:S(2)}) %collective-permute-start.23) | collective-permute-done | bytes 160 | tf_op jit(solution)/shard_map/ppermute | solution.py:546
  103.9 1.3 %collective-permute-start.24 = (f32[2,8,4]{1,2,0:T(4,128)S(1)}, f32[2,8,4]{1,2,0:T(4,128)S(1)}, u32[]{:S(2)}, u32[]{:S(2)}) collective-permute-start(f32[2,8,4]{1,2,0:T(4,128)S(1)} %maximum_select_fusion), channel_id=1, source_target_pairs={{0,8},{1,9},{2,10},{3,11},{4,12},{5,13},{6,14},{7,15}} | collective-permute-start | bytes 776 | tf_op jit(solution)/shard_map/ppermute | solution.py:550
  105.2 1.3 %collective-permute-start.25 = (f32[2,8,4]{1,2,0:T(4,128)S(1)}, f32[2,8,4]{1,2,0:T(4,128)S(1)}, u32[]{:S(2)}, u32[]{:S(2)}) collective-permute-start(f32[2,8,4]{1,2,0:T(4,128)S(1)} %maximum_select_fusion), channel_id=1, source_target_pairs={{0,16},{1,17},{2,18},{3,19},{4,20},{5,21},{6,22},{7,23}} | collective-permute-start | bytes 776 | tf_op jit(solution)/shard_map/ppermute | solution.py:550
  106.5 1.3 %collective-permute-start.26 = (f32[2,8,4]{1,2,0:T(4,128)S(1)}, f32[2,8,4]{1,2,0:T(4,128)S(1)}, u32[]{:S(2)}, u32[]{:S(2)}) collective-permute-start(f32[2,8,4]{1,2,0:T(4,128)S(1)} %maximum_select_fusion), channel_id=1, source_target_pairs={{0,24},{1,25},{2,26},{3,27},{4,28},{5,29},{6,30},{7,31}} | collective-permute-start | bytes 776 | tf_op jit(solution)/shard_map/ppermute | solution.py:550
  107.8 1.3 %collective-permute-done.26 = f32[2,8,4]{1,2,0:T(4,128)S(1)} collective-permute-done((f32[2,8,4]{1,2,0:T(4,128)S(1)}, f32[2,8,4]{1,2,0:T(4,128)S(1)}, u32[]{:S(2)}, u32[]{:S(2)}) %collective-permute-start.26) | collective-permute-done | bytes 288 | tf_op jit(solution)/shard_map/ppermute | solution.py:550
  109.1 0.6 slice.24
  109.7 0.6 copy.15
  (55 shorter events, 1.2 us)
Async XLA Ops:
  0.6 0.9 copy-start.7
  1.5 0.7 copy-start.8
  2.3 0.7 copy-start.9
  3.0 0.7 copy-start.10
  3.7 0.7 copy-start.11
  4.3 0.7 copy-start.12
  5.5 10.3 %collective-permute-start = (bf16[30,8,128]{2,1,0:T(8,128)(2,1)S(1)}, bf16[30,8,128]{2,1,0:T(8,128)(2,1)S(1)}, u32[]{:S(2)}, u32[]{:S(2)}) collective-permute-start(bf16[30,8,128]{2,1,0:T(8,128)(2,1)S(1)} %get-tuple-element.40), channel_id=1, source_target_pairs={{0,1},{1,0},{2,3},{3,2},{4,5},{5,4},{6,7},{7,6},{8,9},{9,8},{10,11... | collective-permute-start | bytes 184328 | tf_op jit(solution)/shard_map/ppermute | solution.py:546
  6.0 9.8 %collective-permute-start.1 = (bf16[30,8,128]{2,1,0:T(8,128)(2,1)S(1)}, bf16[30,8,128]{2,1,0:T(8,128)(2,1)S(1)}, u32[]{:S(2)}, u32[]{:S(2)}) collective-permute-start(bf16[30,8,128]{2,1,0:T(8,128)(2,1)S(1)} %get-tuple-element.39.mine_ref), channel_id=1, source_target_pairs={{0,6},{1,3},{2,0},{3,5},{4,2},{5,7},{6,4},{7,1},{8,14},{9,11},{10,... | collective-permute-start | bytes 184328 | tf_op jit(solution)/shard_map/ppermute | solution.py:546
  10.7 5.4 %collective-permute-start.2 = (bf16[30,8,128]{2,1,0:T(8,128)(2,1)S(1)}, bf16[30,8,128]{2,1,0:T(8,128)(2,1)S(1)}, u32[]{:S(2)}, u32[]{:S(2)}) collective-permute-start(bf16[30,8,128]{2,1,0:T(8,128)(2,1)S(1)} %get-tuple-element.40), channel_id=1, source_target_pairs={{0,7},{1,2},{2,1},{3,4},{4,3},{5,6},{6,5},{7,0},{8,15},{9,10},{10,... | collective-permute-start | bytes 184328 | tf_op jit(solution)/shard_map/ppermute | solution.py:546
  10.7 1.7 %copy-start.4 = (bf16[1,2,768,768]{3,2,1,0:T(8,128)(2,1)S(1)}, bf16[1,2,768,768]{3,2,1,0:T(8,128)(2,1)}, u32[]{:S(2)}) copy-start(bf16[1,2,768,768]{3,2,1,0:T(8,128)(2,1)} %param.18) | copy-start | bytes 7077892
  12.4 1.4 %copy-start.5 = (bf16[1,2,640,640]{3,2,1,0:T(8,128)(2,1)S(1)}, bf16[1,2,640,640]{3,2,1,0:T(8,128)(2,1)}, u32[]{:S(2)}) copy-start(bf16[1,2,640,640]{3,2,1,0:T(8,128)(2,1)} %param.19) | copy-start | bytes 4915204
  13.8 1.4 %copy-start.6 = (bf16[1,896,896]{2,1,0:T(8,128)(2,1)S(1)}, bf16[1,896,896]{2,1,0:T(8,128)(2,1)}, u32[]{:S(2)}) copy-start(bf16[1,896,896]{2,1,0:T(8,128)(2,1)} %param.17) | copy-start | bytes 4816900
  15.2 0.9 copy-start.13
  15.8 17.9 %copy-start = (bf16[2,640,640]{2,1,0:T(8,128)(2,1)}, bf16[2,640,640]{2,1,0:T(8,128)(2,1)S(1)}, u32[]{:S(2)}) copy-start(bf16[2,640,640]{2,1,0:T(8,128)(2,1)S(1)} %get-tuple-element.48.two_ref) | copy-start | bytes 4915204
  15.8 17.9 %copy-start.2 = (bf16[896,896]{1,0:T(8,128)(2,1)}, bf16[896,896]{1,0:T(8,128)(2,1)S(1)}, u32[]{:S(2)}) copy-start(bf16[896,896]{1,0:T(8,128)(2,1)S(1)} %get-tuple-element.46.zero_ref) | copy-start | bytes 4816900
  18.3 7.1 %collective-permute-start.4 = (bf16[29,16,128]{2,1,0:T(8,128)(2,1)S(1)}, bf16[29,16,128]{2,1,0:T(8,128)(2,1)S(1)}, u32[]{:S(2)}, u32[]{:S(2)}) collective-permute-start(bf16[29,16,128]{2,1,0:T(8,128)(2,1)S(1)} %get-tuple-element.50), channel_id=1, source_target_pairs={{0,8},{1,9},{2,10},{3,11},{4,12},{5,13},{6,14},{7,15}} | collective-permute-start | bytes 356360 | tf_op jit(solution)/shard_map/ppermute | solution.py:550
  20.0 3.6 %collective-permute-start.3 = (bf16[29,8,128]{2,1,0:T(8,128)(2,1)S(1)}, bf16[29,8,128]{2,1,0:T(8,128)(2,1)S(1)}, u32[]{:S(2)}, u32[]{:S(2)}) collective-permute-start(bf16[29,8,128]{2,1,0:T(8,128)(2,1)S(1)} %get-tuple-element.49), channel_id=1, source_target_pairs={{0,10},{1,11},{2,12},{3,13},{4,14},{5,15},{6,8},{7,9}} | collective-permute-start | bytes 178184 | tf_op jit(solution)/shard_map/ppermute | solution.py:550
  21.3 4.1 %collective-permute-start.5 = (bf16[29,8,128]{2,1,0:T(8,128)(2,1)S(1)}, bf16[29,8,128]{2,1,0:T(8,128)(2,1)S(1)}, u32[]{:S(2)}, u32[]{:S(2)}) collective-permute-start(bf16[29,8,128]{2,1,0:T(8,128)(2,1)S(1)} %get-tuple-element.51), channel_id=1, source_target_pairs={{0,14},{1,15},{2,8},{3,9},{4,10},{5,11},{6,12},{7,13}} | collective-permute-start | bytes 178184 | tf_op jit(solution)/shard_map/ppermute | solution.py:550
  25.4 2.0 %collective-permute-start.7 = (bf16[29,16,128]{2,1,0:T(8,128)(2,1)S(1)}, bf16[29,16,128]{2,1,0:T(8,128)(2,1)S(1)}, u32[]{:S(2)}, u32[]{:S(2)}) collective-permute-start(bf16[29,16,128]{2,1,0:T(8,128)(2,1)S(1)} %get-tuple-element.53), channel_id=1, source_target_pairs={{8,16},{9,17},{10,18},{11,19},{12,20},{13,21},{14,22},{15,23}} | collective-permute-start | bytes 356360 | tf_op jit(solution)/shard_map/ppermute | solution.py:550
  26.1 1.4 %collective-permute-start.6 = (bf16[29,8,128]{2,1,0:T(8,128)(2,1)S(1)}, bf16[29,8,128]{2,1,0:T(8,128)(2,1)S(1)}, u32[]{:S(2)}, u32[]{:S(2)}) collective-permute-start(bf16[29,8,128]{2,1,0:T(8,128)(2,1)S(1)} %get-tuple-element.52), channel_id=1, source_target_pairs={{8,18},{9,19},{10,20},{11,21},{12,22},{13,23},{14,16},{15,17}} | collective-permute-start | bytes 178184 | tf_op jit(solution)/shard_map/ppermute | solution.py:550
  26.7 2.8 %copy-start.14 = (f32[128]{0:T(128)S(1)}, f32[128]{0:T(128)}, u32[]{:S(2)}) copy-start(f32[128]{0:T(128)} %param.20) | copy-start | bytes 1540
  26.8 0.7 collective-permute-start.8
  27.5 2.0 %collective-permute-start.10 = (bf16[29,16,128]{2,1,0:T(8,128)(2,1)S(1)}, bf16[29,16,128]{2,1,0:T(8,128)(2,1)S(1)}, u32[]{:S(2)}, u32[]{:S(2)}) collective-permute-start(bf16[29,16,128]{2,1,0:T(8,128)(2,1)S(1)} %get-tuple-element.56), channel_id=1, source_target_pairs={{16,24},{17,25},{18,26},{19,27},{20,28},{21,29},{22,30},{23,31}} | collective-permute-start | bytes 356360 | tf_op jit(solution)/shard_map/ppermute | solution.py:550
  28.2 1.3 %collective-permute-start.11 = (bf16[29,8,128]{2,1,0:T(8,128)(2,1)S(1)}, bf16[29,8,128]{2,1,0:T(8,128)(2,1)S(1)}, u32[]{:S(2)}, u32[]{:S(2)}) collective-permute-start(bf16[29,8,128]{2,1,0:T(8,128)(2,1)S(1)} %get-tuple-element.57), channel_id=1, source_target_pairs={{16,30},{17,31},{18,24},{19,25},{20,26},{21,27},{22,28},{23,29}} | collective-permute-start | bytes 178184 | tf_op jit(solution)/shard_map/ppermute | solution.py:550
  28.8 0.7 collective-permute-start.9
  29.6 2.0 %collective-permute-start.12 = (bf16[30,16,128]{2,1,0:T(8,128)(2,1)S(1)}, bf16[30,16,128]{2,1,0:T(8,128)(2,1)S(1)}, u32[]{:S(2)}, u32[]{:S(2)}) collective-permute-start(bf16[30,16,128]{2,1,0:T(8,128)(2,1)S(1)} %get-tuple-element.60), channel_id=1, source_target_pairs={{24,16},{25,17},{26,18},{27,19},{28,20},{29,21},{30,22},{31,23}} | collective-permute-start | bytes 368648 | tf_op jit(solution)/shard_map/ppermute | solution.py:550
  30.3 1.3 %collective-permute-start.13 = (bf16[30,8,128]{2,1,0:T(8,128)(2,1)S(1)}, bf16[30,8,128]{2,1,0:T(8,128)(2,1)S(1)}, u32[]{:S(2)}, u32[]{:S(2)}) collective-permute-start(bf16[30,8,128]{2,1,0:T(8,128)(2,1)S(1)} %get-tuple-element.61), channel_id=1, source_target_pairs={{24,18},{25,19},{26,20},{27,21},{28,22},{29,23},{30,16},{31,17}} | collective-permute-start | bytes 184328 | tf_op jit(solution)/shard_map/ppermute | solution.py:550
  30.9 0.7 collective-permute-start.14
  31.7 2.0 %collective-permute-start.15 = (bf16[30,16,128]{2,1,0:T(8,128)(2,1)S(1)}, bf16[30,16,128]{2,1,0:T(8,128)(2,1)S(1)}, u32[]{:S(2)}, u32[]{:S(2)}) collective-permute-start(bf16[30,16,128]{2,1,0:T(8,128)(2,1)S(1)} %get-tuple-element.64), channel_id=1, source_target_pairs={{16,8},{17,9},{18,10},{19,11},{20,12},{21,13},{22,14},{23,15}} | collective-permute-start | bytes 368648 | tf_op jit(solution)/shard_map/ppermute | solution.py:550
  32.3 1.3 %collective-permute-start.16 = (bf16[30,8,128]{2,1,0:T(8,128)(2,1)S(1)}, bf16[30,8,128]{2,1,0:T(8,128)(2,1)S(1)}, u32[]{:S(2)}, u32[]{:S(2)}) collective-permute-start(bf16[30,8,128]{2,1,0:T(8,128)(2,1)S(1)} %get-tuple-element.65), channel_id=1, source_target_pairs={{16,10},{17,11},{18,12},{19,13},{20,14},{21,15},{22,8},{23,9}} | collective-permute-start | bytes 184328 | tf_op jit(solution)/shard_map/ppermute | solution.py:550
  33.0 0.7 collective-permute-start.17
  34.6 51.4 %collective-permute-start.18 = (bf16[30,16,128]{2,1,0:T(8,128)(2,1)}, bf16[30,16,128]{2,1,0:T(8,128)(2,1)}, u32[]{:S(2)}, u32[]{:S(2)}) collective-permute-start(bf16[30,16,128]{2,1,0:T(8,128)(2,1)} %get-tuple-element.68), channel_id=1, source_target_pairs={{8,0},{9,1},{10,2},{11,3},{12,4},{13,5},{14,6},{15,7}} | collective-permute-start | bytes 368648 | tf_op jit(solution)/shard_map/ppermute | solution.py:550
  35.9 50.1 %collective-permute-start.19 = (bf16[30,8,128]{2,1,0:T(8,128)(2,1)}, bf16[30,8,128]{2,1,0:T(8,128)(2,1)}, u32[]{:S(2)}, u32[]{:S(2)}) collective-permute-start(bf16[30,8,128]{2,1,0:T(8,128)(2,1)} %get-tuple-element.69), channel_id=1, source_target_pairs={{8,2},{9,3},{10,4},{11,5},{12,6},{13,7},{14,0},{15,1}} | collective-permute-start | bytes 184328 | tf_op jit(solution)/shard_map/ppermute | solution.py:550
  37.2 48.8 %collective-permute-start.20 = (bf16[30,8,128]{2,1,0:T(8,128)(2,1)}, bf16[30,8,128]{2,1,0:T(8,128)(2,1)}, u32[]{:S(2)}, u32[]{:S(2)}) collective-permute-start(bf16[30,8,128]{2,1,0:T(8,128)(2,1)} %get-tuple-element.70), channel_id=1, source_target_pairs={{8,6},{9,7},{10,0},{11,1},{12,2},{13,3},{14,4},{15,5}} | collective-permute-start | bytes 184328 | tf_op jit(solution)/shard_map/ppermute | solution.py:550
  86.0 1.4 %copy-start.1 = (bf16[2,640,640]{2,1,0:T(8,128)(2,1)S(1)}, bf16[2,640,640]{2,1,0:T(8,128)(2,1)}, u32[]{:S(2)}) copy-start(bf16[2,640,640]{2,1,0:T(8,128)(2,1)} %copy-done) | copy-start | bytes 4915204
  87.5 1.4 %copy-start.3 = (bf16[896,896]{1,0:T(8,128)(2,1)S(1)}, bf16[896,896]{1,0:T(8,128)(2,1)}, u32[]{:S(2)}) copy-start(bf16[896,896]{1,0:T(8,128)(2,1)} %copy-done.2) | copy-start | bytes 4816900
  92.2 9.7 %collective-permute-start.21 = (f32[8,4]{1,0:T(8,128)S(1)}, f32[8,4]{1,0:T(8,128)S(1)}, u32[]{:S(2)}, u32[]{:S(2)}) collective-permute-start(f32[8,4]{1,0:T(8,128)S(1)} %bitcast.22), channel_id=1, source_target_pairs={{0,2},{1,7},{2,4},{3,1},{4,6},{5,3},{6,0},{7,5}} | collective-permute-start | bytes 392 | tf_op jit(solution)/shard_map/ppermute | solution.py:546
  95.1 6.9 %collective-permute-start.22 = (f32[8,4]{1,0:T(8,128)S(1)}, f32[8,4]{1,0:T(8,128)S(1)}, u32[]{:S(2)}, u32[]{:S(2)}) collective-permute-start(f32[8,4]{1,0:T(8,128)S(1)} %bitcast.21), channel_id=1, source_target_pairs={{0,1},{1,0},{2,3},{3,2},{4,5},{5,4},{6,7},{7,6}} | collective-permute-start | bytes 392 | tf_op jit(solution)/shard_map/ppermute | solution.py:546
  97.1 6.7 %collective-permute-start.23 = (f32[8,4]{1,0:T(8,128)S(1)}, f32[8,4]{1,0:T(8,128)S(1)}, u32[]{:S(2)}, u32[]{:S(2)}) collective-permute-start(f32[8,4]{1,0:T(8,128)S(1)} %bitcast.20), channel_id=1, source_target_pairs={{0,7},{1,2},{2,1},{3,4},{4,3},{5,6},{6,5},{7,0}} | collective-permute-start | bytes 392 | tf_op jit(solution)/shard_map/ppermute | solution.py:546
  103.9 3.9 %collective-permute-start.24 = (f32[2,8,4]{1,2,0:T(4,128)S(1)}, f32[2,8,4]{1,2,0:T(4,128)S(1)}, u32[]{:S(2)}, u32[]{:S(2)}) collective-permute-start(f32[2,8,4]{1,2,0:T(4,128)S(1)} %maximum_select_fusion), channel_id=1, source_target_pairs={{0,8},{1,9},{2,10},{3,11},{4,12},{5,13},{6,14},{7,15}} | collective-permute-start | bytes 776 | tf_op jit(solution)/shard_map/ppermute | solution.py:550
  105.2 2.6 %collective-permute-start.25 = (f32[2,8,4]{1,2,0:T(4,128)S(1)}, f32[2,8,4]{1,2,0:T(4,128)S(1)}, u32[]{:S(2)}, u32[]{:S(2)}) collective-permute-start(f32[2,8,4]{1,2,0:T(4,128)S(1)} %maximum_select_fusion), channel_id=1, source_target_pairs={{0,16},{1,17},{2,18},{3,19},{4,20},{5,21},{6,22},{7,23}} | collective-permute-start | bytes 776 | tf_op jit(solution)/shard_map/ppermute | solution.py:550
  106.5 2.6 %collective-permute-start.26 = (f32[2,8,4]{1,2,0:T(4,128)S(1)}, f32[2,8,4]{1,2,0:T(4,128)S(1)}, u32[]{:S(2)}, u32[]{:S(2)}) collective-permute-start(f32[2,8,4]{1,2,0:T(4,128)S(1)} %maximum_select_fusion), channel_id=1, source_target_pairs={{0,24},{1,25},{2,26},{3,27},{4,28},{5,29},{6,30},{7,31}} | collective-permute-start | bytes 776 | tf_op jit(solution)/shard_map/ppermute | solution.py:550

commit v2 on v1

--- a/solution.py
+++ b/solution.py
@@ -79,10 +79,14 @@
 
 
 def picked_group(refs, hot, first, count):
-    blocks = []
-    for k in range(first, first + count):
-        blocks.append(jnp.concatenate([ref[k].astype(F32) for ref in refs], axis=0).astype(BF16))
+    blocks = [jnp.concatenate([ref[k] for ref in refs], axis=0) for k in range(first, first + count)]
     return dot(hot, jnp.concatenate(blocks, axis=1))
+
+
+def own_rows(refs, k):
+    low, high = (ref[k].astype(F32) for ref in refs)
+    slab = low.shape[0] // 2
+    return jnp.concatenate([low[slab:], high[:slab]], axis=0)
 
 
 def pool(value, rows):
@@ -146,7 +150,7 @@
 
 
 def backward(
-    upstream, carried, pooled, refs, hot_ref, hot_t_ref, geo_ref, zero_ref, one_ref, two_ref, sz, rows, last, outs
+    upstream, pooled, refs, hot_ref, hot_t_ref, geo_ref, zero_ref, one_ref, two_ref, sz, rows, last, outs
 ):
     hot = hot_ref[...]
     hot_t = hot_t_ref[...]
@@ -187,12 +191,10 @@
         for n in range(len(blocks)):
             k = first + n
             part = back[:, sz.cols(n)]
-            middle = part[slab : slab + rows]
             if not last or k == 0:
-                middle = middle + upstream[k]
-            outs[0][k] = part[:slab].astype(BF16)
-            outs[1][k] = middle.astype(BF16)
-            outs[2][k] = part[slab + rows :].astype(BF16)
+                part = part + around(upstream[k], slab)
+            outs[0][k] = part[:rows].astype(BF16)
+            outs[1][k] = part[rows:].astype(BF16)
 
     q_len = jnp.zeros((edges, sz.c), F32)
     group = picked_group(refs, hot, 0, sz.zero)
@@ -260,13 +262,32 @@
     lane = lax.broadcasted_iota(jnp.int32, (edges, sz.c), 1)
     change = jnp.where(lane == 0, dx, jnp.where(lane == 1, dy, jnp.where(lane == 2, dz_, 0.0)))
     moved = sum(dot(hot_t, part) for part in split3(change))
-    own = moved[slab : slab + rows] - pool(change, rows) + carried
-    return moved[:slab], own, moved[slab + rows :]
-
-
-def send_back(moved, outs, sz):
-    for ref, value in zip(outs, moved):
-        ref[sz.coefs] = encode(value).astype(BF16)
+    return moved - around(pool(change, rows), slab)
+
+
+def around(own, slab):
+    edge = jnp.zeros((slab, own.shape[1]), F32)
+    return jnp.concatenate([edge, own, edge], axis=0)
+
+
+def first_slab(slabs):
+    slab_now = lax.axis_index("space")
+    batch = lax.rem(slab_now, 2)
+    shift = lax.rem(lax.axis_index("segment"), 2)
+    return lax.rem(slab_now - batch + shift - 1 + slabs, slabs), batch
+
+
+def publish(values, slabs, out_ref):
+    window, c = values.shape
+    count = out_ref.shape[1]
+    start, batch = first_slab(slabs)
+    row = lax.broadcasted_iota(jnp.int32, (window, count), 0)
+    column = lax.broadcasted_iota(jnp.int32, (window, count), 1)
+    target = lax.rem(start * (window // 4) + row, count // 2) + batch * (count // 2)
+    hot = (column == target).astype(BF16)
+    turned = jnp.transpose(jnp.concatenate([values, jnp.zeros((c - window, c), F32)], axis=0))
+    turned = turned[: out_ref.shape[0], :window]
+    out_ref[...] = sum(dot(part, hot) for part in split3(turned))
 
 
 def pack_kernel(
@@ -318,13 +339,13 @@
 
 def open_kernel(
     slabs, neighbours, mine_ref, partner_ref, straight_ref, cross_ref, rate_ref,
-    left_ref, own_ref, right_ref, hot_ref, hot_t_ref, geo_ref, seed_ref
+    low_ref, high_ref, hot_ref, hot_t_ref, geo_ref, seed_ref
 ):
-    slab_now = lax.axis_index("space")
-    batch = lax.rem(slab_now, 2)
+    start, batch = first_slab(slabs)
     even = batch == 0
-    coefs = own_ref.shape[0]
-    rows, c = own_ref.shape[1:]
+    level = lax.rem(lax.axis_index("segment"), 2) == 0
+    coefs = low_ref.shape[0]
+    rows, c = low_ref.shape[1:]
     per_slab = rows // 2
     window = 2 * rows
     edges = rows * neighbours
@@ -335,16 +356,19 @@
     def parts(k):
         mine, partner = mine_ref[k].astype(F32), partner_ref[k].astype(F32)
         straight, cross = straight_ref[k].astype(F32), cross_ref[k].astype(F32)
-        own = jnp.concatenate([choose(mine, partner), choose(partner, mine)], axis=0)
-        return choose(cross, straight), own, choose(straight, cross)
+        low, high = choose(mine, partner), choose(partner, mine)
+        after, last = choose(straight, cross), choose(cross, straight)
+        return [
+            jnp.where(level, last, low), jnp.where(level, low, high), jnp.where(level, high, after),
+            jnp.where(level, after, last),
+        ]
 
     @pl.when(lax.axis_index("segment") == 0)
     def _():
         for k in range(coefs):
-            left, own, right = parts(k)
-            left_ref[k] = left.astype(BF16)
-            own_ref[k] = own.astype(BF16)
-            right_ref[k] = right.astype(BF16)
+            slab = parts(k)
+            low_ref[k] = jnp.concatenate(slab[:2], axis=0).astype(BF16)
+            high_ref[k] = jnp.concatenate(slab[2:], axis=0).astype(BF16)
 
     extra = jnp.concatenate(parts(coefs), axis=0)
     numbers = decode(extra)
@@ -352,8 +376,7 @@
     own_extra = extra[per_slab : per_slab + rows]
     low = pltpu.roll(own_extra, c - 8, 1)
     index = own_extra.astype(jnp.int32) * BASE + low.astype(jnp.int32)
-    first_slab = slab_now - batch
-    place = lax.rem(index // per_slab - first_slab + (1 + slabs), slabs) * per_slab + index % per_slab
+    place = lax.rem(index // per_slab - start + slabs, slabs) * per_slab + index % per_slab
     columns = lax.broadcasted_iota(jnp.int32, (rows, c), 1)
     hot = jnp.concatenate(
         [
@@ -365,12 +388,12 @@
     hot_ref[...] = hot.astype(BF16)[:, :window]
     hot_t_ref[...] = jnp.transpose(hot).astype(BF16)[:window]
     hot = hot.astype(BF16)[:, :window]
-    level = lax.broadcasted_iota(jnp.int32, (window, c), 0) // per_slab - 1
+    lift = lax.broadcasted_iota(jnp.int32, (window, c), 0) // per_slab - 1
     offset = []
     for n in range(3):
         column = jnp.broadcast_to(numbers[:, n : n + 1], (window, c))
         if n == 2:
-            column = column + SLAB_DEPTH * level.astype(F32)
+            column = column + SLAB_DEPTH * lift.astype(F32)
         there = sum(dot(hot, part) for part in split3(column))
         offset.append(there - jnp.concatenate([column[per_slab : per_slab + rows]] * neighbours, axis=0))
     flat = offset[0] * offset[0] + offset[1] * offset[1] + 1.0
@@ -406,92 +429,74 @@
 
 
 def forward_kernel(
-    tick, sz, left_ref, own_ref, right_ref, hot_ref, geo_ref, zero_ref, one_ref, two_ref,
-    out_ref, low_ref, high_ref, pooled_ref
+    tick, sz, low_ref, high_ref, hot_ref, geo_ref, zero_ref, one_ref, two_ref, out_ref, pooled_ref
 ):
     @pl.when(lax.axis_index("segment") == tick)
     def _():
-        rows = own_ref.shape[1]
-        slab = rows // 2
-        refs = (left_ref, own_ref, right_ref)
+        rows = low_ref.shape[1]
+        refs = (low_ref, high_ref)
         pooled = forward(refs, hot_ref, geo_ref, zero_ref, one_ref, two_ref, sz, rows, False)
         signal = signal_of(pooled, sz)
         gate, lifted = silu_parts(signal)
         for k in range(sz.coefs):
             pooled_ref[k] = pooled[k]
             added = lifted if k == 0 else gate * pooled[k]
-            updated = own_ref[k].astype(F32) + added
-            out_ref[k] = updated.astype(BF16)
-            low_ref[k] = updated[:slab].astype(BF16)
-            high_ref[k] = updated[slab:].astype(BF16)
+            out_ref[k] = (own_rows(refs, k) + added).astype(BF16)
 
 
 def turn_kernel(
-    tick, sz, left_ref, own_ref, right_ref, hot_ref, hot_t_ref, geo_ref, zero_ref, one_ref, two_ref,
-    read_ref, seed_ref, *outs
+    tick, sz, slabs, low_ref, high_ref, hot_ref, hot_t_ref, geo_ref, zero_ref, one_ref, two_ref,
+    read_ref, seed_ref, sums_ref, *outs
 ):
     @pl.when(lax.axis_index("segment") == tick)
     def _():
-        rows = own_ref.shape[1]
-        refs = (left_ref, own_ref, right_ref)
+        rows = low_ref.shape[1]
+        refs = (low_ref, high_ref)
         pooled = forward(refs, hot_ref, geo_ref, zero_ref, one_ref, two_ref, sz, rows, True)
         signal = signal_of(pooled, sz)
         _, lifted = silu_parts(signal)
-        updated = own_ref[0].astype(F32) + lifted
+        updated = own_rows(refs, 0) + lifted
         gate, active = silu_parts(updated)
         read = read_ref[...]
         energy = jnp.sum(read * active, axis=1, keepdims=True)
         lane = lax.broadcasted_iota(jnp.int32, (rows, sz.c), 1)
-        carried = jnp.where(lane == 3, energy, 0.0)
+        energy = around(jnp.where(lane == 3, energy, 0.0), rows // 2)
         upstream = [seed_ref[...] * read * (gate + updated * gate * (1.0 - gate))]
         moved = backward(
-            upstream, carried, pooled, refs, hot_ref, hot_t_ref, geo_ref, zero_ref, one_ref, two_ref, sz, rows, True, outs
+            upstream, pooled, refs, hot_ref, hot_t_ref, geo_ref, zero_ref, one_ref, two_ref, sz, rows, True, outs
         )
-        send_back(moved, outs, sz)
+        publish(moved + energy, slabs, sums_ref)
 
 
 def backward_kernel(
-    tick, sz, up_own_ref, up_low_ref, up_high_ref, pooled_ref, left_ref, own_ref, right_ref, hot_ref, hot_t_ref, geo_ref,
-    zero_ref, one_ref, two_ref, *outs
+    tick, sz, slabs, up_low_ref, up_high_ref, pooled_ref, low_ref, high_ref, hot_ref, hot_t_ref, geo_ref,
+    zero_ref, one_ref, two_ref, *more
 ):
+    earlier = () if tick else more[: lax.axis_size("segment") - 1]
+    sums_ref, *outs = more[len(earlier) :]
+
     @pl.when(lax.axis_index("segment") == tick)
     def _():
-        rows = own_ref.shape[1]
-        refs = (left_ref, own_ref, right_ref)
-
-        def arrived(k):
-            halves = jnp.concatenate([up_low_ref[k].astype(F32), up_high_ref[k].astype(F32)], axis=0)
-            return up_own_ref[k].astype(F32) + halves
-
-        upstream = [arrived(k) for k in range(sz.coefs)]
-        halves = jnp.concatenate(
-            [decode(up_low_ref[sz.coefs].astype(F32)), decode(up_high_ref[sz.coefs].astype(F32))], axis=0
-        )
-        carried = decode(up_own_ref[sz.coefs].astype(F32)) + halves
+        rows = low_ref.shape[1]
+        refs = (low_ref, high_ref)
+        upstream = [up_low_ref[k].astype(F32) + up_high_ref[k].astype(F32) for k in range(sz.coefs)]
         pooled = [pooled_ref[k] for k in range(sz.coefs)]
         moved = backward(
-            upstream, carried, pooled, refs, hot_ref, hot_t_ref, geo_ref, zero_ref, one_ref, two_ref, sz, rows, False,
+            upstream, pooled, refs, hot_ref, hot_t_ref, geo_ref, zero_ref, one_ref, two_ref, sz, rows, False,
             outs if tick else None,
         )
-        if tick:
-            send_back(moved, outs, sz)
-        else:
-            share(moved, outs)
-
-
-def share(moved, outs):
-    left, own, right = moved
-    slab = left.shape[0]
-    even = lax.rem(lax.axis_index("space"), 2) == 0
-    low, high = own[:slab], own[slab:]
-    outs[0][...] = jnp.where(even, low, high)
-    outs[1][...] = jnp.where(even, high, low)
-    outs[2][...] = jnp.where(even, right, left)
-    outs[3][...] = jnp.where(even, left, right)
+        publish(moved, slabs, sums_ref)
+
+    for n, ref in enumerate(earlier):
+
+        @pl.when(lax.axis_index("segment") == n + 1)
+        def _(ref=ref):
+            sums_ref[...] = ref[...]
 
 
 def call(body, operands, shapes, name, spaces=None, scratch=()):
     spaces = spaces or [pltpu.VMEM] * len(operands)
+    operands = [pltpu.with_memory_space_constraint(value, space) for value, space in zip(operands, spaces)]
     return pl.pallas_call(
         body,
         out_shape=shapes,
@@ -518,8 +523,6 @@
 ):
     segments = lax.axis_size("segment")
     slabs = lax.axis_size("space")
-    segment_now = lax.axis_index("segment")
-    even = lax.rem(lax.axis_index("space"), 2) == 0
     batches, per_slab = species.shape
     coefs, channels = node_states.shape[2:]
     neighbours = sources.shape[2]
@@ -529,21 +532,9 @@
     axes = ("segment", "space")
     shape = jax.ShapeDtypeStruct
 
-    def to_partner(i):
-        return i + 1 - 2 * (i % 2)
-
-    def outward(i):
-        return (i + (2 if i % 2 else -2)) % slabs
-
-    def inward(i):
-        return (i + (-2 if i % 2 else 2)) % slabs
-
-    def across(i):
-        return (i + (1 if i % 2 else -1)) % slabs
-
-    def within(value, target, only=None):
-        chosen = range(segments) if only is None else [only]
-        return lax.ppermute(value, axes, [(s * slabs + i, s * slabs + target(i)) for s in chosen for i in range(slabs)])
+    def within(value, target):
+        pairs = [(s * slabs + i, s * slabs + target(s % 2, i) % slabs) for s in range(segments) for i in range(slabs)]
+        return lax.ppermute(value, axes, pairs)
 
     def hop(value, start, stop, by):
         pairs = [(start * slabs + i, stop * slabs + (i + by) % slabs) for i in range(slabs)]
@@ -557,67 +548,58 @@
         pack_kernel, raw, [packed, packed], "pack", [pltpu.HBM] * len(raw),
         [pltpu.VMEM(v.shape, v.dtype) for v in raw] + [pltpu.SemaphoreType.DMA((len(raw),))],
     )
-    partner = within(other, to_partner)
-    straight = within(mine, outward)
-    cross = within(other, across)
+    partner = within(other, lambda odd, i: i + 1 - 2 * (i % 2))
+    straight = within(mine, lambda odd, i: i - 2 if odd or i % 2 == 0 else i + 2)
+    cross = within(other, lambda odd, i: i - 1 if i % 2 == 0 else i - 3 if odd else i + 1)
     weights = [zero_weight[0], one_weight[0], two_weight[0]]
     weights = call(
         stage_kernel, weights, [pltpu.VMEM(w.shape, w.dtype) for w in weights], "stage", [pltpu.HBM] * 3,
         [pltpu.SemaphoreType.DMA((3,))],
     )
     whole = shape((coefs, rows, channels), BF16)
-    half = shape((coefs, per_slab, channels), BF16)
-    left, own, right, hot, hot_t, geo, seeds = call(
+    low, high, hot, hot_t, geo, seeds = call(
         functools.partial(open_kernel, slabs, neighbours),
         [mine, partner, straight, cross, radial_rate],
         [
-            half, whole, half, shape((edges, 2 * rows), BF16), shape((2 * rows, edges), BF16),
+            whole, whole, shape((edges, 2 * rows), BF16), shape((2 * rows, edges), BF16),
             shape((10 * edges, channels), F32), shape((rows, channels), F32),
         ],
         "open",
     )
-    around = [(left, own, right)]
+    around_all = [(low, high)]
     kept = []
     for tick in range(segments - 1):
-        out, low, high, pooled = call(
+        out, pooled = call(
             functools.partial(forward_kernel, tick, sz),
-            [*around[tick], hot, geo, *weights],
-            [whole, half, half, shape((coefs, rows, channels), F32)],
+            [*around_all[tick], hot, geo, *weights],
+            [whole, shape((coefs, rows, channels), F32)],
             "forward",
         )
         kept.append(pooled)
-        own = hop(out, tick, tick + 1, 0)
-        right = hop(low, tick, tick + 1, -2)
-        left = hop(high, tick, tick + 1, 2)
-        around.append((left, own, right))
+        ways = (2, 0) if tick % 2 else (0, -2)
+        around_all.append(tuple(hop(out, tick, tick + 1, by) for by in ways))
     final = segments - 1
-    whole_more = shape((coefs + 1, rows, channels), BF16)
-    last_shape = [shape((per_slab, channels), F32)] * 4
-    parts = call(
-        functools.partial(turn_kernel, final, sz),
-        [*around[final], hot, hot_t, geo, *weights, read_weight.reshape(1, channels), seeds],
-        [packed, whole_more, packed],
+    sums = shape((8, batches * slabs * per_slab), F32)
+    sums_last, *parts = call(
+        functools.partial(turn_kernel, final, sz, slabs),
+        [*around_all[final], hot, hot_t, geo, *weights, read_weight.reshape(1, channels), seeds],
+        [sums, whole, whole],
         "turn",
     )
+    every = [sums_last]
     for tick in reversed(range(segments - 1)):
-        left, own, right = parts
-        up_own = hop(own, tick + 1, tick, 0)
-        up_low = hop(right, tick + 1, tick, 2)
-        up_high = hop(left, tick + 1, tick, -2)
-        parts = call(
-            functools.partial(backward_kernel, tick, sz),
-            [up_own, up_low, up_high, kept[tick], *around[tick], hot, hot_t, geo, *weights],
-            [packed, whole_more, packed] if tick else last_shape,
+        ways = (2, 0) if tick % 2 else (0, -2)
+        up = [hop(part, tick + 1, tick, -by) for part, by in zip(parts, ways)]
+        sums_now, *parts = call(
+            functools.partial(backward_kernel, tick, sz, slabs),
+            [*up, kept[tick], *around_all[tick], hot, hot_t, geo, *weights] + ([] if tick else every),
+            [sums, whole, whole] if tick else [sums],
             "backward",
         )
-    here, theirs, straight, cross = (value[:, :4] for value in parts)
-    here = here + within(straight, inward, 0)
-    there = within(theirs, to_partner, 0) + within(cross, across, 0)
-    both = jnp.where(even, jnp.stack([here, there]), jnp.stack([there, here]))
-    total = jnp.where(segment_now == 0, both, 0.0)
-    for stop in range(1, segments):
-        total = total + hop(both, 0, stop, 0)
-    return total[..., 3], total[..., :3].transpose(0, 2, 1)
+        every.insert(0, sums_now)
+    total = lax.psum(every[0][:4], axes).reshape(4, batches, slabs * per_slab)
+    mine = lax.dynamic_slice_in_dim(total, lax.axis_index("space") * per_slab, per_slab, 2)
+    return mine[3], mine[:3].transpose(1, 0, 2)
 
 
 def solution(mesh):

time: 111 us -> 125 us (1.13)
  blocking collectives: 0 us -> 38.5 us
  starting transfers between devices: 35.8 us -> 17.3 us
  local copies, waits for them, and re-layouts: 13.1 us -> 4.24 us
  Pallas kernels: 7.46 us -> 10.5 us
    psum x0 -> x1, blocking collectives: none -> 38.5 us  [on_device(): total = lax.psum(every[0][:4], axes).reshape(4, batches, slabs * per_slab)]
    ppermute x6 -> x3, starting transfers between devices: 14.9 us -> 5.23 us  [within(): return lax.ppermute(value, axes, pairs)]
    unnamed x31 -> x12, local copies, waits for them, and re-layouts: 12.3 us -> 2.86 us
    ppermute x21 -> x12, starting transfers between devices: 20.9 us -> 12 us  [hop(): return lax.ppermute(value, axes, pairs)]
    pallas_call x10, Pallas kernels: 7.46 us -> 10.5 us  [call(): pl.pallas_call(body, out_shape=shapes, in_specs=[pl.BlockSpec(memory_spac...]
    ppermute x6 -> x3, waiting for transfers between devices: 2.09 us -> 2.68 us  [within(): return lax.ppermute(value, axes, pairs)]
    ppermute x21 -> x12, waiting for transfers between devices: 50.7 us -> 50.4 us  [hop(): return lax.ppermute(value, axes, pairs)]
  transfers between devices with their start and end apart: 27 -> 15, of which waited for: 5 -> 5; matrix products, arithmetic and copies ran while one was open for 0% -> 0% of each run, Pallas kernels for 0% -> 2%
where the time goes in v2:
time: 125 us; the launch traced here: 124 us
  waiting for transfers between devices  53.1 us (42%)
  blocking collectives  38.5 us (31%)
  starting transfers between devices  17.3 us (14%)
  Pallas kernels  10.5 us (8%)
  local copies, waits for them, and re-layouts  4.24 us (3%)
    ppermute x12, waiting for transfers between devices, hop(): return lax.ppermute(value, axes, pairs)  50.4 us
    psum x1, blocking collectives, on_device(): total = lax.psum(every[0][:4], axes).reshape(4, batches, slabs * per_slab)  38.5 us
    ppermute x12, starting transfers between devices, hop(): return lax.ppermute(value, axes, pairs)  12 us
    pallas_call x10, Pallas kernels, call(): pl.pallas_call(body, out_shape=shapes, in_specs=[pl.BlockSpec(memory_spac...  10.5 us
    ppermute x3, starting transfers between devices, within(): return lax.ppermute(value, axes, pairs)  5.23 us
    unnamed x12, local copies, waits for them, and re-layouts  2.86 us
    ppermute x3, waiting for transfers between devices, within(): return lax.ppermute(value, axes, pairs)  2.68 us
  transfers between devices with their start and end apart: 15, of which 5 were waited for; matrix products, arithmetic and copies ran while one was open for 0% of the time, Pallas kernels for 2%

profile of v2, /device:TPU:0, one launch (start us, length us, event | category | flops | bytes accessed | tf_op | source)
XLA Modules:
  0.0 124.4 jit_solution(7957422056788953933)
XLA Ops:
  0.6 1.2 pack.1
  1.8 0.5 collective-permute-start
  2.4 4.7 %collective-permute-start.1 = (bf16[30,8,128]{2,1,0:T(8,128)(2,1)S(1)}, bf16[30,8,128]{2,1,0:T(8,128)(2,1)S(1)}, u32[]{:S(2)}, u32[]{:S(2)}) collective-permute-start(bf16[30,8,128]{2,1,0:T(8,128)(2,1)S(1)} %get-tuple-element.28.mine_ref), channel_id=1, source_target_pairs={{0,6},{1,3},{2,0},{3,5},{4,2},{5,7},{6,4},{7,1},{8,14},{9,15},{10,... | collective-permute-start | bytes 184328 | tf_op jit(solution)/shard_map/ppermute | solution.py:537
  7.0 0.1 collective-permute-start.2
  7.1 2.7 %stage.1 = (bf16[896,896]{1,0:T(8,128)(2,1)S(1)}, bf16[2,768,768]{2,1,0:T(8,128)(2,1)S(1)}, bf16[2,640,640]{2,1,0:T(8,128)(2,1)S(1)}) custom-call(bf16[896,896]{1,0:T(8,128)(2,1)} %bitcast.13, bf16[2,768,768]{2,1,0:T(8,128)(2,1)} %bitcast.11, bf16[2,640,640]{2,1,0:T(8,128)(2,1)} %bitcast.12), custom_call_target="tpu_custom_call" | custom-call | tf_op jit(solution)/shard_map/stage/pallas_call | solution.py:500
  9.8 0.0 copy-start
  9.8 0.0 copy-start.2
  9.8 0.0 collective-permute-done.partner_ref
  9.8 0.0 collective-permute-done.1.straight_ref
  9.8 2.7 %collective-permute-done.2.cross_ref = bf16[30,8,128]{2,1,0:T(8,128)(2,1)S(1)} collective-permute-done((bf16[30,8,128]{2,1,0:T(8,128)(2,1)S(1)}, bf16[30,8,128]{2,1,0:T(8,128)(2,1)S(1)}, u32[]{:S(2)}, u32[]{:S(2)}) %collective-permute-start.2) | collective-permute-done | bytes 61472 | tf_op jit(solution)/shard_map/ppermute | solution.py:537
  12.5 0.0 copy-done.4
  12.5 0.5 open.1
  13.0 1.7 %forward.3 = (bf16[29,16,128]{2,1,0:T(8,128)(2,1)S(1)}, f32[29,16,128]{2,1,0:T(8,128)S(1)}) custom-call(bf16[29,16,128]{2,1,0:T(8,128)(2,1)S(1)} %get-tuple-element.30.low_ref, bf16[29,16,128]{2,1,0:T(8,128)(2,1)S(1)} %get-tuple-element.31.high_ref, bf16[128,32]{1,0:T(8,128)(2,1)S(1)} %get-tuple-element.32.hot_ref, ...), custom_call_target="tpu_custom_call" | custom-call | tf_op jit(solution)/shard_map/forward/pallas_call | solution.py:500
  14.7 1.3 %collective-permute-start.3 = (bf16[29,16,128]{2,1,0:T(8,128)(2,1)S(1)}, bf16[29,16,128]{2,1,0:T(8,128)(2,1)S(1)}, u32[]{:S(2)}, u32[]{:S(2)}) collective-permute-start(bf16[29,16,128]{2,1,0:T(8,128)(2,1)S(1)} %get-tuple-element.37), channel_id=1, source_target_pairs={{0,8},{1,9},{2,10},{3,11},{4,12},{5,13},{6,14},{7,15}} | collective-permute-start | bytes 356360 | tf_op jit(solution)/shard_map/ppermute | solution.py:541
  16.0 2.7 %collective-permute-start.4 = (bf16[29,16,128]{2,1,0:T(8,128)(2,1)S(1)}, bf16[29,16,128]{2,1,0:T(8,128)(2,1)S(1)}, u32[]{:S(2)}, u32[]{:S(2)}) collective-permute-start(bf16[29,16,128]{2,1,0:T(8,128)(2,1)S(1)} %get-tuple-element.37), channel_id=1, source_target_pairs={{0,14},{1,15},{2,8},{3,9},{4,10},{5,11},{6,12},{7,13}} | collective-permute-start | bytes 356360 | tf_op jit(solution)/shard_map/ppermute | solution.py:541
  18.7 2.2 %collective-permute-done.3.low_ref = bf16[29,16,128]{2,1,0:T(8,128)(2,1)S(1)} collective-permute-done((bf16[29,16,128]{2,1,0:T(8,128)(2,1)S(1)}, bf16[29,16,128]{2,1,0:T(8,128)(2,1)S(1)}, u32[]{:S(2)}, u32[]{:S(2)}) %collective-permute-start.3) | collective-permute-done | bytes 118816 | tf_op jit(solution)/shard_map/ppermute | solution.py:541
  20.9 0.7 collective-permute-done.4.high_ref
  21.6 0.8 collective-permute-start.5
  22.4 0.7 collective-permute-start.6
  23.1 0.0 collective-permute-done.5.low_ref
  23.1 0.0 collective-permute-done.6.high_ref
  23.1 0.7 collective-permute-start.7
  23.8 0.7 collective-permute-start.8
  24.5 0.0 collective-permute-done.7.low_ref
  24.5 0.0 collective-permute-done.8.high_ref
  24.5 0.0 copy-done.5
  24.5 0.7 collective-permute-start.10
  25.2 0.7 collective-permute-start.9
  25.9 0.0 collective-permute-done.10.up_high_ref
  25.9 0.0 collective-permute-done.9.up_low_ref
  25.9 0.7 collective-permute-start.11
  26.6 0.7 collective-permute-start.12
  27.3 0.0 collective-permute-done.11.up_low_ref
  27.3 0.0 collective-permute-done.12.up_high_ref
  27.3 0.0 copy-done
  27.3 0.0 copy-done.2
  27.3 0.9 backward.4
  28.2 1.3 %collective-permute-start.13 = (bf16[29,16,128]{2,1,0:T(8,128)(2,1)}, bf16[29,16,128]{2,1,0:T(8,128)(2,1)}, u32[]{:S(2)}, u32[]{:S(2)}) collective-permute-start(bf16[29,16,128]{2,1,0:T(8,128)(2,1)} %get-tuple-element.48), channel_id=1, source_target_pairs={{8,0},{9,1},{10,2},{11,3},{12,4},{13,5},{14,6},{15,7}} | collective-permute-start | bytes 356360 | tf_op jit(solution)/shard_map/ppermute | solution.py:541
  29.5 1.3 %collective-permute-start.14 = (bf16[29,16,128]{2,1,0:T(8,128)(2,1)}, bf16[29,16,128]{2,1,0:T(8,128)(2,1)}, u32[]{:S(2)}, u32[]{:S(2)}) collective-permute-start(bf16[29,16,128]{2,1,0:T(8,128)(2,1)} %get-tuple-element.49), channel_id=1, source_target_pairs={{8,2},{9,3},{10,4},{11,5},{12,6},{13,7},{14,0},{15,1}} | collective-permute-start | bytes 356360 | tf_op jit(solution)/shard_map/ppermute | solution.py:541
  30.8 46.1 %collective-permute-done.13.up_low_ref = bf16[29,16,128]{2,1,0:T(8,128)(2,1)} collective-permute-done((bf16[29,16,128]{2,1,0:T(8,128)(2,1)}, bf16[29,16,128]{2,1,0:T(8,128)(2,1)}, u32[]{:S(2)}, u32[]{:S(2)}) %collective-permute-start.13) | collective-permute-done | bytes 118816 | tf_op jit(solution)/shard_map/ppermute | solution.py:541
  76.9 1.3 %collective-permute-done.14.up_high_ref = bf16[29,16,128]{2,1,0:T(8,128)(2,1)} collective-permute-done((bf16[29,16,128]{2,1,0:T(8,128)(2,1)}, bf16[29,16,128]{2,1,0:T(8,128)(2,1)}, u32[]{:S(2)}, u32[]{:S(2)}) %collective-permute-start.14) | collective-permute-done | bytes 118816 | tf_op jit(solution)/shard_map/ppermute | solution.py:541
  78.2 1.4 %copy-done.1 = bf16[2,640,640]{2,1,0:T(8,128)(2,1)S(1)} copy-done((bf16[2,640,640]{2,1,0:T(8,128)(2,1)S(1)}, bf16[2,640,640]{2,1,0:T(8,128)(2,1)}, u32[]{:S(2)}) %copy-start.1) | copy-done | bytes 1638424
  79.7 1.4 %copy-done.3 = bf16[896,896]{1,0:T(8,128)(2,1)S(1)} copy-done((bf16[896,896]{1,0:T(8,128)(2,1)S(1)}, bf16[896,896]{1,0:T(8,128)(2,1)}, u32[]{:S(2)}) %copy-start.3) | copy-done | bytes 1605656
  81.1 3.4 %backward.5 = f32[8,128]{1,0:T(8,128)S(1)} custom-call(bf16[29,16,128]{2,1,0:T(8,128)(2,1)} %collective-permute-done.13.up_low_ref, bf16[29,16,128]{2,1,0:T(8,128)(2,1)} %collective-permute-done.14.up_high_ref, f32[29,16,128]{2,1,0:T(8,128)S(1)} %get-tuple-element.50.pooled_ref, bf16[29,16,128]{2,1,0:T(8,128)(2,1)S(1)} %get-tuple-element.30.low_ref, ...), custom_call_target="tpu_custom_call" | custom-call | tf_op jit(solution)/shard_map/backward/pallas_call | solution.py:500
  84.5 0.1 reshape.11
  84.6 38.5 %psum.7 = f32[4,2,64]{2,1,0:T(2,128)S(1)} all-reduce(f32[4,2,64]{2,1,0:T(2,128)S(1)} %reshape.11), channel_id=1, replica_groups=mesh['segment'=4,'space'=8] {'segment','space'}, use_global_device_ids=true, to_apply=%region_0.0 | all-reduce | flops 512 | bytes 4096 | tf_op jit(solution)/shard_map/psum | solution.py:600
  123.1 0.7 dynamic-slice_bitcast_fusion
  123.8 0.6 dynamic-slice_bitcast_fusion.1
  (9 shorter events, 0.1 us)
Async XLA Ops:
  1.8 7.9 %collective-permute-start = (bf16[30,8,128]{2,1,0:T(8,128)(2,1)S(1)}, bf16[30,8,128]{2,1,0:T(8,128)(2,1)S(1)}, u32[]{:S(2)}, u32[]{:S(2)}) collective-permute-start(bf16[30,8,128]{2,1,0:T(8,128)(2,1)S(1)} %get-tuple-element.29), channel_id=1, source_target_pairs={{0,1},{1,0},{2,3},{3,2},{4,5},{5,4},{6,7},{7,6},{8,9},{9,8},{10,11... | collective-permute-start | bytes 184328 | tf_op jit(solution)/shard_map/ppermute | solution.py:537
  2.4 7.4 %collective-permute-start.1 = (bf16[30,8,128]{2,1,0:T(8,128)(2,1)S(1)}, bf16[30,8,128]{2,1,0:T(8,128)(2,1)S(1)}, u32[]{:S(2)}, u32[]{:S(2)}) collective-permute-start(bf16[30,8,128]{2,1,0:T(8,128)(2,1)S(1)} %get-tuple-element.28.mine_ref), channel_id=1, source_target_pairs={{0,6},{1,3},{2,0},{3,5},{4,2},{5,7},{6,4},{7,1},{8,14},{9,15},{10,... | collective-permute-start | bytes 184328 | tf_op jit(solution)/shard_map/ppermute | solution.py:537
  7.0 5.4 %collective-permute-start.2 = (bf16[30,8,128]{2,1,0:T(8,128)(2,1)S(1)}, bf16[30,8,128]{2,1,0:T(8,128)(2,1)S(1)}, u32[]{:S(2)}, u32[]{:S(2)}) collective-permute-start(bf16[30,8,128]{2,1,0:T(8,128)(2,1)S(1)} %get-tuple-element.29), channel_id=1, source_target_pairs={{0,7},{1,2},{2,1},{3,4},{4,3},{5,6},{6,5},{7,0},{8,15},{9,14},{10,... | collective-permute-start | bytes 184328 | tf_op jit(solution)/shard_map/ppermute | solution.py:537
  7.1 5.4 %copy-start.4 = (f32[1,128]{1,0:T(1,128)S(1)}, f32[1,128]{1,0:T(1,128)}, u32[]{:S(2)}) copy-start(f32[1,128]{1,0:T(1,128)} %rate_ref.1) | copy-start | bytes 1540
  9.8 17.5 %copy-start = (bf16[2,640,640]{2,1,0:T(8,128)(2,1)}, bf16[2,640,640]{2,1,0:T(8,128)(2,1)S(1)}, u32[]{:S(2)}) copy-start(bf16[2,640,640]{2,1,0:T(8,128)(2,1)S(1)} %get-tuple-element.36.two_ref) | copy-start | bytes 4915204
  9.8 17.5 %copy-start.2 = (bf16[896,896]{1,0:T(8,128)(2,1)}, bf16[896,896]{1,0:T(8,128)(2,1)S(1)}, u32[]{:S(2)}) copy-start(bf16[896,896]{1,0:T(8,128)(2,1)S(1)} %get-tuple-element.34.zero_ref) | copy-start | bytes 4816900
  14.7 6.2 %collective-permute-start.3 = (bf16[29,16,128]{2,1,0:T(8,128)(2,1)S(1)}, bf16[29,16,128]{2,1,0:T(8,128)(2,1)S(1)}, u32[]{:S(2)}, u32[]{:S(2)}) collective-permute-start(bf16[29,16,128]{2,1,0:T(8,128)(2,1)S(1)} %get-tuple-element.37), channel_id=1, source_target_pairs={{0,8},{1,9},{2,10},{3,11},{4,12},{5,13},{6,14},{7,15}} | collective-permute-start | bytes 356360 | tf_op jit(solution)/shard_map/ppermute | solution.py:541
  16.0 5.6 %collective-permute-start.4 = (bf16[29,16,128]{2,1,0:T(8,128)(2,1)S(1)}, bf16[29,16,128]{2,1,0:T(8,128)(2,1)S(1)}, u32[]{:S(2)}, u32[]{:S(2)}) collective-permute-start(bf16[29,16,128]{2,1,0:T(8,128)(2,1)S(1)} %get-tuple-element.37), channel_id=1, source_target_pairs={{0,14},{1,15},{2,8},{3,9},{4,10},{5,11},{6,12},{7,13}} | collective-permute-start | bytes 356360 | tf_op jit(solution)/shard_map/ppermute | solution.py:541
  21.6 2.9 %copy-start.5 = (f32[128]{0:T(128)S(1)}, f32[128]{0:T(128)}, u32[]{:S(2)}) copy-start(f32[128]{0:T(128)} %param.20) | copy-start | bytes 1540
  21.6 1.5 %collective-permute-start.5 = (bf16[29,16,128]{2,1,0:T(8,128)(2,1)S(1)}, bf16[29,16,128]{2,1,0:T(8,128)(2,1)S(1)}, u32[]{:S(2)}, u32[]{:S(2)}) collective-permute-start(bf16[29,16,128]{2,1,0:T(8,128)(2,1)S(1)} %get-tuple-element.38), channel_id=1, source_target_pairs={{8,18},{9,19},{10,20},{11,21},{12,22},{13,23},{14,16},{15,17}} | collective-permute-start | bytes 356360 | tf_op jit(solution)/shard_map/ppermute | solution.py:541
  22.4 0.7 collective-permute-start.6
  23.1 1.4 %collective-permute-start.7 = (bf16[29,16,128]{2,1,0:T(8,128)(2,1)S(1)}, bf16[29,16,128]{2,1,0:T(8,128)(2,1)S(1)}, u32[]{:S(2)}, u32[]{:S(2)}) collective-permute-start(bf16[29,16,128]{2,1,0:T(8,128)(2,1)S(1)} %get-tuple-element.39), channel_id=1, source_target_pairs={{16,24},{17,25},{18,26},{19,27},{20,28},{21,29},{22,30},{23,31}} | collective-permute-start | bytes 356360 | tf_op jit(solution)/shard_map/ppermute | solution.py:541
  23.8 0.7 collective-permute-start.8
  24.5 1.4 %collective-permute-start.10 = (bf16[29,16,128]{2,1,0:T(8,128)(2,1)S(1)}, bf16[29,16,128]{2,1,0:T(8,128)(2,1)S(1)}, u32[]{:S(2)}, u32[]{:S(2)}) collective-permute-start(bf16[29,16,128]{2,1,0:T(8,128)(2,1)S(1)} %get-tuple-element.43), channel_id=1, source_target_pairs={{24,18},{25,19},{26,20},{27,21},{28,22},{29,23},{30,16},{31,17}} | collective-permute-start | bytes 356360 | tf_op jit(solution)/shard_map/ppermute | solution.py:541
  25.2 0.7 collective-permute-start.9
  25.9 1.4 %collective-permute-start.11 = (bf16[29,16,128]{2,1,0:T(8,128)(2,1)S(1)}, bf16[29,16,128]{2,1,0:T(8,128)(2,1)S(1)}, u32[]{:S(2)}, u32[]{:S(2)}) collective-permute-start(bf16[29,16,128]{2,1,0:T(8,128)(2,1)S(1)} %get-tuple-element.45), channel_id=1, source_target_pairs={{16,14},{17,15},{18,8},{19,9},{20,10},{21,11},{22,12},{23,13}} | collective-permute-start | bytes 356360 | tf_op jit(solution)/shard_map/ppermute | solution.py:541
  26.6 0.7 collective-permute-start.12
  28.2 48.7 %collective-permute-start.13 = (bf16[29,16,128]{2,1,0:T(8,128)(2,1)}, bf16[29,16,128]{2,1,0:T(8,128)(2,1)}, u32[]{:S(2)}, u32[]{:S(2)}) collective-permute-start(bf16[29,16,128]{2,1,0:T(8,128)(2,1)} %get-tuple-element.48), channel_id=1, source_target_pairs={{8,0},{9,1},{10,2},{11,3},{12,4},{13,5},{14,6},{15,7}} | collective-permute-start | bytes 356360 | tf_op jit(solution)/shard_map/ppermute | solution.py:541
  29.5 48.7 %collective-permute-start.14 = (bf16[29,16,128]{2,1,0:T(8,128)(2,1)}, bf16[29,16,128]{2,1,0:T(8,128)(2,1)}, u32[]{:S(2)}, u32[]{:S(2)}) collective-permute-start(bf16[29,16,128]{2,1,0:T(8,128)(2,1)} %get-tuple-element.49), channel_id=1, source_target_pairs={{8,2},{9,3},{10,4},{11,5},{12,6},{13,7},{14,0},{15,1}} | collective-permute-start | bytes 356360 | tf_op jit(solution)/shard_map/ppermute | solution.py:541
  78.2 1.4 %copy-start.1 = (bf16[2,640,640]{2,1,0:T(8,128)(2,1)S(1)}, bf16[2,640,640]{2,1,0:T(8,128)(2,1)}, u32[]{:S(2)}) copy-start(bf16[2,640,640]{2,1,0:T(8,128)(2,1)} %copy-done) | copy-start | bytes 4915204
  79.7 1.4 %copy-start.3 = (bf16[896,896]{1,0:T(8,128)(2,1)S(1)}, bf16[896,896]{1,0:T(8,128)(2,1)}, u32[]{:S(2)}) copy-start(bf16[896,896]{1,0:T(8,128)(2,1)} %copy-done.2) | copy-start | bytes 4816900

commit v3 on v2

--- a/solution.py
+++ b/solution.py
@@ -277,17 +277,46 @@
     return lax.rem(slab_now - batch + shift - 1 + slabs, slabs), batch
 
 
-def publish(values, slabs, out_ref):
-    window, c = values.shape
-    count = out_ref.shape[1]
-    start, batch = first_slab(slabs)
-    row = lax.broadcasted_iota(jnp.int32, (window, count), 0)
-    column = lax.broadcasted_iota(jnp.int32, (window, count), 1)
-    target = lax.rem(start * (window // 4) + row, count // 2) + batch * (count // 2)
-    hot = (column == target).astype(BF16)
-    turned = jnp.transpose(jnp.concatenate([values, jnp.zeros((c - window, c), F32)], axis=0))
-    turned = turned[: out_ref.shape[0], :window]
-    out_ref[...] = sum(dot(part, hot) for part in split3(turned))
+def send_back(moved, outs, sz):
+    rows = moved.shape[0] // 2
+    coded = encode(moved).astype(BF16)
+    outs[0][sz.coefs] = coded[:rows]
+    outs[1][sz.coefs] = coded[rows:]
+
+
+def share(moved, outs):
+    slab = moved.shape[0] // 4
+    left, low, high, right = (moved[n * slab : (n + 1) * slab] for n in range(4))
+    even = lax.rem(lax.axis_index("space"), 2) == 0
+    outs[0][...] = jnp.where(even, low, high)
+    outs[1][...] = jnp.where(even, high, low)
+    outs[2][...] = jnp.where(even, right, left)
+    outs[3][...] = jnp.where(even, left, right)
+
+
+def join_kernel(here_ref, theirs_ref, straight_ref, cross_ref, both_ref):
+    slab = here_ref.shape[0]
+    even = lax.rem(lax.axis_index("space"), 2) == 0
+    here = here_ref[...] + straight_ref[...]
+    there = theirs_ref[...] + cross_ref[...]
+    both_ref[:slab, :] = jnp.where(even, here, there)
+    both_ref[slab:, :] = jnp.where(even, there, here)
+
+
+def close_kernel(*refs):
+    *sums_refs, energies_ref, places_ref = refs
+    slab = energies_ref.shape[1]
+    for n, ref in enumerate(sums_refs):
+
+        @pl.when(lax.axis_index("segment") == n)
+        def _(ref=ref):
+            sums = ref[...]
+            rows, c = sums.shape
+            turned = jnp.transpose(jnp.concatenate([sums, jnp.zeros((c - rows, c), F32)], axis=0))
+            for b in range(2):
+                energies_ref[b : b + 1, :] = turned[3:4, b * slab : (b + 1) * slab]
+                for n in range(3):
+                    places_ref[n, b : b + 1, :] = turned[n : n + 1, b * slab : (b + 1) * slab]
 
 
 def pack_kernel(
@@ -445,8 +474,8 @@
 
 
 def turn_kernel(
-    tick, sz, slabs, low_ref, high_ref, hot_ref, hot_t_ref, geo_ref, zero_ref, one_ref, two_ref,
-    read_ref, seed_ref, sums_ref, *outs
+    tick, sz, low_ref, high_ref, hot_ref, hot_t_ref, geo_ref, zero_ref, one_ref, two_ref,
+    read_ref, seed_ref, *outs
 ):
     @pl.when(lax.axis_index("segment") == tick)
     def _():
@@ -465,16 +494,13 @@
         moved = backward(
             upstream, pooled, refs, hot_ref, hot_t_ref, geo_ref, zero_ref, one_ref, two_ref, sz, rows, True, outs
         )
-        publish(moved + energy, slabs, sums_ref)
+        send_back(moved + energy, outs, sz)
 
 
 def backward_kernel(
-    tick, sz, slabs, up_low_ref, up_high_ref, pooled_ref, low_ref, high_ref, hot_ref, hot_t_ref, geo_ref,
-    zero_ref, one_ref, two_ref, *more
+    tick, sz, up_low_ref, up_high_ref, pooled_ref, low_ref, high_ref, hot_ref, hot_t_ref, geo_ref,
+    zero_ref, one_ref, two_ref, *outs
 ):
-    earlier = () if tick else more[: lax.axis_size("segment") - 1]
-    sums_ref, *outs = more[len(earlier) :]
-
     @pl.when(lax.axis_index("segment") == tick)
     def _():
         rows = low_ref.shape[1]
@@ -485,13 +511,12 @@
             upstream, pooled, refs, hot_ref, hot_t_ref, geo_ref, zero_ref, one_ref, two_ref, sz, rows, False,
             outs if tick else None,
         )
-        publish(moved, slabs, sums_ref)
-
-    for n, ref in enumerate(earlier):
-
-        @pl.when(lax.axis_index("segment") == n + 1)
-        def _(ref=ref):
-            sums_ref[...] = ref[...]
+        carried = decode(up_low_ref[sz.coefs].astype(F32)) + decode(up_high_ref[sz.coefs].astype(F32))
+        moved = moved + around(carried, rows // 2)
+        if tick:
+            send_back(moved, outs, sz)
+        else:
+            share(moved, outs)
 
 
 def call(body, operands, shapes, name, spaces=None, scratch=()):
@@ -532,8 +557,8 @@
     axes = ("segment", "space")
     shape = jax.ShapeDtypeStruct
 
-    def within(value, target):
-        pairs = [(s * slabs + i, s * slabs + target(s % 2, i) % slabs) for s in range(segments) for i in range(slabs)]
+    def within(value, target, count):
+        pairs = [(s * slabs + i, s * slabs + target(s % 2, i) % slabs) for s in range(count) for i in range(slabs)]
         return lax.ppermute(value, axes, pairs)
 
     def hop(value, start, stop, by):
@@ -548,9 +573,9 @@
         pack_kernel, raw, [packed, packed], "pack", [pltpu.HBM] * len(raw),
         [pltpu.VMEM(v.shape, v.dtype) for v in raw] + [pltpu.SemaphoreType.DMA((len(raw),))],
     )
-    partner = within(other, lambda odd, i: i + 1 - 2 * (i % 2))
-    straight = within(mine, lambda odd, i: i - 2 if odd or i % 2 == 0 else i + 2)
-    cross = within(other, lambda odd, i: i - 1 if i % 2 == 0 else i - 3 if odd else i + 1)
+    partner = within(other, lambda odd, i: i + 1 - 2 * (i % 2), segments)
+    straight = within(mine, lambda odd, i: i - 2 if odd or i % 2 == 0 else i + 2, segments)
+    cross = within(other, lambda odd, i: i - 1 if i % 2 == 0 else i - 3 if odd else i + 1, segments)
     weights = [zero_weight[0], one_weight[0], two_weight[0]]
     weights = call(
         stage_kernel, weights, [pltpu.VMEM(w.shape, w.dtype) for w in weights], "stage", [pltpu.HBM] * 3,
@@ -579,27 +604,33 @@
         ways = (2, 0) if tick % 2 else (0, -2)
         around_all.append(tuple(hop(out, tick, tick + 1, by) for by in ways))
     final = segments - 1
-    sums = shape((8, batches * slabs * per_slab), F32)
-    sums_last, *parts = call(
-        functools.partial(turn_kernel, final, sz, slabs),
+    whole_more = shape((coefs + 1, rows, channels), BF16)
+    slab_sums = shape((per_slab, channels), F32)
+    parts = call(
+        functools.partial(turn_kernel, final, sz),
         [*around_all[final], hot, hot_t, geo, *weights, read_weight.reshape(1, channels), seeds],
-        [sums, whole, whole],
+        [whole_more, whole_more],
         "turn",
     )
-    every = [sums_last]
     for tick in reversed(range(segments - 1)):
         ways = (2, 0) if tick % 2 else (0, -2)
         up = [hop(part, tick + 1, tick, -by) for part, by in zip(parts, ways)]
-        sums_now, *parts = call(
-            functools.partial(backward_kernel, tick, sz, slabs),
-            [*up, kept[tick], *around_all[tick], hot, hot_t, geo, *weights] + ([] if tick else every),
-            [sums, whole, whole] if tick else [sums],
+        parts = call(
+            functools.partial(backward_kernel, tick, sz),
+            [*up, kept[tick], *around_all[tick], hot, hot_t, geo, *weights],
+            [whole_more, whole_more] if tick else [slab_sums] * 4,
             "backward",
         )
-        every.insert(0, sums_now)
-    total = lax.psum(every[0][:4], axes).reshape(4, batches, slabs * per_slab)
-    mine = lax.dynamic_slice_in_dim(total, lax.axis_index("space") * per_slab, per_slab, 2)
-    return mine[3], mine[:3].transpose(1, 0, 2)
+    here, theirs, straight, cross = parts
+    theirs = within(theirs, lambda odd, i: i + 1 - 2 * (i % 2), 1)
+    straight = within(straight, lambda odd, i: i - 2 if i % 2 else i + 2, 1)
+    cross = within(cross, lambda odd, i: i + 1 if i % 2 else i - 1, 1)
+    (both,) = call(join_kernel, [here, theirs, straight, cross], [shape((rows, channels), F32)], "join")
+    copies = [both] + [hop(both, 0, stop, 0) for stop in range(1, segments)]
+    energies, gradients = call(
+        close_kernel, copies, [shape((batches, per_slab), F32), shape((3, batches, per_slab), F32)], "close"
+    )
+    return energies, gradients.transpose(1, 0, 2)
 
 
 def solution(mesh):

time: 125 us -> 100 us (0.80)
  blocking collectives: 38.5 us -> 0 us
  starting transfers between devices: 17.3 us -> 28.3 us
  waiting for transfers between devices: 53.1 us -> 61.1 us
  local copies, waits for them, and re-layouts: 4.24 us -> 0.01 us
    psum x1 -> x0, blocking collectives: 38.5 us -> none  [on_device(): total = lax.psum(every[0][:4], axes).reshape(4, batches, slabs * per_slab)]
    ppermute x3 -> x6, starting transfers between devices: 5.23 us -> 12.9 us  [within(): return lax.ppermute(value, axes, pairs)]
    ppermute x12 -> x15, waiting for transfers between devices: 50.4 us -> 55.5 us  [hop(): return lax.ppermute(value, axes, pairs)]
    ppermute x12 -> x15, starting transfers between devices: 12 us -> 15.4 us  [hop(): return lax.ppermute(value, axes, pairs)]
    ppermute x3 -> x6, waiting for transfers between devices: 2.68 us -> 5.56 us  [within(): return lax.ppermute(value, axes, pairs)]
    unnamed x12 -> x4, local copies, waits for them, and re-layouts: 2.86 us -> 0.01 us
    pallas_call x10 -> x12, Pallas kernels: 10.5 us -> 9.4 us  [call(): pl.pallas_call(body, out_shape=shapes, in_specs=[pl.BlockSpec(memory_spac...]
  transfers between devices with their start and end apart: 15 -> 21, of which waited for: 5 -> 8; matrix products, arithmetic and copies ran while one was open for 0% -> 0% of each run, Pallas kernels for 2% -> 3%
where the time goes in v3:
time: 100 us; the launch traced here: 99.7 us
  waiting for transfers between devices  61.1 us (61%)
  starting transfers between devices  28.3 us (28%)
  Pallas kernels  9.4 us (9%)
    ppermute x15, waiting for transfers between devices, hop(): return lax.ppermute(value, axes, pairs)  55.5 us
    ppermute x15, starting transfers between devices, hop(): return lax.ppermute(value, axes, pairs)  15.4 us
    ppermute x6, starting transfers between devices, within(): return lax.ppermute(value, axes, pairs)  12.9 us
    pallas_call x12, Pallas kernels, call(): pl.pallas_call(body, out_shape=shapes, in_specs=[pl.BlockSpec(memory_spac...  9.4 us
    ppermute x6, waiting for transfers between devices, within(): return lax.ppermute(value, axes, pairs)  5.56 us
  transfers between devices with their start and end apart: 21, of which 8 were waited for; matrix products, arithmetic and copies ran while one was open for 0% of the time, Pallas kernels for 3%

profile of v3, /device:TPU:0, one launch (start us, length us, event | category | flops | bytes accessed | tf_op | source)
XLA Modules:
  0.0 99.7 jit_solution(1113277878034538262)
XLA Ops:
  0.6 1.2 %pack.1 = (bf16[30,8,128]{2,1,0:T(8,128)(2,1)S(1)}, bf16[30,8,128]{2,1,0:T(8,128)(2,1)S(1)}) custom-call(bf16[2,29,8,128]{3,2,1,0:T(8,128)(2,1)} %bitcast.11, f32[3,2,8]{2,1,0:T(2,128)} %bitcast.12, s32[2,8]{1,0:T(2,128)} %species_hbm.1, s32[2,8,8]{2,1,0:T(8,128)} %sources_hbm.1, f32[2,8]{1,0:T(2,128)} %grad_hbm.1, bf16[100,128]{1,0:T(8,128)(2,1)} %table_hbm.1), custom_call_target="tpu_custom_call" | custom-call | tf_op jit(solution)/shard_map/pack/pallas_call | solution.py:525
  1.8 5.1 %collective-permute-start.1 = (bf16[30,8,128]{2,1,0:T(8,128)(2,1)S(1)}, bf16[30,8,128]{2,1,0:T(8,128)(2,1)S(1)}, u32[]{:S(2)}, u32[]{:S(2)}) collective-permute-start(bf16[30,8,128]{2,1,0:T(8,128)(2,1)S(1)} %get-tuple-element.31.mine_ref), channel_id=1, source_target_pairs={{0,6},{1,3},{2,0},{3,5},{4,2},{5,7},{6,4},{7,1},{8,14},{9,15},{10,... | collective-permute-start | bytes 184328 | tf_op jit(solution)/shard_map/ppermute | solution.py:562
  6.9 0.0 collective-permute-start.2
  7.0 0.0 collective-permute-start
  7.0 2.7 %stage.1 = (bf16[896,896]{1,0:T(8,128)(2,1)S(1)}, bf16[2,768,768]{2,1,0:T(8,128)(2,1)S(1)}, bf16[2,640,640]{2,1,0:T(8,128)(2,1)S(1)}) custom-call(bf16[896,896]{1,0:T(8,128)(2,1)} %bitcast.10, bf16[2,768,768]{2,1,0:T(8,128)(2,1)} %bitcast.8, bf16[2,640,640]{2,1,0:T(8,128)(2,1)} %bitcast.9), custom_call_target="tpu_custom_call" | custom-call | tf_op jit(solution)/shard_map/stage/pallas_call | solution.py:525
  9.6 0.0 collective-permute-done.1.straight_ref
  9.6 2.8 %collective-permute-done.2.cross_ref = bf16[30,8,128]{2,1,0:T(8,128)(2,1)S(1)} collective-permute-done((bf16[30,8,128]{2,1,0:T(8,128)(2,1)S(1)}, bf16[30,8,128]{2,1,0:T(8,128)(2,1)S(1)}, u32[]{:S(2)}, u32[]{:S(2)}) %collective-permute-start.2) | collective-permute-done | bytes 61472 | tf_op jit(solution)/shard_map/ppermute | solution.py:562
  12.4 0.0 collective-permute-done.partner_ref
  12.4 0.5 open.1
  12.9 1.7 %forward.3 = (bf16[29,16,128]{2,1,0:T(8,128)(2,1)S(1)}, f32[29,16,128]{2,1,0:T(8,128)S(1)}) custom-call(bf16[29,16,128]{2,1,0:T(8,128)(2,1)S(1)} %get-tuple-element.33.low_ref, bf16[29,16,128]{2,1,0:T(8,128)(2,1)S(1)} %get-tuple-element.34.high_ref, bf16[128,32]{1,0:T(8,128)(2,1)S(1)} %get-tuple-element.35.hot_ref, ...), custom_call_target="tpu_custom_call" | custom-call | tf_op jit(solution)/shard_map/forward/pallas_call | solution.py:525
  14.6 2.2 %collective-permute-start.4 = (bf16[29,16,128]{2,1,0:T(8,128)(2,1)S(1)}, bf16[29,16,128]{2,1,0:T(8,128)(2,1)S(1)}, u32[]{:S(2)}, u32[]{:S(2)}) collective-permute-start(bf16[29,16,128]{2,1,0:T(8,128)(2,1)S(1)} %get-tuple-element.40), channel_id=1, source_target_pairs={{0,14},{1,15},{2,8},{3,9},{4,10},{5,11},{6,12},{7,13}} | collective-permute-start | bytes 356360 | tf_op jit(solution)/shard_map/ppermute | solution.py:566
  16.9 1.3 %collective-permute-start.3 = (bf16[29,16,128]{2,1,0:T(8,128)(2,1)S(1)}, bf16[29,16,128]{2,1,0:T(8,128)(2,1)S(1)}, u32[]{:S(2)}, u32[]{:S(2)}) collective-permute-start(bf16[29,16,128]{2,1,0:T(8,128)(2,1)S(1)} %get-tuple-element.40), channel_id=1, source_target_pairs={{0,8},{1,9},{2,10},{3,11},{4,12},{5,13},{6,14},{7,15}} | collective-permute-start | bytes 356360 | tf_op jit(solution)/shard_map/ppermute | solution.py:566
  18.2 1.8 %collective-permute-done.4.high_ref = bf16[29,16,128]{2,1,0:T(8,128)(2,1)S(1)} collective-permute-done((bf16[29,16,128]{2,1,0:T(8,128)(2,1)S(1)}, bf16[29,16,128]{2,1,0:T(8,128)(2,1)S(1)}, u32[]{:S(2)}, u32[]{:S(2)}) %collective-permute-start.4) | collective-permute-done | bytes 118816 | tf_op jit(solution)/shard_map/ppermute | solution.py:566
  20.0 1.3 %collective-permute-done.3.low_ref = bf16[29,16,128]{2,1,0:T(8,128)(2,1)S(1)} collective-permute-done((bf16[29,16,128]{2,1,0:T(8,128)(2,1)S(1)}, bf16[29,16,128]{2,1,0:T(8,128)(2,1)S(1)}, u32[]{:S(2)}, u32[]{:S(2)}) %collective-permute-start.3) | collective-permute-done | bytes 118816 | tf_op jit(solution)/shard_map/ppermute | solution.py:566
  21.3 0.8 collective-permute-start.6
  22.1 0.7 collective-permute-start.5
  22.7 0.0 collective-permute-done.6.high_ref
  22.7 0.0 collective-permute-done.5.low_ref
  22.8 0.7 collective-permute-start.8
  23.5 0.7 collective-permute-start.7
  24.1 0.0 collective-permute-done.8.high_ref
  24.1 0.0 collective-permute-done.7.low_ref
  24.2 0.7 collective-permute-start.9
  24.9 0.7 collective-permute-start.10
  25.5 0.0 collective-permute-done.9.up_low_ref
  25.6 0.0 collective-permute-done.10.up_high_ref
  25.6 0.7 collective-permute-start.11
  26.3 0.7 collective-permute-start.12
  27.0 0.0 collective-permute-done.12.up_high_ref
  27.0 0.2 backward.4
  27.2 1.3 %collective-permute-start.13 = (bf16[30,16,128]{2,1,0:T(8,128)(2,1)S(1)}, bf16[30,16,128]{2,1,0:T(8,128)(2,1)S(1)}, u32[]{:S(2)}, u32[]{:S(2)}) collective-permute-start(bf16[30,16,128]{2,1,0:T(8,128)(2,1)S(1)} %get-tuple-element.51), channel_id=1, source_target_pairs={{8,0},{9,1},{10,2},{11,3},{12,4},{13,5},{14,6},{15,7}} | collective-permute-start | bytes 368648 | tf_op jit(solution)/shard_map/ppermute | solution.py:566
  28.5 1.3 %collective-permute-start.14 = (bf16[30,16,128]{2,1,0:T(8,128)(2,1)S(1)}, bf16[30,16,128]{2,1,0:T(8,128)(2,1)S(1)}, u32[]{:S(2)}, u32[]{:S(2)}) collective-permute-start(bf16[30,16,128]{2,1,0:T(8,128)(2,1)S(1)} %get-tuple-element.52), channel_id=1, source_target_pairs={{8,2},{9,3},{10,4},{11,5},{12,6},{13,7},{14,0},{15,1}} | collective-permute-start | bytes 368648 | tf_op jit(solution)/shard_map/ppermute | solution.py:566
  29.8 45.2 %collective-permute-done.13.up_low_ref = bf16[30,16,128]{2,1,0:T(8,128)(2,1)S(1)} collective-permute-done((bf16[30,16,128]{2,1,0:T(8,128)(2,1)S(1)}, bf16[30,16,128]{2,1,0:T(8,128)(2,1)S(1)}, u32[]{:S(2)}, u32[]{:S(2)}) %collective-permute-start.13) | collective-permute-done | bytes 122912 | tf_op jit(solution)/shard_map/ppermute | solution.py:566
  75.0 5.8 %collective-permute-done.14.up_high_ref = bf16[30,16,128]{2,1,0:T(8,128)(2,1)S(1)} collective-permute-done((bf16[30,16,128]{2,1,0:T(8,128)(2,1)S(1)}, bf16[30,16,128]{2,1,0:T(8,128)(2,1)S(1)}, u32[]{:S(2)}, u32[]{:S(2)}) %collective-permute-start.14) | collective-permute-done | bytes 122912 | tf_op jit(solution)/shard_map/ppermute | solution.py:566
  80.9 2.3 %backward.5 = (f32[8,128]{1,0:T(8,128)S(1)}, f32[8,128]{1,0:T(8,128)S(1)}, f32[8,128]{1,0:T(8,128)S(1)}, f32[8,128]{1,0:T(8,128)S(1)}) custom-call(bf16[30,16,128]{2,1,0:T(8,128)(2,1)S(1)} %collective-permute-done.13.up_low_ref, bf16[30,16,128]{2,1,0:T(8,128)(2,1)S(1)} %collective-permute-done.14.up_high_ref, ...), custom_call_target="tpu_custom_call" | custom-call | tf_op jit(solution)/shard_map/backward/pallas_call | solution.py:525
  83.2 1.9 %collective-permute-start.15 = (f32[8,128]{1,0:T(8,128)S(1)}, f32[8,128]{1,0:T(8,128)S(1)}, u32[]{:S(2)}, u32[]{:S(2)}) collective-permute-start(f32[8,128]{1,0:T(8,128)S(1)} %get-tuple-element.55), channel_id=1, source_target_pairs={{0,1},{1,0},{2,3},{3,2},{4,5},{5,4},{6,7},{7,6}} | collective-permute-start | bytes 12296 | tf_op jit(solution)/shard_map/ppermute | solution.py:562
  85.1 1.9 %collective-permute-start.16 = (f32[8,128]{1,0:T(8,128)S(1)}, f32[8,128]{1,0:T(8,128)S(1)}, u32[]{:S(2)}, u32[]{:S(2)}) collective-permute-start(f32[8,128]{1,0:T(8,128)S(1)} %get-tuple-element.56), channel_id=1, source_target_pairs={{0,2},{1,7},{2,4},{3,1},{4,6},{5,3},{6,0},{7,5}} | collective-permute-start | bytes 12296 | tf_op jit(solution)/shard_map/ppermute | solution.py:562
  87.1 3.9 %collective-permute-start.17 = (f32[8,128]{1,0:T(8,128)S(1)}, f32[8,128]{1,0:T(8,128)S(1)}, u32[]{:S(2)}, u32[]{:S(2)}) collective-permute-start(f32[8,128]{1,0:T(8,128)S(1)} %get-tuple-element.57), channel_id=1, source_target_pairs={{0,7},{1,2},{2,1},{3,4},{4,3},{5,6},{6,5},{7,0}} | collective-permute-start | bytes 12296 | tf_op jit(solution)/shard_map/ppermute | solution.py:562
  91.0 0.0 collective-permute-done.15.theirs_ref
  91.0 1.4 %collective-permute-done.16.straight_ref = f32[8,128]{1,0:T(8,128)S(1)} collective-permute-done((f32[8,128]{1,0:T(8,128)S(1)}, f32[8,128]{1,0:T(8,128)S(1)}, u32[]{:S(2)}, u32[]{:S(2)}) %collective-permute-start.16) | collective-permute-done | bytes 4128 | tf_op jit(solution)/shard_map/ppermute | solution.py:562
  92.4 1.4 %collective-permute-done.17.cross_ref = f32[8,128]{1,0:T(8,128)S(1)} collective-permute-done((f32[8,128]{1,0:T(8,128)S(1)}, f32[8,128]{1,0:T(8,128)S(1)}, u32[]{:S(2)}, u32[]{:S(2)}) %collective-permute-start.17) | collective-permute-done | bytes 4128 | tf_op jit(solution)/shard_map/ppermute | solution.py:562
  93.8 1.3 %collective-permute-start.20 = (f32[16,128]{1,0:T(8,128)S(1)}, f32[16,128]{1,0:T(8,128)S(1)}, u32[]{:S(2)}, u32[]{:S(2)}) collective-permute-start(f32[16,128]{1,0:T(8,128)S(1)} %join.1.refs_0_), channel_id=1, source_target_pairs={{0,24},{1,25},{2,26},{3,27},{4,28},{5,29},{6,30},{7,31}} | collective-permute-start | bytes 24584 | tf_op jit(solution)/shard_map/ppermute | solution.py:566
  95.1 1.3 %collective-permute-start.19 = (f32[16,128]{1,0:T(8,128)S(1)}, f32[16,128]{1,0:T(8,128)S(1)}, u32[]{:S(2)}, u32[]{:S(2)}) collective-permute-start(f32[16,128]{1,0:T(8,128)S(1)} %join.1.refs_0_), channel_id=1, source_target_pairs={{0,16},{1,17},{2,18},{3,19},{4,20},{5,21},{6,22},{7,23}} | collective-permute-start | bytes 24584 | tf_op jit(solution)/shard_map/ppermute | solution.py:566
  96.4 1.3 %collective-permute-start.18 = (f32[16,128]{1,0:T(8,128)S(1)}, f32[16,128]{1,0:T(8,128)S(1)}, u32[]{:S(2)}, u32[]{:S(2)}) collective-permute-start(f32[16,128]{1,0:T(8,128)S(1)} %join.1.refs_0_), channel_id=1, source_target_pairs={{0,8},{1,9},{2,10},{3,11},{4,12},{5,13},{6,14},{7,15}} | collective-permute-start | bytes 24584 | tf_op jit(solution)/shard_map/ppermute | solution.py:566
  97.7 0.0 collective-permute-done.20.refs_3_
  97.7 0.0 collective-permute-done.19.refs_2_
  97.7 1.3 %collective-permute-done.18.refs_1_ = f32[16,128]{1,0:T(8,128)S(1)} collective-permute-done((f32[16,128]{1,0:T(8,128)S(1)}, f32[16,128]{1,0:T(8,128)S(1)}, u32[]{:S(2)}, u32[]{:S(2)}) %collective-permute-start.18) | collective-permute-done | bytes 8224 | tf_op jit(solution)/shard_map/ppermute | solution.py:566
  99.0 0.7 close.1
  (10 shorter events, 0.1 us)
Async XLA Ops:
  1.8 7.8 %collective-permute-start.1 = (bf16[30,8,128]{2,1,0:T(8,128)(2,1)S(1)}, bf16[30,8,128]{2,1,0:T(8,128)(2,1)S(1)}, u32[]{:S(2)}, u32[]{:S(2)}) collective-permute-start(bf16[30,8,128]{2,1,0:T(8,128)(2,1)S(1)} %get-tuple-element.31.mine_ref), channel_id=1, source_target_pairs={{0,6},{1,3},{2,0},{3,5},{4,2},{5,7},{6,4},{7,1},{8,14},{9,15},{10,... | collective-permute-start | bytes 184328 | tf_op jit(solution)/shard_map/ppermute | solution.py:562
  6.9 5.4 %collective-permute-start.2 = (bf16[30,8,128]{2,1,0:T(8,128)(2,1)S(1)}, bf16[30,8,128]{2,1,0:T(8,128)(2,1)S(1)}, u32[]{:S(2)}, u32[]{:S(2)}) collective-permute-start(bf16[30,8,128]{2,1,0:T(8,128)(2,1)S(1)} %get-tuple-element.32), channel_id=1, source_target_pairs={{0,7},{1,2},{2,1},{3,4},{4,3},{5,6},{6,5},{7,0},{8,15},{9,14},{10,... | collective-permute-start | bytes 184328 | tf_op jit(solution)/shard_map/ppermute | solution.py:562
  7.0 5.4 %collective-permute-start = (bf16[30,8,128]{2,1,0:T(8,128)(2,1)S(1)}, bf16[30,8,128]{2,1,0:T(8,128)(2,1)S(1)}, u32[]{:S(2)}, u32[]{:S(2)}) collective-permute-start(bf16[30,8,128]{2,1,0:T(8,128)(2,1)S(1)} %get-tuple-element.32), channel_id=1, source_target_pairs={{0,1},{1,0},{2,3},{3,2},{4,5},{5,4},{6,7},{7,6},{8,9},{9,8},{10,11... | collective-permute-start | bytes 184328 | tf_op jit(solution)/shard_map/ppermute | solution.py:562
  7.0 5.4 %copy-start = (f32[1,128]{1,0:T(1,128)S(1)}, f32[1,128]{1,0:T(1,128)}, u32[]{:S(2)}) copy-start(f32[1,128]{1,0:T(1,128)} %rate_ref.1) | copy-start | bytes 1540
  14.6 5.3 %collective-permute-start.4 = (bf16[29,16,128]{2,1,0:T(8,128)(2,1)S(1)}, bf16[29,16,128]{2,1,0:T(8,128)(2,1)S(1)}, u32[]{:S(2)}, u32[]{:S(2)}) collective-permute-start(bf16[29,16,128]{2,1,0:T(8,128)(2,1)S(1)} %get-tuple-element.40), channel_id=1, source_target_pairs={{0,14},{1,15},{2,8},{3,9},{4,10},{5,11},{6,12},{7,13}} | collective-permute-start | bytes 356360 | tf_op jit(solution)/shard_map/ppermute | solution.py:566
  16.9 4.4 %collective-permute-start.3 = (bf16[29,16,128]{2,1,0:T(8,128)(2,1)S(1)}, bf16[29,16,128]{2,1,0:T(8,128)(2,1)S(1)}, u32[]{:S(2)}, u32[]{:S(2)}) collective-permute-start(bf16[29,16,128]{2,1,0:T(8,128)(2,1)S(1)} %get-tuple-element.40), channel_id=1, source_target_pairs={{0,8},{1,9},{2,10},{3,11},{4,12},{5,13},{6,14},{7,15}} | collective-permute-start | bytes 356360 | tf_op jit(solution)/shard_map/ppermute | solution.py:566
  21.3 2.9 %copy-start.1 = (f32[128]{0:T(128)S(1)}, f32[128]{0:T(128)}, u32[]{:S(2)}) copy-start(f32[128]{0:T(128)} %param.20) | copy-start | bytes 1540
  21.3 1.5 %collective-permute-start.6 = (bf16[29,16,128]{2,1,0:T(8,128)(2,1)S(1)}, bf16[29,16,128]{2,1,0:T(8,128)(2,1)S(1)}, u32[]{:S(2)}, u32[]{:S(2)}) collective-permute-start(bf16[29,16,128]{2,1,0:T(8,128)(2,1)S(1)} %get-tuple-element.41), channel_id=1, source_target_pairs={{8,16},{9,17},{10,18},{11,19},{12,20},{13,21},{14,22},{15,23}} | collective-permute-start | bytes 356360 | tf_op jit(solution)/shard_map/ppermute | solution.py:566
  22.1 0.7 collective-permute-start.5
  22.8 1.4 %collective-permute-start.8 = (bf16[29,16,128]{2,1,0:T(8,128)(2,1)S(1)}, bf16[29,16,128]{2,1,0:T(8,128)(2,1)S(1)}, u32[]{:S(2)}, u32[]{:S(2)}) collective-permute-start(bf16[29,16,128]{2,1,0:T(8,128)(2,1)S(1)} %get-tuple-element.42), channel_id=1, source_target_pairs={{16,30},{17,31},{18,24},{19,25},{20,26},{21,27},{22,28},{23,29}} | collective-permute-start | bytes 356360 | tf_op jit(solution)/shard_map/ppermute | solution.py:566
  23.5 0.7 collective-permute-start.7
  24.2 1.4 %collective-permute-start.9 = (bf16[30,16,128]{2,1,0:T(8,128)(2,1)S(1)}, bf16[30,16,128]{2,1,0:T(8,128)(2,1)S(1)}, u32[]{:S(2)}, u32[]{:S(2)}) collective-permute-start(bf16[30,16,128]{2,1,0:T(8,128)(2,1)S(1)} %get-tuple-element.45), channel_id=1, source_target_pairs={{24,16},{25,17},{26,18},{27,19},{28,20},{29,21},{30,22},{31,23}} | collective-permute-start | bytes 368648 | tf_op jit(solution)/shard_map/ppermute | solution.py:566
  24.9 0.7 collective-permute-start.10
  25.6 1.4 %collective-permute-start.11 = (bf16[30,16,128]{2,1,0:T(8,128)(2,1)S(1)}, bf16[30,16,128]{2,1,0:T(8,128)(2,1)S(1)}, u32[]{:S(2)}, u32[]{:S(2)}) collective-permute-start(bf16[30,16,128]{2,1,0:T(8,128)(2,1)S(1)} %get-tuple-element.48), channel_id=1, source_target_pairs={{16,14},{17,15},{18,8},{19,9},{20,10},{21,11},{22,12},{23,13}} | collective-permute-start | bytes 368648 | tf_op jit(solution)/shard_map/ppermute | solution.py:566
  26.3 0.7 collective-permute-start.12
  27.2 47.8 %collective-permute-start.13 = (bf16[30,16,128]{2,1,0:T(8,128)(2,1)S(1)}, bf16[30,16,128]{2,1,0:T(8,128)(2,1)S(1)}, u32[]{:S(2)}, u32[]{:S(2)}) collective-permute-start(bf16[30,16,128]{2,1,0:T(8,128)(2,1)S(1)} %get-tuple-element.51), channel_id=1, source_target_pairs={{8,0},{9,1},{10,2},{11,3},{12,4},{13,5},{14,6},{15,7}} | collective-permute-start | bytes 368648 | tf_op jit(solution)/shard_map/ppermute | solution.py:566
  28.5 52.4 %collective-permute-start.14 = (bf16[30,16,128]{2,1,0:T(8,128)(2,1)S(1)}, bf16[30,16,128]{2,1,0:T(8,128)(2,1)S(1)}, u32[]{:S(2)}, u32[]{:S(2)}) collective-permute-start(bf16[30,16,128]{2,1,0:T(8,128)(2,1)S(1)} %get-tuple-element.52), channel_id=1, source_target_pairs={{8,2},{9,3},{10,4},{11,5},{12,6},{13,7},{14,0},{15,1}} | collective-permute-start | bytes 368648 | tf_op jit(solution)/shard_map/ppermute | solution.py:566
  83.2 7.8 %collective-permute-start.15 = (f32[8,128]{1,0:T(8,128)S(1)}, f32[8,128]{1,0:T(8,128)S(1)}, u32[]{:S(2)}, u32[]{:S(2)}) collective-permute-start(f32[8,128]{1,0:T(8,128)S(1)} %get-tuple-element.55), channel_id=1, source_target_pairs={{0,1},{1,0},{2,3},{3,2},{4,5},{5,4},{6,7},{7,6}} | collective-permute-start | bytes 12296 | tf_op jit(solution)/shard_map/ppermute | solution.py:562
  85.1 7.3 %collective-permute-start.16 = (f32[8,128]{1,0:T(8,128)S(1)}, f32[8,128]{1,0:T(8,128)S(1)}, u32[]{:S(2)}, u32[]{:S(2)}) collective-permute-start(f32[8,128]{1,0:T(8,128)S(1)} %get-tuple-element.56), channel_id=1, source_target_pairs={{0,2},{1,7},{2,4},{3,1},{4,6},{5,3},{6,0},{7,5}} | collective-permute-start | bytes 12296 | tf_op jit(solution)/shard_map/ppermute | solution.py:562
  87.1 6.7 %collective-permute-start.17 = (f32[8,128]{1,0:T(8,128)S(1)}, f32[8,128]{1,0:T(8,128)S(1)}, u32[]{:S(2)}, u32[]{:S(2)}) collective-permute-start(f32[8,128]{1,0:T(8,128)S(1)} %get-tuple-element.57), channel_id=1, source_target_pairs={{0,7},{1,2},{2,1},{3,4},{4,3},{5,6},{6,5},{7,0}} | collective-permute-start | bytes 12296 | tf_op jit(solution)/shard_map/ppermute | solution.py:562
  93.8 3.9 %collective-permute-start.20 = (f32[16,128]{1,0:T(8,128)S(1)}, f32[16,128]{1,0:T(8,128)S(1)}, u32[]{:S(2)}, u32[]{:S(2)}) collective-permute-start(f32[16,128]{1,0:T(8,128)S(1)} %join.1.refs_0_), channel_id=1, source_target_pairs={{0,24},{1,25},{2,26},{3,27},{4,28},{5,29},{6,30},{7,31}} | collective-permute-start | bytes 24584 | tf_op jit(solution)/shard_map/ppermute | solution.py:566
  95.1 2.6 %collective-permute-start.19 = (f32[16,128]{1,0:T(8,128)S(1)}, f32[16,128]{1,0:T(8,128)S(1)}, u32[]{:S(2)}, u32[]{:S(2)}) collective-permute-start(f32[16,128]{1,0:T(8,128)S(1)} %join.1.refs_0_), channel_id=1, source_target_pairs={{0,16},{1,17},{2,18},{3,19},{4,20},{5,21},{6,22},{7,23}} | collective-permute-start | bytes 24584 | tf_op jit(solution)/shard_map/ppermute | solution.py:566
  96.4 2.6 %collective-permute-start.18 = (f32[16,128]{1,0:T(8,128)S(1)}, f32[16,128]{1,0:T(8,128)S(1)}, u32[]{:S(2)}, u32[]{:S(2)}) collective-permute-start(f32[16,128]{1,0:T(8,128)S(1)} %join.1.refs_0_), channel_id=1, source_target_pairs={{0,8},{1,9},{2,10},{3,11},{4,12},{5,13},{6,14},{7,15}} | collective-permute-start | bytes 24584 | tf_op jit(solution)/shard_map/ppermute | solution.py:566

commit v4 on v3

--- a/solution.py
+++ b/solution.py
@@ -446,15 +446,23 @@
         geo_ref[n * edges : (n + 1) * edges, :] = value
 
 
-def stage_kernel(zero_hbm, one_hbm, two_hbm, zero_ref, one_ref, two_ref, sems):
-    copies = [
-        pltpu.make_async_copy(source, target, sems.at[n])
-        for n, (source, target) in enumerate(((zero_hbm, zero_ref), (one_hbm, one_ref), (two_hbm, two_ref)))
-    ]
-    for copy in copies:
-        copy.start()
-    for copy in copies:
-        copy.wait()
+def works_late():
+    return (lax.axis_index("segment") == 0) & (lax.rem(lax.axis_index("space"), 2) == 1)
+
+
+def stage_kernel(late, zero_hbm, one_hbm, two_hbm, *more):
+    zero_ref, one_ref, two_ref, sems = more[-4:]
+
+    @pl.when(works_late() == late)
+    def _():
+        pairs = [(zero_hbm, zero_ref)]
+        for source, target in ((one_hbm, one_ref), (two_hbm, two_ref)):
+            pairs += [(source.at[n], target.at[n]) for n in range(2)]
+        copies = [pltpu.make_async_copy(source, target, sems.at[n]) for n, (source, target) in enumerate(pairs)]
+        for copy in copies:
+            copy.start()
+        for copy in copies:
+            copy.wait()
 
 
 def forward_kernel(
@@ -519,7 +527,7 @@
             share(moved, outs)
 
 
-def call(body, operands, shapes, name, spaces=None, scratch=()):
+def call(body, operands, shapes, name, spaces=None, scratch=(), aliases=None):
     spaces = spaces or [pltpu.VMEM] * len(operands)
     operands = [pltpu.with_memory_space_constraint(value, space) for value, space in zip(operands, spaces)]
     return pl.pallas_call(
@@ -528,6 +536,7 @@
         in_specs=[pl.BlockSpec(memory_space=space) for space in spaces],
         out_specs=[pl.BlockSpec(memory_space=pltpu.VMEM) for _ in shapes],
         scratch_shapes=list(scratch),
+        input_output_aliases=aliases or {},
         compiler_params=pltpu.CompilerParams(vmem_limit_bytes=VMEM_LIMIT),
         name=name,
     )(*operands)
@@ -576,11 +585,11 @@
     partner = within(other, lambda odd, i: i + 1 - 2 * (i % 2), segments)
     straight = within(mine, lambda odd, i: i - 2 if odd or i % 2 == 0 else i + 2, segments)
     cross = within(other, lambda odd, i: i - 1 if i % 2 == 0 else i - 3 if odd else i + 1, segments)
-    weights = [zero_weight[0], one_weight[0], two_weight[0]]
-    weights = call(
-        stage_kernel, weights, [pltpu.VMEM(w.shape, w.dtype) for w in weights], "stage", [pltpu.HBM] * 3,
-        [pltpu.SemaphoreType.DMA((3,))],
-    )
+    stored = [zero_weight[0], one_weight[0], two_weight[0]]
+    spaces = [pltpu.HBM] * 3
+    on_chip = [pltpu.VMEM(w.shape, w.dtype) for w in stored]
+    sems = [pltpu.SemaphoreType.DMA((5,))]
+    weights = call(functools.partial(stage_kernel, False), stored, on_chip, "stage", spaces, sems)
     whole = shape((coefs, rows, channels), BF16)
     low, high, hot, hot_t, geo, seeds = call(
         functools.partial(open_kernel, slabs, neighbours),
@@ -590,6 +599,10 @@
             shape((10 * edges, channels), F32), shape((rows, channels), F32),
         ],
         "open",
+    )
+    weights = call(
+        functools.partial(stage_kernel, True), [*stored, *weights, seeds], on_chip, "stage_late",
+        spaces + [pltpu.VMEM] * 4, sems, {3: 0, 4: 1, 5: 2},
     )
     around_all = [(low, high)]
     kept = []

time: 100 us -> 102 us (1.020)
  waiting for transfers between devices: 61.1 us -> 63.2 us
    ppermute x15, waiting for transfers between devices: 55.5 us -> 56.8 us  [hop(): return lax.ppermute(value, axes, pairs)]
    pallas_call x12 -> x13, Pallas kernels: 9.4 us -> 9.44 us  [call(): pl.pallas_call(body, out_shape=shapes, in_specs=[pl.BlockSpec(memory_spac...]
where the time goes in v4:
time: 102 us; the launch traced here: 101 us
  waiting for transfers between devices  63.2 us (62%)
  starting transfers between devices  27.6 us (27%)
  Pallas kernels  9.44 us (9%)
    ppermute x15, waiting for transfers between devices, hop(): return lax.ppermute(value, axes, pairs)  56.8 us
    ppermute x15, starting transfers between devices, hop(): return lax.ppermute(value, axes, pairs)  15.4 us
    ppermute x6, starting transfers between devices, within(): return lax.ppermute(value, axes, pairs)  12.1 us
    pallas_call x13, Pallas kernels, call(): pl.pallas_call(body, out_shape=shapes, in_specs=[pl.BlockSpec(memory_spac...  9.44 us
    ppermute x6, waiting for transfers between devices, within(): return lax.ppermute(value, axes, pairs)  6.3 us
  transfers between devices with their start and end apart: 21, of which 8 were waited for; matrix products, arithmetic and copies ran while one was open for 0% of the time, Pallas kernels for 3%

profile of v4, /device:TPU:0, one launch (start us, length us, event | category | flops | bytes accessed | tf_op | source)
XLA Modules:
  0.0 101.1 jit_solution(2954770420363095051)
XLA Ops:
  0.6 1.2 %pack.1 = (bf16[30,8,128]{2,1,0:T(8,128)(2,1)S(1)}, bf16[30,8,128]{2,1,0:T(8,128)(2,1)S(1)}) custom-call(bf16[2,29,8,128]{3,2,1,0:T(8,128)(2,1)} %bitcast.14, f32[3,2,8]{2,1,0:T(2,128)} %bitcast.15, s32[2,8]{1,0:T(2,128)} %species_hbm.1, s32[2,8,8]{2,1,0:T(8,128)} %sources_hbm.1, f32[2,8]{1,0:T(2,128)} %grad_hbm.1, bf16[100,128]{1,0:T(8,128)(2,1)} %table_hbm.1), custom_call_target="tpu_custom_call" | custom-call | tf_op jit(solution)/shard_map/pack/pallas_call | solution.py:533
  1.8 5.1 %collective-permute-start.1 = (bf16[30,8,128]{2,1,0:T(8,128)(2,1)S(1)}, bf16[30,8,128]{2,1,0:T(8,128)(2,1)S(1)}, u32[]{:S(2)}, u32[]{:S(2)}) collective-permute-start(bf16[30,8,128]{2,1,0:T(8,128)(2,1)S(1)} %get-tuple-element.34.mine_ref), channel_id=1, source_target_pairs={{0,6},{1,3},{2,0},{3,5},{4,2},{5,7},{6,4},{7,1},{8,14},{9,15},{10,... | collective-permute-start | bytes 184328 | tf_op jit(solution)/shard_map/ppermute | solution.py:571
  6.9 0.0 collective-permute-start.2
  7.0 0.0 collective-permute-start
  7.0 2.6 %stage.1 = (bf16[896,896]{1,0:T(8,128)(2,1)S(1)}, bf16[2,768,768]{2,1,0:T(8,128)(2,1)S(1)}, bf16[2,640,640]{2,1,0:T(8,128)(2,1)S(1)}) custom-call(bf16[896,896]{1,0:T(8,128)(2,1)} %bitcast.12, bf16[2,768,768]{2,1,0:T(8,128)(2,1)} %bitcast.8, bf16[2,640,640]{2,1,0:T(8,128)(2,1)} %bitcast.10), custom_call_target="tpu_custom_call" | custom-call | tf_op jit(solution)/shard_map/stage/pallas_call | solution.py:533
  9.6 0.0 collective-permute-done.1.straight_ref
  9.6 2.8 %collective-permute-done.2.cross_ref = bf16[30,8,128]{2,1,0:T(8,128)(2,1)S(1)} collective-permute-done((bf16[30,8,128]{2,1,0:T(8,128)(2,1)S(1)}, bf16[30,8,128]{2,1,0:T(8,128)(2,1)S(1)}, u32[]{:S(2)}, u32[]{:S(2)}) %collective-permute-start.2) | collective-permute-done | bytes 61472 | tf_op jit(solution)/shard_map/ppermute | solution.py:571
  12.4 0.0 collective-permute-done.partner_ref
  12.4 0.5 open.1
  12.9 0.1 stage_late.1
  13.0 1.7 %forward.3 = (bf16[29,16,128]{2,1,0:T(8,128)(2,1)S(1)}, f32[29,16,128]{2,1,0:T(8,128)S(1)}) custom-call(bf16[29,16,128]{2,1,0:T(8,128)(2,1)S(1)} %get-tuple-element.36.low_ref, bf16[29,16,128]{2,1,0:T(8,128)(2,1)S(1)} %get-tuple-element.37.high_ref, bf16[128,32]{1,0:T(8,128)(2,1)S(1)} %get-tuple-element.38.hot_ref, ...), custom_call_target="tpu_custom_call" | custom-call | tf_op jit(solution)/shard_map/forward/pallas_call | solution.py:533
  14.7 2.2 %collective-permute-start.4 = (bf16[29,16,128]{2,1,0:T(8,128)(2,1)S(1)}, bf16[29,16,128]{2,1,0:T(8,128)(2,1)S(1)}, u32[]{:S(2)}, u32[]{:S(2)}) collective-permute-start(bf16[29,16,128]{2,1,0:T(8,128)(2,1)S(1)} %get-tuple-element.47), channel_id=1, source_target_pairs={{0,14},{1,15},{2,8},{3,9},{4,10},{5,11},{6,12},{7,13}} | collective-permute-start | bytes 356360 | tf_op jit(solution)/shard_map/ppermute | solution.py:575
  16.9 1.3 %collective-permute-start.3 = (bf16[29,16,128]{2,1,0:T(8,128)(2,1)S(1)}, bf16[29,16,128]{2,1,0:T(8,128)(2,1)S(1)}, u32[]{:S(2)}, u32[]{:S(2)}) collective-permute-start(bf16[29,16,128]{2,1,0:T(8,128)(2,1)S(1)} %get-tuple-element.47), channel_id=1, source_target_pairs={{0,8},{1,9},{2,10},{3,11},{4,12},{5,13},{6,14},{7,15}} | collective-permute-start | bytes 356360 | tf_op jit(solution)/shard_map/ppermute | solution.py:575
  18.3 1.8 %collective-permute-done.4.high_ref = bf16[29,16,128]{2,1,0:T(8,128)(2,1)S(1)} collective-permute-done((bf16[29,16,128]{2,1,0:T(8,128)(2,1)S(1)}, bf16[29,16,128]{2,1,0:T(8,128)(2,1)S(1)}, u32[]{:S(2)}, u32[]{:S(2)}) %collective-permute-start.4) | collective-permute-done | bytes 118816 | tf_op jit(solution)/shard_map/ppermute | solution.py:575
  20.0 1.3 %collective-permute-done.3.low_ref = bf16[29,16,128]{2,1,0:T(8,128)(2,1)S(1)} collective-permute-done((bf16[29,16,128]{2,1,0:T(8,128)(2,1)S(1)}, bf16[29,16,128]{2,1,0:T(8,128)(2,1)S(1)}, u32[]{:S(2)}, u32[]{:S(2)}) %collective-permute-start.3) | collective-permute-done | bytes 118816 | tf_op jit(solution)/shard_map/ppermute | solution.py:575
  21.3 0.8 collective-permute-start.6
  22.1 0.7 collective-permute-start.5
  22.8 0.0 collective-permute-done.6.high_ref
  22.8 0.0 collective-permute-done.5.low_ref
  22.9 0.7 collective-permute-start.8
  23.5 0.7 collective-permute-start.7
  24.2 0.0 collective-permute-done.8.high_ref
  24.2 0.0 collective-permute-done.7.low_ref
  24.3 0.7 collective-permute-start.9
  24.9 0.7 collective-permute-start.10
  25.6 0.0 collective-permute-done.9.up_low_ref
  25.6 0.0 collective-permute-done.10.up_high_ref
  25.7 0.7 collective-permute-start.11
  26.3 0.7 collective-permute-start.12
  27.0 0.0 collective-permute-done.11.up_low_ref
  27.0 0.2 backward.4
  27.2 1.3 %collective-permute-start.13 = (bf16[30,16,128]{2,1,0:T(8,128)(2,1)S(1)}, bf16[30,16,128]{2,1,0:T(8,128)(2,1)S(1)}, u32[]{:S(2)}, u32[]{:S(2)}) collective-permute-start(bf16[30,16,128]{2,1,0:T(8,128)(2,1)S(1)} %get-tuple-element.57), channel_id=1, source_target_pairs={{8,0},{9,1},{10,2},{11,3},{12,4},{13,5},{14,6},{15,7}} | collective-permute-start | bytes 368648 | tf_op jit(solution)/shard_map/ppermute | solution.py:575
  28.5 1.3 %collective-permute-start.14 = (bf16[30,16,128]{2,1,0:T(8,128)(2,1)S(1)}, bf16[30,16,128]{2,1,0:T(8,128)(2,1)S(1)}, u32[]{:S(2)}, u32[]{:S(2)}) collective-permute-start(bf16[30,16,128]{2,1,0:T(8,128)(2,1)S(1)} %get-tuple-element.58), channel_id=1, source_target_pairs={{8,2},{9,3},{10,4},{11,5},{12,6},{13,7},{14,0},{15,1}} | collective-permute-start | bytes 368648 | tf_op jit(solution)/shard_map/ppermute | solution.py:575
  29.8 46.5 %collective-permute-done.13.up_low_ref = bf16[30,16,128]{2,1,0:T(8,128)(2,1)S(1)} collective-permute-done((bf16[30,16,128]{2,1,0:T(8,128)(2,1)S(1)}, bf16[30,16,128]{2,1,0:T(8,128)(2,1)S(1)}, u32[]{:S(2)}, u32[]{:S(2)}) %collective-permute-start.13) | collective-permute-done | bytes 122912 | tf_op jit(solution)/shard_map/ppermute | solution.py:575
  76.4 5.9 %collective-permute-done.14.up_high_ref = bf16[30,16,128]{2,1,0:T(8,128)(2,1)S(1)} collective-permute-done((bf16[30,16,128]{2,1,0:T(8,128)(2,1)S(1)}, bf16[30,16,128]{2,1,0:T(8,128)(2,1)S(1)}, u32[]{:S(2)}, u32[]{:S(2)}) %collective-permute-start.14) | collective-permute-done | bytes 122912 | tf_op jit(solution)/shard_map/ppermute | solution.py:575
  82.3 2.3 %backward.5 = (f32[8,128]{1,0:T(8,128)S(1)}, f32[8,128]{1,0:T(8,128)S(1)}, f32[8,128]{1,0:T(8,128)S(1)}, f32[8,128]{1,0:T(8,128)S(1)}) custom-call(bf16[30,16,128]{2,1,0:T(8,128)(2,1)S(1)} %collective-permute-done.13.up_low_ref, bf16[30,16,128]{2,1,0:T(8,128)(2,1)S(1)} %collective-permute-done.14.up_high_ref, ...), custom_call_target="tpu_custom_call" | custom-call | tf_op jit(solution)/shard_map/backward/pallas_call | solution.py:533
  84.6 1.9 %collective-permute-start.15 = (f32[8,128]{1,0:T(8,128)S(1)}, f32[8,128]{1,0:T(8,128)S(1)}, u32[]{:S(2)}, u32[]{:S(2)}) collective-permute-start(f32[8,128]{1,0:T(8,128)S(1)} %get-tuple-element.61), channel_id=1, source_target_pairs={{0,1},{1,0},{2,3},{3,2},{4,5},{5,4},{6,7},{7,6}} | collective-permute-start | bytes 12296 | tf_op jit(solution)/shard_map/ppermute | solution.py:571
  86.5 1.9 %collective-permute-start.16 = (f32[8,128]{1,0:T(8,128)S(1)}, f32[8,128]{1,0:T(8,128)S(1)}, u32[]{:S(2)}, u32[]{:S(2)}) collective-permute-start(f32[8,128]{1,0:T(8,128)S(1)} %get-tuple-element.62), channel_id=1, source_target_pairs={{0,2},{1,7},{2,4},{3,1},{4,6},{5,3},{6,0},{7,5}} | collective-permute-start | bytes 12296 | tf_op jit(solution)/shard_map/ppermute | solution.py:571
  88.5 3.2 %collective-permute-start.17 = (f32[8,128]{1,0:T(8,128)S(1)}, f32[8,128]{1,0:T(8,128)S(1)}, u32[]{:S(2)}, u32[]{:S(2)}) collective-permute-start(f32[8,128]{1,0:T(8,128)S(1)} %get-tuple-element.63), channel_id=1, source_target_pairs={{0,7},{1,2},{2,1},{3,4},{4,3},{5,6},{6,5},{7,0}} | collective-permute-start | bytes 12296 | tf_op jit(solution)/shard_map/ppermute | solution.py:571
  91.6 0.0 collective-permute-done.15.theirs_ref
  91.7 2.2 %collective-permute-done.16.straight_ref = f32[8,128]{1,0:T(8,128)S(1)} collective-permute-done((f32[8,128]{1,0:T(8,128)S(1)}, f32[8,128]{1,0:T(8,128)S(1)}, u32[]{:S(2)}, u32[]{:S(2)}) %collective-permute-start.16) | collective-permute-done | bytes 4128 | tf_op jit(solution)/shard_map/ppermute | solution.py:571
  93.8 1.4 %collective-permute-done.17.cross_ref = f32[8,128]{1,0:T(8,128)S(1)} collective-permute-done((f32[8,128]{1,0:T(8,128)S(1)}, f32[8,128]{1,0:T(8,128)S(1)}, u32[]{:S(2)}, u32[]{:S(2)}) %collective-permute-start.17) | collective-permute-done | bytes 4128 | tf_op jit(solution)/shard_map/ppermute | solution.py:571
  95.2 1.3 %collective-permute-start.20 = (f32[16,128]{1,0:T(8,128)S(1)}, f32[16,128]{1,0:T(8,128)S(1)}, u32[]{:S(2)}, u32[]{:S(2)}) collective-permute-start(f32[16,128]{1,0:T(8,128)S(1)} %join.1.refs_0_), channel_id=1, source_target_pairs={{0,24},{1,25},{2,26},{3,27},{4,28},{5,29},{6,30},{7,31}} | collective-permute-start | bytes 24584 | tf_op jit(solution)/shard_map/ppermute | solution.py:575
  96.5 1.3 %collective-permute-start.19 = (f32[16,128]{1,0:T(8,128)S(1)}, f32[16,128]{1,0:T(8,128)S(1)}, u32[]{:S(2)}, u32[]{:S(2)}) collective-permute-start(f32[16,128]{1,0:T(8,128)S(1)} %join.1.refs_0_), channel_id=1, source_target_pairs={{0,16},{1,17},{2,18},{3,19},{4,20},{5,21},{6,22},{7,23}} | collective-permute-start | bytes 24584 | tf_op jit(solution)/shard_map/ppermute | solution.py:575
  97.8 1.3 %collective-permute-start.18 = (f32[16,128]{1,0:T(8,128)S(1)}, f32[16,128]{1,0:T(8,128)S(1)}, u32[]{:S(2)}, u32[]{:S(2)}) collective-permute-start(f32[16,128]{1,0:T(8,128)S(1)} %join.1.refs_0_), channel_id=1, source_target_pairs={{0,8},{1,9},{2,10},{3,11},{4,12},{5,13},{6,14},{7,15}} | collective-permute-start | bytes 24584 | tf_op jit(solution)/shard_map/ppermute | solution.py:575
  99.1 0.0 collective-permute-done.19.refs_2_
  99.1 1.3 %collective-permute-done.18.refs_1_ = f32[16,128]{1,0:T(8,128)S(1)} collective-permute-done((f32[16,128]{1,0:T(8,128)S(1)}, f32[16,128]{1,0:T(8,128)S(1)}, u32[]{:S(2)}, u32[]{:S(2)}) %collective-permute-start.18) | collective-permute-done | bytes 8224 | tf_op jit(solution)/shard_map/ppermute | solution.py:575
  100.4 0.7 close.1
  (11 shorter events, 0.1 us)
Async XLA Ops:
  1.8 7.8 %collective-permute-start.1 = (bf16[30,8,128]{2,1,0:T(8,128)(2,1)S(1)}, bf16[30,8,128]{2,1,0:T(8,128)(2,1)S(1)}, u32[]{:S(2)}, u32[]{:S(2)}) collective-permute-start(bf16[30,8,128]{2,1,0:T(8,128)(2,1)S(1)} %get-tuple-element.34.mine_ref), channel_id=1, source_target_pairs={{0,6},{1,3},{2,0},{3,5},{4,2},{5,7},{6,4},{7,1},{8,14},{9,15},{10,... | collective-permute-start | bytes 184328 | tf_op jit(solution)/shard_map/ppermute | solution.py:571
  6.9 5.4 %collective-permute-start.2 = (bf16[30,8,128]{2,1,0:T(8,128)(2,1)S(1)}, bf16[30,8,128]{2,1,0:T(8,128)(2,1)S(1)}, u32[]{:S(2)}, u32[]{:S(2)}) collective-permute-start(bf16[30,8,128]{2,1,0:T(8,128)(2,1)S(1)} %get-tuple-element.35), channel_id=1, source_target_pairs={{0,7},{1,2},{2,1},{3,4},{4,3},{5,6},{6,5},{7,0},{8,15},{9,14},{10,... | collective-permute-start | bytes 184328 | tf_op jit(solution)/shard_map/ppermute | solution.py:571
  7.0 5.4 %collective-permute-start = (bf16[30,8,128]{2,1,0:T(8,128)(2,1)S(1)}, bf16[30,8,128]{2,1,0:T(8,128)(2,1)S(1)}, u32[]{:S(2)}, u32[]{:S(2)}) collective-permute-start(bf16[30,8,128]{2,1,0:T(8,128)(2,1)S(1)} %get-tuple-element.35), channel_id=1, source_target_pairs={{0,1},{1,0},{2,3},{3,2},{4,5},{5,4},{6,7},{7,6},{8,9},{9,8},{10,11... | collective-permute-start | bytes 184328 | tf_op jit(solution)/shard_map/ppermute | solution.py:571
  7.0 5.4 %copy-start = (f32[1,128]{1,0:T(1,128)S(1)}, f32[1,128]{1,0:T(1,128)}, u32[]{:S(2)}) copy-start(f32[1,128]{1,0:T(1,128)} %rate_ref.1) | copy-start | bytes 1540
  14.7 5.3 %collective-permute-start.4 = (bf16[29,16,128]{2,1,0:T(8,128)(2,1)S(1)}, bf16[29,16,128]{2,1,0:T(8,128)(2,1)S(1)}, u32[]{:S(2)}, u32[]{:S(2)}) collective-permute-start(bf16[29,16,128]{2,1,0:T(8,128)(2,1)S(1)} %get-tuple-element.47), channel_id=1, source_target_pairs={{0,14},{1,15},{2,8},{3,9},{4,10},{5,11},{6,12},{7,13}} | collective-permute-start | bytes 356360 | tf_op jit(solution)/shard_map/ppermute | solution.py:575
  16.9 4.4 %collective-permute-start.3 = (bf16[29,16,128]{2,1,0:T(8,128)(2,1)S(1)}, bf16[29,16,128]{2,1,0:T(8,128)(2,1)S(1)}, u32[]{:S(2)}, u32[]{:S(2)}) collective-permute-start(bf16[29,16,128]{2,1,0:T(8,128)(2,1)S(1)} %get-tuple-element.47), channel_id=1, source_target_pairs={{0,8},{1,9},{2,10},{3,11},{4,12},{5,13},{6,14},{7,15}} | collective-permute-start | bytes 356360 | tf_op jit(solution)/shard_map/ppermute | solution.py:575
  21.3 2.9 %copy-start.1 = (f32[128]{0:T(128)S(1)}, f32[128]{0:T(128)}, u32[]{:S(2)}) copy-start(f32[128]{0:T(128)} %param.20) | copy-start | bytes 1540
  21.3 1.5 %collective-permute-start.6 = (bf16[29,16,128]{2,1,0:T(8,128)(2,1)S(1)}, bf16[29,16,128]{2,1,0:T(8,128)(2,1)S(1)}, u32[]{:S(2)}, u32[]{:S(2)}) collective-permute-start(bf16[29,16,128]{2,1,0:T(8,128)(2,1)S(1)} %get-tuple-element.48), channel_id=1, source_target_pairs={{8,16},{9,17},{10,18},{11,19},{12,20},{13,21},{14,22},{15,23}} | collective-permute-start | bytes 356360 | tf_op jit(solution)/shard_map/ppermute | solution.py:575
  22.1 0.7 collective-permute-start.5
  22.9 1.4 %collective-permute-start.8 = (bf16[29,16,128]{2,1,0:T(8,128)(2,1)S(1)}, bf16[29,16,128]{2,1,0:T(8,128)(2,1)S(1)}, u32[]{:S(2)}, u32[]{:S(2)}) collective-permute-start(bf16[29,16,128]{2,1,0:T(8,128)(2,1)S(1)} %get-tuple-element.49), channel_id=1, source_target_pairs={{16,30},{17,31},{18,24},{19,25},{20,26},{21,27},{22,28},{23,29}} | collective-permute-start | bytes 356360 | tf_op jit(solution)/shard_map/ppermute | solution.py:575
  23.5 0.7 collective-permute-start.7
  24.3 1.4 %collective-permute-start.9 = (bf16[30,16,128]{2,1,0:T(8,128)(2,1)S(1)}, bf16[30,16,128]{2,1,0:T(8,128)(2,1)S(1)}, u32[]{:S(2)}, u32[]{:S(2)}) collective-permute-start(bf16[30,16,128]{2,1,0:T(8,128)(2,1)S(1)} %get-tuple-element.51), channel_id=1, source_target_pairs={{24,16},{25,17},{26,18},{27,19},{28,20},{29,21},{30,22},{31,23}} | collective-permute-start | bytes 368648 | tf_op jit(solution)/shard_map/ppermute | solution.py:575
  24.9 0.7 collective-permute-start.10
  25.7 1.4 %collective-permute-start.11 = (bf16[30,16,128]{2,1,0:T(8,128)(2,1)S(1)}, bf16[30,16,128]{2,1,0:T(8,128)(2,1)S(1)}, u32[]{:S(2)}, u32[]{:S(2)}) collective-permute-start(bf16[30,16,128]{2,1,0:T(8,128)(2,1)S(1)} %get-tuple-element.54), channel_id=1, source_target_pairs={{16,14},{17,15},{18,8},{19,9},{20,10},{21,11},{22,12},{23,13}} | collective-permute-start | bytes 368648 | tf_op jit(solution)/shard_map/ppermute | solution.py:575
  26.3 0.7 collective-permute-start.12
  27.2 49.1 %collective-permute-start.13 = (bf16[30,16,128]{2,1,0:T(8,128)(2,1)S(1)}, bf16[30,16,128]{2,1,0:T(8,128)(2,1)S(1)}, u32[]{:S(2)}, u32[]{:S(2)}) collective-permute-start(bf16[30,16,128]{2,1,0:T(8,128)(2,1)S(1)} %get-tuple-element.57), channel_id=1, source_target_pairs={{8,0},{9,1},{10,2},{11,3},{12,4},{13,5},{14,6},{15,7}} | collective-permute-start | bytes 368648 | tf_op jit(solution)/shard_map/ppermute | solution.py:575
  28.5 53.7 %collective-permute-start.14 = (bf16[30,16,128]{2,1,0:T(8,128)(2,1)S(1)}, bf16[30,16,128]{2,1,0:T(8,128)(2,1)S(1)}, u32[]{:S(2)}, u32[]{:S(2)}) collective-permute-start(bf16[30,16,128]{2,1,0:T(8,128)(2,1)S(1)} %get-tuple-element.58), channel_id=1, source_target_pairs={{8,2},{9,3},{10,4},{11,5},{12,6},{13,7},{14,0},{15,1}} | collective-permute-start | bytes 368648 | tf_op jit(solution)/shard_map/ppermute | solution.py:575
  84.6 7.1 %collective-permute-start.15 = (f32[8,128]{1,0:T(8,128)S(1)}, f32[8,128]{1,0:T(8,128)S(1)}, u32[]{:S(2)}, u32[]{:S(2)}) collective-permute-start(f32[8,128]{1,0:T(8,128)S(1)} %get-tuple-element.61), channel_id=1, source_target_pairs={{0,1},{1,0},{2,3},{3,2},{4,5},{5,4},{6,7},{7,6}} | collective-permute-start | bytes 12296 | tf_op jit(solution)/shard_map/ppermute | solution.py:571
  86.5 7.3 %collective-permute-start.16 = (f32[8,128]{1,0:T(8,128)S(1)}, f32[8,128]{1,0:T(8,128)S(1)}, u32[]{:S(2)}, u32[]{:S(2)}) collective-permute-start(f32[8,128]{1,0:T(8,128)S(1)} %get-tuple-element.62), channel_id=1, source_target_pairs={{0,2},{1,7},{2,4},{3,1},{4,6},{5,3},{6,0},{7,5}} | collective-permute-start | bytes 12296 | tf_op jit(solution)/shard_map/ppermute | solution.py:571
  88.5 6.7 %collective-permute-start.17 = (f32[8,128]{1,0:T(8,128)S(1)}, f32[8,128]{1,0:T(8,128)S(1)}, u32[]{:S(2)}, u32[]{:S(2)}) collective-permute-start(f32[8,128]{1,0:T(8,128)S(1)} %get-tuple-element.63), channel_id=1, source_target_pairs={{0,7},{1,2},{2,1},{3,4},{4,3},{5,6},{6,5},{7,0}} | collective-permute-start | bytes 12296 | tf_op jit(solution)/shard_map/ppermute | solution.py:571
  95.2 3.9 %collective-permute-start.20 = (f32[16,128]{1,0:T(8,128)S(1)}, f32[16,128]{1,0:T(8,128)S(1)}, u32[]{:S(2)}, u32[]{:S(2)}) collective-permute-start(f32[16,128]{1,0:T(8,128)S(1)} %join.1.refs_0_), channel_id=1, source_target_pairs={{0,24},{1,25},{2,26},{3,27},{4,28},{5,29},{6,30},{7,31}} | collective-permute-start | bytes 24584 | tf_op jit(solution)/shard_map/ppermute | solution.py:575
  96.5 2.6 %collective-permute-start.19 = (f32[16,128]{1,0:T(8,128)S(1)}, f32[16,128]{1,0:T(8,128)S(1)}, u32[]{:S(2)}, u32[]{:S(2)}) collective-permute-start(f32[16,128]{1,0:T(8,128)S(1)} %join.1.refs_0_), channel_id=1, source_target_pairs={{0,16},{1,17},{2,18},{3,19},{4,20},{5,21},{6,22},{7,23}} | collective-permute-start | bytes 24584 | tf_op jit(solution)/shard_map/ppermute | solution.py:575
  97.8 2.6 %collective-permute-start.18 = (f32[16,128]{1,0:T(8,128)S(1)}, f32[16,128]{1,0:T(8,128)S(1)}, u32[]{:S(2)}, u32[]{:S(2)}) collective-permute-start(f32[16,128]{1,0:T(8,128)S(1)} %join.1.refs_0_), channel_id=1, source_target_pairs={{0,8},{1,9},{2,10},{3,11},{4,12},{5,13},{6,14},{7,15}} | collective-permute-start | bytes 24584 | tf_op jit(solution)/shard_map/ppermute | solution.py:575

commit v5 on v4

--- a/solution.py
+++ b/solution.py
@@ -446,14 +446,15 @@
         geo_ref[n * edges : (n + 1) * edges, :] = value
 
 
-def works_late():
-    return (lax.axis_index("segment") == 0) & (lax.rem(lax.axis_index("space"), 2) == 1)
-
-
-def stage_kernel(late, zero_hbm, one_hbm, two_hbm, *more):
+def turn_to_stage():
+    odd = lax.rem(lax.axis_index("space"), 2)
+    return jnp.where(lax.axis_index("segment") == 0, odd, 2)
+
+
+def stage_kernel(moment, zero_hbm, one_hbm, two_hbm, *more):
     zero_ref, one_ref, two_ref, sems = more[-4:]
 
-    @pl.when(works_late() == late)
+    @pl.when(turn_to_stage() == moment)
     def _():
         pairs = [(zero_hbm, zero_ref)]
         for source, target in ((one_hbm, one_ref), (two_hbm, two_ref)):
@@ -589,7 +590,7 @@
     spaces = [pltpu.HBM] * 3
     on_chip = [pltpu.VMEM(w.shape, w.dtype) for w in stored]
     sems = [pltpu.SemaphoreType.DMA((5,))]
-    weights = call(functools.partial(stage_kernel, False), stored, on_chip, "stage", spaces, sems)
+    weights = call(functools.partial(stage_kernel, 0), stored, on_chip, "stage", spaces, sems)
     whole = shape((coefs, rows, channels), BF16)
     low, high, hot, hot_t, geo, seeds = call(
         functools.partial(open_kernel, slabs, neighbours),
@@ -600,10 +601,14 @@
         ],
         "open",
     )
-    weights = call(
-        functools.partial(stage_kernel, True), [*stored, *weights, seeds], on_chip, "stage_late",
-        spaces + [pltpu.VMEM] * 4, sems, {3: 0, 4: 1, 5: 2},
-    )
+
+    def stage_more(moment, weights, after):
+        return call(
+            functools.partial(stage_kernel, moment), [*stored, *weights, after], on_chip, "stage",
+            spaces + [pltpu.VMEM] * 4, sems, {3: 0, 4: 1, 5: 2},
+        )
+
+    weights = stage_more(1, weights, seeds)
     around_all = [(low, high)]
     kept = []
     for tick in range(segments - 1):
@@ -614,6 +619,8 @@
             "forward",
         )
         kept.append(pooled)
+        if tick == 0:
+            weights = stage_more(2, weights, out)
         ways = (2, 0) if tick % 2 else (0, -2)
         around_all.append(tuple(hop(out, tick, tick + 1, by) for by in ways))
     final = segments - 1

time: 102 us -> 102 us (level)
    pallas_call x13 -> x14, Pallas kernels: 9.44 us -> 9.53 us  [call(): pl.pallas_call(body, out_shape=shapes, in_specs=[pl.BlockSpec(memory_spac...]
where the time goes in v5:
time: 102 us; the launch traced here: 101 us
  waiting for transfers between devices  63.2 us (62%)
  starting transfers between devices  27.6 us (27%)
  Pallas kernels  9.53 us (9%)
    ppermute x15, waiting for transfers between devices, hop(): return lax.ppermute(value, axes, pairs)  57 us
    ppermute x15, starting transfers between devices, hop(): return lax.ppermute(value, axes, pairs)  15.4 us
    ppermute x6, starting transfers between devices, within(): return lax.ppermute(value, axes, pairs)  12.2 us
    pallas_call x14, Pallas kernels, call(): pl.pallas_call(body, out_shape=shapes, in_specs=[pl.BlockSpec(memory_spac...  9.53 us
    ppermute x6, waiting for transfers between devices, within(): return lax.ppermute(value, axes, pairs)  6.25 us
  transfers between devices with their start and end apart: 21, of which 8 were waited for; matrix products, arithmetic and copies ran while one was open for 0% of the time, Pallas kernels for 3%

profile of v5, /device:TPU:0, one launch (start us, length us, event | category | flops | bytes accessed | tf_op | source)
XLA Modules:
  0.0 101.4 jit_solution(2209001804070704883)
XLA Ops:
  0.6 1.2 %pack.1 = (bf16[30,8,128]{2,1,0:T(8,128)(2,1)S(1)}, bf16[30,8,128]{2,1,0:T(8,128)(2,1)S(1)}) custom-call(bf16[2,29,8,128]{3,2,1,0:T(8,128)(2,1)} %bitcast.17, f32[3,2,8]{2,1,0:T(2,128)} %bitcast.18, s32[2,8]{1,0:T(2,128)} %species_hbm.1, s32[2,8,8]{2,1,0:T(8,128)} %sources_hbm.1, f32[2,8]{1,0:T(2,128)} %grad_hbm.1, bf16[100,128]{1,0:T(8,128)(2,1)} %table_hbm.1), custom_call_target="tpu_custom_call" | custom-call | tf_op jit(solution)/shard_map/pack/pallas_call | solution.py:534
  1.8 5.1 %collective-permute-start.1 = (bf16[30,8,128]{2,1,0:T(8,128)(2,1)S(1)}, bf16[30,8,128]{2,1,0:T(8,128)(2,1)S(1)}, u32[]{:S(2)}, u32[]{:S(2)}) collective-permute-start(bf16[30,8,128]{2,1,0:T(8,128)(2,1)S(1)} %get-tuple-element.37.mine_ref), channel_id=1, source_target_pairs={{0,6},{1,3},{2,0},{3,5},{4,2},{5,7},{6,4},{7,1},{8,14},{9,15},{10,... | collective-permute-start | bytes 184328 | tf_op jit(solution)/shard_map/ppermute | solution.py:572
  6.9 0.0 collective-permute-start.2
  7.0 0.0 collective-permute-start
  7.0 2.6 %stage.3 = (bf16[896,896]{1,0:T(8,128)(2,1)S(1)}, bf16[2,768,768]{2,1,0:T(8,128)(2,1)S(1)}, bf16[2,640,640]{2,1,0:T(8,128)(2,1)S(1)}) custom-call(bf16[896,896]{1,0:T(8,128)(2,1)} %bitcast.14, bf16[2,768,768]{2,1,0:T(8,128)(2,1)} %bitcast.8, bf16[2,640,640]{2,1,0:T(8,128)(2,1)} %bitcast.11), custom_call_target="tpu_custom_call" | custom-call | tf_op jit(solution)/shard_map/stage/pallas_call | solution.py:534
  9.6 0.0 collective-permute-done.1.straight_ref
  9.6 2.8 %collective-permute-done.2.cross_ref = bf16[30,8,128]{2,1,0:T(8,128)(2,1)S(1)} collective-permute-done((bf16[30,8,128]{2,1,0:T(8,128)(2,1)S(1)}, bf16[30,8,128]{2,1,0:T(8,128)(2,1)S(1)}, u32[]{:S(2)}, u32[]{:S(2)}) %collective-permute-start.2) | collective-permute-done | bytes 61472 | tf_op jit(solution)/shard_map/ppermute | solution.py:572
  12.4 0.5 open.1
  12.9 0.1 stage.4
  13.0 1.7 %forward.3 = (bf16[29,16,128]{2,1,0:T(8,128)(2,1)S(1)}, f32[29,16,128]{2,1,0:T(8,128)S(1)}) custom-call(bf16[29,16,128]{2,1,0:T(8,128)(2,1)S(1)} %get-tuple-element.39.low_ref, bf16[29,16,128]{2,1,0:T(8,128)(2,1)S(1)} %get-tuple-element.40.high_ref, bf16[128,32]{1,0:T(8,128)(2,1)S(1)} %get-tuple-element.41.hot_ref, ...), custom_call_target="tpu_custom_call" | custom-call | tf_op jit(solution)/shard_map/forward/pallas_call | solution.py:534
  14.7 2.2 %collective-permute-start.4 = (bf16[29,16,128]{2,1,0:T(8,128)(2,1)S(1)}, bf16[29,16,128]{2,1,0:T(8,128)(2,1)S(1)}, u32[]{:S(2)}, u32[]{:S(2)}) collective-permute-start(bf16[29,16,128]{2,1,0:T(8,128)(2,1)S(1)} %get-tuple-element.50.more_3_), channel_id=1, source_target_pairs={{0,14},{1,15},{2,8},{3,9},{4,10},{5,11},{6,12},{7,13}} | collective-permute-start | bytes 356360 | tf_op jit(solution)/shard_map/ppermute | solution.py:576
  16.9 1.3 %collective-permute-start.3 = (bf16[29,16,128]{2,1,0:T(8,128)(2,1)S(1)}, bf16[29,16,128]{2,1,0:T(8,128)(2,1)S(1)}, u32[]{:S(2)}, u32[]{:S(2)}) collective-permute-start(bf16[29,16,128]{2,1,0:T(8,128)(2,1)S(1)} %get-tuple-element.50.more_3_), channel_id=1, source_target_pairs={{0,8},{1,9},{2,10},{3,11},{4,12},{5,13},{6,14},{7,15}} | collective-permute-start | bytes 356360 | tf_op jit(solution)/shard_map/ppermute | solution.py:576
  18.3 0.1 stage.5
  18.3 1.7 %collective-permute-done.4.high_ref = bf16[29,16,128]{2,1,0:T(8,128)(2,1)S(1)} collective-permute-done((bf16[29,16,128]{2,1,0:T(8,128)(2,1)S(1)}, bf16[29,16,128]{2,1,0:T(8,128)(2,1)S(1)}, u32[]{:S(2)}, u32[]{:S(2)}) %collective-permute-start.4) | collective-permute-done | bytes 118816 | tf_op jit(solution)/shard_map/ppermute | solution.py:576
  20.0 1.3 %collective-permute-done.3.low_ref = bf16[29,16,128]{2,1,0:T(8,128)(2,1)S(1)} collective-permute-done((bf16[29,16,128]{2,1,0:T(8,128)(2,1)S(1)}, bf16[29,16,128]{2,1,0:T(8,128)(2,1)S(1)}, u32[]{:S(2)}, u32[]{:S(2)}) %collective-permute-start.3) | collective-permute-done | bytes 118816 | tf_op jit(solution)/shard_map/ppermute | solution.py:576
  21.3 0.8 collective-permute-start.6
  22.1 0.7 collective-permute-start.5
  22.8 0.0 collective-permute-done.6.high_ref
  22.8 0.0 collective-permute-done.5.low_ref
  22.9 0.7 collective-permute-start.8
  23.5 0.7 collective-permute-start.7
  24.2 0.0 collective-permute-done.7.low_ref
  24.3 0.7 collective-permute-start.9
  24.9 0.7 collective-permute-start.10
  25.6 0.0 collective-permute-done.10.up_high_ref
  25.7 0.7 collective-permute-start.11
  26.3 0.7 collective-permute-start.12
  27.0 0.0 collective-permute-done.11.up_low_ref
  27.0 0.0 collective-permute-done.12.up_high_ref
  27.0 0.2 backward.4
  27.2 1.3 %collective-permute-start.13 = (bf16[30,16,128]{2,1,0:T(8,128)(2,1)S(1)}, bf16[30,16,128]{2,1,0:T(8,128)(2,1)S(1)}, u32[]{:S(2)}, u32[]{:S(2)}) collective-permute-start(bf16[30,16,128]{2,1,0:T(8,128)(2,1)S(1)} %get-tuple-element.63), channel_id=1, source_target_pairs={{8,0},{9,1},{10,2},{11,3},{12,4},{13,5},{14,6},{15,7}} | collective-permute-start | bytes 368648 | tf_op jit(solution)/shard_map/ppermute | solution.py:576
  28.5 1.3 %collective-permute-start.14 = (bf16[30,16,128]{2,1,0:T(8,128)(2,1)S(1)}, bf16[30,16,128]{2,1,0:T(8,128)(2,1)S(1)}, u32[]{:S(2)}, u32[]{:S(2)}) collective-permute-start(bf16[30,16,128]{2,1,0:T(8,128)(2,1)S(1)} %get-tuple-element.64), channel_id=1, source_target_pairs={{8,2},{9,3},{10,4},{11,5},{12,6},{13,7},{14,0},{15,1}} | collective-permute-start | bytes 368648 | tf_op jit(solution)/shard_map/ppermute | solution.py:576
  29.8 46.6 %collective-permute-done.13.up_low_ref = bf16[30,16,128]{2,1,0:T(8,128)(2,1)S(1)} collective-permute-done((bf16[30,16,128]{2,1,0:T(8,128)(2,1)S(1)}, bf16[30,16,128]{2,1,0:T(8,128)(2,1)S(1)}, u32[]{:S(2)}, u32[]{:S(2)}) %collective-permute-start.13) | collective-permute-done | bytes 122912 | tf_op jit(solution)/shard_map/ppermute | solution.py:576
  76.5 6.0 %collective-permute-done.14.up_high_ref = bf16[30,16,128]{2,1,0:T(8,128)(2,1)S(1)} collective-permute-done((bf16[30,16,128]{2,1,0:T(8,128)(2,1)S(1)}, bf16[30,16,128]{2,1,0:T(8,128)(2,1)S(1)}, u32[]{:S(2)}, u32[]{:S(2)}) %collective-permute-start.14) | collective-permute-done | bytes 122912 | tf_op jit(solution)/shard_map/ppermute | solution.py:576
  82.5 2.3 %backward.5 = (f32[8,128]{1,0:T(8,128)S(1)}, f32[8,128]{1,0:T(8,128)S(1)}, f32[8,128]{1,0:T(8,128)S(1)}, f32[8,128]{1,0:T(8,128)S(1)}) custom-call(bf16[30,16,128]{2,1,0:T(8,128)(2,1)S(1)} %collective-permute-done.13.up_low_ref, bf16[30,16,128]{2,1,0:T(8,128)(2,1)S(1)} %collective-permute-done.14.up_high_ref, ...), custom_call_target="tpu_custom_call" | custom-call | tf_op jit(solution)/shard_map/backward/pallas_call | solution.py:534
  84.8 1.9 %collective-permute-start.15 = (f32[8,128]{1,0:T(8,128)S(1)}, f32[8,128]{1,0:T(8,128)S(1)}, u32[]{:S(2)}, u32[]{:S(2)}) collective-permute-start(f32[8,128]{1,0:T(8,128)S(1)} %get-tuple-element.67), channel_id=1, source_target_pairs={{0,1},{1,0},{2,3},{3,2},{4,5},{5,4},{6,7},{7,6}} | collective-permute-start | bytes 12296 | tf_op jit(solution)/shard_map/ppermute | solution.py:572
  86.8 1.9 %collective-permute-start.16 = (f32[8,128]{1,0:T(8,128)S(1)}, f32[8,128]{1,0:T(8,128)S(1)}, u32[]{:S(2)}, u32[]{:S(2)}) collective-permute-start(f32[8,128]{1,0:T(8,128)S(1)} %get-tuple-element.68), channel_id=1, source_target_pairs={{0,2},{1,7},{2,4},{3,1},{4,6},{5,3},{6,0},{7,5}} | collective-permute-start | bytes 12296 | tf_op jit(solution)/shard_map/ppermute | solution.py:572
  88.7 3.2 %collective-permute-start.17 = (f32[8,128]{1,0:T(8,128)S(1)}, f32[8,128]{1,0:T(8,128)S(1)}, u32[]{:S(2)}, u32[]{:S(2)}) collective-permute-start(f32[8,128]{1,0:T(8,128)S(1)} %get-tuple-element.69), channel_id=1, source_target_pairs={{0,7},{1,2},{2,1},{3,4},{4,3},{5,6},{6,5},{7,0}} | collective-permute-start | bytes 12296 | tf_op jit(solution)/shard_map/ppermute | solution.py:572
  91.9 0.0 collective-permute-done.15.theirs_ref
  91.9 2.1 %collective-permute-done.16.straight_ref = f32[8,128]{1,0:T(8,128)S(1)} collective-permute-done((f32[8,128]{1,0:T(8,128)S(1)}, f32[8,128]{1,0:T(8,128)S(1)}, u32[]{:S(2)}, u32[]{:S(2)}) %collective-permute-start.16) | collective-permute-done | bytes 4128 | tf_op jit(solution)/shard_map/ppermute | solution.py:572
  94.1 1.4 %collective-permute-done.17.cross_ref = f32[8,128]{1,0:T(8,128)S(1)} collective-permute-done((f32[8,128]{1,0:T(8,128)S(1)}, f32[8,128]{1,0:T(8,128)S(1)}, u32[]{:S(2)}, u32[]{:S(2)}) %collective-permute-start.17) | collective-permute-done | bytes 4128 | tf_op jit(solution)/shard_map/ppermute | solution.py:572
  95.4 1.3 %collective-permute-start.20 = (f32[16,128]{1,0:T(8,128)S(1)}, f32[16,128]{1,0:T(8,128)S(1)}, u32[]{:S(2)}, u32[]{:S(2)}) collective-permute-start(f32[16,128]{1,0:T(8,128)S(1)} %join.1.refs_0_), channel_id=1, source_target_pairs={{0,24},{1,25},{2,26},{3,27},{4,28},{5,29},{6,30},{7,31}} | collective-permute-start | bytes 24584 | tf_op jit(solution)/shard_map/ppermute | solution.py:576
  96.7 1.3 %collective-permute-start.19 = (f32[16,128]{1,0:T(8,128)S(1)}, f32[16,128]{1,0:T(8,128)S(1)}, u32[]{:S(2)}, u32[]{:S(2)}) collective-permute-start(f32[16,128]{1,0:T(8,128)S(1)} %join.1.refs_0_), channel_id=1, source_target_pairs={{0,16},{1,17},{2,18},{3,19},{4,20},{5,21},{6,22},{7,23}} | collective-permute-start | bytes 24584 | tf_op jit(solution)/shard_map/ppermute | solution.py:576
  98.0 1.3 %collective-permute-start.18 = (f32[16,128]{1,0:T(8,128)S(1)}, f32[16,128]{1,0:T(8,128)S(1)}, u32[]{:S(2)}, u32[]{:S(2)}) collective-permute-start(f32[16,128]{1,0:T(8,128)S(1)} %join.1.refs_0_), channel_id=1, source_target_pairs={{0,8},{1,9},{2,10},{3,11},{4,12},{5,13},{6,14},{7,15}} | collective-permute-start | bytes 24584 | tf_op jit(solution)/shard_map/ppermute | solution.py:576
  99.3 0.0 collective-permute-done.20.refs_3_
  99.3 0.0 collective-permute-done.19.refs_2_
  99.3 1.3 %collective-permute-done.18.refs_1_ = f32[16,128]{1,0:T(8,128)S(1)} collective-permute-done((f32[16,128]{1,0:T(8,128)S(1)}, f32[16,128]{1,0:T(8,128)S(1)}, u32[]{:S(2)}, u32[]{:S(2)}) %collective-permute-start.18) | collective-permute-done | bytes 8224 | tf_op jit(solution)/shard_map/ppermute | solution.py:576
  100.6 0.7 close.1
  (12 shorter events, 0.1 us)
Async XLA Ops:
  1.8 7.8 %collective-permute-start.1 = (bf16[30,8,128]{2,1,0:T(8,128)(2,1)S(1)}, bf16[30,8,128]{2,1,0:T(8,128)(2,1)S(1)}, u32[]{:S(2)}, u32[]{:S(2)}) collective-permute-start(bf16[30,8,128]{2,1,0:T(8,128)(2,1)S(1)} %get-tuple-element.37.mine_ref), channel_id=1, source_target_pairs={{0,6},{1,3},{2,0},{3,5},{4,2},{5,7},{6,4},{7,1},{8,14},{9,15},{10,... | collective-permute-start | bytes 184328 | tf_op jit(solution)/shard_map/ppermute | solution.py:572
  6.9 5.4 %collective-permute-start.2 = (bf16[30,8,128]{2,1,0:T(8,128)(2,1)S(1)}, bf16[30,8,128]{2,1,0:T(8,128)(2,1)S(1)}, u32[]{:S(2)}, u32[]{:S(2)}) collective-permute-start(bf16[30,8,128]{2,1,0:T(8,128)(2,1)S(1)} %get-tuple-element.38), channel_id=1, source_target_pairs={{0,7},{1,2},{2,1},{3,4},{4,3},{5,6},{6,5},{7,0},{8,15},{9,14},{10,... | collective-permute-start | bytes 184328 | tf_op jit(solution)/shard_map/ppermute | solution.py:572
  7.0 5.4 %collective-permute-start = (bf16[30,8,128]{2,1,0:T(8,128)(2,1)S(1)}, bf16[30,8,128]{2,1,0:T(8,128)(2,1)S(1)}, u32[]{:S(2)}, u32[]{:S(2)}) collective-permute-start(bf16[30,8,128]{2,1,0:T(8,128)(2,1)S(1)} %get-tuple-element.38), channel_id=1, source_target_pairs={{0,1},{1,0},{2,3},{3,2},{4,5},{5,4},{6,7},{7,6},{8,9},{9,8},{10,11... | collective-permute-start | bytes 184328 | tf_op jit(solution)/shard_map/ppermute | solution.py:572
  7.0 5.4 %copy-start = (f32[1,128]{1,0:T(1,128)S(1)}, f32[1,128]{1,0:T(1,128)}, u32[]{:S(2)}) copy-start(f32[1,128]{1,0:T(1,128)} %rate_ref.1) | copy-start | bytes 1540
  14.7 5.3 %collective-permute-start.4 = (bf16[29,16,128]{2,1,0:T(8,128)(2,1)S(1)}, bf16[29,16,128]{2,1,0:T(8,128)(2,1)S(1)}, u32[]{:S(2)}, u32[]{:S(2)}) collective-permute-start(bf16[29,16,128]{2,1,0:T(8,128)(2,1)S(1)} %get-tuple-element.50.more_3_), channel_id=1, source_target_pairs={{0,14},{1,15},{2,8},{3,9},{4,10},{5,11},{6,12},{7,13}} | collective-permute-start | bytes 356360 | tf_op jit(solution)/shard_map/ppermute | solution.py:576
  16.9 4.4 %collective-permute-start.3 = (bf16[29,16,128]{2,1,0:T(8,128)(2,1)S(1)}, bf16[29,16,128]{2,1,0:T(8,128)(2,1)S(1)}, u32[]{:S(2)}, u32[]{:S(2)}) collective-permute-start(bf16[29,16,128]{2,1,0:T(8,128)(2,1)S(1)} %get-tuple-element.50.more_3_), channel_id=1, source_target_pairs={{0,8},{1,9},{2,10},{3,11},{4,12},{5,13},{6,14},{7,15}} | collective-permute-start | bytes 356360 | tf_op jit(solution)/shard_map/ppermute | solution.py:576
  21.3 2.9 %copy-start.1 = (f32[128]{0:T(128)S(1)}, f32[128]{0:T(128)}, u32[]{:S(2)}) copy-start(f32[128]{0:T(128)} %param.20) | copy-start | bytes 1540
  21.3 1.5 %collective-permute-start.6 = (bf16[29,16,128]{2,1,0:T(8,128)(2,1)S(1)}, bf16[29,16,128]{2,1,0:T(8,128)(2,1)S(1)}, u32[]{:S(2)}, u32[]{:S(2)}) collective-permute-start(bf16[29,16,128]{2,1,0:T(8,128)(2,1)S(1)} %get-tuple-element.54), channel_id=1, source_target_pairs={{8,16},{9,17},{10,18},{11,19},{12,20},{13,21},{14,22},{15,23}} | collective-permute-start | bytes 356360 | tf_op jit(solution)/shard_map/ppermute | solution.py:576
  22.1 0.7 collective-permute-start.5
  22.9 1.4 %collective-permute-start.8 = (bf16[29,16,128]{2,1,0:T(8,128)(2,1)S(1)}, bf16[29,16,128]{2,1,0:T(8,128)(2,1)S(1)}, u32[]{:S(2)}, u32[]{:S(2)}) collective-permute-start(bf16[29,16,128]{2,1,0:T(8,128)(2,1)S(1)} %get-tuple-element.55), channel_id=1, source_target_pairs={{16,30},{17,31},{18,24},{19,25},{20,26},{21,27},{22,28},{23,29}} | collective-permute-start | bytes 356360 | tf_op jit(solution)/shard_map/ppermute | solution.py:576
  23.5 0.7 collective-permute-start.7
  24.3 1.4 %collective-permute-start.9 = (bf16[30,16,128]{2,1,0:T(8,128)(2,1)S(1)}, bf16[30,16,128]{2,1,0:T(8,128)(2,1)S(1)}, u32[]{:S(2)}, u32[]{:S(2)}) collective-permute-start(bf16[30,16,128]{2,1,0:T(8,128)(2,1)S(1)} %get-tuple-element.57), channel_id=1, source_target_pairs={{24,16},{25,17},{26,18},{27,19},{28,20},{29,21},{30,22},{31,23}} | collective-permute-start | bytes 368648 | tf_op jit(solution)/shard_map/ppermute | solution.py:576
  24.9 0.7 collective-permute-start.10
  25.7 1.4 %collective-permute-start.11 = (bf16[30,16,128]{2,1,0:T(8,128)(2,1)S(1)}, bf16[30,16,128]{2,1,0:T(8,128)(2,1)S(1)}, u32[]{:S(2)}, u32[]{:S(2)}) collective-permute-start(bf16[30,16,128]{2,1,0:T(8,128)(2,1)S(1)} %get-tuple-element.60), channel_id=1, source_target_pairs={{16,14},{17,15},{18,8},{19,9},{20,10},{21,11},{22,12},{23,13}} | collective-permute-start | bytes 368648 | tf_op jit(solution)/shard_map/ppermute | solution.py:576
  26.3 0.7 collective-permute-start.12
  27.2 49.2 %collective-permute-start.13 = (bf16[30,16,128]{2,1,0:T(8,128)(2,1)S(1)}, bf16[30,16,128]{2,1,0:T(8,128)(2,1)S(1)}, u32[]{:S(2)}, u32[]{:S(2)}) collective-permute-start(bf16[30,16,128]{2,1,0:T(8,128)(2,1)S(1)} %get-tuple-element.63), channel_id=1, source_target_pairs={{8,0},{9,1},{10,2},{11,3},{12,4},{13,5},{14,6},{15,7}} | collective-permute-start | bytes 368648 | tf_op jit(solution)/shard_map/ppermute | solution.py:576
  28.5 53.9 %collective-permute-start.14 = (bf16[30,16,128]{2,1,0:T(8,128)(2,1)S(1)}, bf16[30,16,128]{2,1,0:T(8,128)(2,1)S(1)}, u32[]{:S(2)}, u32[]{:S(2)}) collective-permute-start(bf16[30,16,128]{2,1,0:T(8,128)(2,1)S(1)} %get-tuple-element.64), channel_id=1, source_target_pairs={{8,2},{9,3},{10,4},{11,5},{12,6},{13,7},{14,0},{15,1}} | collective-permute-start | bytes 368648 | tf_op jit(solution)/shard_map/ppermute | solution.py:576
  84.8 7.1 %collective-permute-start.15 = (f32[8,128]{1,0:T(8,128)S(1)}, f32[8,128]{1,0:T(8,128)S(1)}, u32[]{:S(2)}, u32[]{:S(2)}) collective-permute-start(f32[8,128]{1,0:T(8,128)S(1)} %get-tuple-element.67), channel_id=1, source_target_pairs={{0,1},{1,0},{2,3},{3,2},{4,5},{5,4},{6,7},{7,6}} | collective-permute-start | bytes 12296 | tf_op jit(solution)/shard_map/ppermute | solution.py:572
  86.8 7.3 %collective-permute-start.16 = (f32[8,128]{1,0:T(8,128)S(1)}, f32[8,128]{1,0:T(8,128)S(1)}, u32[]{:S(2)}, u32[]{:S(2)}) collective-permute-start(f32[8,128]{1,0:T(8,128)S(1)} %get-tuple-element.68), channel_id=1, source_target_pairs={{0,2},{1,7},{2,4},{3,1},{4,6},{5,3},{6,0},{7,5}} | collective-permute-start | bytes 12296 | tf_op jit(solution)/shard_map/ppermute | solution.py:572
  88.7 6.7 %collective-permute-start.17 = (f32[8,128]{1,0:T(8,128)S(1)}, f32[8,128]{1,0:T(8,128)S(1)}, u32[]{:S(2)}, u32[]{:S(2)}) collective-permute-start(f32[8,128]{1,0:T(8,128)S(1)} %get-tuple-element.69), channel_id=1, source_target_pairs={{0,7},{1,2},{2,1},{3,4},{4,3},{5,6},{6,5},{7,0}} | collective-permute-start | bytes 12296 | tf_op jit(solution)/shard_map/ppermute | solution.py:572
  95.4 3.9 %collective-permute-start.20 = (f32[16,128]{1,0:T(8,128)S(1)}, f32[16,128]{1,0:T(8,128)S(1)}, u32[]{:S(2)}, u32[]{:S(2)}) collective-permute-start(f32[16,128]{1,0:T(8,128)S(1)} %join.1.refs_0_), channel_id=1, source_target_pairs={{0,24},{1,25},{2,26},{3,27},{4,28},{5,29},{6,30},{7,31}} | collective-permute-start | bytes 24584 | tf_op jit(solution)/shard_map/ppermute | solution.py:576
  96.7 2.6 %collective-permute-start.19 = (f32[16,128]{1,0:T(8,128)S(1)}, f32[16,128]{1,0:T(8,128)S(1)}, u32[]{:S(2)}, u32[]{:S(2)}) collective-permute-start(f32[16,128]{1,0:T(8,128)S(1)} %join.1.refs_0_), channel_id=1, source_target_pairs={{0,16},{1,17},{2,18},{3,19},{4,20},{5,21},{6,22},{7,23}} | collective-permute-start | bytes 24584 | tf_op jit(solution)/shard_map/ppermute | solution.py:576
  98.0 2.6 %collective-permute-start.18 = (f32[16,128]{1,0:T(8,128)S(1)}, f32[16,128]{1,0:T(8,128)S(1)}, u32[]{:S(2)}, u32[]{:S(2)}) collective-permute-start(f32[16,128]{1,0:T(8,128)S(1)} %join.1.refs_0_), channel_id=1, source_target_pairs={{0,8},{1,9},{2,10},{3,11},{4,12},{5,13},{6,14},{7,15}} | collective-permute-start | bytes 24584 | tf_op jit(solution)/shard_map/ppermute | solution.py:576

commit v6 on v5

--- a/solution.py
+++ b/solution.py
@@ -447,8 +447,9 @@
 
 
 def turn_to_stage():
+    segment = lax.axis_index("segment")
     odd = lax.rem(lax.axis_index("space"), 2)
-    return jnp.where(lax.axis_index("segment") == 0, odd, 2)
+    return jnp.where(segment == 0, odd, jnp.where(segment == 1, 2 + odd, 2))
 
 
 def stage_kernel(moment, zero_hbm, one_hbm, two_hbm, *more):
@@ -623,6 +624,8 @@
             weights = stage_more(2, weights, out)
         ways = (2, 0) if tick % 2 else (0, -2)
         around_all.append(tuple(hop(out, tick, tick + 1, by) for by in ways))
+        if tick == 0:
+            weights = stage_more(3, weights, around_all[1][0])
     final = segments - 1
     whole_more = shape((coefs + 1, rows, channels), BF16)
     slab_sums = shape((per_slab, channels), F32)

time: 102 us -> 101 us (level)
  starting transfers between devices: 27.6 us -> 26.5 us
    ppermute x6, waiting for transfers between devices: 6.25 us -> 7.41 us  [within(): return lax.ppermute(value, axes, pairs)]
    ppermute x6, starting transfers between devices: 12.2 us -> 11 us  [within(): return lax.ppermute(value, axes, pairs)]
    pallas_call x14 -> x15, Pallas kernels: 9.53 us -> 9.57 us  [call(): pl.pallas_call(body, out_shape=shapes, in_specs=[pl.BlockSpec(memory_spac...]
where the time goes in v6:
time: 101 us
  waiting for transfers between devices  63.5 us (63%)
  starting transfers between devices  26.5 us (26%)
  Pallas kernels  9.57 us (9%)
    ppermute x15, waiting for transfers between devices, hop(): return lax.ppermute(value, axes, pairs)  56.1 us
    ppermute x15, starting transfers between devices, hop(): return lax.ppermute(value, axes, pairs)  15.4 us
    ppermute x6, starting transfers between devices, within(): return lax.ppermute(value, axes, pairs)  11 us
    pallas_call x15, Pallas kernels, call(): pl.pallas_call(body, out_shape=shapes, in_specs=[pl.BlockSpec(memory_spac...  9.57 us
    ppermute x6, waiting for transfers between devices, within(): return lax.ppermute(value, axes, pairs)  7.41 us
  transfers between devices with their start and end apart: 21, of which 8 were waited for; matrix products, arithmetic and copies ran while one was open for 0% of the time, Pallas kernels for 3%

profile of v6, /device:TPU:0, one launch (start us, length us, event | category | flops | bytes accessed | tf_op | source)
XLA Modules:
  0.0 100.6 jit_solution(8949490288652739581)
XLA Ops:
  0.6 1.2 %pack.1 = (bf16[30,8,128]{2,1,0:T(8,128)(2,1)S(1)}, bf16[30,8,128]{2,1,0:T(8,128)(2,1)S(1)}) custom-call(bf16[2,29,8,128]{3,2,1,0:T(8,128)(2,1)} %bitcast.20, f32[3,2,8]{2,1,0:T(2,128)} %bitcast.21, s32[2,8]{1,0:T(2,128)} %species_hbm.1, s32[2,8,8]{2,1,0:T(8,128)} %sources_hbm.1, f32[2,8]{1,0:T(2,128)} %grad_hbm.1, bf16[100,128]{1,0:T(8,128)(2,1)} %table_hbm.1), custom_call_target="tpu_custom_call" | custom-call | tf_op jit(solution)/shard_map/pack/pallas_call | solution.py:535
  1.8 5.1 %collective-permute-start.1 = (bf16[30,8,128]{2,1,0:T(8,128)(2,1)S(1)}, bf16[30,8,128]{2,1,0:T(8,128)(2,1)S(1)}, u32[]{:S(2)}, u32[]{:S(2)}) collective-permute-start(bf16[30,8,128]{2,1,0:T(8,128)(2,1)S(1)} %get-tuple-element.40.mine_ref), channel_id=1, source_target_pairs={{0,6},{1,3},{2,0},{3,5},{4,2},{5,7},{6,4},{7,1},{8,14},{9,15},{10,... | collective-permute-start | bytes 184328 | tf_op jit(solution)/shard_map/ppermute | solution.py:573
  6.9 0.0 collective-permute-start.2
  7.0 0.0 collective-permute-start
  7.0 2.6 %stage.4 = (bf16[896,896]{1,0:T(8,128)(2,1)S(1)}, bf16[2,768,768]{2,1,0:T(8,128)(2,1)S(1)}, bf16[2,640,640]{2,1,0:T(8,128)(2,1)S(1)}) custom-call(bf16[896,896]{1,0:T(8,128)(2,1)} %bitcast.16, bf16[2,768,768]{2,1,0:T(8,128)(2,1)} %bitcast.8, bf16[2,640,640]{2,1,0:T(8,128)(2,1)} %bitcast.12), custom_call_target="tpu_custom_call" | custom-call | tf_op jit(solution)/shard_map/stage/pallas_call | solution.py:535
  9.6 0.0 collective-permute-done.1.straight_ref
  9.6 2.8 %collective-permute-done.2.cross_ref = bf16[30,8,128]{2,1,0:T(8,128)(2,1)S(1)} collective-permute-done((bf16[30,8,128]{2,1,0:T(8,128)(2,1)S(1)}, bf16[30,8,128]{2,1,0:T(8,128)(2,1)S(1)}, u32[]{:S(2)}, u32[]{:S(2)}) %collective-permute-start.2) | collective-permute-done | bytes 61472 | tf_op jit(solution)/shard_map/ppermute | solution.py:573
  12.4 0.0 collective-permute-done.partner_ref
  12.4 0.5 open.1
  12.9 0.1 stage.5
  13.0 1.7 %forward.3 = (bf16[29,16,128]{2,1,0:T(8,128)(2,1)S(1)}, f32[29,16,128]{2,1,0:T(8,128)S(1)}) custom-call(bf16[29,16,128]{2,1,0:T(8,128)(2,1)S(1)} %get-tuple-element.42.low_ref, bf16[29,16,128]{2,1,0:T(8,128)(2,1)S(1)} %get-tuple-element.43.high_ref, bf16[128,32]{1,0:T(8,128)(2,1)S(1)} %get-tuple-element.44.hot_ref, ...), custom_call_target="tpu_custom_call" | custom-call | tf_op jit(solution)/shard_map/forward/pallas_call | solution.py:535
  14.7 1.3 %collective-permute-start.3 = (bf16[29,16,128]{2,1,0:T(8,128)(2,1)S(1)}, bf16[29,16,128]{2,1,0:T(8,128)(2,1)S(1)}, u32[]{:S(2)}, u32[]{:S(2)}) collective-permute-start(bf16[29,16,128]{2,1,0:T(8,128)(2,1)S(1)} %get-tuple-element.53.more_3_), channel_id=1, source_target_pairs={{0,8},{1,9},{2,10},{3,11},{4,12},{5,13},{6,14},{7,15}} | collective-permute-start | bytes 356360 | tf_op jit(solution)/shard_map/ppermute | solution.py:577
  16.0 2.2 %collective-permute-start.4 = (bf16[29,16,128]{2,1,0:T(8,128)(2,1)S(1)}, bf16[29,16,128]{2,1,0:T(8,128)(2,1)S(1)}, u32[]{:S(2)}, u32[]{:S(2)}) collective-permute-start(bf16[29,16,128]{2,1,0:T(8,128)(2,1)S(1)} %get-tuple-element.53.more_3_), channel_id=1, source_target_pairs={{0,14},{1,15},{2,8},{3,9},{4,10},{5,11},{6,12},{7,13}} | collective-permute-start | bytes 356360 | tf_op jit(solution)/shard_map/ppermute | solution.py:577
  18.2 0.1 stage.6
  18.3 2.6 %collective-permute-done.3.more_3_.low_ref = bf16[29,16,128]{2,1,0:T(8,128)(2,1)S(1)} collective-permute-done((bf16[29,16,128]{2,1,0:T(8,128)(2,1)S(1)}, bf16[29,16,128]{2,1,0:T(8,128)(2,1)S(1)}, u32[]{:S(2)}, u32[]{:S(2)}) %collective-permute-start.3) | collective-permute-done | bytes 118816 | tf_op jit(solution)/shard_map/ppermute | solution.py:577
  20.9 0.4 collective-permute-done.4.high_ref
  21.3 0.8 collective-permute-start.6
  22.1 0.7 collective-permute-start.5
  22.8 0.0 collective-permute-done.6.high_ref
  22.8 0.0 collective-permute-done.5.low_ref
  22.9 0.7 collective-permute-start.8
  23.5 0.7 collective-permute-start.7
  24.2 0.0 collective-permute-done.7.low_ref
  24.3 0.7 collective-permute-start.9
  24.9 0.7 collective-permute-start.10
  25.6 0.0 collective-permute-done.10.up_high_ref
  25.7 0.7 collective-permute-start.11
  26.3 0.7 collective-permute-start.12
  27.0 0.0 collective-permute-done.11.up_low_ref
  27.0 0.2 backward.4
  27.2 1.3 %collective-permute-start.13 = (bf16[30,16,128]{2,1,0:T(8,128)(2,1)S(1)}, bf16[30,16,128]{2,1,0:T(8,128)(2,1)S(1)}, u32[]{:S(2)}, u32[]{:S(2)}) collective-permute-start(bf16[30,16,128]{2,1,0:T(8,128)(2,1)S(1)} %get-tuple-element.69), channel_id=1, source_target_pairs={{8,0},{9,1},{10,2},{11,3},{12,4},{13,5},{14,6},{15,7}} | collective-permute-start | bytes 368648 | tf_op jit(solution)/shard_map/ppermute | solution.py:577
  28.5 1.3 %collective-permute-start.14 = (bf16[30,16,128]{2,1,0:T(8,128)(2,1)S(1)}, bf16[30,16,128]{2,1,0:T(8,128)(2,1)S(1)}, u32[]{:S(2)}, u32[]{:S(2)}) collective-permute-start(bf16[30,16,128]{2,1,0:T(8,128)(2,1)S(1)} %get-tuple-element.70), channel_id=1, source_target_pairs={{8,2},{9,3},{10,4},{11,5},{12,6},{13,7},{14,0},{15,1}} | collective-permute-start | bytes 368648 | tf_op jit(solution)/shard_map/ppermute | solution.py:577
  29.8 45.8 %collective-permute-done.13.up_low_ref = bf16[30,16,128]{2,1,0:T(8,128)(2,1)S(1)} collective-permute-done((bf16[30,16,128]{2,1,0:T(8,128)(2,1)S(1)}, bf16[30,16,128]{2,1,0:T(8,128)(2,1)S(1)}, u32[]{:S(2)}, u32[]{:S(2)}) %collective-permute-start.13) | collective-permute-done | bytes 122912 | tf_op jit(solution)/shard_map/ppermute | solution.py:577
  75.7 6.0 %collective-permute-done.14.up_high_ref = bf16[30,16,128]{2,1,0:T(8,128)(2,1)S(1)} collective-permute-done((bf16[30,16,128]{2,1,0:T(8,128)(2,1)S(1)}, bf16[30,16,128]{2,1,0:T(8,128)(2,1)S(1)}, u32[]{:S(2)}, u32[]{:S(2)}) %collective-permute-start.14) | collective-permute-done | bytes 122912 | tf_op jit(solution)/shard_map/ppermute | solution.py:577
  81.7 2.3 %backward.5 = (f32[8,128]{1,0:T(8,128)S(1)}, f32[8,128]{1,0:T(8,128)S(1)}, f32[8,128]{1,0:T(8,128)S(1)}, f32[8,128]{1,0:T(8,128)S(1)}) custom-call(bf16[30,16,128]{2,1,0:T(8,128)(2,1)S(1)} %collective-permute-done.13.up_low_ref, bf16[30,16,128]{2,1,0:T(8,128)(2,1)S(1)} %collective-permute-done.14.up_high_ref, ...), custom_call_target="tpu_custom_call" | custom-call | tf_op jit(solution)/shard_map/backward/pallas_call | solution.py:535
  84.0 1.9 %collective-permute-start.15 = (f32[8,128]{1,0:T(8,128)S(1)}, f32[8,128]{1,0:T(8,128)S(1)}, u32[]{:S(2)}, u32[]{:S(2)}) collective-permute-start(f32[8,128]{1,0:T(8,128)S(1)} %get-tuple-element.73), channel_id=1, source_target_pairs={{0,1},{1,0},{2,3},{3,2},{4,5},{5,4},{6,7},{7,6}} | collective-permute-start | bytes 12296 | tf_op jit(solution)/shard_map/ppermute | solution.py:573
  86.0 1.9 %collective-permute-start.16 = (f32[8,128]{1,0:T(8,128)S(1)}, f32[8,128]{1,0:T(8,128)S(1)}, u32[]{:S(2)}, u32[]{:S(2)}) collective-permute-start(f32[8,128]{1,0:T(8,128)S(1)} %get-tuple-element.74), channel_id=1, source_target_pairs={{0,2},{1,7},{2,4},{3,1},{4,6},{5,3},{6,0},{7,5}} | collective-permute-start | bytes 12296 | tf_op jit(solution)/shard_map/ppermute | solution.py:573
  87.9 2.1 %collective-permute-start.17 = (f32[8,128]{1,0:T(8,128)S(1)}, f32[8,128]{1,0:T(8,128)S(1)}, u32[]{:S(2)}, u32[]{:S(2)}) collective-permute-start(f32[8,128]{1,0:T(8,128)S(1)} %get-tuple-element.75), channel_id=1, source_target_pairs={{0,7},{1,2},{2,1},{3,4},{4,3},{5,6},{6,5},{7,0}} | collective-permute-start | bytes 12296 | tf_op jit(solution)/shard_map/ppermute | solution.py:573
  90.0 0.0 collective-permute-done.15.theirs_ref
  90.0 3.3 %collective-permute-done.16.straight_ref = f32[8,128]{1,0:T(8,128)S(1)} collective-permute-done((f32[8,128]{1,0:T(8,128)S(1)}, f32[8,128]{1,0:T(8,128)S(1)}, u32[]{:S(2)}, u32[]{:S(2)}) %collective-permute-start.16) | collective-permute-done | bytes 4128 | tf_op jit(solution)/shard_map/ppermute | solution.py:573
  93.3 1.4 %collective-permute-done.17.cross_ref = f32[8,128]{1,0:T(8,128)S(1)} collective-permute-done((f32[8,128]{1,0:T(8,128)S(1)}, f32[8,128]{1,0:T(8,128)S(1)}, u32[]{:S(2)}, u32[]{:S(2)}) %collective-permute-start.17) | collective-permute-done | bytes 4128 | tf_op jit(solution)/shard_map/ppermute | solution.py:573
  94.6 1.3 %collective-permute-start.20 = (f32[16,128]{1,0:T(8,128)S(1)}, f32[16,128]{1,0:T(8,128)S(1)}, u32[]{:S(2)}, u32[]{:S(2)}) collective-permute-start(f32[16,128]{1,0:T(8,128)S(1)} %join.1.refs_0_), channel_id=1, source_target_pairs={{0,24},{1,25},{2,26},{3,27},{4,28},{5,29},{6,30},{7,31}} | collective-permute-start | bytes 24584 | tf_op jit(solution)/shard_map/ppermute | solution.py:577
  95.9 1.3 %collective-permute-start.19 = (f32[16,128]{1,0:T(8,128)S(1)}, f32[16,128]{1,0:T(8,128)S(1)}, u32[]{:S(2)}, u32[]{:S(2)}) collective-permute-start(f32[16,128]{1,0:T(8,128)S(1)} %join.1.refs_0_), channel_id=1, source_target_pairs={{0,16},{1,17},{2,18},{3,19},{4,20},{5,21},{6,22},{7,23}} | collective-permute-start | bytes 24584 | tf_op jit(solution)/shard_map/ppermute | solution.py:577
  97.2 1.3 %collective-permute-start.18 = (f32[16,128]{1,0:T(8,128)S(1)}, f32[16,128]{1,0:T(8,128)S(1)}, u32[]{:S(2)}, u32[]{:S(2)}) collective-permute-start(f32[16,128]{1,0:T(8,128)S(1)} %join.1.refs_0_), channel_id=1, source_target_pairs={{0,8},{1,9},{2,10},{3,11},{4,12},{5,13},{6,14},{7,15}} | collective-permute-start | bytes 24584 | tf_op jit(solution)/shard_map/ppermute | solution.py:577
  98.5 0.0 collective-permute-done.20.refs_3_
  98.5 0.0 collective-permute-done.19.refs_2_
  98.5 1.3 %collective-permute-done.18.refs_1_ = f32[16,128]{1,0:T(8,128)S(1)} collective-permute-done((f32[16,128]{1,0:T(8,128)S(1)}, f32[16,128]{1,0:T(8,128)S(1)}, u32[]{:S(2)}, u32[]{:S(2)}) %collective-permute-start.18) | collective-permute-done | bytes 8224 | tf_op jit(solution)/shard_map/ppermute | solution.py:577
  99.8 0.7 close.1
  (13 shorter events, 0.1 us)
Async XLA Ops:
  1.8 7.8 %collective-permute-start.1 = (bf16[30,8,128]{2,1,0:T(8,128)(2,1)S(1)}, bf16[30,8,128]{2,1,0:T(8,128)(2,1)S(1)}, u32[]{:S(2)}, u32[]{:S(2)}) collective-permute-start(bf16[30,8,128]{2,1,0:T(8,128)(2,1)S(1)} %get-tuple-element.40.mine_ref), channel_id=1, source_target_pairs={{0,6},{1,3},{2,0},{3,5},{4,2},{5,7},{6,4},{7,1},{8,14},{9,15},{10,... | collective-permute-start | bytes 184328 | tf_op jit(solution)/shard_map/ppermute | solution.py:573
  6.9 5.4 %collective-permute-start.2 = (bf16[30,8,128]{2,1,0:T(8,128)(2,1)S(1)}, bf16[30,8,128]{2,1,0:T(8,128)(2,1)S(1)}, u32[]{:S(2)}, u32[]{:S(2)}) collective-permute-start(bf16[30,8,128]{2,1,0:T(8,128)(2,1)S(1)} %get-tuple-element.41), channel_id=1, source_target_pairs={{0,7},{1,2},{2,1},{3,4},{4,3},{5,6},{6,5},{7,0},{8,15},{9,14},{10,... | collective-permute-start | bytes 184328 | tf_op jit(solution)/shard_map/ppermute | solution.py:573
  7.0 5.4 %collective-permute-start = (bf16[30,8,128]{2,1,0:T(8,128)(2,1)S(1)}, bf16[30,8,128]{2,1,0:T(8,128)(2,1)S(1)}, u32[]{:S(2)}, u32[]{:S(2)}) collective-permute-start(bf16[30,8,128]{2,1,0:T(8,128)(2,1)S(1)} %get-tuple-element.41), channel_id=1, source_target_pairs={{0,1},{1,0},{2,3},{3,2},{4,5},{5,4},{6,7},{7,6},{8,9},{9,8},{10,11... | collective-permute-start | bytes 184328 | tf_op jit(solution)/shard_map/ppermute | solution.py:573
  7.0 5.4 %copy-start = (f32[1,128]{1,0:T(1,128)S(1)}, f32[1,128]{1,0:T(1,128)}, u32[]{:S(2)}) copy-start(f32[1,128]{1,0:T(1,128)} %rate_ref.1) | copy-start | bytes 1540
  14.7 6.2 %collective-permute-start.3 = (bf16[29,16,128]{2,1,0:T(8,128)(2,1)S(1)}, bf16[29,16,128]{2,1,0:T(8,128)(2,1)S(1)}, u32[]{:S(2)}, u32[]{:S(2)}) collective-permute-start(bf16[29,16,128]{2,1,0:T(8,128)(2,1)S(1)} %get-tuple-element.53.more_3_), channel_id=1, source_target_pairs={{0,8},{1,9},{2,10},{3,11},{4,12},{5,13},{6,14},{7,15}} | collective-permute-start | bytes 356360 | tf_op jit(solution)/shard_map/ppermute | solution.py:577
  16.0 5.3 %collective-permute-start.4 = (bf16[29,16,128]{2,1,0:T(8,128)(2,1)S(1)}, bf16[29,16,128]{2,1,0:T(8,128)(2,1)S(1)}, u32[]{:S(2)}, u32[]{:S(2)}) collective-permute-start(bf16[29,16,128]{2,1,0:T(8,128)(2,1)S(1)} %get-tuple-element.53.more_3_), channel_id=1, source_target_pairs={{0,14},{1,15},{2,8},{3,9},{4,10},{5,11},{6,12},{7,13}} | collective-permute-start | bytes 356360 | tf_op jit(solution)/shard_map/ppermute | solution.py:577
  21.3 2.9 %copy-start.1 = (f32[128]{0:T(128)S(1)}, f32[128]{0:T(128)}, u32[]{:S(2)}) copy-start(f32[128]{0:T(128)} %param.20) | copy-start | bytes 1540
  21.3 1.5 %collective-permute-start.6 = (bf16[29,16,128]{2,1,0:T(8,128)(2,1)S(1)}, bf16[29,16,128]{2,1,0:T(8,128)(2,1)S(1)}, u32[]{:S(2)}, u32[]{:S(2)}) collective-permute-start(bf16[29,16,128]{2,1,0:T(8,128)(2,1)S(1)} %get-tuple-element.60), channel_id=1, source_target_pairs={{8,16},{9,17},{10,18},{11,19},{12,20},{13,21},{14,22},{15,23}} | collective-permute-start | bytes 356360 | tf_op jit(solution)/shard_map/ppermute | solution.py:577
  22.1 0.7 collective-permute-start.5
  22.9 1.4 %collective-permute-start.8 = (bf16[29,16,128]{2,1,0:T(8,128)(2,1)S(1)}, bf16[29,16,128]{2,1,0:T(8,128)(2,1)S(1)}, u32[]{:S(2)}, u32[]{:S(2)}) collective-permute-start(bf16[29,16,128]{2,1,0:T(8,128)(2,1)S(1)} %get-tuple-element.61), channel_id=1, source_target_pairs={{16,30},{17,31},{18,24},{19,25},{20,26},{21,27},{22,28},{23,29}} | collective-permute-start | bytes 356360 | tf_op jit(solution)/shard_map/ppermute | solution.py:577
  23.5 0.7 collective-permute-start.7
  24.3 1.4 %collective-permute-start.9 = (bf16[30,16,128]{2,1,0:T(8,128)(2,1)S(1)}, bf16[30,16,128]{2,1,0:T(8,128)(2,1)S(1)}, u32[]{:S(2)}, u32[]{:S(2)}) collective-permute-start(bf16[30,16,128]{2,1,0:T(8,128)(2,1)S(1)} %get-tuple-element.63), channel_id=1, source_target_pairs={{24,16},{25,17},{26,18},{27,19},{28,20},{29,21},{30,22},{31,23}} | collective-permute-start | bytes 368648 | tf_op jit(solution)/shard_map/ppermute | solution.py:577
  24.9 0.7 collective-permute-start.10
  25.7 1.4 %collective-permute-start.11 = (bf16[30,16,128]{2,1,0:T(8,128)(2,1)S(1)}, bf16[30,16,128]{2,1,0:T(8,128)(2,1)S(1)}, u32[]{:S(2)}, u32[]{:S(2)}) collective-permute-start(bf16[30,16,128]{2,1,0:T(8,128)(2,1)S(1)} %get-tuple-element.66), channel_id=1, source_target_pairs={{16,14},{17,15},{18,8},{19,9},{20,10},{21,11},{22,12},{23,13}} | collective-permute-start | bytes 368648 | tf_op jit(solution)/shard_map/ppermute | solution.py:577
  26.3 0.7 collective-permute-start.12
  27.2 48.4 %collective-permute-start.13 = (bf16[30,16,128]{2,1,0:T(8,128)(2,1)S(1)}, bf16[30,16,128]{2,1,0:T(8,128)(2,1)S(1)}, u32[]{:S(2)}, u32[]{:S(2)}) collective-permute-start(bf16[30,16,128]{2,1,0:T(8,128)(2,1)S(1)} %get-tuple-element.69), channel_id=1, source_target_pairs={{8,0},{9,1},{10,2},{11,3},{12,4},{13,5},{14,6},{15,7}} | collective-permute-start | bytes 368648 | tf_op jit(solution)/shard_map/ppermute | solution.py:577
  28.5 53.1 %collective-permute-start.14 = (bf16[30,16,128]{2,1,0:T(8,128)(2,1)S(1)}, bf16[30,16,128]{2,1,0:T(8,128)(2,1)S(1)}, u32[]{:S(2)}, u32[]{:S(2)}) collective-permute-start(bf16[30,16,128]{2,1,0:T(8,128)(2,1)S(1)} %get-tuple-element.70), channel_id=1, source_target_pairs={{8,2},{9,3},{10,4},{11,5},{12,6},{13,7},{14,0},{15,1}} | collective-permute-start | bytes 368648 | tf_op jit(solution)/shard_map/ppermute | solution.py:577
  84.0 6.0 %collective-permute-start.15 = (f32[8,128]{1,0:T(8,128)S(1)}, f32[8,128]{1,0:T(8,128)S(1)}, u32[]{:S(2)}, u32[]{:S(2)}) collective-permute-start(f32[8,128]{1,0:T(8,128)S(1)} %get-tuple-element.73), channel_id=1, source_target_pairs={{0,1},{1,0},{2,3},{3,2},{4,5},{5,4},{6,7},{7,6}} | collective-permute-start | bytes 12296 | tf_op jit(solution)/shard_map/ppermute | solution.py:573
  86.0 7.3 %collective-permute-start.16 = (f32[8,128]{1,0:T(8,128)S(1)}, f32[8,128]{1,0:T(8,128)S(1)}, u32[]{:S(2)}, u32[]{:S(2)}) collective-permute-start(f32[8,128]{1,0:T(8,128)S(1)} %get-tuple-element.74), channel_id=1, source_target_pairs={{0,2},{1,7},{2,4},{3,1},{4,6},{5,3},{6,0},{7,5}} | collective-permute-start | bytes 12296 | tf_op jit(solution)/shard_map/ppermute | solution.py:573
  87.9 6.7 %collective-permute-start.17 = (f32[8,128]{1,0:T(8,128)S(1)}, f32[8,128]{1,0:T(8,128)S(1)}, u32[]{:S(2)}, u32[]{:S(2)}) collective-permute-start(f32[8,128]{1,0:T(8,128)S(1)} %get-tuple-element.75), channel_id=1, source_target_pairs={{0,7},{1,2},{2,1},{3,4},{4,3},{5,6},{6,5},{7,0}} | collective-permute-start | bytes 12296 | tf_op jit(solution)/shard_map/ppermute | solution.py:573
  94.6 3.9 %collective-permute-start.20 = (f32[16,128]{1,0:T(8,128)S(1)}, f32[16,128]{1,0:T(8,128)S(1)}, u32[]{:S(2)}, u32[]{:S(2)}) collective-permute-start(f32[16,128]{1,0:T(8,128)S(1)} %join.1.refs_0_), channel_id=1, source_target_pairs={{0,24},{1,25},{2,26},{3,27},{4,28},{5,29},{6,30},{7,31}} | collective-permute-start | bytes 24584 | tf_op jit(solution)/shard_map/ppermute | solution.py:577
  95.9 2.6 %collective-permute-start.19 = (f32[16,128]{1,0:T(8,128)S(1)}, f32[16,128]{1,0:T(8,128)S(1)}, u32[]{:S(2)}, u32[]{:S(2)}) collective-permute-start(f32[16,128]{1,0:T(8,128)S(1)} %join.1.refs_0_), channel_id=1, source_target_pairs={{0,16},{1,17},{2,18},{3,19},{4,20},{5,21},{6,22},{7,23}} | collective-permute-start | bytes 24584 | tf_op jit(solution)/shard_map/ppermute | solution.py:577
  97.2 2.6 %collective-permute-start.18 = (f32[16,128]{1,0:T(8,128)S(1)}, f32[16,128]{1,0:T(8,128)S(1)}, u32[]{:S(2)}, u32[]{:S(2)}) collective-permute-start(f32[16,128]{1,0:T(8,128)S(1)} %join.1.refs_0_), channel_id=1, source_target_pairs={{0,8},{1,9},{2,10},{3,11},{4,12},{5,13},{6,14},{7,15}} | collective-permute-start | bytes 24584 | tf_op jit(solution)/shard_map/ppermute | solution.py:577

commit v7 on v5

--- a/solution.py
+++ b/solution.py
@@ -270,11 +270,19 @@
     return jnp.concatenate([edge, own, edge], axis=0)
 
 
+def place_of(pair, pairs, segment):
+    if segment == 0:
+        return pair
+    return 2 * pair if pair < pairs // 2 else 2 * (pairs - 1 - pair) + 1
+
+
 def first_slab(slabs):
     slab_now = lax.axis_index("space")
-    batch = lax.rem(slab_now, 2)
-    shift = lax.rem(lax.axis_index("segment"), 2)
-    return lax.rem(slab_now - batch + shift - 1 + slabs, slabs), batch
+    segment = lax.axis_index("segment")
+    chip = slab_now // 2
+    folded = jnp.where(lax.rem(chip, 2) == 0, chip // 2, slabs // 2 - 1 - chip // 2)
+    pair = jnp.where(segment == 0, chip, folded)
+    return lax.rem(2 * pair + lax.rem(segment, 2) - 1 + slabs, slabs), lax.rem(slab_now, 2)
 
 
 def send_back(moved, outs, sz):
@@ -323,14 +331,18 @@
     node_hbm, places_hbm, species_hbm, sources_hbm, grad_hbm, table_hbm, mine_ref, other_ref,
     states, places, species, sources, grads, table, sems
 ):
-    slab_now = lax.axis_index("space")
-    batch = lax.rem(slab_now, 2)
+    @pl.when(lax.axis_index("segment") == 0)
+    def _():
+        pack(
+            (node_hbm, places_hbm, species_hbm, sources_hbm, grad_hbm, table_hbm), mine_ref, other_ref,
+            states, places, species, sources, grads, table, sems,
+        )
+
+
+def pack(given, mine_ref, other_ref, states, places, species, sources, grads, table, sems):
+    batch = lax.rem(lax.axis_index("space"), 2)
     copies = []
-    pairs = (
-        (node_hbm, states), (places_hbm, places), (species_hbm, species), (sources_hbm, sources),
-        (grad_hbm, grads), (table_hbm, table),
-    )
-    for n, (source, target) in enumerate(pairs):
+    for n, (source, target) in enumerate(zip(given, (states, places, species, sources, grads, table))):
         copies.append(pltpu.make_async_copy(source, target, sems.at[n]))
         copies[-1].start()
     for copy in copies:
@@ -366,42 +378,29 @@
         ref[coefs] = jnp.where(chosen == 0, both[0][1].astype(F32), both[1][1].astype(F32)).astype(BF16)
 
 
-def open_kernel(
-    slabs, neighbours, mine_ref, partner_ref, straight_ref, cross_ref, rate_ref,
-    low_ref, high_ref, hot_ref, hot_t_ref, geo_ref, seed_ref
-):
-    start, batch = first_slab(slabs)
-    even = batch == 0
-    level = lax.rem(lax.axis_index("segment"), 2) == 0
-    coefs = low_ref.shape[0]
-    rows, c = low_ref.shape[1:]
-    per_slab = rows // 2
-    window = 2 * rows
-    edges = rows * neighbours
-
-    def choose(a, b):
-        return jnp.where(even, a, b)
-
-    def parts(k):
-        mine, partner = mine_ref[k].astype(F32), partner_ref[k].astype(F32)
-        straight, cross = straight_ref[k].astype(F32), cross_ref[k].astype(F32)
-        low, high = choose(mine, partner), choose(partner, mine)
-        after, last = choose(straight, cross), choose(cross, straight)
-        return [
-            jnp.where(level, last, low), jnp.where(level, low, high), jnp.where(level, high, after),
-            jnp.where(level, after, last),
-        ]
-
+def open_kernel(mine_ref, partner_ref, straight_ref, cross_ref, low_ref, high_ref):
     @pl.when(lax.axis_index("segment") == 0)
     def _():
-        for k in range(coefs):
-            slab = parts(k)
-            low_ref[k] = jnp.concatenate(slab[:2], axis=0).astype(BF16)
-            high_ref[k] = jnp.concatenate(slab[2:], axis=0).astype(BF16)
-
-    extra = jnp.concatenate(parts(coefs), axis=0)
+        even = lax.rem(lax.axis_index("space"), 2) == 0
+
+        def choose(a, b):
+            return jnp.where(even, a, b)
+
+        for k in range(low_ref.shape[0]):
+            mine, partner = mine_ref[k].astype(F32), partner_ref[k].astype(F32)
+            straight, cross = straight_ref[k].astype(F32), cross_ref[k].astype(F32)
+            low_ref[k] = jnp.concatenate([choose(cross, straight), choose(mine, partner)], axis=0).astype(BF16)
+            high_ref[k] = jnp.concatenate([choose(partner, mine), choose(straight, cross)], axis=0).astype(BF16)
+
+
+def edges_of(refs, coefs, slabs, neighbours, rate_ref, hot_ref, hot_t_ref, geo_ref):
+    start, _ = first_slab(slabs)
+    extra = jnp.concatenate([ref[coefs].astype(F32) for ref in refs], axis=0)
+    window, c = extra.shape
+    rows = window // 2
+    per_slab = rows // 2
+    edges = rows * neighbours
     numbers = decode(extra)
-    seed_ref[...] = jnp.broadcast_to(numbers[per_slab : per_slab + rows, 3:4], (rows, c))
     own_extra = extra[per_slab : per_slab + rows]
     low = pltpu.roll(own_extra, c - 8, 1)
     index = own_extra.astype(jnp.int32) * BASE + low.astype(jnp.int32)
@@ -414,9 +413,9 @@
         ],
         axis=0,
     )
-    hot_ref[...] = hot.astype(BF16)[:, :window]
     hot_t_ref[...] = jnp.transpose(hot).astype(BF16)[:window]
     hot = hot.astype(BF16)[:, :window]
+    hot_ref[...] = hot
     lift = lax.broadcasted_iota(jnp.int32, (window, c), 0) // per_slab - 1
     offset = []
     for n in range(3):
@@ -444,11 +443,12 @@
     ]
     for n, value in enumerate(values):
         geo_ref[n * edges : (n + 1) * edges, :] = value
+    return numbers[per_slab : per_slab + rows]
 
 
 def turn_to_stage():
     odd = lax.rem(lax.axis_index("space"), 2)
-    return jnp.where(lax.axis_index("segment") == 0, odd, 2)
+    return jnp.where(lax.axis_index("segment") == 0, odd, 0)
 
 
 def stage_kernel(moment, zero_hbm, one_hbm, two_hbm, *more):
@@ -467,12 +467,14 @@
 
 
 def forward_kernel(
-    tick, sz, low_ref, high_ref, hot_ref, geo_ref, zero_ref, one_ref, two_ref, out_ref, pooled_ref
+    tick, sz, slabs, neighbours, low_ref, high_ref, rate_ref, zero_ref, one_ref, two_ref,
+    out_ref, pooled_ref, hot_ref, hot_t_ref, geo_ref
 ):
     @pl.when(lax.axis_index("segment") == tick)
     def _():
         rows = low_ref.shape[1]
         refs = (low_ref, high_ref)
+        edges_of(refs, sz.coefs, slabs, neighbours, rate_ref, hot_ref, hot_t_ref, geo_ref)
         pooled = forward(refs, hot_ref, geo_ref, zero_ref, one_ref, two_ref, sz, rows, False)
         signal = signal_of(pooled, sz)
         gate, lifted = silu_parts(signal)
@@ -480,16 +482,19 @@
             pooled_ref[k] = pooled[k]
             added = lifted if k == 0 else gate * pooled[k]
             out_ref[k] = (own_rows(refs, k) + added).astype(BF16)
+        out_ref[sz.coefs] = own_rows(refs, sz.coefs).astype(BF16)
 
 
 def turn_kernel(
-    tick, sz, low_ref, high_ref, hot_ref, hot_t_ref, geo_ref, zero_ref, one_ref, two_ref,
-    read_ref, seed_ref, *outs
+    tick, sz, slabs, neighbours, low_ref, high_ref, rate_ref, zero_ref, one_ref, two_ref, read_ref,
+    back_low_ref, back_high_ref, hot_ref, hot_t_ref, geo_ref
 ):
     @pl.when(lax.axis_index("segment") == tick)
     def _():
         rows = low_ref.shape[1]
         refs = (low_ref, high_ref)
+        outs = (back_low_ref, back_high_ref)
+        own = edges_of(refs, sz.coefs, slabs, neighbours, rate_ref, hot_ref, hot_t_ref, geo_ref)
         pooled = forward(refs, hot_ref, geo_ref, zero_ref, one_ref, two_ref, sz, rows, True)
         signal = signal_of(pooled, sz)
         _, lifted = silu_parts(signal)
@@ -499,7 +504,7 @@
         energy = jnp.sum(read * active, axis=1, keepdims=True)
         lane = lax.broadcasted_iota(jnp.int32, (rows, sz.c), 1)
         energy = around(jnp.where(lane == 3, energy, 0.0), rows // 2)
-        upstream = [seed_ref[...] * read * (gate + updated * gate * (1.0 - gate))]
+        upstream = [own[:, 3:4] * read * (gate + updated * gate * (1.0 - gate))]
         moved = backward(
             upstream, pooled, refs, hot_ref, hot_t_ref, geo_ref, zero_ref, one_ref, two_ref, sz, rows, True, outs
         )
@@ -567,13 +572,16 @@
     axes = ("segment", "space")
     shape = jax.ShapeDtypeStruct
 
-    def within(value, target, count):
-        pairs = [(s * slabs + i, s * slabs + target(s % 2, i) % slabs) for s in range(count) for i in range(slabs)]
-        return lax.ppermute(value, axes, pairs)
+    pairs = slabs // 2
+
+    def within(value, target):
+        return lax.ppermute(value, axes, [(i, target(i) % slabs) for i in range(slabs)])
 
     def hop(value, start, stop, by):
-        pairs = [(start * slabs + i, stop * slabs + (i + by) % slabs) for i in range(slabs)]
-        return lax.ppermute(value, axes, pairs)
+        ways = [(place_of(q, pairs, start), place_of((q + by) % pairs, pairs, stop)) for q in range(pairs)]
+        return lax.ppermute(
+            value, axes, [(start * slabs + 2 * a + c, stop * slabs + 2 * b + c) for a, b in ways for c in range(2)]
+        )
 
     raw = [
         node_states.transpose(0, 2, 1, 3), places.transpose(1, 0, 2), species, sources, energy_grad, species_table,
@@ -583,70 +591,60 @@
         pack_kernel, raw, [packed, packed], "pack", [pltpu.HBM] * len(raw),
         [pltpu.VMEM(v.shape, v.dtype) for v in raw] + [pltpu.SemaphoreType.DMA((len(raw),))],
     )
-    partner = within(other, lambda odd, i: i + 1 - 2 * (i % 2), segments)
-    straight = within(mine, lambda odd, i: i - 2 if odd or i % 2 == 0 else i + 2, segments)
-    cross = within(other, lambda odd, i: i - 1 if i % 2 == 0 else i - 3 if odd else i + 1, segments)
+    partner = within(other, lambda i: i + 1 - 2 * (i % 2))
+    straight = within(mine, lambda i: i + 2 if i % 2 else i - 2)
+    cross = within(other, lambda i: i + 1 if i % 2 else i - 1)
     stored = [zero_weight[0], one_weight[0], two_weight[0]]
     spaces = [pltpu.HBM] * 3
     on_chip = [pltpu.VMEM(w.shape, w.dtype) for w in stored]
     sems = [pltpu.SemaphoreType.DMA((5,))]
     weights = call(functools.partial(stage_kernel, 0), stored, on_chip, "stage", spaces, sems)
-    whole = shape((coefs, rows, channels), BF16)
-    low, high, hot, hot_t, geo, seeds = call(
-        functools.partial(open_kernel, slabs, neighbours),
-        [mine, partner, straight, cross, radial_rate],
-        [
-            whole, whole, shape((edges, 2 * rows), BF16), shape((2 * rows, edges), BF16),
-            shape((10 * edges, channels), F32), shape((rows, channels), F32),
-        ],
-        "open",
-    )
-
-    def stage_more(moment, weights, after):
-        return call(
-            functools.partial(stage_kernel, moment), [*stored, *weights, after], on_chip, "stage",
-            spaces + [pltpu.VMEM] * 4, sems, {3: 0, 4: 1, 5: 2},
-        )
-
-    weights = stage_more(1, weights, seeds)
-    around_all = [(low, high)]
+    whole = shape((coefs + 1, rows, channels), BF16)
+    around_all = [call(open_kernel, [mine, partner, straight, cross], [whole, whole], "open")]
+    weights = call(
+        functools.partial(stage_kernel, 1), [*stored, *weights, around_all[0][0]], on_chip, "stage",
+        spaces + [pltpu.VMEM] * 4, sems, {3: 0, 4: 1, 5: 2},
+    )
+    edge_shapes = [
+        shape((edges, 2 * rows), BF16), shape((2 * rows, edges), BF16), shape((10 * edges, channels), F32),
+    ]
     kept = []
     for tick in range(segments - 1):
-        out, pooled = call(
-            functools.partial(forward_kernel, tick, sz),
-            [*around_all[tick], hot, geo, *weights],
-            [whole, shape((coefs, rows, channels), F32)],
+        out, *residuals = call(
+            functools.partial(forward_kernel, tick, sz, slabs, neighbours),
+            [*around_all[tick], radial_rate, *weights],
+            [whole, shape((coefs, rows, channels), F32), *edge_shapes],
             "forward",
         )
-        kept.append(pooled)
-        if tick == 0:
-            weights = stage_more(2, weights, out)
-        ways = (2, 0) if tick % 2 else (0, -2)
-        around_all.append(tuple(hop(out, tick, tick + 1, by) for by in ways))
+        kept.append(residuals)
+        ways = (1, 0) if tick % 2 else (0, -1)
+        around_all.append([hop(out, tick, tick + 1, by) for by in ways])
     final = segments - 1
-    whole_more = shape((coefs + 1, rows, channels), BF16)
     slab_sums = shape((per_slab, channels), F32)
     parts = call(
-        functools.partial(turn_kernel, final, sz),
-        [*around_all[final], hot, hot_t, geo, *weights, read_weight.reshape(1, channels), seeds],
-        [whole_more, whole_more],
+        functools.partial(turn_kernel, final, sz, slabs, neighbours),
+        [*around_all[final], radial_rate, *weights, read_weight.reshape(1, channels)],
+        [whole, whole, *edge_shapes],
         "turn",
-    )
+    )[:2]
     for tick in reversed(range(segments - 1)):
-        ways = (2, 0) if tick % 2 else (0, -2)
+        ways = (1, 0) if tick % 2 else (0, -1)
         up = [hop(part, tick + 1, tick, -by) for part, by in zip(parts, ways)]
+        pooled, *residuals = kept[tick]
         parts = call(
             functools.partial(backward_kernel, tick, sz),
-            [*up, kept[tick], *around_all[tick], hot, hot_t, geo, *weights],
-            [whole_more, whole_more] if tick else [slab_sums] * 4,
+            [*up, pooled, *around_all[tick], *residuals, *weights],
+            [whole, whole] if tick else [slab_sums] * 4,
             "backward",
         )
     here, theirs, straight, cross = parts
-    theirs = within(theirs, lambda odd, i: i + 1 - 2 * (i % 2), 1)
-    straight = within(straight, lambda odd, i: i - 2 if i % 2 else i + 2, 1)
-    cross = within(cross, lambda odd, i: i + 1 if i % 2 else i - 1, 1)
+    theirs = within(theirs, lambda i: i + 1 - 2 * (i % 2))
+    straight = within(straight, lambda i: i - 2 if i % 2 else i + 2)
+    cross = within(cross, lambda i: i + 1 if i % 2 else i - 1)
     (both,) = call(join_kernel, [here, theirs, straight, cross], [shape((rows, channels), F32)], "join")
-    copies = [both] + [hop(both, 0, stop, 0) for stop in range(1, segments)]
+    copies = [both] + [
+        lax.ppermute(both, axes, [(i, stop * slabs + i) for i in range(slabs)]) for stop in range(1, segments)
+    ]
     energies, gradients = call(
         close_kernel, copies, [shape((batches, per_slab), F32), shape((3, batches, per_slab), F32)], "close"
     )

time: 102 us -> 106 us (1.039)
  starting transfers between devices: 27.6 us -> 34.8 us
  waiting for transfers between devices: 63.2 us -> 58.6 us
    ppermute x21, starting transfers between devices: 27.6 us -> 34.8 us  [the longest x6 20.3 us: within(): lax.ppermute(value, axes, [(i, target(i) % slabs) for i in range(slabs)])]
    ppermute x21, waiting for transfers between devices: 63.2 us -> 58.6 us  [the longest x12 54.2 us: hop(): lax.ppermute(value, axes, [(start * slabs + 2 * a + c, stop * slabs + 2 *...]
    pallas_call x14 -> x13, Pallas kernels: 9.53 us -> 10.1 us  [call(): pl.pallas_call(body, out_shape=shapes, in_specs=[pl.BlockSpec(memory_spac...]
  transfers between devices with their start and end apart: 21 -> 21, of which waited for: 8 -> 6; matrix products, arithmetic and copies ran while one was open for 0% -> 0% of each run, Pallas kernels for 3% -> 3%
where the time goes in v7:
time: 106 us; the launch traced here: 105 us
  waiting for transfers between devices  58.6 us (55%)
  starting transfers between devices  34.8 us (33%)
  Pallas kernels  10.1 us (10%)
    ppermute x12, waiting for transfers between devices, hop(): lax.ppermute(value, axes, [(start * slabs + 2 * a + c, stop * slabs + 2 *...  54.2 us
    ppermute x6, starting transfers between devices, within(): lax.ppermute(value, axes, [(i, target(i) % slabs) for i in range(slabs)])  20.3 us
    ppermute x12, starting transfers between devices, hop(): lax.ppermute(value, axes, [(start * slabs + 2 * a + c, stop * slabs + 2 *...  10.6 us
    pallas_call x13, Pallas kernels, call(): pl.pallas_call(body, out_shape=shapes, in_specs=[pl.BlockSpec(memory_spac...  10.1 us
    ppermute x3, starting transfers between devices, on_device(): lax.ppermute(both, axes, [(i, stop * slabs + i) for i in range(slabs)])  3.86 us
    ppermute x6, waiting for transfers between devices, within(): lax.ppermute(value, axes, [(i, target(i) % slabs) for i in range(slabs)])  3.08 us
  transfers between devices with their start and end apart: 21, of which 6 were waited for; matrix products, arithmetic and copies ran while one was open for 0% of the time, Pallas kernels for 3%

profile of v7, /device:TPU:0, one launch (start us, length us, event | category | flops | bytes accessed | tf_op | source)
XLA Modules:
  0.0 105.1 jit_solution(6309966133086607975)
XLA Ops:
  0.6 1.2 %pack.1 = (bf16[30,8,128]{2,1,0:T(8,128)(2,1)S(1)}, bf16[30,8,128]{2,1,0:T(8,128)(2,1)S(1)}) custom-call(bf16[2,29,8,128]{3,2,1,0:T(8,128)(2,1)} %bitcast.14, f32[3,2,8]{2,1,0:T(2,128)} %bitcast.15, s32[2,8]{1,0:T(2,128)} %species_hbm.1, s32[2,8,8]{2,1,0:T(8,128)} %sources_hbm.1, f32[2,8]{1,0:T(2,128)} %grad_hbm.1, bf16[100,128]{1,0:T(8,128)(2,1)} %table_hbm.1), custom_call_target="tpu_custom_call" | custom-call | tf_op jit(solution)/shard_map/pack/pallas_call | solution.py:539
  1.9 7.0 %collective-permute-start.1 = (bf16[30,8,128]{2,1,0:T(8,128)(2,1)S(1)}, bf16[30,8,128]{2,1,0:T(8,128)(2,1)S(1)}, u32[]{:S(2)}, u32[]{:S(2)}) collective-permute-start(bf16[30,8,128]{2,1,0:T(8,128)(2,1)S(1)} %get-tuple-element.39.mine_ref), channel_id=1, source_target_pairs={{0,6},{1,3},{2,0},{3,5},{4,2},{5,7},{6,4},{7,1}} | collective-permute-start | bytes 184328 | tf_op jit(solution)/shard_map/ppermute | solution.py:578
  8.8 1.9 %collective-permute-start.2 = (bf16[30,8,128]{2,1,0:T(8,128)(2,1)S(1)}, bf16[30,8,128]{2,1,0:T(8,128)(2,1)S(1)}, u32[]{:S(2)}, u32[]{:S(2)}) collective-permute-start(bf16[30,8,128]{2,1,0:T(8,128)(2,1)S(1)} %get-tuple-element.40), channel_id=1, source_target_pairs={{0,7},{1,2},{2,1},{3,4},{4,3},{5,6},{6,5},{7,0}} | collective-permute-start | bytes 184328 | tf_op jit(solution)/shard_map/ppermute | solution.py:578
  10.8 1.9 %collective-permute-start = (bf16[30,8,128]{2,1,0:T(8,128)(2,1)S(1)}, bf16[30,8,128]{2,1,0:T(8,128)(2,1)S(1)}, u32[]{:S(2)}, u32[]{:S(2)}) collective-permute-start(bf16[30,8,128]{2,1,0:T(8,128)(2,1)S(1)} %get-tuple-element.40), channel_id=1, source_target_pairs={{0,1},{1,0},{2,3},{3,2},{4,5},{5,4},{6,7},{7,6}} | collective-permute-start | bytes 184328 | tf_op jit(solution)/shard_map/ppermute | solution.py:578
  12.7 2.6 %stage.2 = (bf16[896,896]{1,0:T(8,128)(2,1)S(1)}, bf16[2,768,768]{2,1,0:T(8,128)(2,1)S(1)}, bf16[2,640,640]{2,1,0:T(8,128)(2,1)S(1)}) custom-call(bf16[896,896]{1,0:T(8,128)(2,1)} %bitcast.12, bf16[2,768,768]{2,1,0:T(8,128)(2,1)} %bitcast.8, bf16[2,640,640]{2,1,0:T(8,128)(2,1)} %bitcast.10), custom_call_target="tpu_custom_call" | custom-call | tf_op jit(solution)/shard_map/stage/pallas_call | solution.py:539
  15.3 0.8 collective-permute-done.2.cross_ref
  16.2 0.0 collective-permute-done.partner_ref
  16.2 0.1 open.1
  16.2 0.0 copy-start
  16.2 0.1 stage.3
  16.3 0.6 copy-done
  16.9 1.9 %forward.3 = (bf16[30,16,128]{2,1,0:T(8,128)(2,1)S(1)}, f32[29,16,128]{2,1,0:T(8,128)S(1)}, bf16[128,32]{1,0:T(8,128)(2,1)S(1)}, bf16[32,128]{1,0:T(8,128)(2,1)S(1)}, f32[1280,128]{1,0:T(8,128)S(1)}) custom-call(bf16[30,16,128]{2,1,0:T(8,128)(2,1)S(1)} %get-tuple-element.41.more_3_.low_ref, bf16[30,16,128]{2,1,0:T(8,128)(2,1)S(1)} %get-tuple-element.42.high_ref, ...), custom_call_target="tpu_custom_call" | custom-call | tf_op jit(solution)/shard_map/forward/pallas_call | solution.py:539
  18.8 1.3 %collective-permute-start.4 = (bf16[30,16,128]{2,1,0:T(8,128)(2,1)S(1)}, bf16[30,16,128]{2,1,0:T(8,128)(2,1)S(1)}, u32[]{:S(2)}, u32[]{:S(2)}) collective-permute-start(bf16[30,16,128]{2,1,0:T(8,128)(2,1)S(1)} %get-tuple-element.49), channel_id=1, source_target_pairs={{0,10},{1,11},{2,8},{3,9},{4,12},{5,13},{6,14},{7,15}} | collective-permute-start | bytes 368648 | tf_op jit(solution)/shard_map/ppermute | solution.py:582
  20.1 1.3 %collective-permute-start.3 = (bf16[30,16,128]{2,1,0:T(8,128)(2,1)S(1)}, bf16[30,16,128]{2,1,0:T(8,128)(2,1)S(1)}, u32[]{:S(2)}, u32[]{:S(2)}) collective-permute-start(bf16[30,16,128]{2,1,0:T(8,128)(2,1)S(1)} %get-tuple-element.49), channel_id=1, source_target_pairs={{0,8},{1,9},{2,12},{3,13},{4,14},{5,15},{6,10},{7,11}} | collective-permute-start | bytes 368648 | tf_op jit(solution)/shard_map/ppermute | solution.py:582
  21.4 1.6 %collective-permute-done.4.high_ref = bf16[30,16,128]{2,1,0:T(8,128)(2,1)S(1)} collective-permute-done((bf16[30,16,128]{2,1,0:T(8,128)(2,1)S(1)}, bf16[30,16,128]{2,1,0:T(8,128)(2,1)S(1)}, u32[]{:S(2)}, u32[]{:S(2)}) %collective-permute-start.4) | collective-permute-done | bytes 122912 | tf_op jit(solution)/shard_map/ppermute | solution.py:582
  23.0 2.0 %collective-permute-done.3.low_ref = bf16[30,16,128]{2,1,0:T(8,128)(2,1)S(1)} collective-permute-done((bf16[30,16,128]{2,1,0:T(8,128)(2,1)S(1)}, bf16[30,16,128]{2,1,0:T(8,128)(2,1)S(1)}, u32[]{:S(2)}, u32[]{:S(2)}) %collective-permute-start.3) | collective-permute-done | bytes 122912 | tf_op jit(solution)/shard_map/ppermute | solution.py:582
  25.1 0.8 collective-permute-start.6
  25.9 0.7 collective-permute-start.5
  26.5 0.0 collective-permute-done.6.high_ref
  26.6 0.7 collective-permute-start.8
  27.3 0.7 collective-permute-start.7
  27.9 0.0 collective-permute-done.8.high_ref
  28.0 0.9 turn.1
  28.9 0.7 collective-permute-start.9
  29.5 0.7 collective-permute-start.10
  30.2 0.0 collective-permute-done.10.up_high_ref
  30.3 0.7 collective-permute-start.11
  30.9 0.7 collective-permute-start.12
  31.6 0.0 collective-permute-done.11.up_low_ref
  31.6 0.0 collective-permute-done.12.up_high_ref
  31.6 0.2 backward.4
  31.8 1.3 %collective-permute-start.13 = (bf16[30,16,128]{2,1,0:T(8,128)(2,1)S(1)}, bf16[30,16,128]{2,1,0:T(8,128)(2,1)S(1)}, u32[]{:S(2)}, u32[]{:S(2)}) collective-permute-start(bf16[30,16,128]{2,1,0:T(8,128)(2,1)S(1)} %get-tuple-element.64), channel_id=1, source_target_pairs={{8,0},{9,1},{12,2},{13,3},{14,4},{15,5},{10,6},{11,7}} | collective-permute-start | bytes 368648 | tf_op jit(solution)/shard_map/ppermute | solution.py:582
  33.1 1.3 %collective-permute-start.14 = (bf16[30,16,128]{2,1,0:T(8,128)(2,1)S(1)}, bf16[30,16,128]{2,1,0:T(8,128)(2,1)S(1)}, u32[]{:S(2)}, u32[]{:S(2)}) collective-permute-start(bf16[30,16,128]{2,1,0:T(8,128)(2,1)S(1)} %get-tuple-element.65), channel_id=1, source_target_pairs={{8,2},{9,3},{12,4},{13,5},{14,6},{15,7},{10,0},{11,1}} | collective-permute-start | bytes 368648 | tf_op jit(solution)/shard_map/ppermute | solution.py:582
  34.4 50.5 %collective-permute-done.13.up_low_ref = bf16[30,16,128]{2,1,0:T(8,128)(2,1)S(1)} collective-permute-done((bf16[30,16,128]{2,1,0:T(8,128)(2,1)S(1)}, bf16[30,16,128]{2,1,0:T(8,128)(2,1)S(1)}, u32[]{:S(2)}, u32[]{:S(2)}) %collective-permute-start.13) | collective-permute-done | bytes 122912 | tf_op jit(solution)/shard_map/ppermute | solution.py:582
  85.0 2.3 %backward.5 = (f32[8,128]{1,0:T(8,128)S(1)}, f32[8,128]{1,0:T(8,128)S(1)}, f32[8,128]{1,0:T(8,128)S(1)}, f32[8,128]{1,0:T(8,128)S(1)}) custom-call(bf16[30,16,128]{2,1,0:T(8,128)(2,1)S(1)} %collective-permute-done.13.up_low_ref, bf16[30,16,128]{2,1,0:T(8,128)(2,1)S(1)} %collective-permute-done.14.up_high_ref, ...), custom_call_target="tpu_custom_call" | custom-call | tf_op jit(solution)/shard_map/backward/pallas_call | solution.py:539
  87.3 1.9 %collective-permute-start.15 = (f32[8,128]{1,0:T(8,128)S(1)}, f32[8,128]{1,0:T(8,128)S(1)}, u32[]{:S(2)}, u32[]{:S(2)}) collective-permute-start(f32[8,128]{1,0:T(8,128)S(1)} %get-tuple-element.71), channel_id=1, source_target_pairs={{0,1},{1,0},{2,3},{3,2},{4,5},{5,4},{6,7},{7,6}} | collective-permute-start | bytes 12296 | tf_op jit(solution)/shard_map/ppermute | solution.py:578
  89.2 3.2 %collective-permute-start.16 = (f32[8,128]{1,0:T(8,128)S(1)}, f32[8,128]{1,0:T(8,128)S(1)}, u32[]{:S(2)}, u32[]{:S(2)}) collective-permute-start(f32[8,128]{1,0:T(8,128)S(1)} %get-tuple-element.72), channel_id=1, source_target_pairs={{0,2},{1,7},{2,4},{3,1},{4,6},{5,3},{6,0},{7,5}} | collective-permute-start | bytes 12296 | tf_op jit(solution)/shard_map/ppermute | solution.py:578
  92.4 4.4 %collective-permute-start.17 = (f32[8,128]{1,0:T(8,128)S(1)}, f32[8,128]{1,0:T(8,128)S(1)}, u32[]{:S(2)}, u32[]{:S(2)}) collective-permute-start(f32[8,128]{1,0:T(8,128)S(1)} %get-tuple-element.73), channel_id=1, source_target_pairs={{0,7},{1,2},{2,1},{3,4},{4,3},{5,6},{6,5},{7,0}} | collective-permute-start | bytes 12296 | tf_op jit(solution)/shard_map/ppermute | solution.py:578
  96.8 0.0 collective-permute-done.15.theirs_ref
  96.9 0.0 collective-permute-done.16.straight_ref
  96.9 2.3 %collective-permute-done.17.cross_ref = f32[8,128]{1,0:T(8,128)S(1)} collective-permute-done((f32[8,128]{1,0:T(8,128)S(1)}, f32[8,128]{1,0:T(8,128)S(1)}, u32[]{:S(2)}, u32[]{:S(2)}) %collective-permute-start.17) | collective-permute-done | bytes 4128 | tf_op jit(solution)/shard_map/ppermute | solution.py:578
  99.1 1.3 %collective-permute-start.20 = (f32[16,128]{1,0:T(8,128)S(1)}, f32[16,128]{1,0:T(8,128)S(1)}, u32[]{:S(2)}, u32[]{:S(2)}) collective-permute-start(f32[16,128]{1,0:T(8,128)S(1)} %join.1.refs_0_), channel_id=1, source_target_pairs={{0,24},{1,25},{2,26},{3,27},{4,28},{5,29},{6,30},{7,31}} | collective-permute-start | bytes 24584 | tf_op jit(solution)/shard_map/ppermute | solution.py:646
  100.4 1.3 %collective-permute-start.19 = (f32[16,128]{1,0:T(8,128)S(1)}, f32[16,128]{1,0:T(8,128)S(1)}, u32[]{:S(2)}, u32[]{:S(2)}) collective-permute-start(f32[16,128]{1,0:T(8,128)S(1)} %join.1.refs_0_), channel_id=1, source_target_pairs={{0,16},{1,17},{2,18},{3,19},{4,20},{5,21},{6,22},{7,23}} | collective-permute-start | bytes 24584 | tf_op jit(solution)/shard_map/ppermute | solution.py:646
  101.7 1.3 %collective-permute-start.18 = (f32[16,128]{1,0:T(8,128)S(1)}, f32[16,128]{1,0:T(8,128)S(1)}, u32[]{:S(2)}, u32[]{:S(2)}) collective-permute-start(f32[16,128]{1,0:T(8,128)S(1)} %join.1.refs_0_), channel_id=1, source_target_pairs={{0,8},{1,9},{2,10},{3,11},{4,12},{5,13},{6,14},{7,15}} | collective-permute-start | bytes 24584 | tf_op jit(solution)/shard_map/ppermute | solution.py:646
  103.0 0.0 collective-permute-done.20.refs_3_
  103.0 0.0 collective-permute-done.19.refs_2_
  103.1 1.3 %collective-permute-done.18.refs_1_ = f32[16,128]{1,0:T(8,128)S(1)} collective-permute-done((f32[16,128]{1,0:T(8,128)S(1)}, f32[16,128]{1,0:T(8,128)S(1)}, u32[]{:S(2)}, u32[]{:S(2)}) %collective-permute-start.18) | collective-permute-done | bytes 8224 | tf_op jit(solution)/shard_map/ppermute | solution.py:646
  104.4 0.7 close.1
  (11 shorter events, 0.1 us)
Async XLA Ops:
  1.9 13.5 %collective-permute-start.1 = (bf16[30,8,128]{2,1,0:T(8,128)(2,1)S(1)}, bf16[30,8,128]{2,1,0:T(8,128)(2,1)S(1)}, u32[]{:S(2)}, u32[]{:S(2)}) collective-permute-start(bf16[30,8,128]{2,1,0:T(8,128)(2,1)S(1)} %get-tuple-element.39.mine_ref), channel_id=1, source_target_pairs={{0,6},{1,3},{2,0},{3,5},{4,2},{5,7},{6,4},{7,1}} | collective-permute-start | bytes 184328 | tf_op jit(solution)/shard_map/ppermute | solution.py:578
  8.8 7.3 %collective-permute-start.2 = (bf16[30,8,128]{2,1,0:T(8,128)(2,1)S(1)}, bf16[30,8,128]{2,1,0:T(8,128)(2,1)S(1)}, u32[]{:S(2)}, u32[]{:S(2)}) collective-permute-start(bf16[30,8,128]{2,1,0:T(8,128)(2,1)S(1)} %get-tuple-element.40), channel_id=1, source_target_pairs={{0,7},{1,2},{2,1},{3,4},{4,3},{5,6},{6,5},{7,0}} | collective-permute-start | bytes 184328 | tf_op jit(solution)/shard_map/ppermute | solution.py:578
  10.8 5.4 %collective-permute-start = (bf16[30,8,128]{2,1,0:T(8,128)(2,1)S(1)}, bf16[30,8,128]{2,1,0:T(8,128)(2,1)S(1)}, u32[]{:S(2)}, u32[]{:S(2)}) collective-permute-start(bf16[30,8,128]{2,1,0:T(8,128)(2,1)S(1)} %get-tuple-element.40), channel_id=1, source_target_pairs={{0,1},{1,0},{2,3},{3,2},{4,5},{5,4},{6,7},{7,6}} | collective-permute-start | bytes 184328 | tf_op jit(solution)/shard_map/ppermute | solution.py:578
  16.2 0.7 copy-start
  18.8 4.2 %collective-permute-start.4 = (bf16[30,16,128]{2,1,0:T(8,128)(2,1)S(1)}, bf16[30,16,128]{2,1,0:T(8,128)(2,1)S(1)}, u32[]{:S(2)}, u32[]{:S(2)}) collective-permute-start(bf16[30,16,128]{2,1,0:T(8,128)(2,1)S(1)} %get-tuple-element.49), channel_id=1, source_target_pairs={{0,10},{1,11},{2,8},{3,9},{4,12},{5,13},{6,14},{7,15}} | collective-permute-start | bytes 368648 | tf_op jit(solution)/shard_map/ppermute | solution.py:582
  20.1 4.9 %collective-permute-start.3 = (bf16[30,16,128]{2,1,0:T(8,128)(2,1)S(1)}, bf16[30,16,128]{2,1,0:T(8,128)(2,1)S(1)}, u32[]{:S(2)}, u32[]{:S(2)}) collective-permute-start(bf16[30,16,128]{2,1,0:T(8,128)(2,1)S(1)} %get-tuple-element.49), channel_id=1, source_target_pairs={{0,8},{1,9},{2,12},{3,13},{4,14},{5,15},{6,10},{7,11}} | collective-permute-start | bytes 368648 | tf_op jit(solution)/shard_map/ppermute | solution.py:582
  25.1 2.9 %copy-start.1 = (f32[128]{0:T(128)S(1)}, f32[128]{0:T(128)}, u32[]{:S(2)}) copy-start(f32[128]{0:T(128)} %param.20) | copy-start | bytes 1540
  25.1 1.5 %collective-permute-start.6 = (bf16[30,16,128]{2,1,0:T(8,128)(2,1)S(1)}, bf16[30,16,128]{2,1,0:T(8,128)(2,1)S(1)}, u32[]{:S(2)}, u32[]{:S(2)}) collective-permute-start(bf16[30,16,128]{2,1,0:T(8,128)(2,1)S(1)} %get-tuple-element.50), channel_id=1, source_target_pairs={{8,16},{9,17},{12,20},{13,21},{14,22},{15,23},{10,18},{11,19}} | collective-permute-start | bytes 368648 | tf_op jit(solution)/shard_map/ppermute | solution.py:582
  25.9 0.7 collective-permute-start.5
  26.6 1.4 %collective-permute-start.8 = (bf16[30,16,128]{2,1,0:T(8,128)(2,1)S(1)}, bf16[30,16,128]{2,1,0:T(8,128)(2,1)S(1)}, u32[]{:S(2)}, u32[]{:S(2)}) collective-permute-start(bf16[30,16,128]{2,1,0:T(8,128)(2,1)S(1)} %get-tuple-element.51), channel_id=1, source_target_pairs={{16,26},{17,27},{20,24},{21,25},{22,28},{23,29},{18,30},{19,31}} | collective-permute-start | bytes 368648 | tf_op jit(solution)/shard_map/ppermute | solution.py:582
  27.3 0.7 collective-permute-start.7
  28.9 1.3 %collective-permute-start.9 = (bf16[30,16,128]{2,1,0:T(8,128)(2,1)S(1)}, bf16[30,16,128]{2,1,0:T(8,128)(2,1)S(1)}, u32[]{:S(2)}, u32[]{:S(2)}) collective-permute-start(bf16[30,16,128]{2,1,0:T(8,128)(2,1)S(1)} %get-tuple-element.52), channel_id=1, source_target_pairs={{24,16},{25,17},{28,20},{29,21},{30,22},{31,23},{26,18},{27,19}} | collective-permute-start | bytes 368648 | tf_op jit(solution)/shard_map/ppermute | solution.py:582
  29.5 0.7 collective-permute-start.10
  30.3 1.4 %collective-permute-start.11 = (bf16[30,16,128]{2,1,0:T(8,128)(2,1)S(1)}, bf16[30,16,128]{2,1,0:T(8,128)(2,1)S(1)}, u32[]{:S(2)}, u32[]{:S(2)}) collective-permute-start(bf16[30,16,128]{2,1,0:T(8,128)(2,1)S(1)} %get-tuple-element.58), channel_id=1, source_target_pairs={{16,10},{17,11},{20,8},{21,9},{22,12},{23,13},{18,14},{19,15}} | collective-permute-start | bytes 368648 | tf_op jit(solution)/shard_map/ppermute | solution.py:582
  30.9 0.7 collective-permute-start.12
  31.8 53.1 %collective-permute-start.13 = (bf16[30,16,128]{2,1,0:T(8,128)(2,1)S(1)}, bf16[30,16,128]{2,1,0:T(8,128)(2,1)S(1)}, u32[]{:S(2)}, u32[]{:S(2)}) collective-permute-start(bf16[30,16,128]{2,1,0:T(8,128)(2,1)S(1)} %get-tuple-element.64), channel_id=1, source_target_pairs={{8,0},{9,1},{12,2},{13,3},{14,4},{15,5},{10,6},{11,7}} | collective-permute-start | bytes 368648 | tf_op jit(solution)/shard_map/ppermute | solution.py:582
  33.1 51.8 %collective-permute-start.14 = (bf16[30,16,128]{2,1,0:T(8,128)(2,1)S(1)}, bf16[30,16,128]{2,1,0:T(8,128)(2,1)S(1)}, u32[]{:S(2)}, u32[]{:S(2)}) collective-permute-start(bf16[30,16,128]{2,1,0:T(8,128)(2,1)S(1)} %get-tuple-element.65), channel_id=1, source_target_pairs={{8,2},{9,3},{12,4},{13,5},{14,6},{15,7},{10,0},{11,1}} | collective-permute-start | bytes 368648 | tf_op jit(solution)/shard_map/ppermute | solution.py:582
  87.3 9.5 %collective-permute-start.15 = (f32[8,128]{1,0:T(8,128)S(1)}, f32[8,128]{1,0:T(8,128)S(1)}, u32[]{:S(2)}, u32[]{:S(2)}) collective-permute-start(f32[8,128]{1,0:T(8,128)S(1)} %get-tuple-element.71), channel_id=1, source_target_pairs={{0,1},{1,0},{2,3},{3,2},{4,5},{5,4},{6,7},{7,6}} | collective-permute-start | bytes 12296 | tf_op jit(solution)/shard_map/ppermute | solution.py:578
  89.2 7.6 %collective-permute-start.16 = (f32[8,128]{1,0:T(8,128)S(1)}, f32[8,128]{1,0:T(8,128)S(1)}, u32[]{:S(2)}, u32[]{:S(2)}) collective-permute-start(f32[8,128]{1,0:T(8,128)S(1)} %get-tuple-element.72), channel_id=1, source_target_pairs={{0,2},{1,7},{2,4},{3,1},{4,6},{5,3},{6,0},{7,5}} | collective-permute-start | bytes 12296 | tf_op jit(solution)/shard_map/ppermute | solution.py:578
  92.4 6.7 %collective-permute-start.17 = (f32[8,128]{1,0:T(8,128)S(1)}, f32[8,128]{1,0:T(8,128)S(1)}, u32[]{:S(2)}, u32[]{:S(2)}) collective-permute-start(f32[8,128]{1,0:T(8,128)S(1)} %get-tuple-element.73), channel_id=1, source_target_pairs={{0,7},{1,2},{2,1},{3,4},{4,3},{5,6},{6,5},{7,0}} | collective-permute-start | bytes 12296 | tf_op jit(solution)/shard_map/ppermute | solution.py:578
  99.1 3.9 %collective-permute-start.20 = (f32[16,128]{1,0:T(8,128)S(1)}, f32[16,128]{1,0:T(8,128)S(1)}, u32[]{:S(2)}, u32[]{:S(2)}) collective-permute-start(f32[16,128]{1,0:T(8,128)S(1)} %join.1.refs_0_), channel_id=1, source_target_pairs={{0,24},{1,25},{2,26},{3,27},{4,28},{5,29},{6,30},{7,31}} | collective-permute-start | bytes 24584 | tf_op jit(solution)/shard_map/ppermute | solution.py:646
  100.4 2.6 %collective-permute-start.19 = (f32[16,128]{1,0:T(8,128)S(1)}, f32[16,128]{1,0:T(8,128)S(1)}, u32[]{:S(2)}, u32[]{:S(2)}) collective-permute-start(f32[16,128]{1,0:T(8,128)S(1)} %join.1.refs_0_), channel_id=1, source_target_pairs={{0,16},{1,17},{2,18},{3,19},{4,20},{5,21},{6,22},{7,23}} | collective-permute-start | bytes 24584 | tf_op jit(solution)/shard_map/ppermute | solution.py:646
  101.7 2.6 %collective-permute-start.18 = (f32[16,128]{1,0:T(8,128)S(1)}, f32[16,128]{1,0:T(8,128)S(1)}, u32[]{:S(2)}, u32[]{:S(2)}) collective-permute-start(f32[16,128]{1,0:T(8,128)S(1)} %join.1.refs_0_), channel_id=1, source_target_pairs={{0,8},{1,9},{2,10},{3,11},{4,12},{5,13},{6,14},{7,15}} | collective-permute-start | bytes 24584 | tf_op jit(solution)/shard_map/ppermute | solution.py:646

commit v8 on v7

--- a/solution.py
+++ b/solution.py
@@ -575,13 +575,16 @@
     pairs = slabs // 2
 
     def within(value, target):
-        return lax.ppermute(value, axes, [(i, target(i) % slabs) for i in range(slabs)])
+        ways = [(s * slabs + i, s * slabs + target(i) % slabs) for s in range(segments) for i in range(slabs)]
+        return lax.ppermute(value, axes, ways)
 
     def hop(value, start, stop, by):
         ways = [(place_of(q, pairs, start), place_of((q + by) % pairs, pairs, stop)) for q in range(pairs)]
-        return lax.ppermute(
-            value, axes, [(start * slabs + 2 * a + c, stop * slabs + 2 * b + c) for a, b in ways for c in range(2)]
-        )
+        ways = [(start * slabs + 2 * a + c, stop * slabs + 2 * b + c) for a, b in ways for c in range(2)]
+        ways += [(b, a) for a, b in ways]
+        moving = {a for a, _ in ways}
+        ways += [(i, i) for i in range(segments * slabs) if i not in moving]
+        return lax.ppermute(value, axes, ways)
 
     raw = [
         node_states.transpose(0, 2, 1, 3), places.transpose(1, 0, 2), species, sources, energy_grad, species_table,
@@ -624,9 +627,10 @@
     parts = call(
         functools.partial(turn_kernel, final, sz, slabs, neighbours),
         [*around_all[final], radial_rate, *weights, read_weight.reshape(1, channels)],
-        [whole, whole, *edge_shapes],
+        [whole, whole],
         "turn",
-    )[:2]
+        scratch=[pltpu.VMEM(v.shape, v.dtype) for v in edge_shapes],
+    )
     for tick in reversed(range(segments - 1)):
         ways = (1, 0) if tick % 2 else (0, -1)
         up = [hop(part, tick + 1, tick, -by) for part, by in zip(parts, ways)]
@@ -643,7 +647,8 @@
     cross = within(cross, lambda i: i + 1 if i % 2 else i - 1)
     (both,) = call(join_kernel, [here, theirs, straight, cross], [shape((rows, channels), F32)], "join")
     copies = [both] + [
-        lax.ppermute(both, axes, [(i, stop * slabs + i) for i in range(slabs)]) for stop in range(1, segments)
+        lax.ppermute(both, "segment", [(s, (s + stop) % segments) for s in range(segments)])
+        for stop in range(1, segments)
     ]
     energies, gradients = call(
         close_kernel, copies, [shape((batches, per_slab), F32), shape((3, batches, per_slab), F32)], "close"

time: 106 us -> 112 us (1.057)
  starting transfers between devices: 34.8 us -> 79.3 us
  waiting for transfers between devices: 58.6 us -> 22.1 us
    ppermute x21, starting transfers between devices: 34.8 us -> 79.3 us  [the longest x12 69.8 us: hop(): return lax.ppermute(value, axes, ways)]
    ppermute x21, waiting for transfers between devices: 58.6 us -> 22.1 us  [the longest x12 11.3 us: hop(): return lax.ppermute(value, axes, ways)]
  transfers between devices with their start and end apart: 21 -> 21, of which waited for: 6 -> 10; matrix products, arithmetic and copies ran while one was open for 0% -> 0% of each run, Pallas kernels for 3% -> 2%
where the time goes in v8:
time: 112 us
  starting transfers between devices  79.3 us (71%)
  waiting for transfers between devices  22.1 us (20%)
  Pallas kernels  9.19 us (8%)
    ppermute x12, starting transfers between devices, hop(): return lax.ppermute(value, axes, ways)  69.8 us
    ppermute x12, waiting for transfers between devices, hop(): return lax.ppermute(value, axes, ways)  11.3 us
    pallas_call x13, Pallas kernels, call(): pl.pallas_call(body, out_shape=shapes, in_specs=[pl.BlockSpec(memory_spac...  9.19 us
    ppermute x6, waiting for transfers between devices, within(): return lax.ppermute(value, axes, ways)  7.62 us
    ppermute x6, starting transfers between devices, within(): return lax.ppermute(value, axes, ways)  7.51 us
    ppermute x3, waiting for transfers between devices, on_device(): lax.ppermute(both, 'segment', [(s, (s + stop) % segments) for s in range(...  3.09 us
  transfers between devices with their start and end apart: 21, of which 10 were waited for; matrix products, arithmetic and copies ran while one was open for 0% of the time, Pallas kernels for 2%

profile of v8, /device:TPU:0, one launch (start us, length us, event | category | flops | bytes accessed | tf_op | source)
XLA Modules:
  0.0 112.0 jit_solution(16823184802590599682)
XLA Ops:
  0.6 1.2 %pack.1 = (bf16[30,8,128]{2,1,0:T(8,128)(2,1)S(1)}, bf16[30,8,128]{2,1,0:T(8,128)(2,1)S(1)}) custom-call(bf16[2,29,8,128]{3,2,1,0:T(8,128)(2,1)} %bitcast.14, f32[3,2,8]{2,1,0:T(2,128)} %bitcast.15, s32[2,8]{1,0:T(2,128)} %species_hbm.1, s32[2,8,8]{2,1,0:T(8,128)} %sources_hbm.1, f32[2,8]{1,0:T(2,128)} %grad_hbm.1, bf16[100,128]{1,0:T(8,128)(2,1)} %table_hbm.1), custom_call_target="tpu_custom_call" | custom-call | tf_op jit(solution)/shard_map/pack/pallas_call | solution.py:539
  1.9 5.1 %collective-permute-start.1 = (bf16[30,8,128]{2,1,0:T(8,128)(2,1)S(1)}, bf16[30,8,128]{2,1,0:T(8,128)(2,1)S(1)}, u32[]{:S(2)}, u32[]{:S(2)}) collective-permute-start(bf16[30,8,128]{2,1,0:T(8,128)(2,1)S(1)} %get-tuple-element.39.mine_ref), channel_id=1, source_target_pairs={{0,6},{1,3},{2,0},{3,5},{4,2},{5,7},{6,4},{7,1},{8,14},{9,11},{10,... | collective-permute-start | bytes 184328 | tf_op jit(solution)/shard_map/ppermute | solution.py:579
  7.0 0.0 collective-permute-start.2
  7.0 2.6 %stage.2 = (bf16[896,896]{1,0:T(8,128)(2,1)S(1)}, bf16[2,768,768]{2,1,0:T(8,128)(2,1)S(1)}, bf16[2,640,640]{2,1,0:T(8,128)(2,1)S(1)}) custom-call(bf16[896,896]{1,0:T(8,128)(2,1)} %bitcast.12, bf16[2,768,768]{2,1,0:T(8,128)(2,1)} %bitcast.8, bf16[2,640,640]{2,1,0:T(8,128)(2,1)} %bitcast.10), custom_call_target="tpu_custom_call" | custom-call | tf_op jit(solution)/shard_map/stage/pallas_call | solution.py:539
  9.6 0.0 collective-permute-done.1.straight_ref
  9.6 2.8 %collective-permute-done.2.cross_ref = bf16[30,8,128]{2,1,0:T(8,128)(2,1)S(1)} collective-permute-done((bf16[30,8,128]{2,1,0:T(8,128)(2,1)S(1)}, bf16[30,8,128]{2,1,0:T(8,128)(2,1)S(1)}, u32[]{:S(2)}, u32[]{:S(2)}) %collective-permute-start.2) | collective-permute-done | bytes 61472 | tf_op jit(solution)/shard_map/ppermute | solution.py:579
  12.4 0.0 collective-permute-done.partner_ref
  12.4 0.1 open.1
  12.5 0.0 copy-start
  12.5 0.1 stage.3
  12.6 0.6 copy-done
  13.1 1.9 %forward.3 = (bf16[30,16,128]{2,1,0:T(8,128)(2,1)S(1)}, f32[29,16,128]{2,1,0:T(8,128)S(1)}, bf16[128,32]{1,0:T(8,128)(2,1)S(1)}, bf16[32,128]{1,0:T(8,128)(2,1)S(1)}, f32[1280,128]{1,0:T(8,128)S(1)}) custom-call(bf16[30,16,128]{2,1,0:T(8,128)(2,1)S(1)} %get-tuple-element.41.more_3_.low_ref, bf16[30,16,128]{2,1,0:T(8,128)(2,1)S(1)} %get-tuple-element.42.high_ref, ...), custom_call_target="tpu_custom_call" | custom-call | tf_op jit(solution)/shard_map/forward/pallas_call | solution.py:539
  15.1 1.9 %collective-permute-start.4 = (bf16[30,16,128]{2,1,0:T(8,128)(2,1)S(1)}, bf16[30,16,128]{2,1,0:T(8,128)(2,1)S(1)}, u32[]{:S(2)}, u32[]{:S(2)}) collective-permute-start(bf16[30,16,128]{2,1,0:T(8,128)(2,1)S(1)} %get-tuple-element.49), channel_id=1, source_target_pairs={{0,10},{1,11},{2,8},{3,9},{4,12},{5,13},{6,14},{7,15},{10,0},{11,1... | collective-permute-start | bytes 368648 | tf_op jit(solution)/shard_map/ppermute | solution.py:587
  17.0 1.9 %collective-permute-start.3 = (bf16[30,16,128]{2,1,0:T(8,128)(2,1)S(1)}, bf16[30,16,128]{2,1,0:T(8,128)(2,1)S(1)}, u32[]{:S(2)}, u32[]{:S(2)}) collective-permute-start(bf16[30,16,128]{2,1,0:T(8,128)(2,1)S(1)} %get-tuple-element.49), channel_id=1, source_target_pairs={{0,8},{1,9},{2,12},{3,13},{4,14},{5,15},{6,10},{7,11},{8,0},{9,1},... | collective-permute-start | bytes 368648 | tf_op jit(solution)/shard_map/ppermute | solution.py:587
  18.9 3.9 %collective-permute-done.4.high_ref = bf16[30,16,128]{2,1,0:T(8,128)(2,1)S(1)} collective-permute-done((bf16[30,16,128]{2,1,0:T(8,128)(2,1)S(1)}, bf16[30,16,128]{2,1,0:T(8,128)(2,1)S(1)}, u32[]{:S(2)}, u32[]{:S(2)}) %collective-permute-start.4) | collective-permute-done | bytes 122912 | tf_op jit(solution)/shard_map/ppermute | solution.py:587
  22.8 1.7 %collective-permute-done.3.low_ref = bf16[30,16,128]{2,1,0:T(8,128)(2,1)S(1)} collective-permute-done((bf16[30,16,128]{2,1,0:T(8,128)(2,1)S(1)}, bf16[30,16,128]{2,1,0:T(8,128)(2,1)S(1)}, u32[]{:S(2)}, u32[]{:S(2)}) %collective-permute-start.3) | collective-permute-done | bytes 122912 | tf_op jit(solution)/shard_map/ppermute | solution.py:587
  24.5 0.8 collective-permute-start.6
  25.3 0.7 collective-permute-start.5
  26.0 0.0 collective-permute-done.6.high_ref
  26.0 0.7 collective-permute-start.8
  26.7 0.7 collective-permute-start.7
  27.4 0.0 collective-permute-done.8.high_ref
  27.4 0.7 collective-permute-start.9
  28.1 0.7 collective-permute-start.10
  28.8 0.0 collective-permute-done.9.up_low_ref
  28.8 0.0 collective-permute-done.10.up_high_ref
  28.8 0.7 collective-permute-start.11
  29.5 0.7 collective-permute-start.12
  30.2 0.0 collective-permute-done.11.up_low_ref
  30.2 0.2 backward.4
  30.4 58.5 %collective-permute-start.13 = (bf16[30,16,128]{2,1,0:T(8,128)(2,1)S(1)}, bf16[30,16,128]{2,1,0:T(8,128)(2,1)S(1)}, u32[]{:S(2)}, u32[]{:S(2)}) collective-permute-start(bf16[30,16,128]{2,1,0:T(8,128)(2,1)S(1)} %get-tuple-element.64), channel_id=1, source_target_pairs={{8,0},{9,1},{12,2},{13,3},{14,4},{15,5},{10,6},{11,7},{0,8},{1,9},... | collective-permute-start | bytes 368648 | tf_op jit(solution)/shard_map/ppermute | solution.py:587
  89.0 1.9 %collective-permute-start.14 = (bf16[30,16,128]{2,1,0:T(8,128)(2,1)S(1)}, bf16[30,16,128]{2,1,0:T(8,128)(2,1)S(1)}, u32[]{:S(2)}, u32[]{:S(2)}) collective-permute-start(bf16[30,16,128]{2,1,0:T(8,128)(2,1)S(1)} %get-tuple-element.65), channel_id=1, source_target_pairs={{8,2},{9,3},{12,4},{13,5},{14,6},{15,7},{10,0},{11,1},{2,8},{3,9},... | collective-permute-start | bytes 368648 | tf_op jit(solution)/shard_map/ppermute | solution.py:587
  90.9 2.1 %collective-permute-done.13.up_low_ref = bf16[30,16,128]{2,1,0:T(8,128)(2,1)S(1)} collective-permute-done((bf16[30,16,128]{2,1,0:T(8,128)(2,1)S(1)}, bf16[30,16,128]{2,1,0:T(8,128)(2,1)S(1)}, u32[]{:S(2)}, u32[]{:S(2)}) %collective-permute-start.13) | collective-permute-done | bytes 122912 | tf_op jit(solution)/shard_map/ppermute | solution.py:587
  93.0 3.6 %collective-permute-done.14.up_high_ref = bf16[30,16,128]{2,1,0:T(8,128)(2,1)S(1)} collective-permute-done((bf16[30,16,128]{2,1,0:T(8,128)(2,1)S(1)}, bf16[30,16,128]{2,1,0:T(8,128)(2,1)S(1)}, u32[]{:S(2)}, u32[]{:S(2)}) %collective-permute-start.14) | collective-permute-done | bytes 122912 | tf_op jit(solution)/shard_map/ppermute | solution.py:587
  96.6 2.3 %backward.5 = (f32[8,128]{1,0:T(8,128)S(1)}, f32[8,128]{1,0:T(8,128)S(1)}, f32[8,128]{1,0:T(8,128)S(1)}, f32[8,128]{1,0:T(8,128)S(1)}) custom-call(bf16[30,16,128]{2,1,0:T(8,128)(2,1)S(1)} %collective-permute-done.13.up_low_ref, bf16[30,16,128]{2,1,0:T(8,128)(2,1)S(1)} %collective-permute-done.14.up_high_ref, ...), custom_call_target="tpu_custom_call" | custom-call | tf_op jit(solution)/shard_map/backward/pallas_call | solution.py:539
  98.9 0.0 collective-permute-start.15
  98.9 2.4 %collective-permute-start.16 = (f32[8,128]{1,0:T(8,128)S(1)}, f32[8,128]{1,0:T(8,128)S(1)}, u32[]{:S(2)}, u32[]{:S(2)}) collective-permute-start(f32[8,128]{1,0:T(8,128)S(1)} %get-tuple-element.72), channel_id=1, source_target_pairs={{0,2},{1,7},{2,4},{3,1},{4,6},{5,3},{6,0},{7,5},{8,10},{9,15},{10,... | collective-permute-start | bytes 12296 | tf_op jit(solution)/shard_map/ppermute | solution.py:579
  101.3 0.0 collective-permute-start.17
  101.3 0.0 collective-permute-done.15.theirs_ref
  101.4 3.1 %collective-permute-done.16.straight_ref = f32[8,128]{1,0:T(8,128)S(1)} collective-permute-done((f32[8,128]{1,0:T(8,128)S(1)}, f32[8,128]{1,0:T(8,128)S(1)}, u32[]{:S(2)}, u32[]{:S(2)}) %collective-permute-start.16) | collective-permute-done | bytes 4128 | tf_op jit(solution)/shard_map/ppermute | solution.py:579
  104.4 1.8 %collective-permute-done.17.cross_ref = f32[8,128]{1,0:T(8,128)S(1)} collective-permute-done((f32[8,128]{1,0:T(8,128)S(1)}, f32[8,128]{1,0:T(8,128)S(1)}, u32[]{:S(2)}, u32[]{:S(2)}) %collective-permute-start.17) | collective-permute-done | bytes 4128 | tf_op jit(solution)/shard_map/ppermute | solution.py:579
  106.2 0.0 collective-permute-start.20
  106.2 0.1 collective-permute-start.19
  106.3 1.9 %collective-permute-start.18 = (f32[16,128]{1,0:T(8,128)S(1)}, f32[16,128]{1,0:T(8,128)S(1)}, u32[]{:S(2)}, u32[]{:S(2)}) collective-permute-start(f32[16,128]{1,0:T(8,128)S(1)} %join.1.refs_0_), channel_id=1, source_target_pairs={{0,8},{8,16},{16,24},{24,0},{1,9},{9,17},{17,25},{25,1},{2,10},{10... | collective-permute-start | bytes 24584 | tf_op jit(solution)/shard_map/ppermute | solution.py:650
  108.2 1.6 %collective-permute-done.20.refs_3_ = f32[16,128]{1,0:T(8,128)S(1)} collective-permute-done((f32[16,128]{1,0:T(8,128)S(1)}, f32[16,128]{1,0:T(8,128)S(1)}, u32[]{:S(2)}, u32[]{:S(2)}) %collective-permute-start.20) | collective-permute-done | bytes 8224 | tf_op jit(solution)/shard_map/ppermute | solution.py:650
  109.8 0.1 collective-permute-done.19.refs_2_
  109.9 1.4 %collective-permute-done.18.refs_1_ = f32[16,128]{1,0:T(8,128)S(1)} collective-permute-done((f32[16,128]{1,0:T(8,128)S(1)}, f32[16,128]{1,0:T(8,128)S(1)}, u32[]{:S(2)}, u32[]{:S(2)}) %collective-permute-start.18) | collective-permute-done | bytes 8224 | tf_op jit(solution)/shard_map/ppermute | solution.py:650
  111.3 0.7 close.1
  (11 shorter events, 0.1 us)
Async XLA Ops:
  1.9 7.7 %collective-permute-start.1 = (bf16[30,8,128]{2,1,0:T(8,128)(2,1)S(1)}, bf16[30,8,128]{2,1,0:T(8,128)(2,1)S(1)}, u32[]{:S(2)}, u32[]{:S(2)}) collective-permute-start(bf16[30,8,128]{2,1,0:T(8,128)(2,1)S(1)} %get-tuple-element.39.mine_ref), channel_id=1, source_target_pairs={{0,6},{1,3},{2,0},{3,5},{4,2},{5,7},{6,4},{7,1},{8,14},{9,11},{10,... | collective-permute-start | bytes 184328 | tf_op jit(solution)/shard_map/ppermute | solution.py:579
  7.0 5.4 %collective-permute-start.2 = (bf16[30,8,128]{2,1,0:T(8,128)(2,1)S(1)}, bf16[30,8,128]{2,1,0:T(8,128)(2,1)S(1)}, u32[]{:S(2)}, u32[]{:S(2)}) collective-permute-start(bf16[30,8,128]{2,1,0:T(8,128)(2,1)S(1)} %get-tuple-element.40), channel_id=1, source_target_pairs={{0,7},{1,2},{2,1},{3,4},{4,3},{5,6},{6,5},{7,0},{8,15},{9,10},{10,... | collective-permute-start | bytes 184328 | tf_op jit(solution)/shard_map/ppermute | solution.py:579
  7.0 5.4 %collective-permute-start = (bf16[30,8,128]{2,1,0:T(8,128)(2,1)S(1)}, bf16[30,8,128]{2,1,0:T(8,128)(2,1)S(1)}, u32[]{:S(2)}, u32[]{:S(2)}) collective-permute-start(bf16[30,8,128]{2,1,0:T(8,128)(2,1)S(1)} %get-tuple-element.40), channel_id=1, source_target_pairs={{0,1},{1,0},{2,3},{3,2},{4,5},{5,4},{6,7},{7,6},{8,9},{9,8},{10,11... | collective-permute-start | bytes 184328 | tf_op jit(solution)/shard_map/ppermute | solution.py:579
  12.5 0.7 copy-start
  15.1 7.8 %collective-permute-start.4 = (bf16[30,16,128]{2,1,0:T(8,128)(2,1)S(1)}, bf16[30,16,128]{2,1,0:T(8,128)(2,1)S(1)}, u32[]{:S(2)}, u32[]{:S(2)}) collective-permute-start(bf16[30,16,128]{2,1,0:T(8,128)(2,1)S(1)} %get-tuple-element.49), channel_id=1, source_target_pairs={{0,10},{1,11},{2,8},{3,9},{4,12},{5,13},{6,14},{7,15},{10,0},{11,1... | collective-permute-start | bytes 368648 | tf_op jit(solution)/shard_map/ppermute | solution.py:587
  17.0 7.5 %collective-permute-start.3 = (bf16[30,16,128]{2,1,0:T(8,128)(2,1)S(1)}, bf16[30,16,128]{2,1,0:T(8,128)(2,1)S(1)}, u32[]{:S(2)}, u32[]{:S(2)}) collective-permute-start(bf16[30,16,128]{2,1,0:T(8,128)(2,1)S(1)} %get-tuple-element.49), channel_id=1, source_target_pairs={{0,8},{1,9},{2,12},{3,13},{4,14},{5,15},{6,10},{7,11},{8,0},{9,1},... | collective-permute-start | bytes 368648 | tf_op jit(solution)/shard_map/ppermute | solution.py:587
  24.5 2.9 %copy-start.1 = (f32[128]{0:T(128)S(1)}, f32[128]{0:T(128)}, u32[]{:S(2)}) copy-start(f32[128]{0:T(128)} %param.20) | copy-start | bytes 1540
  24.5 1.5 %collective-permute-start.6 = (bf16[30,16,128]{2,1,0:T(8,128)(2,1)S(1)}, bf16[30,16,128]{2,1,0:T(8,128)(2,1)S(1)}, u32[]{:S(2)}, u32[]{:S(2)}) collective-permute-start(bf16[30,16,128]{2,1,0:T(8,128)(2,1)S(1)} %get-tuple-element.50), channel_id=1, source_target_pairs={{8,16},{9,17},{12,20},{13,21},{14,22},{15,23},{10,18},{11,19},{16,... | collective-permute-start | bytes 368648 | tf_op jit(solution)/shard_map/ppermute | solution.py:587
  25.3 0.7 collective-permute-start.5
  26.0 1.4 %collective-permute-start.8 = (bf16[30,16,128]{2,1,0:T(8,128)(2,1)S(1)}, bf16[30,16,128]{2,1,0:T(8,128)(2,1)S(1)}, u32[]{:S(2)}, u32[]{:S(2)}) collective-permute-start(bf16[30,16,128]{2,1,0:T(8,128)(2,1)S(1)} %get-tuple-element.51), channel_id=1, source_target_pairs={{16,26},{17,27},{20,24},{21,25},{22,28},{23,29},{18,30},{19,31},{2... | collective-permute-start | bytes 368648 | tf_op jit(solution)/shard_map/ppermute | solution.py:587
  26.7 0.7 collective-permute-start.7
  27.4 1.4 %collective-permute-start.9 = (bf16[30,16,128]{2,1,0:T(8,128)(2,1)S(1)}, bf16[30,16,128]{2,1,0:T(8,128)(2,1)S(1)}, u32[]{:S(2)}, u32[]{:S(2)}) collective-permute-start(bf16[30,16,128]{2,1,0:T(8,128)(2,1)S(1)} %get-tuple-element.52), channel_id=1, source_target_pairs={{24,16},{25,17},{28,20},{29,21},{30,22},{31,23},{26,18},{27,19},{1... | collective-permute-start | bytes 368648 | tf_op jit(solution)/shard_map/ppermute | solution.py:587
  28.1 0.7 collective-permute-start.10
  28.8 1.4 %collective-permute-start.11 = (bf16[30,16,128]{2,1,0:T(8,128)(2,1)S(1)}, bf16[30,16,128]{2,1,0:T(8,128)(2,1)S(1)}, u32[]{:S(2)}, u32[]{:S(2)}) collective-permute-start(bf16[30,16,128]{2,1,0:T(8,128)(2,1)S(1)} %get-tuple-element.58), channel_id=1, source_target_pairs={{16,10},{17,11},{20,8},{21,9},{22,12},{23,13},{18,14},{19,15},{10,... | collective-permute-start | bytes 368648 | tf_op jit(solution)/shard_map/ppermute | solution.py:587
  29.5 0.7 collective-permute-start.12
  30.4 62.6 %collective-permute-start.13 = (bf16[30,16,128]{2,1,0:T(8,128)(2,1)S(1)}, bf16[30,16,128]{2,1,0:T(8,128)(2,1)S(1)}, u32[]{:S(2)}, u32[]{:S(2)}) collective-permute-start(bf16[30,16,128]{2,1,0:T(8,128)(2,1)S(1)} %get-tuple-element.64), channel_id=1, source_target_pairs={{8,0},{9,1},{12,2},{13,3},{14,4},{15,5},{10,6},{11,7},{0,8},{1,9},... | collective-permute-start | bytes 368648 | tf_op jit(solution)/shard_map/ppermute | solution.py:587
  89.0 7.7 %collective-permute-start.14 = (bf16[30,16,128]{2,1,0:T(8,128)(2,1)S(1)}, bf16[30,16,128]{2,1,0:T(8,128)(2,1)S(1)}, u32[]{:S(2)}, u32[]{:S(2)}) collective-permute-start(bf16[30,16,128]{2,1,0:T(8,128)(2,1)S(1)} %get-tuple-element.65), channel_id=1, source_target_pairs={{8,2},{9,3},{12,4},{13,5},{14,6},{15,7},{10,0},{11,1},{2,8},{3,9},... | collective-permute-start | bytes 368648 | tf_op jit(solution)/shard_map/ppermute | solution.py:587
  98.9 2.4 %collective-permute-start.15 = (f32[8,128]{1,0:T(8,128)S(1)}, f32[8,128]{1,0:T(8,128)S(1)}, u32[]{:S(2)}, u32[]{:S(2)}) collective-permute-start(f32[8,128]{1,0:T(8,128)S(1)} %get-tuple-element.71), channel_id=1, source_target_pairs={{0,1},{1,0},{2,3},{3,2},{4,5},{5,4},{6,7},{7,6},{8,9},{9,8},{10,11... | collective-permute-start | bytes 12296 | tf_op jit(solution)/shard_map/ppermute | solution.py:579
  98.9 5.5 %collective-permute-start.16 = (f32[8,128]{1,0:T(8,128)S(1)}, f32[8,128]{1,0:T(8,128)S(1)}, u32[]{:S(2)}, u32[]{:S(2)}) collective-permute-start(f32[8,128]{1,0:T(8,128)S(1)} %get-tuple-element.72), channel_id=1, source_target_pairs={{0,2},{1,7},{2,4},{3,1},{4,6},{5,3},{6,0},{7,5},{8,10},{9,15},{10,... | collective-permute-start | bytes 12296 | tf_op jit(solution)/shard_map/ppermute | solution.py:579
  101.3 4.8 %collective-permute-start.17 = (f32[8,128]{1,0:T(8,128)S(1)}, f32[8,128]{1,0:T(8,128)S(1)}, u32[]{:S(2)}, u32[]{:S(2)}) collective-permute-start(f32[8,128]{1,0:T(8,128)S(1)} %get-tuple-element.73), channel_id=1, source_target_pairs={{0,7},{1,2},{2,1},{3,4},{4,3},{5,6},{6,5},{7,0},{8,15},{9,10},{10,... | collective-permute-start | bytes 12296 | tf_op jit(solution)/shard_map/ppermute | solution.py:579
  106.2 3.7 %collective-permute-start.20 = (f32[16,128]{1,0:T(8,128)S(1)}, f32[16,128]{1,0:T(8,128)S(1)}, u32[]{:S(2)}, u32[]{:S(2)}) collective-permute-start(f32[16,128]{1,0:T(8,128)S(1)} %join.1.refs_0_), channel_id=1, source_target_pairs={{0,24},{8,0},{16,8},{24,16},{1,25},{9,1},{17,9},{25,17},{2,26},{10... | collective-permute-start | bytes 24584 | tf_op jit(solution)/shard_map/ppermute | solution.py:650
  106.2 3.7 %collective-permute-start.19 = (f32[16,128]{1,0:T(8,128)S(1)}, f32[16,128]{1,0:T(8,128)S(1)}, u32[]{:S(2)}, u32[]{:S(2)}) collective-permute-start(f32[16,128]{1,0:T(8,128)S(1)} %join.1.refs_0_), channel_id=1, source_target_pairs={{0,16},{8,24},{16,0},{24,8},{1,17},{9,25},{17,1},{25,9},{2,18},{10... | collective-permute-start | bytes 24584 | tf_op jit(solution)/shard_map/ppermute | solution.py:650
  106.3 5.0 %collective-permute-start.18 = (f32[16,128]{1,0:T(8,128)S(1)}, f32[16,128]{1,0:T(8,128)S(1)}, u32[]{:S(2)}, u32[]{:S(2)}) collective-permute-start(f32[16,128]{1,0:T(8,128)S(1)} %join.1.refs_0_), channel_id=1, source_target_pairs={{0,8},{8,16},{16,24},{24,0},{1,9},{9,17},{17,25},{25,1},{2,10},{10... | collective-permute-start | bytes 24584 | tf_op jit(solution)/shard_map/ppermute | solution.py:650

commit v9 on v8

--- a/solution.py
+++ b/solution.py
@@ -578,12 +578,13 @@
         ways = [(s * slabs + i, s * slabs + target(i) % slabs) for s in range(segments) for i in range(slabs)]
         return lax.ppermute(value, axes, ways)
 
-    def hop(value, start, stop, by):
-        ways = [(place_of(q, pairs, start), place_of((q + by) % pairs, pairs, stop)) for q in range(pairs)]
-        ways = [(start * slabs + 2 * a + c, stop * slabs + 2 * b + c) for a, b in ways for c in range(2)]
-        ways += [(b, a) for a, b in ways]
-        moving = {a for a, _ in ways}
-        ways += [(i, i) for i in range(segments * slabs) if i not in moving]
+    def hop(value, step, by):
+        ways = []
+        for start in range(segments):
+            stop = (start + step) % segments
+            for q in range(pairs):
+                a, b = place_of(q, pairs, start), place_of((q + by) % pairs, pairs, stop)
+                ways += [(start * slabs + 2 * a + c, stop * slabs + 2 * b + c) for c in range(2)]
         return lax.ppermute(value, axes, ways)
 
     raw = [
@@ -621,7 +622,7 @@
         )
         kept.append(residuals)
         ways = (1, 0) if tick % 2 else (0, -1)
-        around_all.append([hop(out, tick, tick + 1, by) for by in ways])
+        around_all.append([hop(out, 1, by) for by in ways])
     final = segments - 1
     slab_sums = shape((per_slab, channels), F32)
     parts = call(
@@ -633,7 +634,7 @@
     )
     for tick in reversed(range(segments - 1)):
         ways = (1, 0) if tick % 2 else (0, -1)
-        up = [hop(part, tick + 1, tick, -by) for part, by in zip(parts, ways)]
+        up = [hop(part, -1, -by) for part, by in zip(parts, ways)]
         pooled, *residuals = kept[tick]
         parts = call(
             functools.partial(backward_kernel, tick, sz),

time: 112 us -> 91.1 us (0.81)
  starting transfers between devices: 79.3 us -> 31.8 us
  waiting for transfers between devices: 22.1 us -> 48.8 us
    ppermute x12, starting transfers between devices: 69.8 us -> 18.4 us  [hop(): return lax.ppermute(value, axes, ways)]
    ppermute x12, waiting for transfers between devices: 11.3 us -> 40.7 us  [hop(): return lax.ppermute(value, axes, ways)]
    ppermute x6, waiting for transfers between devices: 7.62 us -> 4.13 us  [within(): return lax.ppermute(value, axes, ways)]
    ppermute x6, starting transfers between devices: 7.51 us -> 9.54 us  [within(): return lax.ppermute(value, axes, ways)]
    ppermute x3, starting transfers between devices: 2.01 us -> 3.9 us  [on_device(): lax.ppermute(both, 'segment', [(s, (s + stop) % segments) for s in range(...]
  transfers between devices with their start and end apart: 21 -> 21, of which waited for: 10 -> 16; matrix products, arithmetic and copies ran while one was open for 0% -> 0% of each run, Pallas kernels for 2% -> 3%
where the time goes in v9:
time: 91.1 us; the launch traced here: 90.9 us
  waiting for transfers between devices  48.8 us (54%)
  starting transfers between devices  31.8 us (35%)
  Pallas kernels  8.94 us (10%)
    ppermute x12, waiting for transfers between devices, hop(): return lax.ppermute(value, axes, ways)  40.7 us
    ppermute x12, starting transfers between devices, hop(): return lax.ppermute(value, axes, ways)  18.4 us
    ppermute x6, starting transfers between devices, within(): return lax.ppermute(value, axes, ways)  9.54 us
    pallas_call x13, Pallas kernels, call(): pl.pallas_call(body, out_shape=shapes, in_specs=[pl.BlockSpec(memory_spac...  8.94 us
    ppermute x6, waiting for transfers between devices, within(): return lax.ppermute(value, axes, ways)  4.13 us
    ppermute x3, waiting for transfers between devices, on_device(): lax.ppermute(both, 'segment', [(s, (s + stop) % segments) for s in range(...  3.99 us
    ppermute x3, starting transfers between devices, on_device(): lax.ppermute(both, 'segment', [(s, (s + stop) % segments) for s in range(...  3.9 us
  transfers between devices with their start and end apart: 21, of which 16 were waited for; matrix products, arithmetic and copies ran while one was open for 0% of the time, Pallas kernels for 3%

profile of v9, /device:TPU:0, one launch (start us, length us, event | category | flops | bytes accessed | tf_op | source)
XLA Modules:
  0.0 90.9 jit_solution(4136302604883931290)
XLA Ops:
  0.6 1.2 %pack.1 = (bf16[30,8,128]{2,1,0:T(8,128)(2,1)S(1)}, bf16[30,8,128]{2,1,0:T(8,128)(2,1)S(1)}) custom-call(bf16[2,29,8,128]{3,2,1,0:T(8,128)(2,1)} %bitcast.14, f32[3,2,8]{2,1,0:T(2,128)} %bitcast.15, s32[2,8]{1,0:T(2,128)} %species_hbm.1, s32[2,8,8]{2,1,0:T(8,128)} %sources_hbm.1, f32[2,8]{1,0:T(2,128)} %grad_hbm.1, bf16[100,128]{1,0:T(8,128)(2,1)} %table_hbm.1), custom_call_target="tpu_custom_call" | custom-call | tf_op jit(solution)/shard_map/pack/pallas_call | solution.py:539
  1.9 5.1 %collective-permute-start.1 = (bf16[30,8,128]{2,1,0:T(8,128)(2,1)S(1)}, bf16[30,8,128]{2,1,0:T(8,128)(2,1)S(1)}, u32[]{:S(2)}, u32[]{:S(2)}) collective-permute-start(bf16[30,8,128]{2,1,0:T(8,128)(2,1)S(1)} %get-tuple-element.39.mine_ref), channel_id=1, source_target_pairs={{0,6},{1,3},{2,0},{3,5},{4,2},{5,7},{6,4},{7,1},{8,14},{9,11},{10,... | collective-permute-start | bytes 184328 | tf_op jit(solution)/shard_map/ppermute | solution.py:579
  7.0 0.0 collective-permute-start.2
  7.0 0.0 collective-permute-start
  7.0 2.6 %stage.2 = (bf16[896,896]{1,0:T(8,128)(2,1)S(1)}, bf16[2,768,768]{2,1,0:T(8,128)(2,1)S(1)}, bf16[2,640,640]{2,1,0:T(8,128)(2,1)S(1)}) custom-call(bf16[896,896]{1,0:T(8,128)(2,1)} %bitcast.12, bf16[2,768,768]{2,1,0:T(8,128)(2,1)} %bitcast.8, bf16[2,640,640]{2,1,0:T(8,128)(2,1)} %bitcast.10), custom_call_target="tpu_custom_call" | custom-call | tf_op jit(solution)/shard_map/stage/pallas_call | solution.py:539
  9.6 0.0 collective-permute-done.1.straight_ref
  9.6 2.8 %collective-permute-done.2.cross_ref = bf16[30,8,128]{2,1,0:T(8,128)(2,1)S(1)} collective-permute-done((bf16[30,8,128]{2,1,0:T(8,128)(2,1)S(1)}, bf16[30,8,128]{2,1,0:T(8,128)(2,1)S(1)}, u32[]{:S(2)}, u32[]{:S(2)}) %collective-permute-start.2) | collective-permute-done | bytes 61472 | tf_op jit(solution)/shard_map/ppermute | solution.py:579
  12.4 0.0 collective-permute-done.partner_ref
  12.4 0.1 open.1
  12.5 0.0 copy-start
  12.5 0.1 stage.3
  12.6 0.6 copy-done
  13.1 1.9 %forward.3 = (bf16[30,16,128]{2,1,0:T(8,128)(2,1)S(1)}, f32[29,16,128]{2,1,0:T(8,128)S(1)}, bf16[128,32]{1,0:T(8,128)(2,1)S(1)}, bf16[32,128]{1,0:T(8,128)(2,1)S(1)}, f32[1280,128]{1,0:T(8,128)S(1)}) custom-call(bf16[30,16,128]{2,1,0:T(8,128)(2,1)S(1)} %get-tuple-element.41.more_3_.low_ref, bf16[30,16,128]{2,1,0:T(8,128)(2,1)S(1)} %get-tuple-element.42.high_ref, ...), custom_call_target="tpu_custom_call" | custom-call | tf_op jit(solution)/shard_map/forward/pallas_call | solution.py:539
  15.1 0.1 collective-permute-start.4
  15.1 0.1 collective-permute-start.3
  15.2 9.3 %collective-permute-done.4.high_ref = bf16[30,16,128]{2,1,0:T(8,128)(2,1)S(1)} collective-permute-done((bf16[30,16,128]{2,1,0:T(8,128)(2,1)S(1)}, bf16[30,16,128]{2,1,0:T(8,128)(2,1)S(1)}, u32[]{:S(2)}, u32[]{:S(2)}) %collective-permute-start.4) | collective-permute-done | bytes 122912 | tf_op jit(solution)/shard_map/ppermute | solution.py:588
  24.5 0.2 collective-permute-done.3.low_ref
  24.6 0.0 collective-permute-start.6
  24.6 0.0 collective-permute-start.5
  24.6 9.0 %collective-permute-done.6.high_ref = bf16[30,16,128]{2,1,0:T(8,128)(2,1)S(1)} collective-permute-done((bf16[30,16,128]{2,1,0:T(8,128)(2,1)S(1)}, bf16[30,16,128]{2,1,0:T(8,128)(2,1)S(1)}, u32[]{:S(2)}, u32[]{:S(2)}) %collective-permute-start.6) | collective-permute-done | bytes 122912 | tf_op jit(solution)/shard_map/ppermute | solution.py:588
  33.7 3.0 %collective-permute-start.8 = (bf16[30,16,128]{2,1,0:T(8,128)(2,1)S(1)}, bf16[30,16,128]{2,1,0:T(8,128)(2,1)S(1)}, u32[]{:S(2)}, u32[]{:S(2)}) collective-permute-start(bf16[30,16,128]{2,1,0:T(8,128)(2,1)S(1)} %get-tuple-element.51), channel_id=1, source_target_pairs={{0,10},{1,11},{2,8},{3,9},{4,12},{5,13},{6,14},{7,15},{8,18},{9,19... | collective-permute-start | bytes 368648 | tf_op jit(solution)/shard_map/ppermute | solution.py:588
  36.7 0.1 collective-permute-start.7
  36.8 7.1 %collective-permute-done.8.high_ref = bf16[30,16,128]{2,1,0:T(8,128)(2,1)S(1)} collective-permute-done((bf16[30,16,128]{2,1,0:T(8,128)(2,1)S(1)}, bf16[30,16,128]{2,1,0:T(8,128)(2,1)S(1)}, u32[]{:S(2)}, u32[]{:S(2)}) %collective-permute-start.8) | collective-permute-done | bytes 122912 | tf_op jit(solution)/shard_map/ppermute | solution.py:588
  43.9 0.1 collective-permute-done.7.low_ref
  44.0 4.1 %collective-permute-start.9 = (bf16[30,16,128]{2,1,0:T(8,128)(2,1)S(1)}, bf16[30,16,128]{2,1,0:T(8,128)(2,1)S(1)}, u32[]{:S(2)}, u32[]{:S(2)}) collective-permute-start(bf16[30,16,128]{2,1,0:T(8,128)(2,1)S(1)} %get-tuple-element.52), channel_id=1, source_target_pairs={{0,24},{1,25},{2,28},{3,29},{4,30},{5,31},{6,26},{7,27},{8,0},{9,1... | collective-permute-start | bytes 368648 | tf_op jit(solution)/shard_map/ppermute | solution.py:588
  48.1 1.8 %collective-permute-start.10 = (bf16[30,16,128]{2,1,0:T(8,128)(2,1)S(1)}, bf16[30,16,128]{2,1,0:T(8,128)(2,1)S(1)}, u32[]{:S(2)}, u32[]{:S(2)}) collective-permute-start(bf16[30,16,128]{2,1,0:T(8,128)(2,1)S(1)} %get-tuple-element.53), channel_id=1, source_target_pairs={{0,28},{1,29},{2,30},{3,31},{4,26},{5,27},{6,24},{7,25},{8,2},{9,3... | collective-permute-start | bytes 368648 | tf_op jit(solution)/shard_map/ppermute | solution.py:588
  49.9 0.6 collective-permute-done.9.up_low_ref
  50.5 3.3 %collective-permute-done.10.up_high_ref = bf16[30,16,128]{2,1,0:T(8,128)(2,1)S(1)} collective-permute-done((bf16[30,16,128]{2,1,0:T(8,128)(2,1)S(1)}, bf16[30,16,128]{2,1,0:T(8,128)(2,1)S(1)}, u32[]{:S(2)}, u32[]{:S(2)}) %collective-permute-start.10) | collective-permute-done | bytes 122912 | tf_op jit(solution)/shard_map/ppermute | solution.py:588
  53.9 7.3 %collective-permute-start.11 = (bf16[30,16,128]{2,1,0:T(8,128)(2,1)S(1)}, bf16[30,16,128]{2,1,0:T(8,128)(2,1)S(1)}, u32[]{:S(2)}, u32[]{:S(2)}) collective-permute-start(bf16[30,16,128]{2,1,0:T(8,128)(2,1)S(1)} %get-tuple-element.58), channel_id=1, source_target_pairs={{0,26},{1,27},{2,24},{3,25},{4,28},{5,29},{6,30},{7,31},{8,6},{9,7... | collective-permute-start | bytes 368648 | tf_op jit(solution)/shard_map/ppermute | solution.py:588
  61.2 3.0 %collective-permute-done.11.up_low_ref = bf16[30,16,128]{2,1,0:T(8,128)(2,1)S(1)} collective-permute-done((bf16[30,16,128]{2,1,0:T(8,128)(2,1)S(1)}, bf16[30,16,128]{2,1,0:T(8,128)(2,1)S(1)}, u32[]{:S(2)}, u32[]{:S(2)}) %collective-permute-start.11) | collective-permute-done | bytes 122912 | tf_op jit(solution)/shard_map/ppermute | solution.py:588
  64.2 1.9 %collective-permute-done.12.up_high_ref = bf16[30,16,128]{2,1,0:T(8,128)(2,1)S(1)} collective-permute-done((bf16[30,16,128]{2,1,0:T(8,128)(2,1)S(1)}, bf16[30,16,128]{2,1,0:T(8,128)(2,1)S(1)}, u32[]{:S(2)}, u32[]{:S(2)}) %collective-permute-start.12) | collective-permute-done | bytes 122912 | tf_op jit(solution)/shard_map/ppermute | solution.py:588
  66.1 1.7 %collective-permute-start.13 = (bf16[30,16,128]{2,1,0:T(8,128)(2,1)S(1)}, bf16[30,16,128]{2,1,0:T(8,128)(2,1)S(1)}, u32[]{:S(2)}, u32[]{:S(2)}) collective-permute-start(bf16[30,16,128]{2,1,0:T(8,128)(2,1)S(1)} %get-tuple-element.64), channel_id=1, source_target_pairs={{0,24},{1,25},{2,28},{3,29},{4,30},{5,31},{6,26},{7,27},{8,0},{9,1... | collective-permute-start | bytes 368648 | tf_op jit(solution)/shard_map/ppermute | solution.py:588
  67.7 0.2 collective-permute-start.14
  68.0 6.2 %collective-permute-done.13.up_low_ref = bf16[30,16,128]{2,1,0:T(8,128)(2,1)S(1)} collective-permute-done((bf16[30,16,128]{2,1,0:T(8,128)(2,1)S(1)}, bf16[30,16,128]{2,1,0:T(8,128)(2,1)S(1)}, u32[]{:S(2)}, u32[]{:S(2)}) %collective-permute-start.13) | collective-permute-done | bytes 122912 | tf_op jit(solution)/shard_map/ppermute | solution.py:588
  74.2 0.0 collective-permute-done.14.up_high_ref
  74.2 2.3 %backward.5 = (f32[8,128]{1,0:T(8,128)S(1)}, f32[8,128]{1,0:T(8,128)S(1)}, f32[8,128]{1,0:T(8,128)S(1)}, f32[8,128]{1,0:T(8,128)S(1)}) custom-call(bf16[30,16,128]{2,1,0:T(8,128)(2,1)S(1)} %collective-permute-done.13.up_low_ref, bf16[30,16,128]{2,1,0:T(8,128)(2,1)S(1)} %collective-permute-done.14.up_high_ref, ...), custom_call_target="tpu_custom_call" | custom-call | tf_op jit(solution)/shard_map/backward/pallas_call | solution.py:539
  76.5 0.0 collective-permute-start.15
  76.5 0.6 collective-permute-start.16
  77.2 3.8 %collective-permute-start.17 = (f32[8,128]{1,0:T(8,128)S(1)}, f32[8,128]{1,0:T(8,128)S(1)}, u32[]{:S(2)}, u32[]{:S(2)}) collective-permute-start(f32[8,128]{1,0:T(8,128)S(1)} %get-tuple-element.73), channel_id=1, source_target_pairs={{0,7},{1,2},{2,1},{3,4},{4,3},{5,6},{6,5},{7,0},{8,15},{9,10},{10,... | collective-permute-start | bytes 12296 | tf_op jit(solution)/shard_map/ppermute | solution.py:579
  81.0 1.0 %collective-permute-done.16.straight_ref = f32[8,128]{1,0:T(8,128)S(1)} collective-permute-done((f32[8,128]{1,0:T(8,128)S(1)}, f32[8,128]{1,0:T(8,128)S(1)}, u32[]{:S(2)}, u32[]{:S(2)}) %collective-permute-start.16) | collective-permute-done | bytes 4128 | tf_op jit(solution)/shard_map/ppermute | solution.py:579
  82.0 0.3 collective-permute-done.17.cross_ref
  82.3 3.3 %collective-permute-start.20 = (f32[16,128]{1,0:T(8,128)S(1)}, f32[16,128]{1,0:T(8,128)S(1)}, u32[]{:S(2)}, u32[]{:S(2)}) collective-permute-start(f32[16,128]{1,0:T(8,128)S(1)} %join.1.refs_0_), channel_id=1, source_target_pairs={{0,24},{8,0},{16,8},{24,16},{1,25},{9,1},{17,9},{25,17},{2,26},{10... | collective-permute-start | bytes 24584 | tf_op jit(solution)/shard_map/ppermute | solution.py:651
  85.6 0.1 collective-permute-start.19
  85.6 0.6 collective-permute-start.18
  86.2 0.7 collective-permute-done.20.refs_3_
  86.9 2.3 %collective-permute-done.19.refs_2_ = f32[16,128]{1,0:T(8,128)S(1)} collective-permute-done((f32[16,128]{1,0:T(8,128)S(1)}, f32[16,128]{1,0:T(8,128)S(1)}, u32[]{:S(2)}, u32[]{:S(2)}) %collective-permute-start.19) | collective-permute-done | bytes 8224 | tf_op jit(solution)/shard_map/ppermute | solution.py:651
  89.2 1.0 %collective-permute-done.18.refs_1_ = f32[16,128]{1,0:T(8,128)S(1)} collective-permute-done((f32[16,128]{1,0:T(8,128)S(1)}, f32[16,128]{1,0:T(8,128)S(1)}, u32[]{:S(2)}, u32[]{:S(2)}) %collective-permute-start.18) | collective-permute-done | bytes 8224 | tf_op jit(solution)/shard_map/ppermute | solution.py:651
  90.2 0.7 close.1
  (11 shorter events, 0.0 us)
Async XLA Ops:
  1.9 7.7 %collective-permute-start.1 = (bf16[30,8,128]{2,1,0:T(8,128)(2,1)S(1)}, bf16[30,8,128]{2,1,0:T(8,128)(2,1)S(1)}, u32[]{:S(2)}, u32[]{:S(2)}) collective-permute-start(bf16[30,8,128]{2,1,0:T(8,128)(2,1)S(1)} %get-tuple-element.39.mine_ref), channel_id=1, source_target_pairs={{0,6},{1,3},{2,0},{3,5},{4,2},{5,7},{6,4},{7,1},{8,14},{9,11},{10,... | collective-permute-start | bytes 184328 | tf_op jit(solution)/shard_map/ppermute | solution.py:579
  7.0 5.4 %collective-permute-start.2 = (bf16[30,8,128]{2,1,0:T(8,128)(2,1)S(1)}, bf16[30,8,128]{2,1,0:T(8,128)(2,1)S(1)}, u32[]{:S(2)}, u32[]{:S(2)}) collective-permute-start(bf16[30,8,128]{2,1,0:T(8,128)(2,1)S(1)} %get-tuple-element.40), channel_id=1, source_target_pairs={{0,7},{1,2},{2,1},{3,4},{4,3},{5,6},{6,5},{7,0},{8,15},{9,10},{10,... | collective-permute-start | bytes 184328 | tf_op jit(solution)/shard_map/ppermute | solution.py:579
  7.0 5.4 %collective-permute-start = (bf16[30,8,128]{2,1,0:T(8,128)(2,1)S(1)}, bf16[30,8,128]{2,1,0:T(8,128)(2,1)S(1)}, u32[]{:S(2)}, u32[]{:S(2)}) collective-permute-start(bf16[30,8,128]{2,1,0:T(8,128)(2,1)S(1)} %get-tuple-element.40), channel_id=1, source_target_pairs={{0,1},{1,0},{2,3},{3,2},{4,5},{5,4},{6,7},{7,6},{8,9},{9,8},{10,11... | collective-permute-start | bytes 184328 | tf_op jit(solution)/shard_map/ppermute | solution.py:579
  12.5 0.7 copy-start
  15.1 9.4 %collective-permute-start.4 = (bf16[30,16,128]{2,1,0:T(8,128)(2,1)S(1)}, bf16[30,16,128]{2,1,0:T(8,128)(2,1)S(1)}, u32[]{:S(2)}, u32[]{:S(2)}) collective-permute-start(bf16[30,16,128]{2,1,0:T(8,128)(2,1)S(1)} %get-tuple-element.49), channel_id=1, source_target_pairs={{0,10},{1,11},{2,8},{3,9},{4,12},{5,13},{6,14},{7,15},{8,18},{9,19... | collective-permute-start | bytes 368648 | tf_op jit(solution)/shard_map/ppermute | solution.py:588
  15.1 9.5 %collective-permute-start.3 = (bf16[30,16,128]{2,1,0:T(8,128)(2,1)S(1)}, bf16[30,16,128]{2,1,0:T(8,128)(2,1)S(1)}, u32[]{:S(2)}, u32[]{:S(2)}) collective-permute-start(bf16[30,16,128]{2,1,0:T(8,128)(2,1)S(1)} %get-tuple-element.49), channel_id=1, source_target_pairs={{0,8},{1,9},{2,12},{3,13},{4,14},{5,15},{6,10},{7,11},{8,16},{9,17... | collective-permute-start | bytes 368648 | tf_op jit(solution)/shard_map/ppermute | solution.py:588
  24.6 19.4 %copy-start.1 = (f32[128]{0:T(128)S(1)}, f32[128]{0:T(128)}, u32[]{:S(2)}) copy-start(f32[128]{0:T(128)} %param.20) | copy-start | bytes 1540
  24.6 9.0 %collective-permute-start.6 = (bf16[30,16,128]{2,1,0:T(8,128)(2,1)S(1)}, bf16[30,16,128]{2,1,0:T(8,128)(2,1)S(1)}, u32[]{:S(2)}, u32[]{:S(2)}) collective-permute-start(bf16[30,16,128]{2,1,0:T(8,128)(2,1)S(1)} %get-tuple-element.50), channel_id=1, source_target_pairs={{0,8},{1,9},{2,12},{3,13},{4,14},{5,15},{6,10},{7,11},{8,16},{9,17... | collective-permute-start | bytes 368648 | tf_op jit(solution)/shard_map/ppermute | solution.py:588
  24.6 9.0 %collective-permute-start.5 = (bf16[30,16,128]{2,1,0:T(8,128)(2,1)S(1)}, bf16[30,16,128]{2,1,0:T(8,128)(2,1)S(1)}, u32[]{:S(2)}, u32[]{:S(2)}) collective-permute-start(bf16[30,16,128]{2,1,0:T(8,128)(2,1)S(1)} %get-tuple-element.50), channel_id=1, source_target_pairs={{0,12},{1,13},{2,14},{3,15},{4,10},{5,11},{6,8},{7,9},{8,20},{9,21... | collective-permute-start | bytes 368648 | tf_op jit(solution)/shard_map/ppermute | solution.py:588
  33.7 10.3 %collective-permute-start.8 = (bf16[30,16,128]{2,1,0:T(8,128)(2,1)S(1)}, bf16[30,16,128]{2,1,0:T(8,128)(2,1)S(1)}, u32[]{:S(2)}, u32[]{:S(2)}) collective-permute-start(bf16[30,16,128]{2,1,0:T(8,128)(2,1)S(1)} %get-tuple-element.51), channel_id=1, source_target_pairs={{0,10},{1,11},{2,8},{3,9},{4,12},{5,13},{6,14},{7,15},{8,18},{9,19... | collective-permute-start | bytes 368648 | tf_op jit(solution)/shard_map/ppermute | solution.py:588
  36.7 7.3 %collective-permute-start.7 = (bf16[30,16,128]{2,1,0:T(8,128)(2,1)S(1)}, bf16[30,16,128]{2,1,0:T(8,128)(2,1)S(1)}, u32[]{:S(2)}, u32[]{:S(2)}) collective-permute-start(bf16[30,16,128]{2,1,0:T(8,128)(2,1)S(1)} %get-tuple-element.51), channel_id=1, source_target_pairs={{0,8},{1,9},{2,12},{3,13},{4,14},{5,15},{6,10},{7,11},{8,16},{9,17... | collective-permute-start | bytes 368648 | tf_op jit(solution)/shard_map/ppermute | solution.py:588
  44.0 6.5 %collective-permute-start.9 = (bf16[30,16,128]{2,1,0:T(8,128)(2,1)S(1)}, bf16[30,16,128]{2,1,0:T(8,128)(2,1)S(1)}, u32[]{:S(2)}, u32[]{:S(2)}) collective-permute-start(bf16[30,16,128]{2,1,0:T(8,128)(2,1)S(1)} %get-tuple-element.52), channel_id=1, source_target_pairs={{0,24},{1,25},{2,28},{3,29},{4,30},{5,31},{6,26},{7,27},{8,0},{9,1... | collective-permute-start | bytes 368648 | tf_op jit(solution)/shard_map/ppermute | solution.py:588
  48.1 5.8 %collective-permute-start.10 = (bf16[30,16,128]{2,1,0:T(8,128)(2,1)S(1)}, bf16[30,16,128]{2,1,0:T(8,128)(2,1)S(1)}, u32[]{:S(2)}, u32[]{:S(2)}) collective-permute-start(bf16[30,16,128]{2,1,0:T(8,128)(2,1)S(1)} %get-tuple-element.53), channel_id=1, source_target_pairs={{0,28},{1,29},{2,30},{3,31},{4,26},{5,27},{6,24},{7,25},{8,2},{9,3... | collective-permute-start | bytes 368648 | tf_op jit(solution)/shard_map/ppermute | solution.py:588
  53.9 10.3 %collective-permute-start.11 = (bf16[30,16,128]{2,1,0:T(8,128)(2,1)S(1)}, bf16[30,16,128]{2,1,0:T(8,128)(2,1)S(1)}, u32[]{:S(2)}, u32[]{:S(2)}) collective-permute-start(bf16[30,16,128]{2,1,0:T(8,128)(2,1)S(1)} %get-tuple-element.58), channel_id=1, source_target_pairs={{0,26},{1,27},{2,24},{3,25},{4,28},{5,29},{6,30},{7,31},{8,6},{9,7... | collective-permute-start | bytes 368648 | tf_op jit(solution)/shard_map/ppermute | solution.py:588
  61.2 4.9 %collective-permute-start.12 = (bf16[30,16,128]{2,1,0:T(8,128)(2,1)S(1)}, bf16[30,16,128]{2,1,0:T(8,128)(2,1)S(1)}, u32[]{:S(2)}, u32[]{:S(2)}) collective-permute-start(bf16[30,16,128]{2,1,0:T(8,128)(2,1)S(1)} %get-tuple-element.59), channel_id=1, source_target_pairs={{0,24},{1,25},{2,28},{3,29},{4,30},{5,31},{6,26},{7,27},{8,0},{9,1... | collective-permute-start | bytes 368648 | tf_op jit(solution)/shard_map/ppermute | solution.py:588
  66.1 8.2 %collective-permute-start.13 = (bf16[30,16,128]{2,1,0:T(8,128)(2,1)S(1)}, bf16[30,16,128]{2,1,0:T(8,128)(2,1)S(1)}, u32[]{:S(2)}, u32[]{:S(2)}) collective-permute-start(bf16[30,16,128]{2,1,0:T(8,128)(2,1)S(1)} %get-tuple-element.64), channel_id=1, source_target_pairs={{0,24},{1,25},{2,28},{3,29},{4,30},{5,31},{6,26},{7,27},{8,0},{9,1... | collective-permute-start | bytes 368648 | tf_op jit(solution)/shard_map/ppermute | solution.py:588
  67.7 6.5 %collective-permute-start.14 = (bf16[30,16,128]{2,1,0:T(8,128)(2,1)S(1)}, bf16[30,16,128]{2,1,0:T(8,128)(2,1)S(1)}, u32[]{:S(2)}, u32[]{:S(2)}) collective-permute-start(bf16[30,16,128]{2,1,0:T(8,128)(2,1)S(1)} %get-tuple-element.65), channel_id=1, source_target_pairs={{0,28},{1,29},{2,30},{3,31},{4,26},{5,27},{6,24},{7,25},{8,2},{9,3... | collective-permute-start | bytes 368648 | tf_op jit(solution)/shard_map/ppermute | solution.py:588
  76.5 4.4 %collective-permute-start.15 = (f32[8,128]{1,0:T(8,128)S(1)}, f32[8,128]{1,0:T(8,128)S(1)}, u32[]{:S(2)}, u32[]{:S(2)}) collective-permute-start(f32[8,128]{1,0:T(8,128)S(1)} %get-tuple-element.71), channel_id=1, source_target_pairs={{0,1},{1,0},{2,3},{3,2},{4,5},{5,4},{6,7},{7,6},{8,9},{9,8},{10,11... | collective-permute-start | bytes 12296 | tf_op jit(solution)/shard_map/ppermute | solution.py:579
  76.5 5.5 %collective-permute-start.16 = (f32[8,128]{1,0:T(8,128)S(1)}, f32[8,128]{1,0:T(8,128)S(1)}, u32[]{:S(2)}, u32[]{:S(2)}) collective-permute-start(f32[8,128]{1,0:T(8,128)S(1)} %get-tuple-element.72), channel_id=1, source_target_pairs={{0,2},{1,7},{2,4},{3,1},{4,6},{5,3},{6,0},{7,5},{8,10},{9,15},{10,... | collective-permute-start | bytes 12296 | tf_op jit(solution)/shard_map/ppermute | solution.py:579
  77.2 5.1 %collective-permute-start.17 = (f32[8,128]{1,0:T(8,128)S(1)}, f32[8,128]{1,0:T(8,128)S(1)}, u32[]{:S(2)}, u32[]{:S(2)}) collective-permute-start(f32[8,128]{1,0:T(8,128)S(1)} %get-tuple-element.73), channel_id=1, source_target_pairs={{0,7},{1,2},{2,1},{3,4},{4,3},{5,6},{6,5},{7,0},{8,15},{9,10},{10,... | collective-permute-start | bytes 12296 | tf_op jit(solution)/shard_map/ppermute | solution.py:579
  82.3 4.6 %collective-permute-start.20 = (f32[16,128]{1,0:T(8,128)S(1)}, f32[16,128]{1,0:T(8,128)S(1)}, u32[]{:S(2)}, u32[]{:S(2)}) collective-permute-start(f32[16,128]{1,0:T(8,128)S(1)} %join.1.refs_0_), channel_id=1, source_target_pairs={{0,24},{8,0},{16,8},{24,16},{1,25},{9,1},{17,9},{25,17},{2,26},{10... | collective-permute-start | bytes 24584 | tf_op jit(solution)/shard_map/ppermute | solution.py:651
  85.6 3.7 %collective-permute-start.19 = (f32[16,128]{1,0:T(8,128)S(1)}, f32[16,128]{1,0:T(8,128)S(1)}, u32[]{:S(2)}, u32[]{:S(2)}) collective-permute-start(f32[16,128]{1,0:T(8,128)S(1)} %join.1.refs_0_), channel_id=1, source_target_pairs={{0,16},{8,24},{16,0},{24,8},{1,17},{9,25},{17,1},{25,9},{2,18},{10... | collective-permute-start | bytes 24584 | tf_op jit(solution)/shard_map/ppermute | solution.py:651
  85.6 4.5 %collective-permute-start.18 = (f32[16,128]{1,0:T(8,128)S(1)}, f32[16,128]{1,0:T(8,128)S(1)}, u32[]{:S(2)}, u32[]{:S(2)}) collective-permute-start(f32[16,128]{1,0:T(8,128)S(1)} %join.1.refs_0_), channel_id=1, source_target_pairs={{0,8},{8,16},{16,24},{24,0},{1,9},{9,17},{17,25},{25,1},{2,10},{10... | collective-permute-start | bytes 24584 | tf_op jit(solution)/shard_map/ppermute | solution.py:651

commit v10 on v9

--- a/solution.py
+++ b/solution.py
@@ -448,7 +448,8 @@
 
 def turn_to_stage():
     odd = lax.rem(lax.axis_index("space"), 2)
-    return jnp.where(lax.axis_index("segment") == 0, odd, 0)
+    segment = lax.axis_index("segment")
+    return jnp.where(segment < 2, odd * (1 + segment), 0)
 
 
 def stage_kernel(moment, zero_hbm, one_hbm, two_hbm, *more):
@@ -605,10 +606,14 @@
     weights = call(functools.partial(stage_kernel, 0), stored, on_chip, "stage", spaces, sems)
     whole = shape((coefs + 1, rows, channels), BF16)
     around_all = [call(open_kernel, [mine, partner, straight, cross], [whole, whole], "open")]
-    weights = call(
-        functools.partial(stage_kernel, 1), [*stored, *weights, around_all[0][0]], on_chip, "stage",
-        spaces + [pltpu.VMEM] * 4, sems, {3: 0, 4: 1, 5: 2},
-    )
+
+    def stage_more(moment, weights, after):
+        return call(
+            functools.partial(stage_kernel, moment), [*stored, *weights, after], on_chip, "stage",
+            spaces + [pltpu.VMEM] * 4, sems, {3: 0, 4: 1, 5: 2},
+        )
+
+    weights = stage_more(1, weights, around_all[0][0])
     edge_shapes = [
         shape((edges, 2 * rows), BF16), shape((2 * rows, edges), BF16), shape((10 * edges, channels), F32),
     ]
@@ -623,6 +628,8 @@
         kept.append(residuals)
         ways = (1, 0) if tick % 2 else (0, -1)
         around_all.append([hop(out, 1, by) for by in ways])
+        if tick == 0:
+            weights = stage_more(2, weights, around_all[1][0])
     final = segments - 1
     slab_sums = shape((per_slab, channels), F32)
     parts = call(

time: 91.1 us -> 94.4 us (1.036)
  starting transfers between devices: 31.8 us -> 33.9 us
  waiting for transfers between devices: 48.8 us -> 50.1 us
    ppermute x12, starting transfers between devices: 18.4 us -> 20.7 us  [hop(): return lax.ppermute(value, axes, ways)]
    pallas_call x13 -> x14, Pallas kernels: 8.94 us -> 8.99 us  [call(): pl.pallas_call(body, out_shape=shapes, in_specs=[pl.BlockSpec(memory_spac...]
  transfers between devices with their start and end apart: 21 -> 21, of which waited for: 16 -> 17; matrix products, arithmetic and copies ran while one was open for 0% -> 0% of each run, Pallas kernels for 3% -> 3%
where the time goes in v10:
time: 94.4 us; the launch traced here: 94.3 us
  waiting for transfers between devices  50.1 us (53%)
  starting transfers between devices  33.9 us (36%)
  Pallas kernels  8.99 us (10%)
    ppermute x12, waiting for transfers between devices, hop(): return lax.ppermute(value, axes, ways)  41.6 us
    ppermute x12, starting transfers between devices, hop(): return lax.ppermute(value, axes, ways)  20.7 us
    ppermute x6, starting transfers between devices, within(): return lax.ppermute(value, axes, ways)  9.29 us
    pallas_call x14, Pallas kernels, call(): pl.pallas_call(body, out_shape=shapes, in_specs=[pl.BlockSpec(memory_spac...  8.99 us
    ppermute x3, waiting for transfers between devices, on_device(): lax.ppermute(both, 'segment', [(s, (s + stop) % segments) for s in range(...  4.29 us
    ppermute x6, waiting for transfers between devices, within(): return lax.ppermute(value, axes, ways)  4.16 us
    ppermute x3, starting transfers between devices, on_device(): lax.ppermute(both, 'segment', [(s, (s + stop) % segments) for s in range(...  3.88 us
  transfers between devices with their start and end apart: 21, of which 17 were waited for; matrix products, arithmetic and copies ran while one was open for 0% of the time, Pallas kernels for 3%

profile of v10, /device:TPU:0, one launch (start us, length us, event | category | flops | bytes accessed | tf_op | source)
XLA Modules:
  0.0 94.3 jit_solution(6843087018313437288)
XLA Ops:
  0.6 1.2 %pack.1 = (bf16[30,8,128]{2,1,0:T(8,128)(2,1)S(1)}, bf16[30,8,128]{2,1,0:T(8,128)(2,1)S(1)}) custom-call(bf16[2,29,8,128]{3,2,1,0:T(8,128)(2,1)} %bitcast.17, f32[3,2,8]{2,1,0:T(2,128)} %bitcast.18, s32[2,8]{1,0:T(2,128)} %species_hbm.1, s32[2,8,8]{2,1,0:T(8,128)} %sources_hbm.1, f32[2,8]{1,0:T(2,128)} %grad_hbm.1, bf16[100,128]{1,0:T(8,128)(2,1)} %table_hbm.1), custom_call_target="tpu_custom_call" | custom-call | tf_op jit(solution)/shard_map/pack/pallas_call | solution.py:540
  1.9 5.1 %collective-permute-start.1 = (bf16[30,8,128]{2,1,0:T(8,128)(2,1)S(1)}, bf16[30,8,128]{2,1,0:T(8,128)(2,1)S(1)}, u32[]{:S(2)}, u32[]{:S(2)}) collective-permute-start(bf16[30,8,128]{2,1,0:T(8,128)(2,1)S(1)} %get-tuple-element.42.mine_ref), channel_id=1, source_target_pairs={{0,6},{1,3},{2,0},{3,5},{4,2},{5,7},{6,4},{7,1},{8,14},{9,11},{10,... | collective-permute-start | bytes 184328 | tf_op jit(solution)/shard_map/ppermute | solution.py:580
  7.0 0.0 collective-permute-start.2
  7.0 0.0 collective-permute-start
  7.0 2.6 %stage.3 = (bf16[896,896]{1,0:T(8,128)(2,1)S(1)}, bf16[2,768,768]{2,1,0:T(8,128)(2,1)S(1)}, bf16[2,640,640]{2,1,0:T(8,128)(2,1)S(1)}) custom-call(bf16[896,896]{1,0:T(8,128)(2,1)} %bitcast.14, bf16[2,768,768]{2,1,0:T(8,128)(2,1)} %bitcast.8, bf16[2,640,640]{2,1,0:T(8,128)(2,1)} %bitcast.11), custom_call_target="tpu_custom_call" | custom-call | tf_op jit(solution)/shard_map/stage/pallas_call | solution.py:540
  9.6 0.0 collective-permute-done.1.straight_ref
  9.6 2.8 %collective-permute-done.2.cross_ref = bf16[30,8,128]{2,1,0:T(8,128)(2,1)S(1)} collective-permute-done((bf16[30,8,128]{2,1,0:T(8,128)(2,1)S(1)}, bf16[30,8,128]{2,1,0:T(8,128)(2,1)S(1)}, u32[]{:S(2)}, u32[]{:S(2)}) %collective-permute-start.2) | collective-permute-done | bytes 61472 | tf_op jit(solution)/shard_map/ppermute | solution.py:580
  12.4 0.0 collective-permute-done.partner_ref
  12.4 0.1 open.1
  12.5 0.0 copy-start
  12.5 0.1 stage.4
  12.6 0.6 copy-done
  13.1 1.9 %forward.3 = (bf16[30,16,128]{2,1,0:T(8,128)(2,1)S(1)}, f32[29,16,128]{2,1,0:T(8,128)S(1)}, bf16[128,32]{1,0:T(8,128)(2,1)S(1)}, bf16[32,128]{1,0:T(8,128)(2,1)S(1)}, f32[1280,128]{1,0:T(8,128)S(1)}) custom-call(bf16[30,16,128]{2,1,0:T(8,128)(2,1)S(1)} %get-tuple-element.44.more_3_.low_ref, bf16[30,16,128]{2,1,0:T(8,128)(2,1)S(1)} %get-tuple-element.45.high_ref, ...), custom_call_target="tpu_custom_call" | custom-call | tf_op jit(solution)/shard_map/forward/pallas_call | solution.py:540
  15.1 0.1 collective-permute-start.3
  15.1 0.1 collective-permute-start.4
  15.2 6.7 %collective-permute-done.3.more_3_.low_ref = bf16[30,16,128]{2,1,0:T(8,128)(2,1)S(1)} collective-permute-done((bf16[30,16,128]{2,1,0:T(8,128)(2,1)S(1)}, bf16[30,16,128]{2,1,0:T(8,128)(2,1)S(1)}, u32[]{:S(2)}, u32[]{:S(2)}) %collective-permute-start.3) | collective-permute-done | bytes 122912 | tf_op jit(solution)/shard_map/ppermute | solution.py:589
  21.9 3.2 %collective-permute-done.4.high_ref = bf16[30,16,128]{2,1,0:T(8,128)(2,1)S(1)} collective-permute-done((bf16[30,16,128]{2,1,0:T(8,128)(2,1)S(1)}, bf16[30,16,128]{2,1,0:T(8,128)(2,1)S(1)}, u32[]{:S(2)}, u32[]{:S(2)}) %collective-permute-start.4) | collective-permute-done | bytes 122912 | tf_op jit(solution)/shard_map/ppermute | solution.py:589
  25.2 0.0 collective-permute-start.5
  25.2 5.8 %collective-permute-done.6.high_ref = bf16[30,16,128]{2,1,0:T(8,128)(2,1)S(1)} collective-permute-done((bf16[30,16,128]{2,1,0:T(8,128)(2,1)S(1)}, bf16[30,16,128]{2,1,0:T(8,128)(2,1)S(1)}, u32[]{:S(2)}, u32[]{:S(2)}) %collective-permute-start.6) | collective-permute-done | bytes 122912 | tf_op jit(solution)/shard_map/ppermute | solution.py:589
  31.0 2.0 %collective-permute-done.5.low_ref = bf16[30,16,128]{2,1,0:T(8,128)(2,1)S(1)} collective-permute-done((bf16[30,16,128]{2,1,0:T(8,128)(2,1)S(1)}, bf16[30,16,128]{2,1,0:T(8,128)(2,1)S(1)}, u32[]{:S(2)}, u32[]{:S(2)}) %collective-permute-start.5) | collective-permute-done | bytes 122912 | tf_op jit(solution)/shard_map/ppermute | solution.py:589
  32.9 5.0 %collective-permute-start.8 = (bf16[30,16,128]{2,1,0:T(8,128)(2,1)S(1)}, bf16[30,16,128]{2,1,0:T(8,128)(2,1)S(1)}, u32[]{:S(2)}, u32[]{:S(2)}) collective-permute-start(bf16[30,16,128]{2,1,0:T(8,128)(2,1)S(1)} %get-tuple-element.57), channel_id=1, source_target_pairs={{0,10},{1,11},{2,8},{3,9},{4,12},{5,13},{6,14},{7,15},{8,18},{9,19... | collective-permute-start | bytes 368648 | tf_op jit(solution)/shard_map/ppermute | solution.py:589
  37.9 1.4 %collective-permute-start.7 = (bf16[30,16,128]{2,1,0:T(8,128)(2,1)S(1)}, bf16[30,16,128]{2,1,0:T(8,128)(2,1)S(1)}, u32[]{:S(2)}, u32[]{:S(2)}) collective-permute-start(bf16[30,16,128]{2,1,0:T(8,128)(2,1)S(1)} %get-tuple-element.57), channel_id=1, source_target_pairs={{0,8},{1,9},{2,12},{3,13},{4,14},{5,15},{6,10},{7,11},{8,16},{9,17... | collective-permute-start | bytes 368648 | tf_op jit(solution)/shard_map/ppermute | solution.py:589
  39.4 4.9 %collective-permute-done.8.high_ref = bf16[30,16,128]{2,1,0:T(8,128)(2,1)S(1)} collective-permute-done((bf16[30,16,128]{2,1,0:T(8,128)(2,1)S(1)}, bf16[30,16,128]{2,1,0:T(8,128)(2,1)S(1)}, u32[]{:S(2)}, u32[]{:S(2)}) %collective-permute-start.8) | collective-permute-done | bytes 122912 | tf_op jit(solution)/shard_map/ppermute | solution.py:589
  44.3 2.1 %collective-permute-done.7.low_ref = bf16[30,16,128]{2,1,0:T(8,128)(2,1)S(1)} collective-permute-done((bf16[30,16,128]{2,1,0:T(8,128)(2,1)S(1)}, bf16[30,16,128]{2,1,0:T(8,128)(2,1)S(1)}, u32[]{:S(2)}, u32[]{:S(2)}) %collective-permute-start.7) | collective-permute-done | bytes 122912 | tf_op jit(solution)/shard_map/ppermute | solution.py:589
  46.4 3.9 %collective-permute-start.9 = (bf16[30,16,128]{2,1,0:T(8,128)(2,1)S(1)}, bf16[30,16,128]{2,1,0:T(8,128)(2,1)S(1)}, u32[]{:S(2)}, u32[]{:S(2)}) collective-permute-start(bf16[30,16,128]{2,1,0:T(8,128)(2,1)S(1)} %get-tuple-element.58), channel_id=1, source_target_pairs={{0,24},{1,25},{2,28},{3,29},{4,30},{5,31},{6,26},{7,27},{8,0},{9,1... | collective-permute-start | bytes 368648 | tf_op jit(solution)/shard_map/ppermute | solution.py:589
  50.4 0.2 collective-permute-start.10
  50.6 2.4 %collective-permute-done.9.up_low_ref = bf16[30,16,128]{2,1,0:T(8,128)(2,1)S(1)} collective-permute-done((bf16[30,16,128]{2,1,0:T(8,128)(2,1)S(1)}, bf16[30,16,128]{2,1,0:T(8,128)(2,1)S(1)}, u32[]{:S(2)}, u32[]{:S(2)}) %collective-permute-start.9) | collective-permute-done | bytes 122912 | tf_op jit(solution)/shard_map/ppermute | solution.py:589
  53.0 3.2 %collective-permute-done.10.up_high_ref = bf16[30,16,128]{2,1,0:T(8,128)(2,1)S(1)} collective-permute-done((bf16[30,16,128]{2,1,0:T(8,128)(2,1)S(1)}, bf16[30,16,128]{2,1,0:T(8,128)(2,1)S(1)}, u32[]{:S(2)}, u32[]{:S(2)}) %collective-permute-start.10) | collective-permute-done | bytes 122912 | tf_op jit(solution)/shard_map/ppermute | solution.py:589
  56.1 8.3 %collective-permute-start.11 = (bf16[30,16,128]{2,1,0:T(8,128)(2,1)S(1)}, bf16[30,16,128]{2,1,0:T(8,128)(2,1)S(1)}, u32[]{:S(2)}, u32[]{:S(2)}) collective-permute-start(bf16[30,16,128]{2,1,0:T(8,128)(2,1)S(1)} %get-tuple-element.64), channel_id=1, source_target_pairs={{0,26},{1,27},{2,24},{3,25},{4,28},{5,29},{6,30},{7,31},{8,6},{9,7... | collective-permute-start | bytes 368648 | tf_op jit(solution)/shard_map/ppermute | solution.py:589
  64.5 0.0 collective-permute-start.12
  64.5 3.0 %collective-permute-done.11.up_low_ref = bf16[30,16,128]{2,1,0:T(8,128)(2,1)S(1)} collective-permute-done((bf16[30,16,128]{2,1,0:T(8,128)(2,1)S(1)}, bf16[30,16,128]{2,1,0:T(8,128)(2,1)S(1)}, u32[]{:S(2)}, u32[]{:S(2)}) %collective-permute-start.11) | collective-permute-done | bytes 122912 | tf_op jit(solution)/shard_map/ppermute | solution.py:589
  67.5 1.9 %collective-permute-done.12.up_high_ref = bf16[30,16,128]{2,1,0:T(8,128)(2,1)S(1)} collective-permute-done((bf16[30,16,128]{2,1,0:T(8,128)(2,1)S(1)}, bf16[30,16,128]{2,1,0:T(8,128)(2,1)S(1)}, u32[]{:S(2)}, u32[]{:S(2)}) %collective-permute-start.12) | collective-permute-done | bytes 122912 | tf_op jit(solution)/shard_map/ppermute | solution.py:589
  69.4 1.7 %collective-permute-start.13 = (bf16[30,16,128]{2,1,0:T(8,128)(2,1)S(1)}, bf16[30,16,128]{2,1,0:T(8,128)(2,1)S(1)}, u32[]{:S(2)}, u32[]{:S(2)}) collective-permute-start(bf16[30,16,128]{2,1,0:T(8,128)(2,1)S(1)} %get-tuple-element.70), channel_id=1, source_target_pairs={{0,24},{1,25},{2,28},{3,29},{4,30},{5,31},{6,26},{7,27},{8,0},{9,1... | collective-permute-start | bytes 368648 | tf_op jit(solution)/shard_map/ppermute | solution.py:589
  71.0 0.0 collective-permute-start.14
  71.0 6.5 %collective-permute-done.13.up_low_ref = bf16[30,16,128]{2,1,0:T(8,128)(2,1)S(1)} collective-permute-done((bf16[30,16,128]{2,1,0:T(8,128)(2,1)S(1)}, bf16[30,16,128]{2,1,0:T(8,128)(2,1)S(1)}, u32[]{:S(2)}, u32[]{:S(2)}) %collective-permute-start.13) | collective-permute-done | bytes 122912 | tf_op jit(solution)/shard_map/ppermute | solution.py:589
  77.5 0.0 collective-permute-done.14.up_high_ref
  77.5 2.3 %backward.5 = (f32[8,128]{1,0:T(8,128)S(1)}, f32[8,128]{1,0:T(8,128)S(1)}, f32[8,128]{1,0:T(8,128)S(1)}, f32[8,128]{1,0:T(8,128)S(1)}) custom-call(bf16[30,16,128]{2,1,0:T(8,128)(2,1)S(1)} %collective-permute-done.13.up_low_ref, bf16[30,16,128]{2,1,0:T(8,128)(2,1)S(1)} %collective-permute-done.14.up_high_ref, ...), custom_call_target="tpu_custom_call" | custom-call | tf_op jit(solution)/shard_map/backward/pallas_call | solution.py:540
  79.8 0.1 collective-permute-start.16
  79.9 4.1 %collective-permute-start.17 = (f32[8,128]{1,0:T(8,128)S(1)}, f32[8,128]{1,0:T(8,128)S(1)}, u32[]{:S(2)}, u32[]{:S(2)}) collective-permute-start(f32[8,128]{1,0:T(8,128)S(1)} %get-tuple-element.79), channel_id=1, source_target_pairs={{0,7},{1,2},{2,1},{3,4},{4,3},{5,6},{6,5},{7,0},{8,15},{9,10},{10,... | collective-permute-start | bytes 12296 | tf_op jit(solution)/shard_map/ppermute | solution.py:580
  84.0 1.3 %collective-permute-done.16.straight_ref = f32[8,128]{1,0:T(8,128)S(1)} collective-permute-done((f32[8,128]{1,0:T(8,128)S(1)}, f32[8,128]{1,0:T(8,128)S(1)}, u32[]{:S(2)}, u32[]{:S(2)}) %collective-permute-start.16) | collective-permute-done | bytes 4128 | tf_op jit(solution)/shard_map/ppermute | solution.py:580
  85.3 0.1 collective-permute-done.17.cross_ref
  85.4 3.2 %collective-permute-start.20 = (f32[16,128]{1,0:T(8,128)S(1)}, f32[16,128]{1,0:T(8,128)S(1)}, u32[]{:S(2)}, u32[]{:S(2)}) collective-permute-start(f32[16,128]{1,0:T(8,128)S(1)} %join.1.refs_0_), channel_id=1, source_target_pairs={{0,24},{8,0},{16,8},{24,16},{1,25},{9,1},{17,9},{25,17},{2,26},{10... | collective-permute-start | bytes 24584 | tf_op jit(solution)/shard_map/ppermute | solution.py:658
  88.6 0.4 collective-permute-start.19
  89.0 0.3 collective-permute-start.18
  89.3 0.7 collective-permute-done.20.refs_3_
  90.0 2.3 %collective-permute-done.19.refs_2_ = f32[16,128]{1,0:T(8,128)S(1)} collective-permute-done((f32[16,128]{1,0:T(8,128)S(1)}, f32[16,128]{1,0:T(8,128)S(1)}, u32[]{:S(2)}, u32[]{:S(2)}) %collective-permute-start.19) | collective-permute-done | bytes 8224 | tf_op jit(solution)/shard_map/ppermute | solution.py:658
  92.3 1.3 %collective-permute-done.18.refs_1_ = f32[16,128]{1,0:T(8,128)S(1)} collective-permute-done((f32[16,128]{1,0:T(8,128)S(1)}, f32[16,128]{1,0:T(8,128)S(1)}, u32[]{:S(2)}, u32[]{:S(2)}) %collective-permute-start.18) | collective-permute-done | bytes 8224 | tf_op jit(solution)/shard_map/ppermute | solution.py:658
  93.6 0.7 close.1
  (12 shorter events, 0.1 us)
Async XLA Ops:
  1.9 7.7 %collective-permute-start.1 = (bf16[30,8,128]{2,1,0:T(8,128)(2,1)S(1)}, bf16[30,8,128]{2,1,0:T(8,128)(2,1)S(1)}, u32[]{:S(2)}, u32[]{:S(2)}) collective-permute-start(bf16[30,8,128]{2,1,0:T(8,128)(2,1)S(1)} %get-tuple-element.42.mine_ref), channel_id=1, source_target_pairs={{0,6},{1,3},{2,0},{3,5},{4,2},{5,7},{6,4},{7,1},{8,14},{9,11},{10,... | collective-permute-start | bytes 184328 | tf_op jit(solution)/shard_map/ppermute | solution.py:580
  7.0 5.4 %collective-permute-start.2 = (bf16[30,8,128]{2,1,0:T(8,128)(2,1)S(1)}, bf16[30,8,128]{2,1,0:T(8,128)(2,1)S(1)}, u32[]{:S(2)}, u32[]{:S(2)}) collective-permute-start(bf16[30,8,128]{2,1,0:T(8,128)(2,1)S(1)} %get-tuple-element.43), channel_id=1, source_target_pairs={{0,7},{1,2},{2,1},{3,4},{4,3},{5,6},{6,5},{7,0},{8,15},{9,10},{10,... | collective-permute-start | bytes 184328 | tf_op jit(solution)/shard_map/ppermute | solution.py:580
  7.0 5.4 %collective-permute-start = (bf16[30,8,128]{2,1,0:T(8,128)(2,1)S(1)}, bf16[30,8,128]{2,1,0:T(8,128)(2,1)S(1)}, u32[]{:S(2)}, u32[]{:S(2)}) collective-permute-start(bf16[30,8,128]{2,1,0:T(8,128)(2,1)S(1)} %get-tuple-element.43), channel_id=1, source_target_pairs={{0,1},{1,0},{2,3},{3,2},{4,5},{5,4},{6,7},{7,6},{8,9},{9,8},{10,11... | collective-permute-start | bytes 184328 | tf_op jit(solution)/shard_map/ppermute | solution.py:580
  12.5 0.7 copy-start
  15.1 6.8 %collective-permute-start.3 = (bf16[30,16,128]{2,1,0:T(8,128)(2,1)S(1)}, bf16[30,16,128]{2,1,0:T(8,128)(2,1)S(1)}, u32[]{:S(2)}, u32[]{:S(2)}) collective-permute-start(bf16[30,16,128]{2,1,0:T(8,128)(2,1)S(1)} %get-tuple-element.52), channel_id=1, source_target_pairs={{0,8},{1,9},{2,12},{3,13},{4,14},{5,15},{6,10},{7,11},{8,16},{9,17... | collective-permute-start | bytes 368648 | tf_op jit(solution)/shard_map/ppermute | solution.py:589
  15.1 10.0 %collective-permute-start.4 = (bf16[30,16,128]{2,1,0:T(8,128)(2,1)S(1)}, bf16[30,16,128]{2,1,0:T(8,128)(2,1)S(1)}, u32[]{:S(2)}, u32[]{:S(2)}) collective-permute-start(bf16[30,16,128]{2,1,0:T(8,128)(2,1)S(1)} %get-tuple-element.52), channel_id=1, source_target_pairs={{0,10},{1,11},{2,8},{3,9},{4,12},{5,13},{6,14},{7,15},{8,18},{9,19... | collective-permute-start | bytes 368648 | tf_op jit(solution)/shard_map/ppermute | solution.py:589
  25.2 21.3 %copy-start.1 = (f32[128]{0:T(128)S(1)}, f32[128]{0:T(128)}, u32[]{:S(2)}) copy-start(f32[128]{0:T(128)} %param.20) | copy-start | bytes 1540
  25.2 5.8 %collective-permute-start.6 = (bf16[30,16,128]{2,1,0:T(8,128)(2,1)S(1)}, bf16[30,16,128]{2,1,0:T(8,128)(2,1)S(1)}, u32[]{:S(2)}, u32[]{:S(2)}) collective-permute-start(bf16[30,16,128]{2,1,0:T(8,128)(2,1)S(1)} %get-tuple-element.56), channel_id=1, source_target_pairs={{0,8},{1,9},{2,12},{3,13},{4,14},{5,15},{6,10},{7,11},{8,16},{9,17... | collective-permute-start | bytes 368648 | tf_op jit(solution)/shard_map/ppermute | solution.py:589
  25.2 7.7 %collective-permute-start.5 = (bf16[30,16,128]{2,1,0:T(8,128)(2,1)S(1)}, bf16[30,16,128]{2,1,0:T(8,128)(2,1)S(1)}, u32[]{:S(2)}, u32[]{:S(2)}) collective-permute-start(bf16[30,16,128]{2,1,0:T(8,128)(2,1)S(1)} %get-tuple-element.56), channel_id=1, source_target_pairs={{0,12},{1,13},{2,14},{3,15},{4,10},{5,11},{6,8},{7,9},{8,20},{9,21... | collective-permute-start | bytes 368648 | tf_op jit(solution)/shard_map/ppermute | solution.py:589
  32.9 11.4 %collective-permute-start.8 = (bf16[30,16,128]{2,1,0:T(8,128)(2,1)S(1)}, bf16[30,16,128]{2,1,0:T(8,128)(2,1)S(1)}, u32[]{:S(2)}, u32[]{:S(2)}) collective-permute-start(bf16[30,16,128]{2,1,0:T(8,128)(2,1)S(1)} %get-tuple-element.57), channel_id=1, source_target_pairs={{0,10},{1,11},{2,8},{3,9},{4,12},{5,13},{6,14},{7,15},{8,18},{9,19... | collective-permute-start | bytes 368648 | tf_op jit(solution)/shard_map/ppermute | solution.py:589
  37.9 8.5 %collective-permute-start.7 = (bf16[30,16,128]{2,1,0:T(8,128)(2,1)S(1)}, bf16[30,16,128]{2,1,0:T(8,128)(2,1)S(1)}, u32[]{:S(2)}, u32[]{:S(2)}) collective-permute-start(bf16[30,16,128]{2,1,0:T(8,128)(2,1)S(1)} %get-tuple-element.57), channel_id=1, source_target_pairs={{0,8},{1,9},{2,12},{3,13},{4,14},{5,15},{6,10},{7,11},{8,16},{9,17... | collective-permute-start | bytes 368648 | tf_op jit(solution)/shard_map/ppermute | solution.py:589
  46.4 6.5 %collective-permute-start.9 = (bf16[30,16,128]{2,1,0:T(8,128)(2,1)S(1)}, bf16[30,16,128]{2,1,0:T(8,128)(2,1)S(1)}, u32[]{:S(2)}, u32[]{:S(2)}) collective-permute-start(bf16[30,16,128]{2,1,0:T(8,128)(2,1)S(1)} %get-tuple-element.58), channel_id=1, source_target_pairs={{0,24},{1,25},{2,28},{3,29},{4,30},{5,31},{6,26},{7,27},{8,0},{9,1... | collective-permute-start | bytes 368648 | tf_op jit(solution)/shard_map/ppermute | solution.py:589
  50.4 5.8 %collective-permute-start.10 = (bf16[30,16,128]{2,1,0:T(8,128)(2,1)S(1)}, bf16[30,16,128]{2,1,0:T(8,128)(2,1)S(1)}, u32[]{:S(2)}, u32[]{:S(2)}) collective-permute-start(bf16[30,16,128]{2,1,0:T(8,128)(2,1)S(1)} %get-tuple-element.59), channel_id=1, source_target_pairs={{0,28},{1,29},{2,30},{3,31},{4,26},{5,27},{6,24},{7,25},{8,2},{9,3... | collective-permute-start | bytes 368648 | tf_op jit(solution)/shard_map/ppermute | solution.py:589
  56.1 11.3 %collective-permute-start.11 = (bf16[30,16,128]{2,1,0:T(8,128)(2,1)S(1)}, bf16[30,16,128]{2,1,0:T(8,128)(2,1)S(1)}, u32[]{:S(2)}, u32[]{:S(2)}) collective-permute-start(bf16[30,16,128]{2,1,0:T(8,128)(2,1)S(1)} %get-tuple-element.64), channel_id=1, source_target_pairs={{0,26},{1,27},{2,24},{3,25},{4,28},{5,29},{6,30},{7,31},{8,6},{9,7... | collective-permute-start | bytes 368648 | tf_op jit(solution)/shard_map/ppermute | solution.py:589
  64.5 4.9 %collective-permute-start.12 = (bf16[30,16,128]{2,1,0:T(8,128)(2,1)S(1)}, bf16[30,16,128]{2,1,0:T(8,128)(2,1)S(1)}, u32[]{:S(2)}, u32[]{:S(2)}) collective-permute-start(bf16[30,16,128]{2,1,0:T(8,128)(2,1)S(1)} %get-tuple-element.65), channel_id=1, source_target_pairs={{0,24},{1,25},{2,28},{3,29},{4,30},{5,31},{6,26},{7,27},{8,0},{9,1... | collective-permute-start | bytes 368648 | tf_op jit(solution)/shard_map/ppermute | solution.py:589
  69.4 8.2 %collective-permute-start.13 = (bf16[30,16,128]{2,1,0:T(8,128)(2,1)S(1)}, bf16[30,16,128]{2,1,0:T(8,128)(2,1)S(1)}, u32[]{:S(2)}, u32[]{:S(2)}) collective-permute-start(bf16[30,16,128]{2,1,0:T(8,128)(2,1)S(1)} %get-tuple-element.70), channel_id=1, source_target_pairs={{0,24},{1,25},{2,28},{3,29},{4,30},{5,31},{6,26},{7,27},{8,0},{9,1... | collective-permute-start | bytes 368648 | tf_op jit(solution)/shard_map/ppermute | solution.py:589
  71.0 6.5 %collective-permute-start.14 = (bf16[30,16,128]{2,1,0:T(8,128)(2,1)S(1)}, bf16[30,16,128]{2,1,0:T(8,128)(2,1)S(1)}, u32[]{:S(2)}, u32[]{:S(2)}) collective-permute-start(bf16[30,16,128]{2,1,0:T(8,128)(2,1)S(1)} %get-tuple-element.71), channel_id=1, source_target_pairs={{0,28},{1,29},{2,30},{3,31},{4,26},{5,27},{6,24},{7,25},{8,2},{9,3... | collective-permute-start | bytes 368648 | tf_op jit(solution)/shard_map/ppermute | solution.py:589
  79.8 4.2 %collective-permute-start.15 = (f32[8,128]{1,0:T(8,128)S(1)}, f32[8,128]{1,0:T(8,128)S(1)}, u32[]{:S(2)}, u32[]{:S(2)}) collective-permute-start(f32[8,128]{1,0:T(8,128)S(1)} %get-tuple-element.77), channel_id=1, source_target_pairs={{0,1},{1,0},{2,3},{3,2},{4,5},{5,4},{6,7},{7,6},{8,9},{9,8},{10,11... | collective-permute-start | bytes 12296 | tf_op jit(solution)/shard_map/ppermute | solution.py:580
  79.8 5.5 %collective-permute-start.16 = (f32[8,128]{1,0:T(8,128)S(1)}, f32[8,128]{1,0:T(8,128)S(1)}, u32[]{:S(2)}, u32[]{:S(2)}) collective-permute-start(f32[8,128]{1,0:T(8,128)S(1)} %get-tuple-element.78), channel_id=1, source_target_pairs={{0,2},{1,7},{2,4},{3,1},{4,6},{5,3},{6,0},{7,5},{8,10},{9,15},{10,... | collective-permute-start | bytes 12296 | tf_op jit(solution)/shard_map/ppermute | solution.py:580
  79.9 5.5 %collective-permute-start.17 = (f32[8,128]{1,0:T(8,128)S(1)}, f32[8,128]{1,0:T(8,128)S(1)}, u32[]{:S(2)}, u32[]{:S(2)}) collective-permute-start(f32[8,128]{1,0:T(8,128)S(1)} %get-tuple-element.79), channel_id=1, source_target_pairs={{0,7},{1,2},{2,1},{3,4},{4,3},{5,6},{6,5},{7,0},{8,15},{9,10},{10,... | collective-permute-start | bytes 12296 | tf_op jit(solution)/shard_map/ppermute | solution.py:580
  85.4 4.6 %collective-permute-start.20 = (f32[16,128]{1,0:T(8,128)S(1)}, f32[16,128]{1,0:T(8,128)S(1)}, u32[]{:S(2)}, u32[]{:S(2)}) collective-permute-start(f32[16,128]{1,0:T(8,128)S(1)} %join.1.refs_0_), channel_id=1, source_target_pairs={{0,24},{8,0},{16,8},{24,16},{1,25},{9,1},{17,9},{25,17},{2,26},{10... | collective-permute-start | bytes 24584 | tf_op jit(solution)/shard_map/ppermute | solution.py:658
  88.6 3.7 %collective-permute-start.19 = (f32[16,128]{1,0:T(8,128)S(1)}, f32[16,128]{1,0:T(8,128)S(1)}, u32[]{:S(2)}, u32[]{:S(2)}) collective-permute-start(f32[16,128]{1,0:T(8,128)S(1)} %join.1.refs_0_), channel_id=1, source_target_pairs={{0,16},{8,24},{16,0},{24,8},{1,17},{9,25},{17,1},{25,9},{2,18},{10... | collective-permute-start | bytes 24584 | tf_op jit(solution)/shard_map/ppermute | solution.py:658
  89.0 4.5 %collective-permute-start.18 = (f32[16,128]{1,0:T(8,128)S(1)}, f32[16,128]{1,0:T(8,128)S(1)}, u32[]{:S(2)}, u32[]{:S(2)}) collective-permute-start(f32[16,128]{1,0:T(8,128)S(1)} %join.1.refs_0_), channel_id=1, source_target_pairs={{0,8},{8,16},{16,24},{24,0},{1,9},{9,17},{17,25},{25,1},{2,10},{10... | collective-permute-start | bytes 24584 | tf_op jit(solution)/shard_map/ppermute | solution.py:658

commit v11 on v9

--- a/solution.py
+++ b/solution.py
@@ -89,31 +89,23 @@
     return jnp.concatenate([low[slab:], high[:slab]], axis=0)
 
 
-def pool(value, rows):
-    total = value[:rows]
-    for start in range(rows, value.shape[0], rows):
-        total = total + value[start : start + rows]
-    return total
-
-
-def geo_at(geo_ref, which, edges):
-    return geo_ref[which * edges : (which + 1) * edges, :]
-
-
-def forward(refs, hot_ref, geo_ref, zero_ref, one_ref, two_ref, sz, rows, last):
+def forward(refs, edge_refs, zero_ref, one_ref, two_ref, sz, rows, last):
+    hot_ref, _, _, geo_ref, turned_ref, scaled_ref = edge_refs
     hot = hot_ref[...]
     edges = hot.shape[0]
     factor = (edges // rows) ** (-0.5)
-    radial = geo_at(geo_ref, 0, edges)
-
-    def scaled(block):
-        return (block * radial).astype(BF16).astype(F32)
+    radial = geo_ref[:edges, :]
+
+    def scaled(first, count):
+        group = picked_group(refs, hot, first, count)
+        blocks = [(group[:, sz.cols(n)] * radial).astype(BF16) for n in range(count)]
+        for n, block in enumerate(blocks):
+            scaled_ref[first + n] = block
+        return jnp.concatenate(blocks, axis=1)
 
     pooled = [None] * sz.coefs
-    group = picked_group(refs, hot, 0, sz.zero)
-    zin = jnp.concatenate(
-        [pool(scaled(group[:, sz.cols(k)]), rows) for k in range(sz.zero)], axis=1
-    )
+    ones = turned_ref[4 * rows : 5 * rows, :].astype(BF16)
+    zin = dot(ones, scaled(0, sz.zero))
     kept = 1 if last else sz.zero
     (zout,) = fine_dot(zin, [zero_ref[:, sz.cols(0, kept)]], dot)
     for k in range(kept):
@@ -121,17 +113,13 @@
     for order in range(2):
         first, count = sz.starts[order], sz.counts[order]
         weight_ref = (one_ref, two_ref)[order]
-        cos = geo_at(geo_ref, 1 + 2 * order, edges)
-        sin = geo_at(geo_ref, 2 + 2 * order, edges)
-        group = picked_group(refs, hot, first, 2 * count)
-        res, ims = [], []
-        for k in range(count):
-            re = scaled(group[:, sz.cols(k)])
-            im = scaled(group[:, sz.cols(count + k)])
-            res.append(pool(cos * re - sin * im, rows))
-            ims.append(pool(sin * re + cos * im, rows))
+        turns = jnp.concatenate(split(turned_ref[2 * order * rows : (2 * order + 2) * rows, :]), axis=0)
+        out = dot(turns, scaled(first, 2 * count))
+        by_cos = out[:rows] + out[2 * rows : 3 * rows]
+        by_sin = out[rows : 2 * rows] + out[3 * rows :]
+        half = count * sz.c
         both = jnp.concatenate(
-            [jnp.concatenate(res, axis=1), jnp.concatenate(ims, axis=1)], axis=0
+            [by_cos[:, :half] - by_sin[:, half:], by_sin[:, :half] + by_cos[:, half:]], axis=0
         )
         a, b = fine_dot(both, [weight_ref[0], weight_ref[1]], dot)
         out_re = (a[:rows] - b[rows:]) * factor
@@ -149,12 +137,9 @@
     return total
 
 
-def backward(
-    upstream, pooled, refs, hot_ref, hot_t_ref, geo_ref, zero_ref, one_ref, two_ref, sz, rows, last, outs
-):
-    hot = hot_ref[...]
-    hot_t = hot_t_ref[...]
-    edges = hot.shape[0]
+def backward(upstream, pooled, edge_refs, rate_ref, zero_ref, one_ref, two_ref, sz, rows, last, outs):
+    _, hot_t_ref, net_ref, geo_ref, turned_ref, scaled_ref = edge_refs
+    edges = hot_t_ref.shape[1]
     slab = rows // 2
     factor = (edges // rows) ** (-0.5)
     signal = signal_of(pooled, sz)
@@ -176,18 +161,19 @@
                 term = term + 2.0 * d_signal * pooled[k]
             d_pooled.append(term * factor)
 
-    radial = geo_at(geo_ref, 0, edges)
-    kept = 1 if last else sz.zero
-    (dz,) = fine_dot(jnp.concatenate(d_pooled[:kept], axis=1), [zero_ref[:, sz.cols(0, kept)]], dot_t)
+    rate = rate_ref[...]
 
     def spread(block):
         return jnp.concatenate([block] * (edges // rows), axis=0)
 
+    def geo(which):
+        return geo_ref[which * edges : (which + 1) * edges, :]
+
+    def source_rows(first, count):
+        return jnp.concatenate([scaled_ref[k] for k in range(first, first + count)], axis=1)
+
     def scatter(first, blocks):
-        if outs is None:
-            return
-        high, low = split(jnp.concatenate(blocks, axis=1))
-        back = dot(hot_t, high) + dot(hot_t, low)
+        back = dot(hot_t_ref[...], jnp.concatenate([block.astype(BF16) for block in blocks], axis=1))
         for n in range(len(blocks)):
             k = first + n
             part = back[:, sz.cols(n)]
@@ -196,21 +182,29 @@
             outs[0][k] = part[:rows].astype(BF16)
             outs[1][k] = part[rows:].astype(BF16)
 
-    q_len = jnp.zeros((edges, sz.c), F32)
-    group = picked_group(refs, hot, 0, sz.zero)
-    blocks = []
-    for k in range(sz.zero):
-        grad = spread(dz[:, sz.cols(k)])
-        q_len = q_len + grad * group[:, sz.cols(k)]
-        blocks.append(grad * radial)
-    q_len = q_len * radial
-    scatter(0, blocks)
-    q_turn = []
+    own_row = lax.broadcasted_iota(jnp.int32, (rows, edges), 0)
+    own_edge = lax.rem(lax.broadcasted_iota(jnp.int32, (rows, edges), 1), rows) == own_row
+
+    def per_edge(products, which, groups):
+        value = products[which * rows : (which + 1) * rows]
+        value = value + products[(groups + which) * rows : (groups + which + 1) * rows]
+        return jnp.sum(jnp.where(own_edge, value, 0.0), axis=0, keepdims=True)
+
+    def by_rate(value):
+        return jnp.concatenate([value[:, sz.cols(n)] * rate for n in range(value.shape[1] // sz.c)], axis=1)
+
+    kept = 1 if last else sz.zero
+    (dz,) = fine_dot(jnp.concatenate(d_pooled[:kept], axis=1), [zero_ref[:, sz.cols(0, kept)]], dot_t)
+    products = dot_t(jnp.concatenate(split(by_rate(dz)), axis=0), source_rows(0, sz.zero))
+    d_len = per_edge(products, 0, 1)
+    if outs is not None:
+        radial = geo(0)
+        scatter(0, [spread(dz[:, sz.cols(k)]) * radial for k in range(sz.zero)])
+    c1, s1 = (turned_ref[5 * rows + n : 5 * rows + n + 1, :] for n in range(2))
+    turned = []
     for order in range(2):
         first, count = sz.starts[order], sz.counts[order]
         weight_ref = (one_ref, two_ref)[order]
-        cos = geo_at(geo_ref, 1 + 2 * order, edges)
-        sin = geo_at(geo_ref, 2 + 2 * order, edges)
         both = jnp.concatenate(
             [
                 jnp.concatenate(d_pooled[first : first + count], axis=1),
@@ -221,48 +215,36 @@
         a, b = fine_dot(both, [weight_ref[0], weight_ref[1]], dot_t)
         d_re = a[:rows] + b[rows:]
         d_im = a[rows:] - b[:rows]
-        group = picked_group(refs, hot, first, 2 * count)
-        q_cos = jnp.zeros((edges, sz.c), F32)
-        q_sin = jnp.zeros((edges, sz.c), F32)
-        cos_r = cos * radial
-        sin_r = sin * radial
-        blocks_re, blocks_im = [], []
-        for k in range(count):
-            re = group[:, sz.cols(k)]
-            im = group[:, sz.cols(count + k)]
-            g_re = spread(d_re[:, sz.cols(k)])
-            g_im = spread(d_im[:, sz.cols(k)])
-            q_cos = q_cos + (re * g_re + im * g_im)
-            q_sin = q_sin + (re * g_im - im * g_re)
-            if outs is not None:
+        straight = jnp.concatenate([d_re, d_im], axis=1)
+        crossed = jnp.concatenate([d_im, -d_re], axis=1)
+        four = jnp.concatenate([straight, crossed, by_rate(straight), by_rate(crossed)], axis=0)
+        products = dot_t(jnp.concatenate(split(four), axis=0), source_rows(first, 2 * count))
+        q_cos, q_sin, r_cos, r_sin = (per_edge(products, n, 4) for n in range(4))
+        cos, sin = (c1, s1) if order == 0 else (c1 * c1 - s1 * s1, 2.0 * c1 * s1)
+        d_len = d_len + cos * r_cos + sin * r_sin
+        turned.append((q_cos, q_sin))
+        if outs is not None:
+            cos_r, sin_r = geo(1 + 2 * order), geo(2 + 2 * order)
+            blocks_re, blocks_im = [], []
+            for k in range(count):
+                g_re, g_im = spread(d_re[:, sz.cols(k)]), spread(d_im[:, sz.cols(k)])
                 blocks_re.append(cos_r * g_re + sin_r * g_im)
                 blocks_im.append(cos_r * g_im - sin_r * g_re)
-        scatter(first, blocks_re + blocks_im)
-        q_cos = q_cos * radial
-        q_sin = q_sin * radial
-        q_len = q_len + cos * q_cos + sin * q_sin
-        q_turn.append((q_cos, q_sin))
-
-    rate = geo_at(geo_ref, 9, edges)
-
-    def total(value):
-        return jnp.sum(value, axis=1, keepdims=True)
-
-    d_len = -total(q_len * rate)
-    (dc1, ds1), (dc2, ds2) = [(total(a), total(b)) for a, b in q_turn]
-    c1, s1 = geo_at(geo_ref, 1, edges), geo_at(geo_ref, 2, edges)
-    ux, uy, uz = (geo_at(geo_ref, 5 + n, edges) for n in range(3))
-    inv_planar = geo_at(geo_ref, 8, edges)
+            scatter(first, blocks_re + blocks_im)
+
+    d_len = -d_len
+    (dc1, ds1), (dc2, ds2) = turned
+    ux, uy, uz, inv_planar = (turned_ref[5 * rows + n : 5 * rows + n + 1, :] for n in range(2, 6))
     dc1 = dc1 + 2.0 * (c1 * dc2 + s1 * ds2)
     ds1 = ds1 + 2.0 * (c1 * ds2 - s1 * dc2)
     along = c1 * dc1 + s1 * ds1
     dx = (dc1 - along * c1) * inv_planar + d_len * ux
     dy = (ds1 - along * s1) * inv_planar + d_len * uy
-    dz_ = d_len * uz
-    lane = lax.broadcasted_iota(jnp.int32, (edges, sz.c), 1)
-    change = jnp.where(lane == 0, dx, jnp.where(lane == 1, dy, jnp.where(lane == 2, dz_, 0.0)))
-    moved = sum(dot(hot_t, part) for part in split3(change))
-    return moved - around(pool(change, rows), slab)
+    change = jnp.where(own_row == 0, dx, jnp.where(own_row == 1, dy, jnp.where(own_row == 2, d_len * uz, 0.0)))
+    moved = sum(dot(part, net_ref[...]) for part in split3(change))
+    lanes = moved.shape[1]
+    moved = jnp.transpose(jnp.concatenate([moved, jnp.zeros((lanes - rows, lanes), F32)], axis=0))
+    return moved[: 2 * rows]
 
 
 def around(own, slab):
@@ -393,7 +375,8 @@
             high_ref[k] = jnp.concatenate([choose(partner, mine), choose(straight, cross)], axis=0).astype(BF16)
 
 
-def edges_of(refs, coefs, slabs, neighbours, rate_ref, hot_ref, hot_t_ref, geo_ref):
+def edges_of(refs, coefs, slabs, neighbours, rate_ref, edge_refs):
+    hot_ref, hot_t_ref, net_ref, geo_ref, turned_ref, _ = edge_refs
     start, _ = first_slab(slabs)
     extra = jnp.concatenate([ref[coefs].astype(F32) for ref in refs], axis=0)
     window, c = extra.shape
@@ -413,6 +396,9 @@
         ],
         axis=0,
     )
+    lane = lax.broadcasted_iota(jnp.int32, (edges, c), 1)
+    atom = lax.rem(lax.broadcasted_iota(jnp.int32, (edges, c), 0), rows)
+    net_ref[...] = (hot - (lane == atom + per_slab).astype(F32)).astype(BF16)
     hot_t_ref[...] = jnp.transpose(hot).astype(BF16)[:window]
     hot = hot.astype(BF16)[:, :window]
     hot_ref[...] = hot
@@ -428,54 +414,41 @@
     length = jnp.sqrt(flat + offset[2] * offset[2])
     planar = jnp.sqrt(flat)
     c1, s1 = offset[0] / planar, offset[1] / planar
-    rate = jnp.broadcast_to(rate_ref[...], (edges, c))
-    values = [
-        jnp.exp(-rate * length),
-        c1,
-        s1,
-        c1 * c1 - s1 * s1,
-        2.0 * c1 * s1,
-        offset[0] / length,
-        offset[1] / length,
-        offset[2] / length,
-        1.0 / planar,
-        rate,
-    ]
-    for n, value in enumerate(values):
+    c2, s2 = c1 * c1 - s1 * s1, 2.0 * c1 * s1
+    radial = jnp.exp(-rate_ref[...] * length)
+    for n, value in enumerate((radial, c1 * radial, s1 * radial, c2 * radial, s2 * radial)):
         geo_ref[n * edges : (n + 1) * edges, :] = value
+    packed = jnp.where(lax.rem(lane, rows) == atom, 1.0, 0.0)
+    for n, value in enumerate((c1, s1, c2, s2)):
+        packed = jnp.where(lane // rows == n, packed * value, packed)
+    singles = (c1, s1, offset[0] / length, offset[1] / length, offset[2] / length, 1.0 / planar)
+    for n, value in enumerate(singles):
+        packed = jnp.where(lane == 5 * rows + n, value, packed)
+    turned_ref[...] = jnp.transpose(packed)
     return numbers[per_slab : per_slab + rows]
 
 
-def turn_to_stage():
-    odd = lax.rem(lax.axis_index("space"), 2)
-    return jnp.where(lax.axis_index("segment") == 0, odd, 0)
-
-
-def stage_kernel(moment, zero_hbm, one_hbm, two_hbm, *more):
-    zero_ref, one_ref, two_ref, sems = more[-4:]
-
-    @pl.when(turn_to_stage() == moment)
-    def _():
-        pairs = [(zero_hbm, zero_ref)]
-        for source, target in ((one_hbm, one_ref), (two_hbm, two_ref)):
-            pairs += [(source.at[n], target.at[n]) for n in range(2)]
-        copies = [pltpu.make_async_copy(source, target, sems.at[n]) for n, (source, target) in enumerate(pairs)]
-        for copy in copies:
-            copy.start()
-        for copy in copies:
-            copy.wait()
+def stage_kernel(zero_hbm, one_hbm, two_hbm, zero_ref, one_ref, two_ref, sems):
+    pairs = [(zero_hbm, zero_ref)]
+    for source, target in ((one_hbm, one_ref), (two_hbm, two_ref)):
+        pairs += [(source.at[n], target.at[n]) for n in range(2)]
+    copies = [pltpu.make_async_copy(source, target, sems.at[n]) for n, (source, target) in enumerate(pairs)]
+    for copy in copies:
+        copy.start()
+    for copy in copies:
+        copy.wait()
 
 
 def forward_kernel(
     tick, sz, slabs, neighbours, low_ref, high_ref, rate_ref, zero_ref, one_ref, two_ref,
-    out_ref, pooled_ref, hot_ref, hot_t_ref, geo_ref
+    out_ref, pooled_ref, *edge_refs
 ):
     @pl.when(lax.axis_index("segment") == tick)
     def _():
         rows = low_ref.shape[1]
         refs = (low_ref, high_ref)
-        edges_of(refs, sz.coefs, slabs, neighbours, rate_ref, hot_ref, hot_t_ref, geo_ref)
-        pooled = forward(refs, hot_ref, geo_ref, zero_ref, one_ref, two_ref, sz, rows, False)
+        edges_of(refs, sz.coefs, slabs, neighbours, rate_ref, edge_refs)
+        pooled = forward(refs, edge_refs, zero_ref, one_ref, two_ref, sz, rows, False)
         signal = signal_of(pooled, sz)
         gate, lifted = silu_parts(signal)
         for k in range(sz.coefs):
@@ -487,15 +460,15 @@
 
 def turn_kernel(
     tick, sz, slabs, neighbours, low_ref, high_ref, rate_ref, zero_ref, one_ref, two_ref, read_ref,
-    back_low_ref, back_high_ref, hot_ref, hot_t_ref, geo_ref
+    back_low_ref, back_high_ref, *edge_refs
 ):
     @pl.when(lax.axis_index("segment") == tick)
     def _():
         rows = low_ref.shape[1]
         refs = (low_ref, high_ref)
         outs = (back_low_ref, back_high_ref)
-        own = edges_of(refs, sz.coefs, slabs, neighbours, rate_ref, hot_ref, hot_t_ref, geo_ref)
-        pooled = forward(refs, hot_ref, geo_ref, zero_ref, one_ref, two_ref, sz, rows, True)
+        own = edges_of(refs, sz.coefs, slabs, neighbours, rate_ref, edge_refs)
+        pooled = forward(refs, edge_refs, zero_ref, one_ref, two_ref, sz, rows, True)
         signal = signal_of(pooled, sz)
         _, lifted = silu_parts(signal)
         updated = own_rows(refs, 0) + lifted
@@ -505,25 +478,21 @@
         lane = lax.broadcasted_iota(jnp.int32, (rows, sz.c), 1)
         energy = around(jnp.where(lane == 3, energy, 0.0), rows // 2)
         upstream = [own[:, 3:4] * read * (gate + updated * gate * (1.0 - gate))]
-        moved = backward(
-            upstream, pooled, refs, hot_ref, hot_t_ref, geo_ref, zero_ref, one_ref, two_ref, sz, rows, True, outs
-        )
+        moved = backward(upstream, pooled, edge_refs, rate_ref, zero_ref, one_ref, two_ref, sz, rows, True, outs)
         send_back(moved + energy, outs, sz)
 
 
-def backward_kernel(
-    tick, sz, up_low_ref, up_high_ref, pooled_ref, low_ref, high_ref, hot_ref, hot_t_ref, geo_ref,
-    zero_ref, one_ref, two_ref, *outs
-):
+def backward_kernel(tick, sz, up_low_ref, up_high_ref, rate_ref, pooled_ref, *more):
+    edge_refs = more[:6]
+    zero_ref, one_ref, two_ref, *outs = more[6:]
+
     @pl.when(lax.axis_index("segment") == tick)
     def _():
-        rows = low_ref.shape[1]
-        refs = (low_ref, high_ref)
+        rows = up_low_ref.shape[1]
         upstream = [up_low_ref[k].astype(F32) + up_high_ref[k].astype(F32) for k in range(sz.coefs)]
         pooled = [pooled_ref[k] for k in range(sz.coefs)]
         moved = backward(
-            upstream, pooled, refs, hot_ref, hot_t_ref, geo_ref, zero_ref, one_ref, two_ref, sz, rows, False,
-            outs if tick else None,
+            upstream, pooled, edge_refs, rate_ref, zero_ref, one_ref, two_ref, sz, rows, False, outs if tick else None
         )
         carried = decode(up_low_ref[sz.coefs].astype(F32)) + decode(up_high_ref[sz.coefs].astype(F32))
         moved = moved + around(carried, rows // 2)
@@ -533,7 +502,7 @@
             share(moved, outs)
 
 
-def call(body, operands, shapes, name, spaces=None, scratch=(), aliases=None):
+def call(body, operands, shapes, name, spaces=None, scratch=()):
     spaces = spaces or [pltpu.VMEM] * len(operands)
     operands = [pltpu.with_memory_space_constraint(value, space) for value, space in zip(operands, spaces)]
     return pl.pallas_call(
@@ -542,7 +511,6 @@
         in_specs=[pl.BlockSpec(memory_space=space) for space in spaces],
         out_specs=[pl.BlockSpec(memory_space=pltpu.VMEM) for _ in shapes],
         scratch_shapes=list(scratch),
-        input_output_aliases=aliases or {},
         compiler_params=pltpu.CompilerParams(vmem_limit_bytes=VMEM_LIMIT),
         name=name,
     )(*operands)
@@ -602,15 +570,12 @@
     spaces = [pltpu.HBM] * 3
     on_chip = [pltpu.VMEM(w.shape, w.dtype) for w in stored]
     sems = [pltpu.SemaphoreType.DMA((5,))]
-    weights = call(functools.partial(stage_kernel, 0), stored, on_chip, "stage", spaces, sems)
+    weights = call(stage_kernel, stored, on_chip, "stage", spaces, sems)
     whole = shape((coefs + 1, rows, channels), BF16)
     around_all = [call(open_kernel, [mine, partner, straight, cross], [whole, whole], "open")]
-    weights = call(
-        functools.partial(stage_kernel, 1), [*stored, *weights, around_all[0][0]], on_chip, "stage",
-        spaces + [pltpu.VMEM] * 4, sems, {3: 0, 4: 1, 5: 2},
-    )
     edge_shapes = [
-        shape((edges, 2 * rows), BF16), shape((2 * rows, edges), BF16), shape((10 * edges, channels), F32),
+        shape((edges, 2 * rows), BF16), shape((2 * rows, edges), BF16), shape((edges, channels), BF16),
+        shape((5 * edges, channels), F32), shape((channels, edges), F32), shape((coefs, edges, channels), BF16),
     ]
     kept = []
     for tick in range(segments - 1):
@@ -638,7 +603,7 @@
         pooled, *residuals = kept[tick]
         parts = call(
             functools.partial(backward_kernel, tick, sz),
-            [*up, pooled, *around_all[tick], *residuals, *weights],
+            [*up, radial_rate, pooled, *residuals, *weights],
             [whole, whole] if tick else [slab_sums] * 4,
             "backward",
         )

time: 91.1 us -> 88.6 us (0.973)
  starting transfers between devices: 31.8 us -> 29.9 us
  Pallas kernels: 8.94 us -> 9.97 us
    ppermute x12, starting transfers between devices: 18.4 us -> 17.3 us  [hop(): return lax.ppermute(value, axes, ways)]
    pallas_call x13 -> x12, Pallas kernels: 8.94 us -> 9.97 us  [call(): pl.pallas_call(body, out_shape=shapes, in_specs=[pl.BlockSpec(memory_spac...]
    ppermute x12, waiting for transfers between devices: 40.7 us -> 39.8 us  [hop(): return lax.ppermute(value, axes, ways)]
  transfers between devices with their start and end apart: 21 -> 21, of which waited for: 16 -> 15; matrix products, arithmetic and copies ran while one was open for 0% -> 0% of each run, Pallas kernels for 3% -> 3%
where the time goes in v11:
time: 88.6 us; the launch traced here: 88.5 us
  waiting for transfers between devices  47.9 us (54%)
  starting transfers between devices  29.9 us (34%)
  Pallas kernels  9.97 us (11%)
    ppermute x12, waiting for transfers between devices, hop(): return lax.ppermute(value, axes, ways)  39.8 us
    ppermute x12, starting transfers between devices, hop(): return lax.ppermute(value, axes, ways)  17.3 us
    pallas_call x12, Pallas kernels, call(): pl.pallas_call(body, out_shape=shapes, in_specs=[pl.BlockSpec(memory_spac...  9.97 us
    ppermute x6, starting transfers between devices, within(): return lax.ppermute(value, axes, ways)  9.41 us
    ppermute x6, waiting for transfers between devices, within(): return lax.ppermute(value, axes, ways)  4.14 us
    ppermute x3, waiting for transfers between devices, on_device(): lax.ppermute(both, 'segment', [(s, (s + stop) % segments) for s in range(...  3.91 us
    ppermute x3, starting transfers between devices, on_device(): lax.ppermute(both, 'segment', [(s, (s + stop) % segments) for s in range(...  3.16 us
  transfers between devices with their start and end apart: 21, of which 15 were waited for; matrix products, arithmetic and copies ran while one was open for 0% of the time, Pallas kernels for 3%

profile of v11, /device:TPU:0, one launch (start us, length us, event | category | flops | bytes accessed | tf_op | source)
XLA Modules:
  0.0 88.5 jit_solution(14575977074322239353)
XLA Ops:
  0.6 1.2 %pack.1 = (bf16[30,8,128]{2,1,0:T(8,128)(2,1)S(1)}, bf16[30,8,128]{2,1,0:T(8,128)(2,1)S(1)}) custom-call(bf16[2,29,8,128]{3,2,1,0:T(8,128)(2,1)} %bitcast.11, f32[3,2,8]{2,1,0:T(2,128)} %bitcast.12, s32[2,8]{1,0:T(2,128)} %species_hbm.1, s32[2,8,8]{2,1,0:T(8,128)} %sources_hbm.1, f32[2,8]{1,0:T(2,128)} %grad_hbm.1, bf16[100,128]{1,0:T(8,128)(2,1)} %table_hbm.1), custom_call_target="tpu_custom_call" | custom-call | tf_op jit(solution)/shard_map/pack/pallas_call | solution.py:508
  1.9 5.1 %collective-permute-start.1 = (bf16[30,8,128]{2,1,0:T(8,128)(2,1)S(1)}, bf16[30,8,128]{2,1,0:T(8,128)(2,1)S(1)}, u32[]{:S(2)}, u32[]{:S(2)}) collective-permute-start(bf16[30,8,128]{2,1,0:T(8,128)(2,1)S(1)} %get-tuple-element.45.mine_ref), channel_id=1, source_target_pairs={{0,6},{1,3},{2,0},{3,5},{4,2},{5,7},{6,4},{7,1},{8,14},{9,11},{10,... | collective-permute-start | bytes 184328 | tf_op jit(solution)/shard_map/ppermute | solution.py:547
  7.0 0.0 collective-permute-start.2
  7.0 0.0 collective-permute-start
  7.0 2.6 %stage.1 = (bf16[896,896]{1,0:T(8,128)(2,1)S(1)}, bf16[2,768,768]{2,1,0:T(8,128)(2,1)S(1)}, bf16[2,640,640]{2,1,0:T(8,128)(2,1)S(1)}) custom-call(bf16[896,896]{1,0:T(8,128)(2,1)} %bitcast.10, bf16[2,768,768]{2,1,0:T(8,128)(2,1)} %bitcast.8, bf16[2,640,640]{2,1,0:T(8,128)(2,1)} %bitcast.9), custom_call_target="tpu_custom_call" | custom-call | tf_op jit(solution)/shard_map/stage/pallas_call | solution.py:508
  9.6 0.0 collective-permute-done.1.straight_ref
  9.6 2.8 %collective-permute-done.2.cross_ref = bf16[30,8,128]{2,1,0:T(8,128)(2,1)S(1)} collective-permute-done((bf16[30,8,128]{2,1,0:T(8,128)(2,1)S(1)}, bf16[30,8,128]{2,1,0:T(8,128)(2,1)S(1)}, u32[]{:S(2)}, u32[]{:S(2)}) %collective-permute-start.2) | collective-permute-done | bytes 61472 | tf_op jit(solution)/shard_map/ppermute | solution.py:547
  12.4 0.0 collective-permute-done.partner_ref
  12.4 0.1 open.1
  12.5 2.3 %forward.3 = (bf16[30,16,128]{2,1,0:T(8,128)(2,1)S(1)}, f32[29,16,128]{2,1,0:T(8,128)S(1)}, bf16[128,32]{1,0:T(8,128)(2,1)S(1)}, bf16[32,128]{1,0:T(8,128)(2,1)S...) custom-call(bf16[30,16,128]{2,1,0:T(8,128)(2,1)S(1)} %get-tuple-elem, ...), custom_call_target="tpu_custom_call" | custom-call | tf_op jit(solution)/shard_map/forward/pallas_call | solution.py:508
  14.8 0.1 collective-permute-start.4
  14.9 0.1 collective-permute-start.3
  14.9 8.8 %collective-permute-done.4.high_ref = bf16[30,16,128]{2,1,0:T(8,128)(2,1)S(1)} collective-permute-done((bf16[30,16,128]{2,1,0:T(8,128)(2,1)S(1)}, bf16[30,16,128]{2,1,0:T(8,128)(2,1)S(1)}, u32[]{:S(2)}, u32[]{:S(2)}) %collective-permute-start.4) | collective-permute-done | bytes 122912 | tf_op jit(solution)/shard_map/ppermute | solution.py:556
  23.8 0.4 collective-permute-done.3.low_ref
  24.2 0.0 collective-permute-start.6
  24.2 0.2 collective-permute-start.5
  24.3 8.2 %collective-permute-done.6.high_ref = bf16[30,16,128]{2,1,0:T(8,128)(2,1)S(1)} collective-permute-done((bf16[30,16,128]{2,1,0:T(8,128)(2,1)S(1)}, bf16[30,16,128]{2,1,0:T(8,128)(2,1)S(1)}, u32[]{:S(2)}, u32[]{:S(2)}) %collective-permute-start.6) | collective-permute-done | bytes 122912 | tf_op jit(solution)/shard_map/ppermute | solution.py:556
  32.6 0.0 collective-permute-done.5.low_ref
  32.6 2.7 %collective-permute-start.8 = (bf16[30,16,128]{2,1,0:T(8,128)(2,1)S(1)}, bf16[30,16,128]{2,1,0:T(8,128)(2,1)S(1)}, u32[]{:S(2)}, u32[]{:S(2)}) collective-permute-start(bf16[30,16,128]{2,1,0:T(8,128)(2,1)S(1)} %get-tuple-element.54), channel_id=1, source_target_pairs={{0,10},{1,11},{2,8},{3,9},{4,12},{5,13},{6,14},{7,15},{8,18},{9,19... | collective-permute-start | bytes 368648 | tf_op jit(solution)/shard_map/ppermute | solution.py:556
  35.2 1.0 %collective-permute-start.7 = (bf16[30,16,128]{2,1,0:T(8,128)(2,1)S(1)}, bf16[30,16,128]{2,1,0:T(8,128)(2,1)S(1)}, u32[]{:S(2)}, u32[]{:S(2)}) collective-permute-start(bf16[30,16,128]{2,1,0:T(8,128)(2,1)S(1)} %get-tuple-element.54), channel_id=1, source_target_pairs={{0,8},{1,9},{2,12},{3,13},{4,14},{5,15},{6,10},{7,11},{8,16},{9,17... | collective-permute-start | bytes 368648 | tf_op jit(solution)/shard_map/ppermute | solution.py:556
  36.2 5.8 %collective-permute-done.8.high_ref = bf16[30,16,128]{2,1,0:T(8,128)(2,1)S(1)} collective-permute-done((bf16[30,16,128]{2,1,0:T(8,128)(2,1)S(1)}, bf16[30,16,128]{2,1,0:T(8,128)(2,1)S(1)}, u32[]{:S(2)}, u32[]{:S(2)}) %collective-permute-start.8) | collective-permute-done | bytes 122912 | tf_op jit(solution)/shard_map/ppermute | solution.py:556
  42.0 0.0 collective-permute-done.7.low_ref
  42.0 5.1 %collective-permute-start.9 = (bf16[30,16,128]{2,1,0:T(8,128)(2,1)S(1)}, bf16[30,16,128]{2,1,0:T(8,128)(2,1)S(1)}, u32[]{:S(2)}, u32[]{:S(2)}) collective-permute-start(bf16[30,16,128]{2,1,0:T(8,128)(2,1)S(1)} %get-tuple-element.55), channel_id=1, source_target_pairs={{0,24},{1,25},{2,28},{3,29},{4,30},{5,31},{6,26},{7,27},{8,0},{9,1... | collective-permute-start | bytes 368648 | tf_op jit(solution)/shard_map/ppermute | solution.py:556
  47.1 0.5 collective-permute-start.10
  47.6 2.0 %collective-permute-done.9.up_low_ref = bf16[30,16,128]{2,1,0:T(8,128)(2,1)S(1)} collective-permute-done((bf16[30,16,128]{2,1,0:T(8,128)(2,1)S(1)}, bf16[30,16,128]{2,1,0:T(8,128)(2,1)S(1)}, u32[]{:S(2)}, u32[]{:S(2)}) %collective-permute-start.9) | collective-permute-done | bytes 122912 | tf_op jit(solution)/shard_map/ppermute | solution.py:556
  49.6 3.3 %collective-permute-done.10.up_high_ref = bf16[30,16,128]{2,1,0:T(8,128)(2,1)S(1)} collective-permute-done((bf16[30,16,128]{2,1,0:T(8,128)(2,1)S(1)}, bf16[30,16,128]{2,1,0:T(8,128)(2,1)S(1)}, u32[]{:S(2)}, u32[]{:S(2)}) %collective-permute-start.10) | collective-permute-done | bytes 122912 | tf_op jit(solution)/shard_map/ppermute | solution.py:556
  52.9 6.1 %collective-permute-start.11 = (bf16[30,16,128]{2,1,0:T(8,128)(2,1)S(1)}, bf16[30,16,128]{2,1,0:T(8,128)(2,1)S(1)}, u32[]{:S(2)}, u32[]{:S(2)}) collective-permute-start(bf16[30,16,128]{2,1,0:T(8,128)(2,1)S(1)} %get-tuple-element.64), channel_id=1, source_target_pairs={{0,26},{1,27},{2,24},{3,25},{4,28},{5,29},{6,30},{7,31},{8,6},{9,7... | collective-permute-start | bytes 368648 | tf_op jit(solution)/shard_map/ppermute | solution.py:556
  59.0 0.0 collective-permute-start.12
  59.0 3.0 %collective-permute-done.11.up_low_ref = bf16[30,16,128]{2,1,0:T(8,128)(2,1)S(1)} collective-permute-done((bf16[30,16,128]{2,1,0:T(8,128)(2,1)S(1)}, bf16[30,16,128]{2,1,0:T(8,128)(2,1)S(1)}, u32[]{:S(2)}, u32[]{:S(2)}) %collective-permute-start.11) | collective-permute-done | bytes 122912 | tf_op jit(solution)/shard_map/ppermute | solution.py:556
  62.0 1.9 %collective-permute-done.12.up_high_ref = bf16[30,16,128]{2,1,0:T(8,128)(2,1)S(1)} collective-permute-done((bf16[30,16,128]{2,1,0:T(8,128)(2,1)S(1)}, bf16[30,16,128]{2,1,0:T(8,128)(2,1)S(1)}, u32[]{:S(2)}, u32[]{:S(2)}) %collective-permute-start.12) | collective-permute-done | bytes 122912 | tf_op jit(solution)/shard_map/ppermute | solution.py:556
  63.9 1.7 %collective-permute-start.13 = (bf16[30,16,128]{2,1,0:T(8,128)(2,1)S(1)}, bf16[30,16,128]{2,1,0:T(8,128)(2,1)S(1)}, u32[]{:S(2)}, u32[]{:S(2)}) collective-permute-start(bf16[30,16,128]{2,1,0:T(8,128)(2,1)S(1)} %get-tuple-element.73), channel_id=1, source_target_pairs={{0,24},{1,25},{2,28},{3,29},{4,30},{5,31},{6,26},{7,27},{8,0},{9,1... | collective-permute-start | bytes 368648 | tf_op jit(solution)/shard_map/ppermute | solution.py:556
  65.6 0.0 collective-permute-start.14
  65.6 6.4 %collective-permute-done.13.up_low_ref = bf16[30,16,128]{2,1,0:T(8,128)(2,1)S(1)} collective-permute-done((bf16[30,16,128]{2,1,0:T(8,128)(2,1)S(1)}, bf16[30,16,128]{2,1,0:T(8,128)(2,1)S(1)}, u32[]{:S(2)}, u32[]{:S(2)}) %collective-permute-start.13) | collective-permute-done | bytes 122912 | tf_op jit(solution)/shard_map/ppermute | solution.py:556
  72.0 0.0 collective-permute-done.14.up_high_ref
  72.0 3.0 %backward.5 = (f32[8,128]{1,0:T(8,128)S(1)}, f32[8,128]{1,0:T(8,128)S(1)}, f32[8,128]{1,0:T(8,128)S(1)}, f32[8,128]{1,0:T(8,128)S(1)}) custom-call(bf16[30,16,128]{2,1,0:T(8,128)(2,1)S(1)} %collective-permute-done.13.up_low_ref, bf16[30,16,128]{2,1,0:T(8,128)(2,1)S(1)} %collective-permute-done.14.up_high_ref, f32[1,128]{1,0:T(1,128)S(1)} %copy-done, ...), custom_call_target="tpu_custom_call" | custom-call | tf_op jit(solution)/shard_map/backward/pallas_call | solution.py:508
  75.0 0.0 collective-permute-start.15
  75.0 0.0 collective-permute-start.16
  75.0 4.3 %collective-permute-start.17 = (f32[8,128]{1,0:T(8,128)S(1)}, f32[8,128]{1,0:T(8,128)S(1)}, u32[]{:S(2)}, u32[]{:S(2)}) collective-permute-start(f32[8,128]{1,0:T(8,128)S(1)} %get-tuple-element.85), channel_id=1, source_target_pairs={{0,7},{1,2},{2,1},{3,4},{4,3},{5,6},{6,5},{7,0},{8,15},{9,10},{10,... | collective-permute-start | bytes 12296 | tf_op jit(solution)/shard_map/ppermute | solution.py:547
  79.3 0.0 collective-permute-done.15.theirs_ref
  79.3 1.1 %collective-permute-done.16.straight_ref = f32[8,128]{1,0:T(8,128)S(1)} collective-permute-done((f32[8,128]{1,0:T(8,128)S(1)}, f32[8,128]{1,0:T(8,128)S(1)}, u32[]{:S(2)}, u32[]{:S(2)}) %collective-permute-start.16) | collective-permute-done | bytes 4128 | tf_op jit(solution)/shard_map/ppermute | solution.py:547
  80.4 0.2 collective-permute-done.17.cross_ref
  80.7 2.5 %collective-permute-start.20 = (f32[16,128]{1,0:T(8,128)S(1)}, f32[16,128]{1,0:T(8,128)S(1)}, u32[]{:S(2)}, u32[]{:S(2)}) collective-permute-start(f32[16,128]{1,0:T(8,128)S(1)} %join.1.refs_0_), channel_id=1, source_target_pairs={{0,24},{8,0},{16,8},{24,16},{1,25},{9,1},{17,9},{25,17},{2,26},{10... | collective-permute-start | bytes 24584 | tf_op jit(solution)/shard_map/ppermute | solution.py:616
  83.2 0.0 collective-permute-start.19
  83.2 0.6 collective-permute-start.18
  83.8 0.7 collective-permute-done.20.refs_3_
  84.5 2.3 %collective-permute-done.19.refs_2_ = f32[16,128]{1,0:T(8,128)S(1)} collective-permute-done((f32[16,128]{1,0:T(8,128)S(1)}, f32[16,128]{1,0:T(8,128)S(1)}, u32[]{:S(2)}, u32[]{:S(2)}) %collective-permute-start.19) | collective-permute-done | bytes 8224 | tf_op jit(solution)/shard_map/ppermute | solution.py:616
  86.8 0.9 %collective-permute-done.18.refs_1_ = f32[16,128]{1,0:T(8,128)S(1)} collective-permute-done((f32[16,128]{1,0:T(8,128)S(1)}, f32[16,128]{1,0:T(8,128)S(1)}, u32[]{:S(2)}, u32[]{:S(2)}) %collective-permute-start.18) | collective-permute-done | bytes 8224 | tf_op jit(solution)/shard_map/ppermute | solution.py:616
  87.7 0.7 close.1
  (10 shorter events, 0.0 us)
Async XLA Ops:
  1.9 7.8 %collective-permute-start.1 = (bf16[30,8,128]{2,1,0:T(8,128)(2,1)S(1)}, bf16[30,8,128]{2,1,0:T(8,128)(2,1)S(1)}, u32[]{:S(2)}, u32[]{:S(2)}) collective-permute-start(bf16[30,8,128]{2,1,0:T(8,128)(2,1)S(1)} %get-tuple-element.45.mine_ref), channel_id=1, source_target_pairs={{0,6},{1,3},{2,0},{3,5},{4,2},{5,7},{6,4},{7,1},{8,14},{9,11},{10,... | collective-permute-start | bytes 184328 | tf_op jit(solution)/shard_map/ppermute | solution.py:547
  7.0 5.4 %collective-permute-start.2 = (bf16[30,8,128]{2,1,0:T(8,128)(2,1)S(1)}, bf16[30,8,128]{2,1,0:T(8,128)(2,1)S(1)}, u32[]{:S(2)}, u32[]{:S(2)}) collective-permute-start(bf16[30,8,128]{2,1,0:T(8,128)(2,1)S(1)} %get-tuple-element.46), channel_id=1, source_target_pairs={{0,7},{1,2},{2,1},{3,4},{4,3},{5,6},{6,5},{7,0},{8,15},{9,10},{10,... | collective-permute-start | bytes 184328 | tf_op jit(solution)/shard_map/ppermute | solution.py:547
  7.0 5.4 %collective-permute-start = (bf16[30,8,128]{2,1,0:T(8,128)(2,1)S(1)}, bf16[30,8,128]{2,1,0:T(8,128)(2,1)S(1)}, u32[]{:S(2)}, u32[]{:S(2)}) collective-permute-start(bf16[30,8,128]{2,1,0:T(8,128)(2,1)S(1)} %get-tuple-element.46), channel_id=1, source_target_pairs={{0,1},{1,0},{2,3},{3,2},{4,5},{5,4},{6,7},{7,6},{8,9},{9,8},{10,11... | collective-permute-start | bytes 184328 | tf_op jit(solution)/shard_map/ppermute | solution.py:547
  7.0 5.5 %copy-start = (f32[1,128]{1,0:T(1,128)S(1)}, f32[1,128]{1,0:T(1,128)}, u32[]{:S(2)}) copy-start(f32[1,128]{1,0:T(1,128)} %rate_ref.13) | copy-start | bytes 1540
  14.8 9.0 %collective-permute-start.4 = (bf16[30,16,128]{2,1,0:T(8,128)(2,1)S(1)}, bf16[30,16,128]{2,1,0:T(8,128)(2,1)S(1)}, u32[]{:S(2)}, u32[]{:S(2)}) collective-permute-start(bf16[30,16,128]{2,1,0:T(8,128)(2,1)S(1)} %get-tuple-element.52), channel_id=1, source_target_pairs={{0,10},{1,11},{2,8},{3,9},{4,12},{5,13},{6,14},{7,15},{8,18},{9,19... | collective-permute-start | bytes 368648 | tf_op jit(solution)/shard_map/ppermute | solution.py:556
  14.9 9.3 %collective-permute-start.3 = (bf16[30,16,128]{2,1,0:T(8,128)(2,1)S(1)}, bf16[30,16,128]{2,1,0:T(8,128)(2,1)S(1)}, u32[]{:S(2)}, u32[]{:S(2)}) collective-permute-start(bf16[30,16,128]{2,1,0:T(8,128)(2,1)S(1)} %get-tuple-element.52), channel_id=1, source_target_pairs={{0,8},{1,9},{2,12},{3,13},{4,14},{5,15},{6,10},{7,11},{8,16},{9,17... | collective-permute-start | bytes 368648 | tf_op jit(solution)/shard_map/ppermute | solution.py:556
  24.1 17.9 %copy-start.1 = (f32[128]{0:T(128)S(1)}, f32[128]{0:T(128)}, u32[]{:S(2)}) copy-start(f32[128]{0:T(128)} %param.20) | copy-start | bytes 1540
  24.2 8.4 %collective-permute-start.6 = (bf16[30,16,128]{2,1,0:T(8,128)(2,1)S(1)}, bf16[30,16,128]{2,1,0:T(8,128)(2,1)S(1)}, u32[]{:S(2)}, u32[]{:S(2)}) collective-permute-start(bf16[30,16,128]{2,1,0:T(8,128)(2,1)S(1)} %get-tuple-element.53), channel_id=1, source_target_pairs={{0,8},{1,9},{2,12},{3,13},{4,14},{5,15},{6,10},{7,11},{8,16},{9,17... | collective-permute-start | bytes 368648 | tf_op jit(solution)/shard_map/ppermute | solution.py:556
  24.2 8.4 %collective-permute-start.5 = (bf16[30,16,128]{2,1,0:T(8,128)(2,1)S(1)}, bf16[30,16,128]{2,1,0:T(8,128)(2,1)S(1)}, u32[]{:S(2)}, u32[]{:S(2)}) collective-permute-start(bf16[30,16,128]{2,1,0:T(8,128)(2,1)S(1)} %get-tuple-element.53), channel_id=1, source_target_pairs={{0,12},{1,13},{2,14},{3,15},{4,10},{5,11},{6,8},{7,9},{8,20},{9,21... | collective-permute-start | bytes 368648 | tf_op jit(solution)/shard_map/ppermute | solution.py:556
  32.6 9.4 %collective-permute-start.8 = (bf16[30,16,128]{2,1,0:T(8,128)(2,1)S(1)}, bf16[30,16,128]{2,1,0:T(8,128)(2,1)S(1)}, u32[]{:S(2)}, u32[]{:S(2)}) collective-permute-start(bf16[30,16,128]{2,1,0:T(8,128)(2,1)S(1)} %get-tuple-element.54), channel_id=1, source_target_pairs={{0,10},{1,11},{2,8},{3,9},{4,12},{5,13},{6,14},{7,15},{8,18},{9,19... | collective-permute-start | bytes 368648 | tf_op jit(solution)/shard_map/ppermute | solution.py:556
  35.2 6.8 %collective-permute-start.7 = (bf16[30,16,128]{2,1,0:T(8,128)(2,1)S(1)}, bf16[30,16,128]{2,1,0:T(8,128)(2,1)S(1)}, u32[]{:S(2)}, u32[]{:S(2)}) collective-permute-start(bf16[30,16,128]{2,1,0:T(8,128)(2,1)S(1)} %get-tuple-element.54), channel_id=1, source_target_pairs={{0,8},{1,9},{2,12},{3,13},{4,14},{5,15},{6,10},{7,11},{8,16},{9,17... | collective-permute-start | bytes 368648 | tf_op jit(solution)/shard_map/ppermute | solution.py:556
  42.0 7.6 %collective-permute-start.9 = (bf16[30,16,128]{2,1,0:T(8,128)(2,1)S(1)}, bf16[30,16,128]{2,1,0:T(8,128)(2,1)S(1)}, u32[]{:S(2)}, u32[]{:S(2)}) collective-permute-start(bf16[30,16,128]{2,1,0:T(8,128)(2,1)S(1)} %get-tuple-element.55), channel_id=1, source_target_pairs={{0,24},{1,25},{2,28},{3,29},{4,30},{5,31},{6,26},{7,27},{8,0},{9,1... | collective-permute-start | bytes 368648 | tf_op jit(solution)/shard_map/ppermute | solution.py:556
  47.1 5.8 %collective-permute-start.10 = (bf16[30,16,128]{2,1,0:T(8,128)(2,1)S(1)}, bf16[30,16,128]{2,1,0:T(8,128)(2,1)S(1)}, u32[]{:S(2)}, u32[]{:S(2)}) collective-permute-start(bf16[30,16,128]{2,1,0:T(8,128)(2,1)S(1)} %get-tuple-element.56), channel_id=1, source_target_pairs={{0,28},{1,29},{2,30},{3,31},{4,26},{5,27},{6,24},{7,25},{8,2},{9,3... | collective-permute-start | bytes 368648 | tf_op jit(solution)/shard_map/ppermute | solution.py:556
  52.9 9.1 %collective-permute-start.11 = (bf16[30,16,128]{2,1,0:T(8,128)(2,1)S(1)}, bf16[30,16,128]{2,1,0:T(8,128)(2,1)S(1)}, u32[]{:S(2)}, u32[]{:S(2)}) collective-permute-start(bf16[30,16,128]{2,1,0:T(8,128)(2,1)S(1)} %get-tuple-element.64), channel_id=1, source_target_pairs={{0,26},{1,27},{2,24},{3,25},{4,28},{5,29},{6,30},{7,31},{8,6},{9,7... | collective-permute-start | bytes 368648 | tf_op jit(solution)/shard_map/ppermute | solution.py:556
  59.0 4.9 %collective-permute-start.12 = (bf16[30,16,128]{2,1,0:T(8,128)(2,1)S(1)}, bf16[30,16,128]{2,1,0:T(8,128)(2,1)S(1)}, u32[]{:S(2)}, u32[]{:S(2)}) collective-permute-start(bf16[30,16,128]{2,1,0:T(8,128)(2,1)S(1)} %get-tuple-element.65), channel_id=1, source_target_pairs={{0,24},{1,25},{2,28},{3,29},{4,30},{5,31},{6,26},{7,27},{8,0},{9,1... | collective-permute-start | bytes 368648 | tf_op jit(solution)/shard_map/ppermute | solution.py:556
  63.9 8.1 %collective-permute-start.13 = (bf16[30,16,128]{2,1,0:T(8,128)(2,1)S(1)}, bf16[30,16,128]{2,1,0:T(8,128)(2,1)S(1)}, u32[]{:S(2)}, u32[]{:S(2)}) collective-permute-start(bf16[30,16,128]{2,1,0:T(8,128)(2,1)S(1)} %get-tuple-element.73), channel_id=1, source_target_pairs={{0,24},{1,25},{2,28},{3,29},{4,30},{5,31},{6,26},{7,27},{8,0},{9,1... | collective-permute-start | bytes 368648 | tf_op jit(solution)/shard_map/ppermute | solution.py:556
  65.6 6.4 %collective-permute-start.14 = (bf16[30,16,128]{2,1,0:T(8,128)(2,1)S(1)}, bf16[30,16,128]{2,1,0:T(8,128)(2,1)S(1)}, u32[]{:S(2)}, u32[]{:S(2)}) collective-permute-start(bf16[30,16,128]{2,1,0:T(8,128)(2,1)S(1)} %get-tuple-element.74), channel_id=1, source_target_pairs={{0,28},{1,29},{2,30},{3,31},{4,26},{5,27},{6,24},{7,25},{8,2},{9,3... | collective-permute-start | bytes 368648 | tf_op jit(solution)/shard_map/ppermute | solution.py:556
  75.0 4.3 %collective-permute-start.15 = (f32[8,128]{1,0:T(8,128)S(1)}, f32[8,128]{1,0:T(8,128)S(1)}, u32[]{:S(2)}, u32[]{:S(2)}) collective-permute-start(f32[8,128]{1,0:T(8,128)S(1)} %get-tuple-element.83), channel_id=1, source_target_pairs={{0,1},{1,0},{2,3},{3,2},{4,5},{5,4},{6,7},{7,6},{8,9},{9,8},{10,11... | collective-permute-start | bytes 12296 | tf_op jit(solution)/shard_map/ppermute | solution.py:547
  75.0 5.4 %collective-permute-start.16 = (f32[8,128]{1,0:T(8,128)S(1)}, f32[8,128]{1,0:T(8,128)S(1)}, u32[]{:S(2)}, u32[]{:S(2)}) collective-permute-start(f32[8,128]{1,0:T(8,128)S(1)} %get-tuple-element.84), channel_id=1, source_target_pairs={{0,2},{1,7},{2,4},{3,1},{4,6},{5,3},{6,0},{7,5},{8,10},{9,15},{10,... | collective-permute-start | bytes 12296 | tf_op jit(solution)/shard_map/ppermute | solution.py:547
  75.0 5.6 %collective-permute-start.17 = (f32[8,128]{1,0:T(8,128)S(1)}, f32[8,128]{1,0:T(8,128)S(1)}, u32[]{:S(2)}, u32[]{:S(2)}) collective-permute-start(f32[8,128]{1,0:T(8,128)S(1)} %get-tuple-element.85), channel_id=1, source_target_pairs={{0,7},{1,2},{2,1},{3,4},{4,3},{5,6},{6,5},{7,0},{8,15},{9,10},{10,... | collective-permute-start | bytes 12296 | tf_op jit(solution)/shard_map/ppermute | solution.py:547
  80.7 3.9 %collective-permute-start.20 = (f32[16,128]{1,0:T(8,128)S(1)}, f32[16,128]{1,0:T(8,128)S(1)}, u32[]{:S(2)}, u32[]{:S(2)}) collective-permute-start(f32[16,128]{1,0:T(8,128)S(1)} %join.1.refs_0_), channel_id=1, source_target_pairs={{0,24},{8,0},{16,8},{24,16},{1,25},{9,1},{17,9},{25,17},{2,26},{10... | collective-permute-start | bytes 24584 | tf_op jit(solution)/shard_map/ppermute | solution.py:616
  83.2 3.7 %collective-permute-start.19 = (f32[16,128]{1,0:T(8,128)S(1)}, f32[16,128]{1,0:T(8,128)S(1)}, u32[]{:S(2)}, u32[]{:S(2)}) collective-permute-start(f32[16,128]{1,0:T(8,128)S(1)} %join.1.refs_0_), channel_id=1, source_target_pairs={{0,16},{8,24},{16,0},{24,8},{1,17},{9,25},{17,1},{25,9},{2,18},{10... | collective-permute-start | bytes 24584 | tf_op jit(solution)/shard_map/ppermute | solution.py:616
  83.2 4.5 %collective-permute-start.18 = (f32[16,128]{1,0:T(8,128)S(1)}, f32[16,128]{1,0:T(8,128)S(1)}, u32[]{:S(2)}, u32[]{:S(2)}) collective-permute-start(f32[16,128]{1,0:T(8,128)S(1)} %join.1.refs_0_), channel_id=1, source_target_pairs={{0,8},{8,16},{16,24},{24,0},{1,9},{9,17},{17,25},{25,1},{2,10},{10... | collective-permute-start | bytes 24584 | tf_op jit(solution)/shard_map/ppermute | solution.py:616

commit v12 on v9

--- a/solution.py
+++ b/solution.py
@@ -100,19 +100,21 @@
     return geo_ref[which * edges : (which + 1) * edges, :]
 
 
-def forward(refs, hot_ref, geo_ref, zero_ref, one_ref, two_ref, sz, rows, last):
+def forward(refs, hot_ref, geo_ref, faded_ref, zero_ref, one_ref, two_ref, sz, rows, last):
     hot = hot_ref[...]
     edges = hot.shape[0]
     factor = (edges // rows) ** (-0.5)
     radial = geo_at(geo_ref, 0, edges)
 
-    def scaled(block):
-        return (block * radial).astype(BF16).astype(F32)
+    def scaled(block, k):
+        faded = block * radial
+        faded_ref[k] = faded
+        return faded.astype(BF16).astype(F32)
 
     pooled = [None] * sz.coefs
     group = picked_group(refs, hot, 0, sz.zero)
     zin = jnp.concatenate(
-        [pool(scaled(group[:, sz.cols(k)]), rows) for k in range(sz.zero)], axis=1
+        [pool(scaled(group[:, sz.cols(k)], k), rows) for k in range(sz.zero)], axis=1
     )
     kept = 1 if last else sz.zero
     (zout,) = fine_dot(zin, [zero_ref[:, sz.cols(0, kept)]], dot)
@@ -126,8 +128,8 @@
         group = picked_group(refs, hot, first, 2 * count)
         res, ims = [], []
         for k in range(count):
-            re = scaled(group[:, sz.cols(k)])
-            im = scaled(group[:, sz.cols(count + k)])
+            re = scaled(group[:, sz.cols(k)], first + k)
+            im = scaled(group[:, sz.cols(count + k)], first + count + k)
             res.append(pool(cos * re - sin * im, rows))
             ims.append(pool(sin * re + cos * im, rows))
         both = jnp.concatenate(
@@ -150,11 +152,10 @@
 
 
 def backward(
-    upstream, pooled, refs, hot_ref, hot_t_ref, geo_ref, zero_ref, one_ref, two_ref, sz, rows, last, outs
+    upstream, pooled, hot_t_ref, geo_ref, faded_ref, zero_ref, one_ref, two_ref, sz, rows, last, outs
 ):
-    hot = hot_ref[...]
     hot_t = hot_t_ref[...]
-    edges = hot.shape[0]
+    edges = hot_t.shape[1]
     slab = rows // 2
     factor = (edges // rows) ** (-0.5)
     signal = signal_of(pooled, sz)
@@ -186,8 +187,7 @@
     def scatter(first, blocks):
         if outs is None:
             return
-        high, low = split(jnp.concatenate(blocks, axis=1))
-        back = dot(hot_t, high) + dot(hot_t, low)
+        back = dot(hot_t, jnp.concatenate([block.astype(BF16) for block in blocks], axis=1))
         for n in range(len(blocks)):
             k = first + n
             part = back[:, sz.cols(n)]
@@ -197,13 +197,12 @@
             outs[1][k] = part[rows:].astype(BF16)
 
     q_len = jnp.zeros((edges, sz.c), F32)
-    group = picked_group(refs, hot, 0, sz.zero)
     blocks = []
     for k in range(sz.zero):
         grad = spread(dz[:, sz.cols(k)])
-        q_len = q_len + grad * group[:, sz.cols(k)]
-        blocks.append(grad * radial)
-    q_len = q_len * radial
+        q_len = q_len + grad * faded_ref[k]
+        if outs is not None:
+            blocks.append(grad * radial)
     scatter(0, blocks)
     q_turn = []
     for order in range(2):
@@ -221,15 +220,14 @@
         a, b = fine_dot(both, [weight_ref[0], weight_ref[1]], dot_t)
         d_re = a[:rows] + b[rows:]
         d_im = a[rows:] - b[:rows]
-        group = picked_group(refs, hot, first, 2 * count)
         q_cos = jnp.zeros((edges, sz.c), F32)
         q_sin = jnp.zeros((edges, sz.c), F32)
         cos_r = cos * radial
         sin_r = sin * radial
         blocks_re, blocks_im = [], []
         for k in range(count):
-            re = group[:, sz.cols(k)]
-            im = group[:, sz.cols(count + k)]
+            re = faded_ref[first + k]
+            im = faded_ref[first + count + k]
             g_re = spread(d_re[:, sz.cols(k)])
             g_im = spread(d_im[:, sz.cols(k)])
             q_cos = q_cos + (re * g_re + im * g_im)
@@ -238,8 +236,6 @@
                 blocks_re.append(cos_r * g_re + sin_r * g_im)
                 blocks_im.append(cos_r * g_im - sin_r * g_re)
         scatter(first, blocks_re + blocks_im)
-        q_cos = q_cos * radial
-        q_sin = q_sin * radial
         q_len = q_len + cos * q_cos + sin * q_sin
         q_turn.append((q_cos, q_sin))
 
@@ -446,36 +442,27 @@
     return numbers[per_slab : per_slab + rows]
 
 
-def turn_to_stage():
-    odd = lax.rem(lax.axis_index("space"), 2)
-    return jnp.where(lax.axis_index("segment") == 0, odd, 0)
-
-
-def stage_kernel(moment, zero_hbm, one_hbm, two_hbm, *more):
-    zero_ref, one_ref, two_ref, sems = more[-4:]
-
-    @pl.when(turn_to_stage() == moment)
-    def _():
-        pairs = [(zero_hbm, zero_ref)]
-        for source, target in ((one_hbm, one_ref), (two_hbm, two_ref)):
-            pairs += [(source.at[n], target.at[n]) for n in range(2)]
-        copies = [pltpu.make_async_copy(source, target, sems.at[n]) for n, (source, target) in enumerate(pairs)]
-        for copy in copies:
-            copy.start()
-        for copy in copies:
-            copy.wait()
+def stage_kernel(zero_hbm, one_hbm, two_hbm, zero_ref, one_ref, two_ref, sems):
+    pairs = [(zero_hbm, zero_ref)]
+    for source, target in ((one_hbm, one_ref), (two_hbm, two_ref)):
+        pairs += [(source.at[n], target.at[n]) for n in range(2)]
+    copies = [pltpu.make_async_copy(source, target, sems.at[n]) for n, (source, target) in enumerate(pairs)]
+    for copy in copies:
+        copy.start()
+    for copy in copies:
+        copy.wait()
 
 
 def forward_kernel(
     tick, sz, slabs, neighbours, low_ref, high_ref, rate_ref, zero_ref, one_ref, two_ref,
-    out_ref, pooled_ref, hot_ref, hot_t_ref, geo_ref
+    out_ref, pooled_ref, hot_t_ref, geo_ref, faded_ref, hot_ref
 ):
     @pl.when(lax.axis_index("segment") == tick)
     def _():
         rows = low_ref.shape[1]
         refs = (low_ref, high_ref)
         edges_of(refs, sz.coefs, slabs, neighbours, rate_ref, hot_ref, hot_t_ref, geo_ref)
-        pooled = forward(refs, hot_ref, geo_ref, zero_ref, one_ref, two_ref, sz, rows, False)
+        pooled = forward(refs, hot_ref, geo_ref, faded_ref, zero_ref, one_ref, two_ref, sz, rows, False)
         signal = signal_of(pooled, sz)
         gate, lifted = silu_parts(signal)
         for k in range(sz.coefs):
@@ -487,7 +474,7 @@
 
 def turn_kernel(
     tick, sz, slabs, neighbours, low_ref, high_ref, rate_ref, zero_ref, one_ref, two_ref, read_ref,
-    back_low_ref, back_high_ref, hot_ref, hot_t_ref, geo_ref
+    back_low_ref, back_high_ref, hot_ref, hot_t_ref, geo_ref, faded_ref
 ):
     @pl.when(lax.axis_index("segment") == tick)
     def _():
@@ -495,7 +482,7 @@
         refs = (low_ref, high_ref)
         outs = (back_low_ref, back_high_ref)
         own = edges_of(refs, sz.coefs, slabs, neighbours, rate_ref, hot_ref, hot_t_ref, geo_ref)
-        pooled = forward(refs, hot_ref, geo_ref, zero_ref, one_ref, two_ref, sz, rows, True)
+        pooled = forward(refs, hot_ref, geo_ref, faded_ref, zero_ref, one_ref, two_ref, sz, rows, True)
         signal = signal_of(pooled, sz)
         _, lifted = silu_parts(signal)
         updated = own_rows(refs, 0) + lifted
@@ -506,23 +493,21 @@
         energy = around(jnp.where(lane == 3, energy, 0.0), rows // 2)
         upstream = [own[:, 3:4] * read * (gate + updated * gate * (1.0 - gate))]
         moved = backward(
-            upstream, pooled, refs, hot_ref, hot_t_ref, geo_ref, zero_ref, one_ref, two_ref, sz, rows, True, outs
+            upstream, pooled, hot_t_ref, geo_ref, faded_ref, zero_ref, one_ref, two_ref, sz, rows, True, outs
         )
         send_back(moved + energy, outs, sz)
 
 
 def backward_kernel(
-    tick, sz, up_low_ref, up_high_ref, pooled_ref, low_ref, high_ref, hot_ref, hot_t_ref, geo_ref,
-    zero_ref, one_ref, two_ref, *outs
+    tick, sz, up_low_ref, up_high_ref, pooled_ref, hot_t_ref, geo_ref, faded_ref, zero_ref, one_ref, two_ref, *outs
 ):
     @pl.when(lax.axis_index("segment") == tick)
     def _():
-        rows = low_ref.shape[1]
-        refs = (low_ref, high_ref)
+        rows = up_low_ref.shape[1]
         upstream = [up_low_ref[k].astype(F32) + up_high_ref[k].astype(F32) for k in range(sz.coefs)]
         pooled = [pooled_ref[k] for k in range(sz.coefs)]
         moved = backward(
-            upstream, pooled, refs, hot_ref, hot_t_ref, geo_ref, zero_ref, one_ref, two_ref, sz, rows, False,
+            upstream, pooled, hot_t_ref, geo_ref, faded_ref, zero_ref, one_ref, two_ref, sz, rows, False,
             outs if tick else None,
         )
         carried = decode(up_low_ref[sz.coefs].astype(F32)) + decode(up_high_ref[sz.coefs].astype(F32))
@@ -533,7 +518,7 @@
             share(moved, outs)
 
 
-def call(body, operands, shapes, name, spaces=None, scratch=(), aliases=None):
+def call(body, operands, shapes, name, spaces=None, scratch=()):
     spaces = spaces or [pltpu.VMEM] * len(operands)
     operands = [pltpu.with_memory_space_constraint(value, space) for value, space in zip(operands, spaces)]
     return pl.pallas_call(
@@ -542,7 +527,6 @@
         in_specs=[pl.BlockSpec(memory_space=space) for space in spaces],
         out_specs=[pl.BlockSpec(memory_space=pltpu.VMEM) for _ in shapes],
         scratch_shapes=list(scratch),
-        input_output_aliases=aliases or {},
         compiler_params=pltpu.CompilerParams(vmem_limit_bytes=VMEM_LIMIT),
         name=name,
     )(*operands)
@@ -602,23 +586,21 @@
     spaces = [pltpu.HBM] * 3
     on_chip = [pltpu.VMEM(w.shape, w.dtype) for w in stored]
     sems = [pltpu.SemaphoreType.DMA((5,))]
-    weights = call(functools.partial(stage_kernel, 0), stored, on_chip, "stage", spaces, sems)
+    weights = call(stage_kernel, stored, on_chip, "stage", spaces, sems)
     whole = shape((coefs + 1, rows, channels), BF16)
     around_all = [call(open_kernel, [mine, partner, straight, cross], [whole, whole], "open")]
-    weights = call(
-        functools.partial(stage_kernel, 1), [*stored, *weights, around_all[0][0]], on_chip, "stage",
-        spaces + [pltpu.VMEM] * 4, sems, {3: 0, 4: 1, 5: 2},
-    )
-    edge_shapes = [
-        shape((edges, 2 * rows), BF16), shape((2 * rows, edges), BF16), shape((10 * edges, channels), F32),
+    kept_shapes = [
+        shape((2 * rows, edges), BF16), shape((10 * edges, channels), F32), shape((coefs, edges, channels), F32),
     ]
+    hot = [pltpu.VMEM((edges, 2 * rows), BF16)]
     kept = []
     for tick in range(segments - 1):
         out, *residuals = call(
             functools.partial(forward_kernel, tick, sz, slabs, neighbours),
             [*around_all[tick], radial_rate, *weights],
-            [whole, shape((coefs, rows, channels), F32), *edge_shapes],
+            [whole, shape((coefs, rows, channels), F32), *kept_shapes],
             "forward",
+            scratch=hot,
         )
         kept.append(residuals)
         ways = (1, 0) if tick % 2 else (0, -1)
@@ -630,7 +612,7 @@
         [*around_all[final], radial_rate, *weights, read_weight.reshape(1, channels)],
         [whole, whole],
         "turn",
-        scratch=[pltpu.VMEM(v.shape, v.dtype) for v in edge_shapes],
+        scratch=hot + [pltpu.VMEM(v.shape, v.dtype) for v in kept_shapes],
     )
     for tick in reversed(range(segments - 1)):
         ways = (1, 0) if tick % 2 else (0, -1)
@@ -638,7 +620,7 @@
         pooled, *residuals = kept[tick]
         parts = call(
             functools.partial(backward_kernel, tick, sz),
-            [*up, pooled, *around_all[tick], *residuals, *weights],
+            [*up, pooled, *residuals, *weights],
             [whole, whole] if tick else [slab_sums] * 4,
             "backward",
         )

time: 91.1 us -> 88.8 us (0.975)
  starting transfers between devices: 31.8 us -> 30 us
    ppermute x12, starting transfers between devices: 18.4 us -> 16.9 us  [hop(): return lax.ppermute(value, axes, ways)]
    pallas_call x13 -> x12, Pallas kernels: 8.94 us -> 8.66 us  [call(): pl.pallas_call(body, out_shape=shapes, in_specs=[pl.BlockSpec(memory_spac...]
  transfers between devices with their start and end apart: 21 -> 21, of which waited for: 16 -> 15; matrix products, arithmetic and copies ran while one was open for 0% -> 0% of each run, Pallas kernels for 3% -> 3%
where the time goes in v12:
time: 88.8 us; the launch traced here: 88.6 us
  waiting for transfers between devices  49.2 us (55%)
  starting transfers between devices  30 us (34%)
  Pallas kernels  8.66 us (10%)
    ppermute x12, waiting for transfers between devices, hop(): return lax.ppermute(value, axes, ways)  40.4 us
    ppermute x12, starting transfers between devices, hop(): return lax.ppermute(value, axes, ways)  16.9 us
    ppermute x6, starting transfers between devices, within(): return lax.ppermute(value, axes, ways)  9.08 us
    pallas_call x12, Pallas kernels, call(): pl.pallas_call(body, out_shape=shapes, in_specs=[pl.BlockSpec(memory_spac...  8.66 us
    ppermute x3, waiting for transfers between devices, on_device(): lax.ppermute(both, 'segment', [(s, (s + stop) % segments) for s in range(...  4.55 us
    ppermute x6, waiting for transfers between devices, within(): return lax.ppermute(value, axes, ways)  4.26 us
    ppermute x3, starting transfers between devices, on_device(): lax.ppermute(both, 'segment', [(s, (s + stop) % segments) for s in range(...  4.05 us
  transfers between devices with their start and end apart: 21, of which 15 were waited for; matrix products, arithmetic and copies ran while one was open for 0% of the time, Pallas kernels for 3%

profile of v12, /device:TPU:0, one launch (start us, length us, event | category | flops | bytes accessed | tf_op | source)
XLA Modules:
  0.0 88.6 jit_solution(16075178054937789166)
XLA Ops:
  0.6 1.2 %pack.1 = (bf16[30,8,128]{2,1,0:T(8,128)(2,1)S(1)}, bf16[30,8,128]{2,1,0:T(8,128)(2,1)S(1)}) custom-call(bf16[2,29,8,128]{3,2,1,0:T(8,128)(2,1)} %bitcast.11, f32[3,2,8]{2,1,0:T(2,128)} %bitcast.12, s32[2,8]{1,0:T(2,128)} %species_hbm.1, s32[2,8,8]{2,1,0:T(8,128)} %sources_hbm.1, f32[2,8]{1,0:T(2,128)} %grad_hbm.1, bf16[100,128]{1,0:T(8,128)(2,1)} %table_hbm.1), custom_call_target="tpu_custom_call" | custom-call | tf_op jit(solution)/shard_map/pack/pallas_call | solution.py:524
  1.9 5.1 %collective-permute-start.1 = (bf16[30,8,128]{2,1,0:T(8,128)(2,1)S(1)}, bf16[30,8,128]{2,1,0:T(8,128)(2,1)S(1)}, u32[]{:S(2)}, u32[]{:S(2)}) collective-permute-start(bf16[30,8,128]{2,1,0:T(8,128)(2,1)S(1)} %get-tuple-element.36.mine_ref), channel_id=1, source_target_pairs={{0,6},{1,3},{2,0},{3,5},{4,2},{5,7},{6,4},{7,1},{8,14},{9,11},{10,... | collective-permute-start | bytes 184328 | tf_op jit(solution)/shard_map/ppermute | solution.py:563
  7.0 0.0 collective-permute-start.2
  7.0 0.0 collective-permute-start
  7.0 2.6 %stage.1 = (bf16[896,896]{1,0:T(8,128)(2,1)S(1)}, bf16[2,768,768]{2,1,0:T(8,128)(2,1)S(1)}, bf16[2,640,640]{2,1,0:T(8,128)(2,1)S(1)}) custom-call(bf16[896,896]{1,0:T(8,128)(2,1)} %bitcast.10, bf16[2,768,768]{2,1,0:T(8,128)(2,1)} %bitcast.8, bf16[2,640,640]{2,1,0:T(8,128)(2,1)} %bitcast.9), custom_call_target="tpu_custom_call" | custom-call | tf_op jit(solution)/shard_map/stage/pallas_call | solution.py:524
  9.6 0.0 collective-permute-done.1.straight_ref
  9.6 2.8 %collective-permute-done.2.cross_ref = bf16[30,8,128]{2,1,0:T(8,128)(2,1)S(1)} collective-permute-done((bf16[30,8,128]{2,1,0:T(8,128)(2,1)S(1)}, bf16[30,8,128]{2,1,0:T(8,128)(2,1)S(1)}, u32[]{:S(2)}, u32[]{:S(2)}) %collective-permute-start.2) | collective-permute-done | bytes 61472 | tf_op jit(solution)/shard_map/ppermute | solution.py:563
  12.4 0.0 collective-permute-done.partner_ref
  12.4 0.1 open.1
  12.5 2.0 %forward.3 = (bf16[30,16,128]{2,1,0:T(8,128)(2,1)S(1)}, f32[29,16,128]{2,1,0:T(8,128)S(1)}, bf16[32,128]{1,0:T(8,128)(2,1)S(1)}, f32[1280,128]{1,0:T(8,128)S(1)}, f32[29,128,128]{2,1,0:T(8,128)S(1)}) custom-call(bf16[30,16,128]{2,1,0:T(8,128)(2,1)S(1)} %get-tuple-element.38.low_ref, bf16[30,16,128]{2,1,0:T(8,128)(2,1)S(1)} %get-tuple-element.39.high_ref, ...), custom_call_target="tpu_custom_call" | custom-call | tf_op jit(solution)/shard_map/forward/pallas_call | solution.py:524
  14.4 0.1 collective-permute-start.4
  14.5 0.1 collective-permute-start.3
  14.6 8.8 %collective-permute-done.4.high_ref = bf16[30,16,128]{2,1,0:T(8,128)(2,1)S(1)} collective-permute-done((bf16[30,16,128]{2,1,0:T(8,128)(2,1)S(1)}, bf16[30,16,128]{2,1,0:T(8,128)(2,1)S(1)}, u32[]{:S(2)}, u32[]{:S(2)}) %collective-permute-start.4) | collective-permute-done | bytes 122912 | tf_op jit(solution)/shard_map/ppermute | solution.py:572
  23.4 0.4 collective-permute-done.3.low_ref
  23.8 0.0 collective-permute-start.6
  23.8 0.2 collective-permute-start.5
  24.0 8.2 %collective-permute-done.6.high_ref = bf16[30,16,128]{2,1,0:T(8,128)(2,1)S(1)} collective-permute-done((bf16[30,16,128]{2,1,0:T(8,128)(2,1)S(1)}, bf16[30,16,128]{2,1,0:T(8,128)(2,1)S(1)}, u32[]{:S(2)}, u32[]{:S(2)}) %collective-permute-start.6) | collective-permute-done | bytes 122912 | tf_op jit(solution)/shard_map/ppermute | solution.py:572
  32.2 0.0 collective-permute-done.5.low_ref
  32.2 2.7 %collective-permute-start.8 = (bf16[30,16,128]{2,1,0:T(8,128)(2,1)S(1)}, bf16[30,16,128]{2,1,0:T(8,128)(2,1)S(1)}, u32[]{:S(2)}, u32[]{:S(2)}) collective-permute-start(bf16[30,16,128]{2,1,0:T(8,128)(2,1)S(1)} %get-tuple-element.45), channel_id=1, source_target_pairs={{0,10},{1,11},{2,8},{3,9},{4,12},{5,13},{6,14},{7,15},{8,18},{9,19... | collective-permute-start | bytes 368648 | tf_op jit(solution)/shard_map/ppermute | solution.py:572
  34.9 0.4 collective-permute-start.7
  35.4 6.3 %collective-permute-done.8.high_ref = bf16[30,16,128]{2,1,0:T(8,128)(2,1)S(1)} collective-permute-done((bf16[30,16,128]{2,1,0:T(8,128)(2,1)S(1)}, bf16[30,16,128]{2,1,0:T(8,128)(2,1)S(1)}, u32[]{:S(2)}, u32[]{:S(2)}) %collective-permute-start.8) | collective-permute-done | bytes 122912 | tf_op jit(solution)/shard_map/ppermute | solution.py:572
  41.7 0.0 collective-permute-done.7.low_ref
  41.7 4.8 %collective-permute-start.9 = (bf16[30,16,128]{2,1,0:T(8,128)(2,1)S(1)}, bf16[30,16,128]{2,1,0:T(8,128)(2,1)S(1)}, u32[]{:S(2)}, u32[]{:S(2)}) collective-permute-start(bf16[30,16,128]{2,1,0:T(8,128)(2,1)S(1)} %get-tuple-element.46), channel_id=1, source_target_pairs={{0,24},{1,25},{2,28},{3,29},{4,30},{5,31},{6,26},{7,27},{8,0},{9,1... | collective-permute-start | bytes 368648 | tf_op jit(solution)/shard_map/ppermute | solution.py:572
  46.5 0.7 collective-permute-start.10
  47.2 1.7 %collective-permute-done.9.up_low_ref = bf16[30,16,128]{2,1,0:T(8,128)(2,1)S(1)} collective-permute-done((bf16[30,16,128]{2,1,0:T(8,128)(2,1)S(1)}, bf16[30,16,128]{2,1,0:T(8,128)(2,1)S(1)}, u32[]{:S(2)}, u32[]{:S(2)}) %collective-permute-start.9) | collective-permute-done | bytes 122912 | tf_op jit(solution)/shard_map/ppermute | solution.py:572
  48.9 3.3 %collective-permute-done.10.up_high_ref = bf16[30,16,128]{2,1,0:T(8,128)(2,1)S(1)} collective-permute-done((bf16[30,16,128]{2,1,0:T(8,128)(2,1)S(1)}, bf16[30,16,128]{2,1,0:T(8,128)(2,1)S(1)}, u32[]{:S(2)}, u32[]{:S(2)}) %collective-permute-start.10) | collective-permute-done | bytes 122912 | tf_op jit(solution)/shard_map/ppermute | solution.py:572
  52.3 6.2 %collective-permute-start.11 = (bf16[30,16,128]{2,1,0:T(8,128)(2,1)S(1)}, bf16[30,16,128]{2,1,0:T(8,128)(2,1)S(1)}, u32[]{:S(2)}, u32[]{:S(2)}) collective-permute-start(bf16[30,16,128]{2,1,0:T(8,128)(2,1)S(1)} %get-tuple-element.52), channel_id=1, source_target_pairs={{0,26},{1,27},{2,24},{3,25},{4,28},{5,29},{6,30},{7,31},{8,6},{9,7... | collective-permute-start | bytes 368648 | tf_op jit(solution)/shard_map/ppermute | solution.py:572
  58.5 0.0 collective-permute-start.12
  58.5 3.0 %collective-permute-done.11.up_low_ref = bf16[30,16,128]{2,1,0:T(8,128)(2,1)S(1)} collective-permute-done((bf16[30,16,128]{2,1,0:T(8,128)(2,1)S(1)}, bf16[30,16,128]{2,1,0:T(8,128)(2,1)S(1)}, u32[]{:S(2)}, u32[]{:S(2)}) %collective-permute-start.11) | collective-permute-done | bytes 122912 | tf_op jit(solution)/shard_map/ppermute | solution.py:572
  61.5 1.9 %collective-permute-done.12.up_high_ref = bf16[30,16,128]{2,1,0:T(8,128)(2,1)S(1)} collective-permute-done((bf16[30,16,128]{2,1,0:T(8,128)(2,1)S(1)}, bf16[30,16,128]{2,1,0:T(8,128)(2,1)S(1)}, u32[]{:S(2)}, u32[]{:S(2)}) %collective-permute-start.12) | collective-permute-done | bytes 122912 | tf_op jit(solution)/shard_map/ppermute | solution.py:572
  63.4 1.7 %collective-permute-start.13 = (bf16[30,16,128]{2,1,0:T(8,128)(2,1)S(1)}, bf16[30,16,128]{2,1,0:T(8,128)(2,1)S(1)}, u32[]{:S(2)}, u32[]{:S(2)}) collective-permute-start(bf16[30,16,128]{2,1,0:T(8,128)(2,1)S(1)} %get-tuple-element.58), channel_id=1, source_target_pairs={{0,24},{1,25},{2,28},{3,29},{4,30},{5,31},{6,26},{7,27},{8,0},{9,1... | collective-permute-start | bytes 368648 | tf_op jit(solution)/shard_map/ppermute | solution.py:572
  65.1 0.0 collective-permute-start.14
  65.1 3.8 %collective-permute-done.13.up_low_ref = bf16[30,16,128]{2,1,0:T(8,128)(2,1)S(1)} collective-permute-done((bf16[30,16,128]{2,1,0:T(8,128)(2,1)S(1)}, bf16[30,16,128]{2,1,0:T(8,128)(2,1)S(1)}, u32[]{:S(2)}, u32[]{:S(2)}) %collective-permute-start.13) | collective-permute-done | bytes 122912 | tf_op jit(solution)/shard_map/ppermute | solution.py:572
  68.9 2.9 %collective-permute-done.14.up_high_ref = bf16[30,16,128]{2,1,0:T(8,128)(2,1)S(1)} collective-permute-done((bf16[30,16,128]{2,1,0:T(8,128)(2,1)S(1)}, bf16[30,16,128]{2,1,0:T(8,128)(2,1)S(1)}, u32[]{:S(2)}, u32[]{:S(2)}) %collective-permute-start.14) | collective-permute-done | bytes 122912 | tf_op jit(solution)/shard_map/ppermute | solution.py:572
  71.8 2.1 %backward.5 = (f32[8,128]{1,0:T(8,128)S(1)}, f32[8,128]{1,0:T(8,128)S(1)}, f32[8,128]{1,0:T(8,128)S(1)}, f32[8,128]{1,0:T(8,128)S(1)}) custom-call(bf16[30,16,128]{2,1,0:T(8,128)(2,1)S(1)} %collective-permute-done.13.up_low_ref, bf16[30,16,128]{2,1,0:T(8,128)(2,1)S(1)} %collective-permute-done.14.up_high_ref, ...), custom_call_target="tpu_custom_call" | custom-call | tf_op jit(solution)/shard_map/backward/pallas_call | solution.py:524
  73.8 0.0 collective-permute-start.15
  73.9 0.1 collective-permute-start.16
  73.9 3.9 %collective-permute-start.17 = (f32[8,128]{1,0:T(8,128)S(1)}, f32[8,128]{1,0:T(8,128)S(1)}, u32[]{:S(2)}, u32[]{:S(2)}) collective-permute-start(f32[8,128]{1,0:T(8,128)S(1)} %get-tuple-element.67), channel_id=1, source_target_pairs={{0,7},{1,2},{2,1},{3,4},{4,3},{5,6},{6,5},{7,0},{8,15},{9,10},{10,... | collective-permute-start | bytes 12296 | tf_op jit(solution)/shard_map/ppermute | solution.py:563
  77.8 0.0 collective-permute-done.15.theirs_ref
  77.8 1.5 %collective-permute-done.16.straight_ref = f32[8,128]{1,0:T(8,128)S(1)} collective-permute-done((f32[8,128]{1,0:T(8,128)S(1)}, f32[8,128]{1,0:T(8,128)S(1)}, u32[]{:S(2)}, u32[]{:S(2)}) %collective-permute-start.16) | collective-permute-done | bytes 4128 | tf_op jit(solution)/shard_map/ppermute | solution.py:563
  79.3 0.0 collective-permute-done.17.cross_ref
  79.3 3.4 %collective-permute-start.20 = (f32[16,128]{1,0:T(8,128)S(1)}, f32[16,128]{1,0:T(8,128)S(1)}, u32[]{:S(2)}, u32[]{:S(2)}) collective-permute-start(f32[16,128]{1,0:T(8,128)S(1)} %join.1.refs_0_), channel_id=1, source_target_pairs={{0,24},{8,0},{16,8},{24,16},{1,25},{9,1},{17,9},{25,17},{2,26},{10... | collective-permute-start | bytes 24584 | tf_op jit(solution)/shard_map/ppermute | solution.py:633
  82.7 0.7 collective-permute-start.19
  83.4 0.0 collective-permute-start.18
  83.4 0.7 collective-permute-done.20.refs_3_
  84.1 2.3 %collective-permute-done.19.refs_2_ = f32[16,128]{1,0:T(8,128)S(1)} collective-permute-done((f32[16,128]{1,0:T(8,128)S(1)}, f32[16,128]{1,0:T(8,128)S(1)}, u32[]{:S(2)}, u32[]{:S(2)}) %collective-permute-start.19) | collective-permute-done | bytes 8224 | tf_op jit(solution)/shard_map/ppermute | solution.py:633
  86.3 1.6 %collective-permute-done.18.refs_1_ = f32[16,128]{1,0:T(8,128)S(1)} collective-permute-done((f32[16,128]{1,0:T(8,128)S(1)}, f32[16,128]{1,0:T(8,128)S(1)}, u32[]{:S(2)}, u32[]{:S(2)}) %collective-permute-start.18) | collective-permute-done | bytes 8224 | tf_op jit(solution)/shard_map/ppermute | solution.py:633
  87.9 0.7 close.1
  (10 shorter events, 0.0 us)
Async XLA Ops:
  1.9 7.8 %collective-permute-start.1 = (bf16[30,8,128]{2,1,0:T(8,128)(2,1)S(1)}, bf16[30,8,128]{2,1,0:T(8,128)(2,1)S(1)}, u32[]{:S(2)}, u32[]{:S(2)}) collective-permute-start(bf16[30,8,128]{2,1,0:T(8,128)(2,1)S(1)} %get-tuple-element.36.mine_ref), channel_id=1, source_target_pairs={{0,6},{1,3},{2,0},{3,5},{4,2},{5,7},{6,4},{7,1},{8,14},{9,11},{10,... | collective-permute-start | bytes 184328 | tf_op jit(solution)/shard_map/ppermute | solution.py:563
  7.0 5.4 %collective-permute-start.2 = (bf16[30,8,128]{2,1,0:T(8,128)(2,1)S(1)}, bf16[30,8,128]{2,1,0:T(8,128)(2,1)S(1)}, u32[]{:S(2)}, u32[]{:S(2)}) collective-permute-start(bf16[30,8,128]{2,1,0:T(8,128)(2,1)S(1)} %get-tuple-element.37), channel_id=1, source_target_pairs={{0,7},{1,2},{2,1},{3,4},{4,3},{5,6},{6,5},{7,0},{8,15},{9,10},{10,... | collective-permute-start | bytes 184328 | tf_op jit(solution)/shard_map/ppermute | solution.py:563
  7.0 5.4 %collective-permute-start = (bf16[30,8,128]{2,1,0:T(8,128)(2,1)S(1)}, bf16[30,8,128]{2,1,0:T(8,128)(2,1)S(1)}, u32[]{:S(2)}, u32[]{:S(2)}) collective-permute-start(bf16[30,8,128]{2,1,0:T(8,128)(2,1)S(1)} %get-tuple-element.37), channel_id=1, source_target_pairs={{0,1},{1,0},{2,3},{3,2},{4,5},{5,4},{6,7},{7,6},{8,9},{9,8},{10,11... | collective-permute-start | bytes 184328 | tf_op jit(solution)/shard_map/ppermute | solution.py:563
  7.0 5.5 %copy-start = (f32[1,128]{1,0:T(1,128)S(1)}, f32[1,128]{1,0:T(1,128)}, u32[]{:S(2)}) copy-start(f32[1,128]{1,0:T(1,128)} %rate_ref.7) | copy-start | bytes 1540
  14.4 9.0 %collective-permute-start.4 = (bf16[30,16,128]{2,1,0:T(8,128)(2,1)S(1)}, bf16[30,16,128]{2,1,0:T(8,128)(2,1)S(1)}, u32[]{:S(2)}, u32[]{:S(2)}) collective-permute-start(bf16[30,16,128]{2,1,0:T(8,128)(2,1)S(1)} %get-tuple-element.43), channel_id=1, source_target_pairs={{0,10},{1,11},{2,8},{3,9},{4,12},{5,13},{6,14},{7,15},{8,18},{9,19... | collective-permute-start | bytes 368648 | tf_op jit(solution)/shard_map/ppermute | solution.py:572
  14.5 9.3 %collective-permute-start.3 = (bf16[30,16,128]{2,1,0:T(8,128)(2,1)S(1)}, bf16[30,16,128]{2,1,0:T(8,128)(2,1)S(1)}, u32[]{:S(2)}, u32[]{:S(2)}) collective-permute-start(bf16[30,16,128]{2,1,0:T(8,128)(2,1)S(1)} %get-tuple-element.43), channel_id=1, source_target_pairs={{0,8},{1,9},{2,12},{3,13},{4,14},{5,15},{6,10},{7,11},{8,16},{9,17... | collective-permute-start | bytes 368648 | tf_op jit(solution)/shard_map/ppermute | solution.py:572
  23.8 17.9 %copy-start.1 = (f32[128]{0:T(128)S(1)}, f32[128]{0:T(128)}, u32[]{:S(2)}) copy-start(f32[128]{0:T(128)} %param.20) | copy-start | bytes 1540
  23.8 8.4 %collective-permute-start.6 = (bf16[30,16,128]{2,1,0:T(8,128)(2,1)S(1)}, bf16[30,16,128]{2,1,0:T(8,128)(2,1)S(1)}, u32[]{:S(2)}, u32[]{:S(2)}) collective-permute-start(bf16[30,16,128]{2,1,0:T(8,128)(2,1)S(1)} %get-tuple-element.44), channel_id=1, source_target_pairs={{0,8},{1,9},{2,12},{3,13},{4,14},{5,15},{6,10},{7,11},{8,16},{9,17... | collective-permute-start | bytes 368648 | tf_op jit(solution)/shard_map/ppermute | solution.py:572
  23.8 8.4 %collective-permute-start.5 = (bf16[30,16,128]{2,1,0:T(8,128)(2,1)S(1)}, bf16[30,16,128]{2,1,0:T(8,128)(2,1)S(1)}, u32[]{:S(2)}, u32[]{:S(2)}) collective-permute-start(bf16[30,16,128]{2,1,0:T(8,128)(2,1)S(1)} %get-tuple-element.44), channel_id=1, source_target_pairs={{0,12},{1,13},{2,14},{3,15},{4,10},{5,11},{6,8},{7,9},{8,20},{9,21... | collective-permute-start | bytes 368648 | tf_op jit(solution)/shard_map/ppermute | solution.py:572
  32.2 9.4 %collective-permute-start.8 = (bf16[30,16,128]{2,1,0:T(8,128)(2,1)S(1)}, bf16[30,16,128]{2,1,0:T(8,128)(2,1)S(1)}, u32[]{:S(2)}, u32[]{:S(2)}) collective-permute-start(bf16[30,16,128]{2,1,0:T(8,128)(2,1)S(1)} %get-tuple-element.45), channel_id=1, source_target_pairs={{0,10},{1,11},{2,8},{3,9},{4,12},{5,13},{6,14},{7,15},{8,18},{9,19... | collective-permute-start | bytes 368648 | tf_op jit(solution)/shard_map/ppermute | solution.py:572
  34.9 6.8 %collective-permute-start.7 = (bf16[30,16,128]{2,1,0:T(8,128)(2,1)S(1)}, bf16[30,16,128]{2,1,0:T(8,128)(2,1)S(1)}, u32[]{:S(2)}, u32[]{:S(2)}) collective-permute-start(bf16[30,16,128]{2,1,0:T(8,128)(2,1)S(1)} %get-tuple-element.45), channel_id=1, source_target_pairs={{0,8},{1,9},{2,12},{3,13},{4,14},{5,15},{6,10},{7,11},{8,16},{9,17... | collective-permute-start | bytes 368648 | tf_op jit(solution)/shard_map/ppermute | solution.py:572
  41.7 7.2 %collective-permute-start.9 = (bf16[30,16,128]{2,1,0:T(8,128)(2,1)S(1)}, bf16[30,16,128]{2,1,0:T(8,128)(2,1)S(1)}, u32[]{:S(2)}, u32[]{:S(2)}) collective-permute-start(bf16[30,16,128]{2,1,0:T(8,128)(2,1)S(1)} %get-tuple-element.46), channel_id=1, source_target_pairs={{0,24},{1,25},{2,28},{3,29},{4,30},{5,31},{6,26},{7,27},{8,0},{9,1... | collective-permute-start | bytes 368648 | tf_op jit(solution)/shard_map/ppermute | solution.py:572
  46.5 5.8 %collective-permute-start.10 = (bf16[30,16,128]{2,1,0:T(8,128)(2,1)S(1)}, bf16[30,16,128]{2,1,0:T(8,128)(2,1)S(1)}, u32[]{:S(2)}, u32[]{:S(2)}) collective-permute-start(bf16[30,16,128]{2,1,0:T(8,128)(2,1)S(1)} %get-tuple-element.47), channel_id=1, source_target_pairs={{0,28},{1,29},{2,30},{3,31},{4,26},{5,27},{6,24},{7,25},{8,2},{9,3... | collective-permute-start | bytes 368648 | tf_op jit(solution)/shard_map/ppermute | solution.py:572
  52.3 9.3 %collective-permute-start.11 = (bf16[30,16,128]{2,1,0:T(8,128)(2,1)S(1)}, bf16[30,16,128]{2,1,0:T(8,128)(2,1)S(1)}, u32[]{:S(2)}, u32[]{:S(2)}) collective-permute-start(bf16[30,16,128]{2,1,0:T(8,128)(2,1)S(1)} %get-tuple-element.52), channel_id=1, source_target_pairs={{0,26},{1,27},{2,24},{3,25},{4,28},{5,29},{6,30},{7,31},{8,6},{9,7... | collective-permute-start | bytes 368648 | tf_op jit(solution)/shard_map/ppermute | solution.py:572
  58.5 4.9 %collective-permute-start.12 = (bf16[30,16,128]{2,1,0:T(8,128)(2,1)S(1)}, bf16[30,16,128]{2,1,0:T(8,128)(2,1)S(1)}, u32[]{:S(2)}, u32[]{:S(2)}) collective-permute-start(bf16[30,16,128]{2,1,0:T(8,128)(2,1)S(1)} %get-tuple-element.53), channel_id=1, source_target_pairs={{0,24},{1,25},{2,28},{3,29},{4,30},{5,31},{6,26},{7,27},{8,0},{9,1... | collective-permute-start | bytes 368648 | tf_op jit(solution)/shard_map/ppermute | solution.py:572
  63.4 5.5 %collective-permute-start.13 = (bf16[30,16,128]{2,1,0:T(8,128)(2,1)S(1)}, bf16[30,16,128]{2,1,0:T(8,128)(2,1)S(1)}, u32[]{:S(2)}, u32[]{:S(2)}) collective-permute-start(bf16[30,16,128]{2,1,0:T(8,128)(2,1)S(1)} %get-tuple-element.58), channel_id=1, source_target_pairs={{0,24},{1,25},{2,28},{3,29},{4,30},{5,31},{6,26},{7,27},{8,0},{9,1... | collective-permute-start | bytes 368648 | tf_op jit(solution)/shard_map/ppermute | solution.py:572
  65.1 6.7 %collective-permute-start.14 = (bf16[30,16,128]{2,1,0:T(8,128)(2,1)S(1)}, bf16[30,16,128]{2,1,0:T(8,128)(2,1)S(1)}, u32[]{:S(2)}, u32[]{:S(2)}) collective-permute-start(bf16[30,16,128]{2,1,0:T(8,128)(2,1)S(1)} %get-tuple-element.59), channel_id=1, source_target_pairs={{0,28},{1,29},{2,30},{3,31},{4,26},{5,27},{6,24},{7,25},{8,2},{9,3... | collective-permute-start | bytes 368648 | tf_op jit(solution)/shard_map/ppermute | solution.py:572
  73.8 4.0 %collective-permute-start.15 = (f32[8,128]{1,0:T(8,128)S(1)}, f32[8,128]{1,0:T(8,128)S(1)}, u32[]{:S(2)}, u32[]{:S(2)}) collective-permute-start(f32[8,128]{1,0:T(8,128)S(1)} %get-tuple-element.65), channel_id=1, source_target_pairs={{0,1},{1,0},{2,3},{3,2},{4,5},{5,4},{6,7},{7,6},{8,9},{9,8},{10,11... | collective-permute-start | bytes 12296 | tf_op jit(solution)/shard_map/ppermute | solution.py:563
  73.9 5.5 %collective-permute-start.16 = (f32[8,128]{1,0:T(8,128)S(1)}, f32[8,128]{1,0:T(8,128)S(1)}, u32[]{:S(2)}, u32[]{:S(2)}) collective-permute-start(f32[8,128]{1,0:T(8,128)S(1)} %get-tuple-element.66), channel_id=1, source_target_pairs={{0,2},{1,7},{2,4},{3,1},{4,6},{5,3},{6,0},{7,5},{8,10},{9,15},{10,... | collective-permute-start | bytes 12296 | tf_op jit(solution)/shard_map/ppermute | solution.py:563
  73.9 5.4 %collective-permute-start.17 = (f32[8,128]{1,0:T(8,128)S(1)}, f32[8,128]{1,0:T(8,128)S(1)}, u32[]{:S(2)}, u32[]{:S(2)}) collective-permute-start(f32[8,128]{1,0:T(8,128)S(1)} %get-tuple-element.67), channel_id=1, source_target_pairs={{0,7},{1,2},{2,1},{3,4},{4,3},{5,6},{6,5},{7,0},{8,15},{9,10},{10,... | collective-permute-start | bytes 12296 | tf_op jit(solution)/shard_map/ppermute | solution.py:563
  79.3 4.7 %collective-permute-start.20 = (f32[16,128]{1,0:T(8,128)S(1)}, f32[16,128]{1,0:T(8,128)S(1)}, u32[]{:S(2)}, u32[]{:S(2)}) collective-permute-start(f32[16,128]{1,0:T(8,128)S(1)} %join.1.refs_0_), channel_id=1, source_target_pairs={{0,24},{8,0},{16,8},{24,16},{1,25},{9,1},{17,9},{25,17},{2,26},{10... | collective-permute-start | bytes 24584 | tf_op jit(solution)/shard_map/ppermute | solution.py:633
  82.7 3.7 %collective-permute-start.19 = (f32[16,128]{1,0:T(8,128)S(1)}, f32[16,128]{1,0:T(8,128)S(1)}, u32[]{:S(2)}, u32[]{:S(2)}) collective-permute-start(f32[16,128]{1,0:T(8,128)S(1)} %join.1.refs_0_), channel_id=1, source_target_pairs={{0,16},{8,24},{16,0},{24,8},{1,17},{9,25},{17,1},{25,9},{2,18},{10... | collective-permute-start | bytes 24584 | tf_op jit(solution)/shard_map/ppermute | solution.py:633
  83.4 4.5 %collective-permute-start.18 = (f32[16,128]{1,0:T(8,128)S(1)}, f32[16,128]{1,0:T(8,128)S(1)}, u32[]{:S(2)}, u32[]{:S(2)}) collective-permute-start(f32[16,128]{1,0:T(8,128)S(1)} %join.1.refs_0_), channel_id=1, source_target_pairs={{0,8},{8,16},{16,24},{24,0},{1,9},{9,17},{17,25},{25,1},{2,10},{10... | collective-permute-start | bytes 24584 | tf_op jit(solution)/shard_map/ppermute | solution.py:633

commit v13 on v12

--- a/solution.py
+++ b/solution.py
@@ -562,13 +562,12 @@
         ways = [(s * slabs + i, s * slabs + target(i) % slabs) for s in range(segments) for i in range(slabs)]
         return lax.ppermute(value, axes, ways)
 
-    def hop(value, step, by):
-        ways = []
-        for start in range(segments):
-            stop = (start + step) % segments
-            for q in range(pairs):
-                a, b = place_of(q, pairs, start), place_of((q + by) % pairs, pairs, stop)
-                ways += [(start * slabs + 2 * a + c, stop * slabs + 2 * b + c) for c in range(2)]
+    def hop(value, start, stop, by):
+        ways = [(place_of(q, pairs, start), place_of((q + by) % pairs, pairs, stop)) for q in range(pairs)]
+        ways = [(start * slabs + 2 * a + c, stop * slabs + 2 * b + c) for a, b in ways for c in range(2)]
+        ways += [(b, a) for a, b in ways]
+        moving = {a for a, _ in ways}
+        ways += [(i, i + 1 - 2 * (i % 2)) for i in range(segments * slabs) if i not in moving]
         return lax.ppermute(value, axes, ways)
 
     raw = [
@@ -604,7 +603,7 @@
         )
         kept.append(residuals)
         ways = (1, 0) if tick % 2 else (0, -1)
-        around_all.append([hop(out, 1, by) for by in ways])
+        around_all.append([hop(out, tick, tick + 1, by) for by in ways])
     final = segments - 1
     slab_sums = shape((per_slab, channels), F32)
     parts = call(
@@ -616,7 +615,7 @@
     )
     for tick in reversed(range(segments - 1)):
         ways = (1, 0) if tick % 2 else (0, -1)
-        up = [hop(part, -1, -by) for part, by in zip(parts, ways)]
+        up = [hop(part, tick + 1, tick, -by) for part, by in zip(parts, ways)]
         pooled, *residuals = kept[tick]
         parts = call(
             functools.partial(backward_kernel, tick, sz),

time: 88.8 us -> 88.8 us (level)
  waiting for transfers between devices: 49.2 us -> 27.3 us
  starting transfers between devices: 30 us -> 51.9 us
    ppermute x12, starting transfers between devices: 16.9 us -> 41.5 us  [hop(): return lax.ppermute(value, axes, ways)]
    ppermute x12, waiting for transfers between devices: 40.4 us -> 16.6 us  [hop(): return lax.ppermute(value, axes, ways)]
    ppermute x6, waiting for transfers between devices: 4.26 us -> 7.61 us  [within(): return lax.ppermute(value, axes, ways)]
    ppermute x3, starting transfers between devices: 4.05 us -> 2.01 us  [on_device(): lax.ppermute(both, 'segment', [(s, (s + stop) % segments) for s in range(...]
    ppermute x3, waiting for transfers between devices: 4.55 us -> 3.09 us  [on_device(): lax.ppermute(both, 'segment', [(s, (s + stop) % segments) for s in range(...]
  transfers between devices with their start and end apart: 21 -> 21, of which waited for: 15 -> 18; matrix products, arithmetic and copies ran while one was open for 0% -> 0% of each run, Pallas kernels for 3% -> 3%
where the time goes in v13:
time: 88.8 us; the launch traced here: 88.6 us
  starting transfers between devices  51.9 us (58%)
  waiting for transfers between devices  27.3 us (31%)
  Pallas kernels  8.65 us (10%)
    ppermute x12, starting transfers between devices, hop(): return lax.ppermute(value, axes, ways)  41.5 us
    ppermute x12, waiting for transfers between devices, hop(): return lax.ppermute(value, axes, ways)  16.6 us
    pallas_call x12, Pallas kernels, call(): pl.pallas_call(body, out_shape=shapes, in_specs=[pl.BlockSpec(memory_spac...  8.65 us
    ppermute x6, starting transfers between devices, within(): return lax.ppermute(value, axes, ways)  8.35 us
    ppermute x6, waiting for transfers between devices, within(): return lax.ppermute(value, axes, ways)  7.61 us
    ppermute x3, waiting for transfers between devices, on_device(): lax.ppermute(both, 'segment', [(s, (s + stop) % segments) for s in range(...  3.09 us
    ppermute x3, starting transfers between devices, on_device(): lax.ppermute(both, 'segment', [(s, (s + stop) % segments) for s in range(...  2.01 us
  transfers between devices with their start and end apart: 21, of which 18 were waited for; matrix products, arithmetic and copies ran while one was open for 0% of the time, Pallas kernels for 3%

profile of v13, /device:TPU:0, one launch (start us, length us, event | category | flops | bytes accessed | tf_op | source)
XLA Modules:
  0.0 88.6 jit_solution(11137145733379170873)
XLA Ops:
  0.6 1.2 %pack.1 = (bf16[30,8,128]{2,1,0:T(8,128)(2,1)S(1)}, bf16[30,8,128]{2,1,0:T(8,128)(2,1)S(1)}) custom-call(bf16[2,29,8,128]{3,2,1,0:T(8,128)(2,1)} %bitcast.11, f32[3,2,8]{2,1,0:T(2,128)} %bitcast.12, s32[2,8]{1,0:T(2,128)} %species_hbm.1, s32[2,8,8]{2,1,0:T(8,128)} %sources_hbm.1, f32[2,8]{1,0:T(2,128)} %grad_hbm.1, bf16[100,128]{1,0:T(8,128)(2,1)} %table_hbm.1), custom_call_target="tpu_custom_call" | custom-call | tf_op jit(solution)/shard_map/pack/pallas_call | solution.py:524
  1.9 5.1 %collective-permute-start.1 = (bf16[30,8,128]{2,1,0:T(8,128)(2,1)S(1)}, bf16[30,8,128]{2,1,0:T(8,128)(2,1)S(1)}, u32[]{:S(2)}, u32[]{:S(2)}) collective-permute-start(bf16[30,8,128]{2,1,0:T(8,128)(2,1)S(1)} %get-tuple-element.36.mine_ref), channel_id=1, source_target_pairs={{0,6},{1,3},{2,0},{3,5},{4,2},{5,7},{6,4},{7,1},{8,14},{9,11},{10,... | collective-permute-start | bytes 184328 | tf_op jit(solution)/shard_map/ppermute | solution.py:563
  7.0 0.0 collective-permute-start.2
  7.0 0.0 collective-permute-start
  7.0 2.6 %stage.1 = (bf16[896,896]{1,0:T(8,128)(2,1)S(1)}, bf16[2,768,768]{2,1,0:T(8,128)(2,1)S(1)}, bf16[2,640,640]{2,1,0:T(8,128)(2,1)S(1)}) custom-call(bf16[896,896]{1,0:T(8,128)(2,1)} %bitcast.10, bf16[2,768,768]{2,1,0:T(8,128)(2,1)} %bitcast.8, bf16[2,640,640]{2,1,0:T(8,128)(2,1)} %bitcast.9), custom_call_target="tpu_custom_call" | custom-call | tf_op jit(solution)/shard_map/stage/pallas_call | solution.py:524
  9.6 0.0 collective-permute-done.1.straight_ref
  9.6 2.8 %collective-permute-done.2.cross_ref = bf16[30,8,128]{2,1,0:T(8,128)(2,1)S(1)} collective-permute-done((bf16[30,8,128]{2,1,0:T(8,128)(2,1)S(1)}, bf16[30,8,128]{2,1,0:T(8,128)(2,1)S(1)}, u32[]{:S(2)}, u32[]{:S(2)}) %collective-permute-start.2) | collective-permute-done | bytes 61472 | tf_op jit(solution)/shard_map/ppermute | solution.py:563
  12.4 0.0 collective-permute-done.partner_ref
  12.4 0.1 open.1
  12.5 2.0 %forward.3 = (bf16[30,16,128]{2,1,0:T(8,128)(2,1)S(1)}, f32[29,16,128]{2,1,0:T(8,128)S(1)}, bf16[32,128]{1,0:T(8,128)(2,1)S(1)}, f32[1280,128]{1,0:T(8,128)S(1)}, f32[29,128,128]{2,1,0:T(8,128)S(1)}) custom-call(bf16[30,16,128]{2,1,0:T(8,128)(2,1)S(1)} %get-tuple-element.38.low_ref, bf16[30,16,128]{2,1,0:T(8,128)(2,1)S(1)} %get-tuple-element.39.high_ref, ...), custom_call_target="tpu_custom_call" | custom-call | tf_op jit(solution)/shard_map/forward/pallas_call | solution.py:524
  14.4 0.1 collective-permute-start.4
  14.5 0.1 collective-permute-start.3
  14.6 5.8 %collective-permute-done.4.high_ref = bf16[30,16,128]{2,1,0:T(8,128)(2,1)S(1)} collective-permute-done((bf16[30,16,128]{2,1,0:T(8,128)(2,1)S(1)}, bf16[30,16,128]{2,1,0:T(8,128)(2,1)S(1)}, u32[]{:S(2)}, u32[]{:S(2)}) %collective-permute-start.4) | collective-permute-done | bytes 122912 | tf_op jit(solution)/shard_map/ppermute | solution.py:571
  20.4 0.7 collective-permute-done.3.low_ref
  21.1 0.0 collective-permute-start.6
  21.1 0.5 collective-permute-start.5
  21.6 0.8 collective-permute-done.6.high_ref
  22.5 0.2 collective-permute-done.5.low_ref
  22.6 0.3 collective-permute-start.8
  23.0 0.2 collective-permute-start.7
  23.1 0.8 collective-permute-done.8.high_ref
  24.0 0.3 collective-permute-done.7.low_ref
  24.3 0.2 collective-permute-start.9
  24.5 0.3 collective-permute-start.10
  24.8 0.8 collective-permute-done.9.up_low_ref
  25.6 0.2 collective-permute-done.10.up_high_ref
  25.8 0.3 collective-permute-start.11
  26.2 0.2 collective-permute-start.12
  26.3 0.8 collective-permute-done.11.up_low_ref
  27.2 0.3 collective-permute-done.12.up_high_ref
  27.5 39.4 %collective-permute-start.13 = (bf16[30,16,128]{2,1,0:T(8,128)(2,1)S(1)}, bf16[30,16,128]{2,1,0:T(8,128)(2,1)S(1)}, u32[]{:S(2)}, u32[]{:S(2)}) collective-permute-start(bf16[30,16,128]{2,1,0:T(8,128)(2,1)S(1)} %get-tuple-element.58), channel_id=1, source_target_pairs={{8,0},{9,1},{12,2},{13,3},{14,4},{15,5},{10,6},{11,7},{0,8},{1,9},... | collective-permute-start | bytes 368648 | tf_op jit(solution)/shard_map/ppermute | solution.py:571
  66.9 0.0 collective-permute-start.14
  66.9 2.9 %collective-permute-done.13.up_low_ref = bf16[30,16,128]{2,1,0:T(8,128)(2,1)S(1)} collective-permute-done((bf16[30,16,128]{2,1,0:T(8,128)(2,1)S(1)}, bf16[30,16,128]{2,1,0:T(8,128)(2,1)S(1)}, u32[]{:S(2)}, u32[]{:S(2)}) %collective-permute-start.13) | collective-permute-done | bytes 122912 | tf_op jit(solution)/shard_map/ppermute | solution.py:571
  69.7 2.9 %collective-permute-done.14.up_high_ref = bf16[30,16,128]{2,1,0:T(8,128)(2,1)S(1)} collective-permute-done((bf16[30,16,128]{2,1,0:T(8,128)(2,1)S(1)}, bf16[30,16,128]{2,1,0:T(8,128)(2,1)S(1)}, u32[]{:S(2)}, u32[]{:S(2)}) %collective-permute-start.14) | collective-permute-done | bytes 122912 | tf_op jit(solution)/shard_map/ppermute | solution.py:571
  72.6 2.1 %backward.5 = (f32[8,128]{1,0:T(8,128)S(1)}, f32[8,128]{1,0:T(8,128)S(1)}, f32[8,128]{1,0:T(8,128)S(1)}, f32[8,128]{1,0:T(8,128)S(1)}) custom-call(bf16[30,16,128]{2,1,0:T(8,128)(2,1)S(1)} %collective-permute-done.13.up_low_ref, bf16[30,16,128]{2,1,0:T(8,128)(2,1)S(1)} %collective-permute-done.14.up_high_ref, ...), custom_call_target="tpu_custom_call" | custom-call | tf_op jit(solution)/shard_map/backward/pallas_call | solution.py:524
  74.7 0.0 collective-permute-start.15
  74.7 3.2 %collective-permute-start.16 = (f32[8,128]{1,0:T(8,128)S(1)}, f32[8,128]{1,0:T(8,128)S(1)}, u32[]{:S(2)}, u32[]{:S(2)}) collective-permute-start(f32[8,128]{1,0:T(8,128)S(1)} %get-tuple-element.66), channel_id=1, source_target_pairs={{0,2},{1,7},{2,4},{3,1},{4,6},{5,3},{6,0},{7,5},{8,10},{9,15},{10,... | collective-permute-start | bytes 12296 | tf_op jit(solution)/shard_map/ppermute | solution.py:563
  77.9 0.0 collective-permute-start.17
  77.9 0.0 collective-permute-done.15.theirs_ref
  77.9 2.2 %collective-permute-done.16.straight_ref = f32[8,128]{1,0:T(8,128)S(1)} collective-permute-done((f32[8,128]{1,0:T(8,128)S(1)}, f32[8,128]{1,0:T(8,128)S(1)}, u32[]{:S(2)}, u32[]{:S(2)}) %collective-permute-start.16) | collective-permute-done | bytes 4128 | tf_op jit(solution)/shard_map/ppermute | solution.py:563
  80.2 2.6 %collective-permute-done.17.cross_ref = f32[8,128]{1,0:T(8,128)S(1)} collective-permute-done((f32[8,128]{1,0:T(8,128)S(1)}, f32[8,128]{1,0:T(8,128)S(1)}, u32[]{:S(2)}, u32[]{:S(2)}) %collective-permute-start.17) | collective-permute-done | bytes 4128 | tf_op jit(solution)/shard_map/ppermute | solution.py:563
  82.8 0.0 collective-permute-start.20
  82.8 0.1 collective-permute-start.19
  82.9 1.9 %collective-permute-start.18 = (f32[16,128]{1,0:T(8,128)S(1)}, f32[16,128]{1,0:T(8,128)S(1)}, u32[]{:S(2)}, u32[]{:S(2)}) collective-permute-start(f32[16,128]{1,0:T(8,128)S(1)} %join.1.refs_0_), channel_id=1, source_target_pairs={{0,8},{8,16},{16,24},{24,0},{1,9},{9,17},{17,25},{25,1},{2,10},{10... | collective-permute-start | bytes 24584 | tf_op jit(solution)/shard_map/ppermute | solution.py:632
  84.8 1.6 %collective-permute-done.20.refs_3_ = f32[16,128]{1,0:T(8,128)S(1)} collective-permute-done((f32[16,128]{1,0:T(8,128)S(1)}, f32[16,128]{1,0:T(8,128)S(1)}, u32[]{:S(2)}, u32[]{:S(2)}) %collective-permute-start.20) | collective-permute-done | bytes 8224 | tf_op jit(solution)/shard_map/ppermute | solution.py:632
  86.4 0.1 collective-permute-done.19.refs_2_
  86.5 1.4 %collective-permute-done.18.refs_1_ = f32[16,128]{1,0:T(8,128)S(1)} collective-permute-done((f32[16,128]{1,0:T(8,128)S(1)}, f32[16,128]{1,0:T(8,128)S(1)}, u32[]{:S(2)}, u32[]{:S(2)}) %collective-permute-start.18) | collective-permute-done | bytes 8224 | tf_op jit(solution)/shard_map/ppermute | solution.py:632
  87.9 0.7 close.1
  (10 shorter events, 0.0 us)
Async XLA Ops:
  1.9 7.8 %collective-permute-start.1 = (bf16[30,8,128]{2,1,0:T(8,128)(2,1)S(1)}, bf16[30,8,128]{2,1,0:T(8,128)(2,1)S(1)}, u32[]{:S(2)}, u32[]{:S(2)}) collective-permute-start(bf16[30,8,128]{2,1,0:T(8,128)(2,1)S(1)} %get-tuple-element.36.mine_ref), channel_id=1, source_target_pairs={{0,6},{1,3},{2,0},{3,5},{4,2},{5,7},{6,4},{7,1},{8,14},{9,11},{10,... | collective-permute-start | bytes 184328 | tf_op jit(solution)/shard_map/ppermute | solution.py:563
  7.0 5.4 %collective-permute-start.2 = (bf16[30,8,128]{2,1,0:T(8,128)(2,1)S(1)}, bf16[30,8,128]{2,1,0:T(8,128)(2,1)S(1)}, u32[]{:S(2)}, u32[]{:S(2)}) collective-permute-start(bf16[30,8,128]{2,1,0:T(8,128)(2,1)S(1)} %get-tuple-element.37), channel_id=1, source_target_pairs={{0,7},{1,2},{2,1},{3,4},{4,3},{5,6},{6,5},{7,0},{8,15},{9,10},{10,... | collective-permute-start | bytes 184328 | tf_op jit(solution)/shard_map/ppermute | solution.py:563
  7.0 5.4 %collective-permute-start = (bf16[30,8,128]{2,1,0:T(8,128)(2,1)S(1)}, bf16[30,8,128]{2,1,0:T(8,128)(2,1)S(1)}, u32[]{:S(2)}, u32[]{:S(2)}) collective-permute-start(bf16[30,8,128]{2,1,0:T(8,128)(2,1)S(1)} %get-tuple-element.37), channel_id=1, source_target_pairs={{0,1},{1,0},{2,3},{3,2},{4,5},{5,4},{6,7},{7,6},{8,9},{9,8},{10,11... | collective-permute-start | bytes 184328 | tf_op jit(solution)/shard_map/ppermute | solution.py:563
  7.0 5.5 %copy-start = (f32[1,128]{1,0:T(1,128)S(1)}, f32[1,128]{1,0:T(1,128)}, u32[]{:S(2)}) copy-start(f32[1,128]{1,0:T(1,128)} %rate_ref.7) | copy-start | bytes 1540
  14.4 5.9 %collective-permute-start.4 = (bf16[30,16,128]{2,1,0:T(8,128)(2,1)S(1)}, bf16[30,16,128]{2,1,0:T(8,128)(2,1)S(1)}, u32[]{:S(2)}, u32[]{:S(2)}) collective-permute-start(bf16[30,16,128]{2,1,0:T(8,128)(2,1)S(1)} %get-tuple-element.43), channel_id=1, source_target_pairs={{0,10},{1,11},{2,8},{3,9},{4,12},{5,13},{6,14},{7,15},{10,0},{11,1... | collective-permute-start | bytes 368648 | tf_op jit(solution)/shard_map/ppermute | solution.py:571
  14.5 6.6 %collective-permute-start.3 = (bf16[30,16,128]{2,1,0:T(8,128)(2,1)S(1)}, bf16[30,16,128]{2,1,0:T(8,128)(2,1)S(1)}, u32[]{:S(2)}, u32[]{:S(2)}) collective-permute-start(bf16[30,16,128]{2,1,0:T(8,128)(2,1)S(1)} %get-tuple-element.43), channel_id=1, source_target_pairs={{0,8},{1,9},{2,12},{3,13},{4,14},{5,15},{6,10},{7,11},{8,0},{9,1},... | collective-permute-start | bytes 368648 | tf_op jit(solution)/shard_map/ppermute | solution.py:571
  21.1 3.2 %copy-start.1 = (f32[128]{0:T(128)S(1)}, f32[128]{0:T(128)}, u32[]{:S(2)}) copy-start(f32[128]{0:T(128)} %param.20) | copy-start | bytes 1540
  21.1 1.3 %collective-permute-start.6 = (bf16[30,16,128]{2,1,0:T(8,128)(2,1)S(1)}, bf16[30,16,128]{2,1,0:T(8,128)(2,1)S(1)}, u32[]{:S(2)}, u32[]{:S(2)}) collective-permute-start(bf16[30,16,128]{2,1,0:T(8,128)(2,1)S(1)} %get-tuple-element.44), channel_id=1, source_target_pairs={{8,16},{9,17},{12,20},{13,21},{14,22},{15,23},{10,18},{11,19},{16,... | collective-permute-start | bytes 368648 | tf_op jit(solution)/shard_map/ppermute | solution.py:571
  21.1 1.5 %collective-permute-start.5 = (bf16[30,16,128]{2,1,0:T(8,128)(2,1)S(1)}, bf16[30,16,128]{2,1,0:T(8,128)(2,1)S(1)}, u32[]{:S(2)}, u32[]{:S(2)}) collective-permute-start(bf16[30,16,128]{2,1,0:T(8,128)(2,1)S(1)} %get-tuple-element.44), channel_id=1, source_target_pairs={{8,20},{9,21},{12,22},{13,23},{14,18},{15,19},{10,16},{11,17},{20,... | collective-permute-start | bytes 368648 | tf_op jit(solution)/shard_map/ppermute | solution.py:571
  22.6 1.3 %collective-permute-start.8 = (bf16[30,16,128]{2,1,0:T(8,128)(2,1)S(1)}, bf16[30,16,128]{2,1,0:T(8,128)(2,1)S(1)}, u32[]{:S(2)}, u32[]{:S(2)}) collective-permute-start(bf16[30,16,128]{2,1,0:T(8,128)(2,1)S(1)} %get-tuple-element.45), channel_id=1, source_target_pairs={{16,26},{17,27},{20,24},{21,25},{22,28},{23,29},{18,30},{19,31},{2... | collective-permute-start | bytes 368648 | tf_op jit(solution)/shard_map/ppermute | solution.py:571
  23.0 1.3 %collective-permute-start.7 = (bf16[30,16,128]{2,1,0:T(8,128)(2,1)S(1)}, bf16[30,16,128]{2,1,0:T(8,128)(2,1)S(1)}, u32[]{:S(2)}, u32[]{:S(2)}) collective-permute-start(bf16[30,16,128]{2,1,0:T(8,128)(2,1)S(1)} %get-tuple-element.45), channel_id=1, source_target_pairs={{16,24},{17,25},{20,28},{21,29},{22,30},{23,31},{18,26},{19,27},{2... | collective-permute-start | bytes 368648 | tf_op jit(solution)/shard_map/ppermute | solution.py:571
  24.3 1.3 %collective-permute-start.9 = (bf16[30,16,128]{2,1,0:T(8,128)(2,1)S(1)}, bf16[30,16,128]{2,1,0:T(8,128)(2,1)S(1)}, u32[]{:S(2)}, u32[]{:S(2)}) collective-permute-start(bf16[30,16,128]{2,1,0:T(8,128)(2,1)S(1)} %get-tuple-element.46), channel_id=1, source_target_pairs={{24,16},{25,17},{28,20},{29,21},{30,22},{31,23},{26,18},{27,19},{1... | collective-permute-start | bytes 368648 | tf_op jit(solution)/shard_map/ppermute | solution.py:571
  24.5 1.3 %collective-permute-start.10 = (bf16[30,16,128]{2,1,0:T(8,128)(2,1)S(1)}, bf16[30,16,128]{2,1,0:T(8,128)(2,1)S(1)}, u32[]{:S(2)}, u32[]{:S(2)}) collective-permute-start(bf16[30,16,128]{2,1,0:T(8,128)(2,1)S(1)} %get-tuple-element.47), channel_id=1, source_target_pairs={{24,20},{25,21},{28,22},{29,23},{30,18},{31,19},{26,16},{27,17},{2... | collective-permute-start | bytes 368648 | tf_op jit(solution)/shard_map/ppermute | solution.py:571
  25.8 1.3 %collective-permute-start.11 = (bf16[30,16,128]{2,1,0:T(8,128)(2,1)S(1)}, bf16[30,16,128]{2,1,0:T(8,128)(2,1)S(1)}, u32[]{:S(2)}, u32[]{:S(2)}) collective-permute-start(bf16[30,16,128]{2,1,0:T(8,128)(2,1)S(1)} %get-tuple-element.52), channel_id=1, source_target_pairs={{16,10},{17,11},{20,8},{21,9},{22,12},{23,13},{18,14},{19,15},{10,... | collective-permute-start | bytes 368648 | tf_op jit(solution)/shard_map/ppermute | solution.py:571
  26.2 1.3 %collective-permute-start.12 = (bf16[30,16,128]{2,1,0:T(8,128)(2,1)S(1)}, bf16[30,16,128]{2,1,0:T(8,128)(2,1)S(1)}, u32[]{:S(2)}, u32[]{:S(2)}) collective-permute-start(bf16[30,16,128]{2,1,0:T(8,128)(2,1)S(1)} %get-tuple-element.53), channel_id=1, source_target_pairs={{16,8},{17,9},{20,12},{21,13},{22,14},{23,15},{18,10},{19,11},{8,1... | collective-permute-start | bytes 368648 | tf_op jit(solution)/shard_map/ppermute | solution.py:571
  27.5 42.2 %collective-permute-start.13 = (bf16[30,16,128]{2,1,0:T(8,128)(2,1)S(1)}, bf16[30,16,128]{2,1,0:T(8,128)(2,1)S(1)}, u32[]{:S(2)}, u32[]{:S(2)}) collective-permute-start(bf16[30,16,128]{2,1,0:T(8,128)(2,1)S(1)} %get-tuple-element.58), channel_id=1, source_target_pairs={{8,0},{9,1},{12,2},{13,3},{14,4},{15,5},{10,6},{11,7},{0,8},{1,9},... | collective-permute-start | bytes 368648 | tf_op jit(solution)/shard_map/ppermute | solution.py:571
  66.9 5.8 %collective-permute-start.14 = (bf16[30,16,128]{2,1,0:T(8,128)(2,1)S(1)}, bf16[30,16,128]{2,1,0:T(8,128)(2,1)S(1)}, u32[]{:S(2)}, u32[]{:S(2)}) collective-permute-start(bf16[30,16,128]{2,1,0:T(8,128)(2,1)S(1)} %get-tuple-element.59), channel_id=1, source_target_pairs={{8,2},{9,3},{12,4},{13,5},{14,6},{15,7},{10,0},{11,1},{2,8},{3,9},... | collective-permute-start | bytes 368648 | tf_op jit(solution)/shard_map/ppermute | solution.py:571
  74.7 3.3 %collective-permute-start.15 = (f32[8,128]{1,0:T(8,128)S(1)}, f32[8,128]{1,0:T(8,128)S(1)}, u32[]{:S(2)}, u32[]{:S(2)}) collective-permute-start(f32[8,128]{1,0:T(8,128)S(1)} %get-tuple-element.65), channel_id=1, source_target_pairs={{0,1},{1,0},{2,3},{3,2},{4,5},{5,4},{6,7},{7,6},{8,9},{9,8},{10,11... | collective-permute-start | bytes 12296 | tf_op jit(solution)/shard_map/ppermute | solution.py:563
  74.7 5.5 %collective-permute-start.16 = (f32[8,128]{1,0:T(8,128)S(1)}, f32[8,128]{1,0:T(8,128)S(1)}, u32[]{:S(2)}, u32[]{:S(2)}) collective-permute-start(f32[8,128]{1,0:T(8,128)S(1)} %get-tuple-element.66), channel_id=1, source_target_pairs={{0,2},{1,7},{2,4},{3,1},{4,6},{5,3},{6,0},{7,5},{8,10},{9,15},{10,... | collective-permute-start | bytes 12296 | tf_op jit(solution)/shard_map/ppermute | solution.py:563
  77.9 4.8 %collective-permute-start.17 = (f32[8,128]{1,0:T(8,128)S(1)}, f32[8,128]{1,0:T(8,128)S(1)}, u32[]{:S(2)}, u32[]{:S(2)}) collective-permute-start(f32[8,128]{1,0:T(8,128)S(1)} %get-tuple-element.67), channel_id=1, source_target_pairs={{0,7},{1,2},{2,1},{3,4},{4,3},{5,6},{6,5},{7,0},{8,15},{9,10},{10,... | collective-permute-start | bytes 12296 | tf_op jit(solution)/shard_map/ppermute | solution.py:563
  82.8 3.7 %collective-permute-start.20 = (f32[16,128]{1,0:T(8,128)S(1)}, f32[16,128]{1,0:T(8,128)S(1)}, u32[]{:S(2)}, u32[]{:S(2)}) collective-permute-start(f32[16,128]{1,0:T(8,128)S(1)} %join.1.refs_0_), channel_id=1, source_target_pairs={{0,24},{8,0},{16,8},{24,16},{1,25},{9,1},{17,9},{25,17},{2,26},{10... | collective-permute-start | bytes 24584 | tf_op jit(solution)/shard_map/ppermute | solution.py:632
  82.8 3.7 %collective-permute-start.19 = (f32[16,128]{1,0:T(8,128)S(1)}, f32[16,128]{1,0:T(8,128)S(1)}, u32[]{:S(2)}, u32[]{:S(2)}) collective-permute-start(f32[16,128]{1,0:T(8,128)S(1)} %join.1.refs_0_), channel_id=1, source_target_pairs={{0,16},{8,24},{16,0},{24,8},{1,17},{9,25},{17,1},{25,9},{2,18},{10... | collective-permute-start | bytes 24584 | tf_op jit(solution)/shard_map/ppermute | solution.py:632
  82.9 5.0 %collective-permute-start.18 = (f32[16,128]{1,0:T(8,128)S(1)}, f32[16,128]{1,0:T(8,128)S(1)}, u32[]{:S(2)}, u32[]{:S(2)}) collective-permute-start(f32[16,128]{1,0:T(8,128)S(1)} %join.1.refs_0_), channel_id=1, source_target_pairs={{0,8},{8,16},{16,24},{24,0},{1,9},{9,17},{17,25},{25,1},{2,10},{10... | collective-permute-start | bytes 24584 | tf_op jit(solution)/shard_map/ppermute | solution.py:632

commit v14 on v13

--- a/solution.py
+++ b/solution.py
@@ -562,10 +562,16 @@
         ways = [(s * slabs + i, s * slabs + target(i) % slabs) for s in range(segments) for i in range(slabs)]
         return lax.ppermute(value, axes, ways)
 
-    def hop(value, start, stop, by):
+    def hop(value, start, stop, by, way):
         ways = [(place_of(q, pairs, start), place_of((q + by) % pairs, pairs, stop)) for q in range(pairs)]
         ways = [(start * slabs + 2 * a + c, stop * slabs + 2 * b + c) for a, b in ways for c in range(2)]
-        ways += [(b, a) for a, b in ways]
+        idle = [s for s in range(segments) if s not in (start, stop)]
+        if idle:
+            third = idle[way % len(idle)]
+            ways += [(stop * slabs + i, third * slabs + i) for i in range(slabs)]
+            ways += [(third * slabs + i, start * slabs + i) for i in range(slabs)]
+        else:
+            ways += [(b, a) for a, b in ways]
         moving = {a for a, _ in ways}
         ways += [(i, i + 1 - 2 * (i % 2)) for i in range(segments * slabs) if i not in moving]
         return lax.ppermute(value, axes, ways)
@@ -603,7 +609,7 @@
         )
         kept.append(residuals)
         ways = (1, 0) if tick % 2 else (0, -1)
-        around_all.append([hop(out, tick, tick + 1, by) for by in ways])
+        around_all.append([hop(out, tick, tick + 1, by, way) for way, by in enumerate(ways)])
     final = segments - 1
     slab_sums = shape((per_slab, channels), F32)
     parts = call(
@@ -615,7 +621,7 @@
     )
     for tick in reversed(range(segments - 1)):
         ways = (1, 0) if tick % 2 else (0, -1)
-        up = [hop(part, tick + 1, tick, -by) for part, by in zip(parts, ways)]
+        up = [hop(part, tick + 1, tick, -by, way) for way, (part, by) in enumerate(zip(parts, ways))]
         pooled, *residuals = kept[tick]
         parts = call(
             functools.partial(backward_kernel, tick, sz),

time: 88.8 us -> 81.1 us (0.913)
  starting transfers between devices: 51.9 us -> 32.8 us
  waiting for transfers between devices: 27.3 us -> 38.8 us
    ppermute x12, starting transfers between devices: 41.5 us -> 21.7 us  [hop(): return lax.ppermute(value, axes, ways)]
    ppermute x12, waiting for transfers between devices: 16.6 us -> 29.6 us  [hop(): return lax.ppermute(value, axes, ways)]
    ppermute x6, waiting for transfers between devices: 7.61 us -> 4.9 us  [within(): return lax.ppermute(value, axes, ways)]
    ppermute x3, waiting for transfers between devices: 3.09 us -> 4.29 us  [on_device(): lax.ppermute(both, 'segment', [(s, (s + stop) % segments) for s in range(...]
  transfers between devices with their start and end apart: 21 -> 21, of which waited for: 18 -> 14; matrix products, arithmetic and copies ran while one was open for 0% -> 0% of each run, Pallas kernels for 3% -> 3%
where the time goes in v14:
time: 81.1 us; the launch traced here: 81 us
  waiting for transfers between devices  38.8 us (48%)
  starting transfers between devices  32.8 us (40%)
  Pallas kernels  8.66 us (11%)
    ppermute x12, waiting for transfers between devices, hop(): return lax.ppermute(value, axes, ways)  29.6 us
    ppermute x12, starting transfers between devices, hop(): return lax.ppermute(value, axes, ways)  21.7 us
    ppermute x6, starting transfers between devices, within(): return lax.ppermute(value, axes, ways)  9.08 us
    pallas_call x12, Pallas kernels, call(): pl.pallas_call(body, out_shape=shapes, in_specs=[pl.BlockSpec(memory_spac...  8.66 us
    ppermute x6, waiting for transfers between devices, within(): return lax.ppermute(value, axes, ways)  4.9 us
    ppermute x3, waiting for transfers between devices, on_device(): lax.ppermute(both, 'segment', [(s, (s + stop) % segments) for s in range(...  4.29 us
    ppermute x3, starting transfers between devices, on_device(): lax.ppermute(both, 'segment', [(s, (s + stop) % segments) for s in range(...  2.02 us
  transfers between devices with their start and end apart: 21, of which 14 were waited for; matrix products, arithmetic and copies ran while one was open for 0% of the time, Pallas kernels for 3%

profile of v14, /device:TPU:0, one launch (start us, length us, event | category | flops | bytes accessed | tf_op | source)
XLA Modules:
  0.0 81.0 jit_solution(8070776909243232618)
XLA Ops:
  0.6 1.2 %pack.1 = (bf16[30,8,128]{2,1,0:T(8,128)(2,1)S(1)}, bf16[30,8,128]{2,1,0:T(8,128)(2,1)S(1)}) custom-call(bf16[2,29,8,128]{3,2,1,0:T(8,128)(2,1)} %bitcast.11, f32[3,2,8]{2,1,0:T(2,128)} %bitcast.12, s32[2,8]{1,0:T(2,128)} %species_hbm.1, s32[2,8,8]{2,1,0:T(8,128)} %sources_hbm.1, f32[2,8]{1,0:T(2,128)} %grad_hbm.1, bf16[100,128]{1,0:T(8,128)(2,1)} %table_hbm.1), custom_call_target="tpu_custom_call" | custom-call | tf_op jit(solution)/shard_map/pack/pallas_call | solution.py:524
  1.9 5.1 %collective-permute-start.1 = (bf16[30,8,128]{2,1,0:T(8,128)(2,1)S(1)}, bf16[30,8,128]{2,1,0:T(8,128)(2,1)S(1)}, u32[]{:S(2)}, u32[]{:S(2)}) collective-permute-start(bf16[30,8,128]{2,1,0:T(8,128)(2,1)S(1)} %get-tuple-element.36.mine_ref), channel_id=1, source_target_pairs={{0,6},{1,3},{2,0},{3,5},{4,2},{5,7},{6,4},{7,1},{8,14},{9,11},{10,... | collective-permute-start | bytes 184328 | tf_op jit(solution)/shard_map/ppermute | solution.py:563
  7.0 0.0 collective-permute-start.2
  7.0 0.0 collective-permute-start
  7.0 2.6 %stage.1 = (bf16[896,896]{1,0:T(8,128)(2,1)S(1)}, bf16[2,768,768]{2,1,0:T(8,128)(2,1)S(1)}, bf16[2,640,640]{2,1,0:T(8,128)(2,1)S(1)}) custom-call(bf16[896,896]{1,0:T(8,128)(2,1)} %bitcast.10, bf16[2,768,768]{2,1,0:T(8,128)(2,1)} %bitcast.8, bf16[2,640,640]{2,1,0:T(8,128)(2,1)} %bitcast.9), custom_call_target="tpu_custom_call" | custom-call | tf_op jit(solution)/shard_map/stage/pallas_call | solution.py:524
  9.6 0.0 collective-permute-done.1.straight_ref
  9.6 2.8 %collective-permute-done.2.cross_ref = bf16[30,8,128]{2,1,0:T(8,128)(2,1)S(1)} collective-permute-done((bf16[30,8,128]{2,1,0:T(8,128)(2,1)S(1)}, bf16[30,8,128]{2,1,0:T(8,128)(2,1)S(1)}, u32[]{:S(2)}, u32[]{:S(2)}) %collective-permute-start.2) | collective-permute-done | bytes 61472 | tf_op jit(solution)/shard_map/ppermute | solution.py:563
  12.4 0.0 collective-permute-done.partner_ref
  12.4 0.1 open.1
  12.5 2.0 %forward.3 = (bf16[30,16,128]{2,1,0:T(8,128)(2,1)S(1)}, f32[29,16,128]{2,1,0:T(8,128)S(1)}, bf16[32,128]{1,0:T(8,128)(2,1)S(1)}, f32[1280,128]{1,0:T(8,128)S(1)}, f32[29,128,128]{2,1,0:T(8,128)S(1)}) custom-call(bf16[30,16,128]{2,1,0:T(8,128)(2,1)S(1)} %get-tuple-element.38.low_ref, bf16[30,16,128]{2,1,0:T(8,128)(2,1)S(1)} %get-tuple-element.39.high_ref, ...), custom_call_target="tpu_custom_call" | custom-call | tf_op jit(solution)/shard_map/forward/pallas_call | solution.py:524
  14.4 0.1 collective-permute-start.4
  14.5 0.1 collective-permute-start.3
  14.6 5.8 %collective-permute-done.4.high_ref = bf16[30,16,128]{2,1,0:T(8,128)(2,1)S(1)} collective-permute-done((bf16[30,16,128]{2,1,0:T(8,128)(2,1)S(1)}, bf16[30,16,128]{2,1,0:T(8,128)(2,1)S(1)}, u32[]{:S(2)}, u32[]{:S(2)}) %collective-permute-start.4) | collective-permute-done | bytes 122912 | tf_op jit(solution)/shard_map/ppermute | solution.py:577
  20.4 0.4 collective-permute-done.3.low_ref
  20.8 0.0 collective-permute-start.6
  20.8 1.2 %collective-permute-start.5 = (bf16[30,16,128]{2,1,0:T(8,128)(2,1)S(1)}, bf16[30,16,128]{2,1,0:T(8,128)(2,1)S(1)}, u32[]{:S(2)}, u32[]{:S(2)}) collective-permute-start(bf16[30,16,128]{2,1,0:T(8,128)(2,1)S(1)} %get-tuple-element.44), channel_id=1, source_target_pairs={{8,20},{9,21},{12,22},{13,23},{14,18},{15,19},{10,16},{11,17},{16,... | collective-permute-start | bytes 368648 | tf_op jit(solution)/shard_map/ppermute | solution.py:577
  22.0 0.1 collective-permute-done.6.high_ref
  22.1 4.4 %collective-permute-done.5.low_ref = bf16[30,16,128]{2,1,0:T(8,128)(2,1)S(1)} collective-permute-done((bf16[30,16,128]{2,1,0:T(8,128)(2,1)S(1)}, bf16[30,16,128]{2,1,0:T(8,128)(2,1)S(1)}, u32[]{:S(2)}, u32[]{:S(2)}) %collective-permute-start.5) | collective-permute-done | bytes 122912 | tf_op jit(solution)/shard_map/ppermute | solution.py:577
  26.5 0.0 collective-permute-start.8
  26.5 4.5 %collective-permute-start.7 = (bf16[30,16,128]{2,1,0:T(8,128)(2,1)S(1)}, bf16[30,16,128]{2,1,0:T(8,128)(2,1)S(1)}, u32[]{:S(2)}, u32[]{:S(2)}) collective-permute-start(bf16[30,16,128]{2,1,0:T(8,128)(2,1)S(1)} %get-tuple-element.45), channel_id=1, source_target_pairs={{16,24},{17,25},{20,28},{21,29},{22,30},{23,31},{18,26},{19,27},{2... | collective-permute-start | bytes 368648 | tf_op jit(solution)/shard_map/ppermute | solution.py:577
  31.0 0.0 collective-permute-done.8.high_ref
  31.0 3.7 %collective-permute-done.7.low_ref = bf16[30,16,128]{2,1,0:T(8,128)(2,1)S(1)} collective-permute-done((bf16[30,16,128]{2,1,0:T(8,128)(2,1)S(1)}, bf16[30,16,128]{2,1,0:T(8,128)(2,1)S(1)}, u32[]{:S(2)}, u32[]{:S(2)}) %collective-permute-start.7) | collective-permute-done | bytes 122912 | tf_op jit(solution)/shard_map/ppermute | solution.py:577
  34.7 7.7 %collective-permute-start.9 = (bf16[30,16,128]{2,1,0:T(8,128)(2,1)S(1)}, bf16[30,16,128]{2,1,0:T(8,128)(2,1)S(1)}, u32[]{:S(2)}, u32[]{:S(2)}) collective-permute-start(bf16[30,16,128]{2,1,0:T(8,128)(2,1)S(1)} %get-tuple-element.46), channel_id=1, source_target_pairs={{24,16},{25,17},{28,20},{29,21},{30,22},{31,23},{26,18},{27,19},{1... | collective-permute-start | bytes 368648 | tf_op jit(solution)/shard_map/ppermute | solution.py:577
  42.4 0.0 collective-permute-start.10
  42.4 2.4 %collective-permute-done.9.up_low_ref = bf16[30,16,128]{2,1,0:T(8,128)(2,1)S(1)} collective-permute-done((bf16[30,16,128]{2,1,0:T(8,128)(2,1)S(1)}, bf16[30,16,128]{2,1,0:T(8,128)(2,1)S(1)}, u32[]{:S(2)}, u32[]{:S(2)}) %collective-permute-start.9) | collective-permute-done | bytes 122912 | tf_op jit(solution)/shard_map/ppermute | solution.py:577
  44.9 0.0 collective-permute-done.10.up_high_ref
  44.9 5.5 %collective-permute-start.11 = (bf16[30,16,128]{2,1,0:T(8,128)(2,1)S(1)}, bf16[30,16,128]{2,1,0:T(8,128)(2,1)S(1)}, u32[]{:S(2)}, u32[]{:S(2)}) collective-permute-start(bf16[30,16,128]{2,1,0:T(8,128)(2,1)S(1)} %get-tuple-element.52), channel_id=1, source_target_pairs={{16,10},{17,11},{20,8},{21,9},{22,12},{23,13},{18,14},{19,15},{8,0... | collective-permute-start | bytes 368648 | tf_op jit(solution)/shard_map/ppermute | solution.py:577
  50.4 0.0 collective-permute-start.12
  50.4 2.4 %collective-permute-done.11.up_low_ref = bf16[30,16,128]{2,1,0:T(8,128)(2,1)S(1)} collective-permute-done((bf16[30,16,128]{2,1,0:T(8,128)(2,1)S(1)}, bf16[30,16,128]{2,1,0:T(8,128)(2,1)S(1)}, u32[]{:S(2)}, u32[]{:S(2)}) %collective-permute-start.11) | collective-permute-done | bytes 122912 | tf_op jit(solution)/shard_map/ppermute | solution.py:577
  52.9 0.0 collective-permute-done.12.up_high_ref
  52.9 2.6 %collective-permute-start.13 = (bf16[30,16,128]{2,1,0:T(8,128)(2,1)S(1)}, bf16[30,16,128]{2,1,0:T(8,128)(2,1)S(1)}, u32[]{:S(2)}, u32[]{:S(2)}) collective-permute-start(bf16[30,16,128]{2,1,0:T(8,128)(2,1)S(1)} %get-tuple-element.58), channel_id=1, source_target_pairs={{8,0},{9,1},{12,2},{13,3},{14,4},{15,5},{10,6},{11,7},{0,16},{1,17... | collective-permute-start | bytes 368648 | tf_op jit(solution)/shard_map/ppermute | solution.py:577
  55.5 0.0 collective-permute-start.14
  55.5 10.2 %collective-permute-done.13.up_low_ref = bf16[30,16,128]{2,1,0:T(8,128)(2,1)S(1)} collective-permute-done((bf16[30,16,128]{2,1,0:T(8,128)(2,1)S(1)}, bf16[30,16,128]{2,1,0:T(8,128)(2,1)S(1)}, u32[]{:S(2)}, u32[]{:S(2)}) %collective-permute-start.13) | collective-permute-done | bytes 122912 | tf_op jit(solution)/shard_map/ppermute | solution.py:577
  65.8 0.0 collective-permute-done.14.up_high_ref
  65.8 2.1 %backward.5 = (f32[8,128]{1,0:T(8,128)S(1)}, f32[8,128]{1,0:T(8,128)S(1)}, f32[8,128]{1,0:T(8,128)S(1)}, f32[8,128]{1,0:T(8,128)S(1)}) custom-call(bf16[30,16,128]{2,1,0:T(8,128)(2,1)S(1)} %collective-permute-done.13.up_low_ref, bf16[30,16,128]{2,1,0:T(8,128)(2,1)S(1)} %collective-permute-done.14.up_high_ref, ...), custom_call_target="tpu_custom_call" | custom-call | tf_op jit(solution)/shard_map/backward/pallas_call | solution.py:524
  67.8 0.0 collective-permute-start.15
  67.8 1.3 %collective-permute-start.16 = (f32[8,128]{1,0:T(8,128)S(1)}, f32[8,128]{1,0:T(8,128)S(1)}, u32[]{:S(2)}, u32[]{:S(2)}) collective-permute-start(f32[8,128]{1,0:T(8,128)S(1)} %get-tuple-element.66), channel_id=1, source_target_pairs={{0,2},{1,7},{2,4},{3,1},{4,6},{5,3},{6,0},{7,5},{8,10},{9,15},{10,... | collective-permute-start | bytes 12296 | tf_op jit(solution)/shard_map/ppermute | solution.py:563
  69.1 2.7 %collective-permute-start.17 = (f32[8,128]{1,0:T(8,128)S(1)}, f32[8,128]{1,0:T(8,128)S(1)}, u32[]{:S(2)}, u32[]{:S(2)}) collective-permute-start(f32[8,128]{1,0:T(8,128)S(1)} %get-tuple-element.67), channel_id=1, source_target_pairs={{0,7},{1,2},{2,1},{3,4},{4,3},{5,6},{6,5},{7,0},{8,15},{9,10},{10,... | collective-permute-start | bytes 12296 | tf_op jit(solution)/shard_map/ppermute | solution.py:563
  71.8 0.0 collective-permute-done.15.theirs_ref
  71.8 1.5 %collective-permute-done.16.straight_ref = f32[8,128]{1,0:T(8,128)S(1)} collective-permute-done((f32[8,128]{1,0:T(8,128)S(1)}, f32[8,128]{1,0:T(8,128)S(1)}, u32[]{:S(2)}, u32[]{:S(2)}) %collective-permute-start.16) | collective-permute-done | bytes 4128 | tf_op jit(solution)/shard_map/ppermute | solution.py:563
  73.3 0.6 collective-permute-done.17.cross_ref
  73.9 0.0 collective-permute-start.20
  73.9 1.8 %collective-permute-start.19 = (f32[16,128]{1,0:T(8,128)S(1)}, f32[16,128]{1,0:T(8,128)S(1)}, u32[]{:S(2)}, u32[]{:S(2)}) collective-permute-start(f32[16,128]{1,0:T(8,128)S(1)} %join.1.refs_0_), channel_id=1, source_target_pairs={{0,16},{8,24},{16,0},{24,8},{1,17},{9,25},{17,1},{25,9},{2,18},{10... | collective-permute-start | bytes 24584 | tf_op jit(solution)/shard_map/ppermute | solution.py:638
  75.7 0.3 collective-permute-start.18
  75.9 1.6 %collective-permute-done.20.refs_3_ = f32[16,128]{1,0:T(8,128)S(1)} collective-permute-done((f32[16,128]{1,0:T(8,128)S(1)}, f32[16,128]{1,0:T(8,128)S(1)}, u32[]{:S(2)}, u32[]{:S(2)}) %collective-permute-start.20) | collective-permute-done | bytes 8224 | tf_op jit(solution)/shard_map/ppermute | solution.py:638
  77.6 0.1 collective-permute-done.19.refs_2_
  77.6 2.6 %collective-permute-done.18.refs_1_ = f32[16,128]{1,0:T(8,128)S(1)} collective-permute-done((f32[16,128]{1,0:T(8,128)S(1)}, f32[16,128]{1,0:T(8,128)S(1)}, u32[]{:S(2)}, u32[]{:S(2)}) %collective-permute-start.18) | collective-permute-done | bytes 8224 | tf_op jit(solution)/shard_map/ppermute | solution.py:638
  80.2 0.7 close.1
  (10 shorter events, 0.0 us)
Async XLA Ops:
  1.9 7.8 %collective-permute-start.1 = (bf16[30,8,128]{2,1,0:T(8,128)(2,1)S(1)}, bf16[30,8,128]{2,1,0:T(8,128)(2,1)S(1)}, u32[]{:S(2)}, u32[]{:S(2)}) collective-permute-start(bf16[30,8,128]{2,1,0:T(8,128)(2,1)S(1)} %get-tuple-element.36.mine_ref), channel_id=1, source_target_pairs={{0,6},{1,3},{2,0},{3,5},{4,2},{5,7},{6,4},{7,1},{8,14},{9,11},{10,... | collective-permute-start | bytes 184328 | tf_op jit(solution)/shard_map/ppermute | solution.py:563
  7.0 5.4 %collective-permute-start.2 = (bf16[30,8,128]{2,1,0:T(8,128)(2,1)S(1)}, bf16[30,8,128]{2,1,0:T(8,128)(2,1)S(1)}, u32[]{:S(2)}, u32[]{:S(2)}) collective-permute-start(bf16[30,8,128]{2,1,0:T(8,128)(2,1)S(1)} %get-tuple-element.37), channel_id=1, source_target_pairs={{0,7},{1,2},{2,1},{3,4},{4,3},{5,6},{6,5},{7,0},{8,15},{9,10},{10,... | collective-permute-start | bytes 184328 | tf_op jit(solution)/shard_map/ppermute | solution.py:563
  7.0 5.4 %collective-permute-start = (bf16[30,8,128]{2,1,0:T(8,128)(2,1)S(1)}, bf16[30,8,128]{2,1,0:T(8,128)(2,1)S(1)}, u32[]{:S(2)}, u32[]{:S(2)}) collective-permute-start(bf16[30,8,128]{2,1,0:T(8,128)(2,1)S(1)} %get-tuple-element.37), channel_id=1, source_target_pairs={{0,1},{1,0},{2,3},{3,2},{4,5},{5,4},{6,7},{7,6},{8,9},{9,8},{10,11... | collective-permute-start | bytes 184328 | tf_op jit(solution)/shard_map/ppermute | solution.py:563
  7.0 5.5 %copy-start = (f32[1,128]{1,0:T(1,128)S(1)}, f32[1,128]{1,0:T(1,128)}, u32[]{:S(2)}) copy-start(f32[1,128]{1,0:T(1,128)} %rate_ref.7) | copy-start | bytes 1540
  14.4 5.9 %collective-permute-start.4 = (bf16[30,16,128]{2,1,0:T(8,128)(2,1)S(1)}, bf16[30,16,128]{2,1,0:T(8,128)(2,1)S(1)}, u32[]{:S(2)}, u32[]{:S(2)}) collective-permute-start(bf16[30,16,128]{2,1,0:T(8,128)(2,1)S(1)} %get-tuple-element.43), channel_id=1, source_target_pairs={{0,10},{1,11},{2,8},{3,9},{4,12},{5,13},{6,14},{7,15},{8,24},{9,25... | collective-permute-start | bytes 368648 | tf_op jit(solution)/shard_map/ppermute | solution.py:577
  14.5 6.2 %collective-permute-start.3 = (bf16[30,16,128]{2,1,0:T(8,128)(2,1)S(1)}, bf16[30,16,128]{2,1,0:T(8,128)(2,1)S(1)}, u32[]{:S(2)}, u32[]{:S(2)}) collective-permute-start(bf16[30,16,128]{2,1,0:T(8,128)(2,1)S(1)} %get-tuple-element.43), channel_id=1, source_target_pairs={{0,8},{1,9},{2,12},{3,13},{4,14},{5,15},{6,10},{7,11},{8,16},{9,17... | collective-permute-start | bytes 368648 | tf_op jit(solution)/shard_map/ppermute | solution.py:577
  20.8 13.9 %copy-start.1 = (f32[128]{0:T(128)S(1)}, f32[128]{0:T(128)}, u32[]{:S(2)}) copy-start(f32[128]{0:T(128)} %param.20) | copy-start | bytes 1540
  20.8 1.3 %collective-permute-start.6 = (bf16[30,16,128]{2,1,0:T(8,128)(2,1)S(1)}, bf16[30,16,128]{2,1,0:T(8,128)(2,1)S(1)}, u32[]{:S(2)}, u32[]{:S(2)}) collective-permute-start(bf16[30,16,128]{2,1,0:T(8,128)(2,1)S(1)} %get-tuple-element.44), channel_id=1, source_target_pairs={{8,16},{9,17},{12,20},{13,21},{14,22},{15,23},{10,18},{11,19},{16,... | collective-permute-start | bytes 368648 | tf_op jit(solution)/shard_map/ppermute | solution.py:577
  20.8 5.7 %collective-permute-start.5 = (bf16[30,16,128]{2,1,0:T(8,128)(2,1)S(1)}, bf16[30,16,128]{2,1,0:T(8,128)(2,1)S(1)}, u32[]{:S(2)}, u32[]{:S(2)}) collective-permute-start(bf16[30,16,128]{2,1,0:T(8,128)(2,1)S(1)} %get-tuple-element.44), channel_id=1, source_target_pairs={{8,20},{9,21},{12,22},{13,23},{14,18},{15,19},{10,16},{11,17},{16,... | collective-permute-start | bytes 368648 | tf_op jit(solution)/shard_map/ppermute | solution.py:577
  26.5 4.5 %collective-permute-start.8 = (bf16[30,16,128]{2,1,0:T(8,128)(2,1)S(1)}, bf16[30,16,128]{2,1,0:T(8,128)(2,1)S(1)}, u32[]{:S(2)}, u32[]{:S(2)}) collective-permute-start(bf16[30,16,128]{2,1,0:T(8,128)(2,1)S(1)} %get-tuple-element.45), channel_id=1, source_target_pairs={{16,26},{17,27},{20,24},{21,25},{22,28},{23,29},{18,30},{19,31},{2... | collective-permute-start | bytes 368648 | tf_op jit(solution)/shard_map/ppermute | solution.py:577
  26.5 8.2 %collective-permute-start.7 = (bf16[30,16,128]{2,1,0:T(8,128)(2,1)S(1)}, bf16[30,16,128]{2,1,0:T(8,128)(2,1)S(1)}, u32[]{:S(2)}, u32[]{:S(2)}) collective-permute-start(bf16[30,16,128]{2,1,0:T(8,128)(2,1)S(1)} %get-tuple-element.45), channel_id=1, source_target_pairs={{16,24},{17,25},{20,28},{21,29},{22,30},{23,31},{18,26},{19,27},{2... | collective-permute-start | bytes 368648 | tf_op jit(solution)/shard_map/ppermute | solution.py:577
  34.7 10.2 %collective-permute-start.9 = (bf16[30,16,128]{2,1,0:T(8,128)(2,1)S(1)}, bf16[30,16,128]{2,1,0:T(8,128)(2,1)S(1)}, u32[]{:S(2)}, u32[]{:S(2)}) collective-permute-start(bf16[30,16,128]{2,1,0:T(8,128)(2,1)S(1)} %get-tuple-element.46), channel_id=1, source_target_pairs={{24,16},{25,17},{28,20},{29,21},{30,22},{31,23},{26,18},{27,19},{1... | collective-permute-start | bytes 368648 | tf_op jit(solution)/shard_map/ppermute | solution.py:577
  42.4 2.4 %collective-permute-start.10 = (bf16[30,16,128]{2,1,0:T(8,128)(2,1)S(1)}, bf16[30,16,128]{2,1,0:T(8,128)(2,1)S(1)}, u32[]{:S(2)}, u32[]{:S(2)}) collective-permute-start(bf16[30,16,128]{2,1,0:T(8,128)(2,1)S(1)} %get-tuple-element.47), channel_id=1, source_target_pairs={{24,20},{25,21},{28,22},{29,23},{30,18},{31,19},{26,16},{27,17},{1... | collective-permute-start | bytes 368648 | tf_op jit(solution)/shard_map/ppermute | solution.py:577
  44.9 8.0 %collective-permute-start.11 = (bf16[30,16,128]{2,1,0:T(8,128)(2,1)S(1)}, bf16[30,16,128]{2,1,0:T(8,128)(2,1)S(1)}, u32[]{:S(2)}, u32[]{:S(2)}) collective-permute-start(bf16[30,16,128]{2,1,0:T(8,128)(2,1)S(1)} %get-tuple-element.52), channel_id=1, source_target_pairs={{16,10},{17,11},{20,8},{21,9},{22,12},{23,13},{18,14},{19,15},{8,0... | collective-permute-start | bytes 368648 | tf_op jit(solution)/shard_map/ppermute | solution.py:577
  50.4 2.4 %collective-permute-start.12 = (bf16[30,16,128]{2,1,0:T(8,128)(2,1)S(1)}, bf16[30,16,128]{2,1,0:T(8,128)(2,1)S(1)}, u32[]{:S(2)}, u32[]{:S(2)}) collective-permute-start(bf16[30,16,128]{2,1,0:T(8,128)(2,1)S(1)} %get-tuple-element.53), channel_id=1, source_target_pairs={{16,8},{17,9},{20,12},{21,13},{22,14},{23,15},{18,10},{19,11},{8,2... | collective-permute-start | bytes 368648 | tf_op jit(solution)/shard_map/ppermute | solution.py:577
  52.9 12.9 %collective-permute-start.13 = (bf16[30,16,128]{2,1,0:T(8,128)(2,1)S(1)}, bf16[30,16,128]{2,1,0:T(8,128)(2,1)S(1)}, u32[]{:S(2)}, u32[]{:S(2)}) collective-permute-start(bf16[30,16,128]{2,1,0:T(8,128)(2,1)S(1)} %get-tuple-element.58), channel_id=1, source_target_pairs={{8,0},{9,1},{12,2},{13,3},{14,4},{15,5},{10,6},{11,7},{0,16},{1,17... | collective-permute-start | bytes 368648 | tf_op jit(solution)/shard_map/ppermute | solution.py:577
  55.5 10.3 %collective-permute-start.14 = (bf16[30,16,128]{2,1,0:T(8,128)(2,1)S(1)}, bf16[30,16,128]{2,1,0:T(8,128)(2,1)S(1)}, u32[]{:S(2)}, u32[]{:S(2)}) collective-permute-start(bf16[30,16,128]{2,1,0:T(8,128)(2,1)S(1)} %get-tuple-element.59), channel_id=1, source_target_pairs={{8,2},{9,3},{12,4},{13,5},{14,6},{15,7},{10,0},{11,1},{0,24},{1,25... | collective-permute-start | bytes 368648 | tf_op jit(solution)/shard_map/ppermute | solution.py:577
  67.8 4.0 %collective-permute-start.15 = (f32[8,128]{1,0:T(8,128)S(1)}, f32[8,128]{1,0:T(8,128)S(1)}, u32[]{:S(2)}, u32[]{:S(2)}) collective-permute-start(f32[8,128]{1,0:T(8,128)S(1)} %get-tuple-element.65), channel_id=1, source_target_pairs={{0,1},{1,0},{2,3},{3,2},{4,5},{5,4},{6,7},{7,6},{8,9},{9,8},{10,11... | collective-permute-start | bytes 12296 | tf_op jit(solution)/shard_map/ppermute | solution.py:563
  67.8 5.5 %collective-permute-start.16 = (f32[8,128]{1,0:T(8,128)S(1)}, f32[8,128]{1,0:T(8,128)S(1)}, u32[]{:S(2)}, u32[]{:S(2)}) collective-permute-start(f32[8,128]{1,0:T(8,128)S(1)} %get-tuple-element.66), channel_id=1, source_target_pairs={{0,2},{1,7},{2,4},{3,1},{4,6},{5,3},{6,0},{7,5},{8,10},{9,15},{10,... | collective-permute-start | bytes 12296 | tf_op jit(solution)/shard_map/ppermute | solution.py:563
  69.1 4.8 %collective-permute-start.17 = (f32[8,128]{1,0:T(8,128)S(1)}, f32[8,128]{1,0:T(8,128)S(1)}, u32[]{:S(2)}, u32[]{:S(2)}) collective-permute-start(f32[8,128]{1,0:T(8,128)S(1)} %get-tuple-element.67), channel_id=1, source_target_pairs={{0,7},{1,2},{2,1},{3,4},{4,3},{5,6},{6,5},{7,0},{8,15},{9,10},{10,... | collective-permute-start | bytes 12296 | tf_op jit(solution)/shard_map/ppermute | solution.py:563
  73.9 3.7 %collective-permute-start.20 = (f32[16,128]{1,0:T(8,128)S(1)}, f32[16,128]{1,0:T(8,128)S(1)}, u32[]{:S(2)}, u32[]{:S(2)}) collective-permute-start(f32[16,128]{1,0:T(8,128)S(1)} %join.1.refs_0_), channel_id=1, source_target_pairs={{0,24},{8,0},{16,8},{24,16},{1,25},{9,1},{17,9},{25,17},{2,26},{10... | collective-permute-start | bytes 24584 | tf_op jit(solution)/shard_map/ppermute | solution.py:638
  73.9 3.7 %collective-permute-start.19 = (f32[16,128]{1,0:T(8,128)S(1)}, f32[16,128]{1,0:T(8,128)S(1)}, u32[]{:S(2)}, u32[]{:S(2)}) collective-permute-start(f32[16,128]{1,0:T(8,128)S(1)} %join.1.refs_0_), channel_id=1, source_target_pairs={{0,16},{8,24},{16,0},{24,8},{1,17},{9,25},{17,1},{25,9},{2,18},{10... | collective-permute-start | bytes 24584 | tf_op jit(solution)/shard_map/ppermute | solution.py:638
  75.7 4.5 %collective-permute-start.18 = (f32[16,128]{1,0:T(8,128)S(1)}, f32[16,128]{1,0:T(8,128)S(1)}, u32[]{:S(2)}, u32[]{:S(2)}) collective-permute-start(f32[16,128]{1,0:T(8,128)S(1)} %join.1.refs_0_), channel_id=1, source_target_pairs={{0,8},{8,16},{16,24},{24,0},{1,9},{9,17},{17,25},{25,1},{2,10},{10... | collective-permute-start | bytes 24584 | tf_op jit(solution)/shard_map/ppermute | solution.py:638

commit v15 on v14

--- a/solution.py
+++ b/solution.py
@@ -634,8 +634,23 @@
     straight = within(straight, lambda i: i - 2 if i % 2 else i + 2)
     cross = within(cross, lambda i: i + 1 if i % 2 else i - 1)
     (both,) = call(join_kernel, [here, theirs, straight, cross], [shape((rows, channels), F32)], "join")
+
+    def across(section, i, stop):
+        if section in (0, stop):
+            return stop - section, i
+        return section, i + 1 - 2 * (i % 2)
+
     copies = [both] + [
-        lax.ppermute(both, "segment", [(s, (s + stop) % segments) for s in range(segments)])
+        lax.ppermute(
+            both,
+            axes,
+            [
+                (s * slabs + i, t * slabs + j)
+                for s in range(segments)
+                for i in range(slabs)
+                for t, j in [across(s, i, stop)]
+            ],
+        )
         for stop in range(1, segments)
     ]
     energies, gradients = call(

time: 81.1 us -> 79.3 us (0.978)
  starting transfers between devices: 32.8 us -> 31.7 us
    ppermute x3, starting transfers between devices: 2.02 us -> 0.98 us  [on_device(): lax.ppermute(both, axes, [(s * slabs + i, t * slabs + j) for s in range(s...]
  transfers between devices with their start and end apart: 21 -> 21, of which waited for: 14 -> 12; matrix products, arithmetic and copies ran while one was open for 0% -> 0% of each run, Pallas kernels for 3% -> 3%
where the time goes in v15:
time: 79.3 us; the launch traced here: 79.2 us
  waiting for transfers between devices  38 us (48%)
  starting transfers between devices  31.7 us (40%)
  Pallas kernels  8.66 us (11%)
    ppermute x12, waiting for transfers between devices, hop(): return lax.ppermute(value, axes, ways)  29.6 us
    ppermute x12, starting transfers between devices, hop(): return lax.ppermute(value, axes, ways)  21.7 us
    ppermute x6, starting transfers between devices, within(): return lax.ppermute(value, axes, ways)  9.08 us
    pallas_call x12, Pallas kernels, call(): pl.pallas_call(body, out_shape=shapes, in_specs=[pl.BlockSpec(memory_spac...  8.66 us
    ppermute x6, waiting for transfers between devices, within(): return lax.ppermute(value, axes, ways)  4.9 us
    ppermute x3, waiting for transfers between devices, on_device(): lax.ppermute(both, axes, [(s * slabs + i, t * slabs + j) for s in range(s...  3.56 us
  transfers between devices with their start and end apart: 21, of which 12 were waited for; matrix products, arithmetic and copies ran while one was open for 0% of the time, Pallas kernels for 3%

profile of v15, /device:TPU:0, one launch (start us, length us, event | category | flops | bytes accessed | tf_op | source)
XLA Modules:
  0.0 79.2 jit_solution(9658735747602172274)
XLA Ops:
  0.6 1.2 %pack.1 = (bf16[30,8,128]{2,1,0:T(8,128)(2,1)S(1)}, bf16[30,8,128]{2,1,0:T(8,128)(2,1)S(1)}) custom-call(bf16[2,29,8,128]{3,2,1,0:T(8,128)(2,1)} %bitcast.11, f32[3,2,8]{2,1,0:T(2,128)} %bitcast.12, s32[2,8]{1,0:T(2,128)} %species_hbm.1, s32[2,8,8]{2,1,0:T(8,128)} %sources_hbm.1, f32[2,8]{1,0:T(2,128)} %grad_hbm.1, bf16[100,128]{1,0:T(8,128)(2,1)} %table_hbm.1), custom_call_target="tpu_custom_call" | custom-call | tf_op jit(solution)/shard_map/pack/pallas_call | solution.py:524
  1.9 5.1 %collective-permute-start.1 = (bf16[30,8,128]{2,1,0:T(8,128)(2,1)S(1)}, bf16[30,8,128]{2,1,0:T(8,128)(2,1)S(1)}, u32[]{:S(2)}, u32[]{:S(2)}) collective-permute-start(bf16[30,8,128]{2,1,0:T(8,128)(2,1)S(1)} %get-tuple-element.36.mine_ref), channel_id=1, source_target_pairs={{0,6},{1,3},{2,0},{3,5},{4,2},{5,7},{6,4},{7,1},{8,14},{9,11},{10,... | collective-permute-start | bytes 184328 | tf_op jit(solution)/shard_map/ppermute | solution.py:563
  7.0 0.0 collective-permute-start.2
  7.0 0.0 collective-permute-start
  7.0 2.6 %stage.1 = (bf16[896,896]{1,0:T(8,128)(2,1)S(1)}, bf16[2,768,768]{2,1,0:T(8,128)(2,1)S(1)}, bf16[2,640,640]{2,1,0:T(8,128)(2,1)S(1)}) custom-call(bf16[896,896]{1,0:T(8,128)(2,1)} %bitcast.10, bf16[2,768,768]{2,1,0:T(8,128)(2,1)} %bitcast.8, bf16[2,640,640]{2,1,0:T(8,128)(2,1)} %bitcast.9), custom_call_target="tpu_custom_call" | custom-call | tf_op jit(solution)/shard_map/stage/pallas_call | solution.py:524
  9.6 0.0 collective-permute-done.1.straight_ref
  9.6 2.8 %collective-permute-done.2.cross_ref = bf16[30,8,128]{2,1,0:T(8,128)(2,1)S(1)} collective-permute-done((bf16[30,8,128]{2,1,0:T(8,128)(2,1)S(1)}, bf16[30,8,128]{2,1,0:T(8,128)(2,1)S(1)}, u32[]{:S(2)}, u32[]{:S(2)}) %collective-permute-start.2) | collective-permute-done | bytes 61472 | tf_op jit(solution)/shard_map/ppermute | solution.py:563
  12.4 0.0 collective-permute-done.partner_ref
  12.4 0.1 open.1
  12.5 2.0 %forward.3 = (bf16[30,16,128]{2,1,0:T(8,128)(2,1)S(1)}, f32[29,16,128]{2,1,0:T(8,128)S(1)}, bf16[32,128]{1,0:T(8,128)(2,1)S(1)}, f32[1280,128]{1,0:T(8,128)S(1)}, f32[29,128,128]{2,1,0:T(8,128)S(1)}) custom-call(bf16[30,16,128]{2,1,0:T(8,128)(2,1)S(1)} %get-tuple-element.38.low_ref, bf16[30,16,128]{2,1,0:T(8,128)(2,1)S(1)} %get-tuple-element.39.high_ref, ...), custom_call_target="tpu_custom_call" | custom-call | tf_op jit(solution)/shard_map/forward/pallas_call | solution.py:524
  14.4 0.1 collective-permute-start.4
  14.5 0.1 collective-permute-start.3
  14.6 5.8 %collective-permute-done.4.high_ref = bf16[30,16,128]{2,1,0:T(8,128)(2,1)S(1)} collective-permute-done((bf16[30,16,128]{2,1,0:T(8,128)(2,1)S(1)}, bf16[30,16,128]{2,1,0:T(8,128)(2,1)S(1)}, u32[]{:S(2)}, u32[]{:S(2)}) %collective-permute-start.4) | collective-permute-done | bytes 122912 | tf_op jit(solution)/shard_map/ppermute | solution.py:577
  20.4 0.4 collective-permute-done.3.low_ref
  20.8 0.0 collective-permute-start.6
  20.8 1.2 %collective-permute-start.5 = (bf16[30,16,128]{2,1,0:T(8,128)(2,1)S(1)}, bf16[30,16,128]{2,1,0:T(8,128)(2,1)S(1)}, u32[]{:S(2)}, u32[]{:S(2)}) collective-permute-start(bf16[30,16,128]{2,1,0:T(8,128)(2,1)S(1)} %get-tuple-element.44), channel_id=1, source_target_pairs={{8,20},{9,21},{12,22},{13,23},{14,18},{15,19},{10,16},{11,17},{16,... | collective-permute-start | bytes 368648 | tf_op jit(solution)/shard_map/ppermute | solution.py:577
  22.0 0.1 collective-permute-done.6.high_ref
  22.1 4.4 %collective-permute-done.5.low_ref = bf16[30,16,128]{2,1,0:T(8,128)(2,1)S(1)} collective-permute-done((bf16[30,16,128]{2,1,0:T(8,128)(2,1)S(1)}, bf16[30,16,128]{2,1,0:T(8,128)(2,1)S(1)}, u32[]{:S(2)}, u32[]{:S(2)}) %collective-permute-start.5) | collective-permute-done | bytes 122912 | tf_op jit(solution)/shard_map/ppermute | solution.py:577
  26.5 0.0 collective-permute-start.8
  26.5 4.5 %collective-permute-start.7 = (bf16[30,16,128]{2,1,0:T(8,128)(2,1)S(1)}, bf16[30,16,128]{2,1,0:T(8,128)(2,1)S(1)}, u32[]{:S(2)}, u32[]{:S(2)}) collective-permute-start(bf16[30,16,128]{2,1,0:T(8,128)(2,1)S(1)} %get-tuple-element.45), channel_id=1, source_target_pairs={{16,24},{17,25},{20,28},{21,29},{22,30},{23,31},{18,26},{19,27},{2... | collective-permute-start | bytes 368648 | tf_op jit(solution)/shard_map/ppermute | solution.py:577
  31.0 0.0 collective-permute-done.8.high_ref
  31.0 3.7 %collective-permute-done.7.low_ref = bf16[30,16,128]{2,1,0:T(8,128)(2,1)S(1)} collective-permute-done((bf16[30,16,128]{2,1,0:T(8,128)(2,1)S(1)}, bf16[30,16,128]{2,1,0:T(8,128)(2,1)S(1)}, u32[]{:S(2)}, u32[]{:S(2)}) %collective-permute-start.7) | collective-permute-done | bytes 122912 | tf_op jit(solution)/shard_map/ppermute | solution.py:577
  34.7 7.7 %collective-permute-start.9 = (bf16[30,16,128]{2,1,0:T(8,128)(2,1)S(1)}, bf16[30,16,128]{2,1,0:T(8,128)(2,1)S(1)}, u32[]{:S(2)}, u32[]{:S(2)}) collective-permute-start(bf16[30,16,128]{2,1,0:T(8,128)(2,1)S(1)} %get-tuple-element.46), channel_id=1, source_target_pairs={{24,16},{25,17},{28,20},{29,21},{30,22},{31,23},{26,18},{27,19},{1... | collective-permute-start | bytes 368648 | tf_op jit(solution)/shard_map/ppermute | solution.py:577
  42.4 0.0 collective-permute-start.10
  42.4 2.4 %collective-permute-done.9.up_low_ref = bf16[30,16,128]{2,1,0:T(8,128)(2,1)S(1)} collective-permute-done((bf16[30,16,128]{2,1,0:T(8,128)(2,1)S(1)}, bf16[30,16,128]{2,1,0:T(8,128)(2,1)S(1)}, u32[]{:S(2)}, u32[]{:S(2)}) %collective-permute-start.9) | collective-permute-done | bytes 122912 | tf_op jit(solution)/shard_map/ppermute | solution.py:577
  44.9 0.0 collective-permute-done.10.up_high_ref
  44.9 5.5 %collective-permute-start.11 = (bf16[30,16,128]{2,1,0:T(8,128)(2,1)S(1)}, bf16[30,16,128]{2,1,0:T(8,128)(2,1)S(1)}, u32[]{:S(2)}, u32[]{:S(2)}) collective-permute-start(bf16[30,16,128]{2,1,0:T(8,128)(2,1)S(1)} %get-tuple-element.52), channel_id=1, source_target_pairs={{16,10},{17,11},{20,8},{21,9},{22,12},{23,13},{18,14},{19,15},{8,0... | collective-permute-start | bytes 368648 | tf_op jit(solution)/shard_map/ppermute | solution.py:577
  50.4 0.0 collective-permute-start.12
  50.4 2.4 %collective-permute-done.11.up_low_ref = bf16[30,16,128]{2,1,0:T(8,128)(2,1)S(1)} collective-permute-done((bf16[30,16,128]{2,1,0:T(8,128)(2,1)S(1)}, bf16[30,16,128]{2,1,0:T(8,128)(2,1)S(1)}, u32[]{:S(2)}, u32[]{:S(2)}) %collective-permute-start.11) | collective-permute-done | bytes 122912 | tf_op jit(solution)/shard_map/ppermute | solution.py:577
  52.9 0.0 collective-permute-done.12.up_high_ref
  52.9 2.6 %collective-permute-start.13 = (bf16[30,16,128]{2,1,0:T(8,128)(2,1)S(1)}, bf16[30,16,128]{2,1,0:T(8,128)(2,1)S(1)}, u32[]{:S(2)}, u32[]{:S(2)}) collective-permute-start(bf16[30,16,128]{2,1,0:T(8,128)(2,1)S(1)} %get-tuple-element.58), channel_id=1, source_target_pairs={{8,0},{9,1},{12,2},{13,3},{14,4},{15,5},{10,6},{11,7},{0,16},{1,17... | collective-permute-start | bytes 368648 | tf_op jit(solution)/shard_map/ppermute | solution.py:577
  55.5 0.0 collective-permute-start.14
  55.5 10.2 %collective-permute-done.13.up_low_ref = bf16[30,16,128]{2,1,0:T(8,128)(2,1)S(1)} collective-permute-done((bf16[30,16,128]{2,1,0:T(8,128)(2,1)S(1)}, bf16[30,16,128]{2,1,0:T(8,128)(2,1)S(1)}, u32[]{:S(2)}, u32[]{:S(2)}) %collective-permute-start.13) | collective-permute-done | bytes 122912 | tf_op jit(solution)/shard_map/ppermute | solution.py:577
  65.8 0.0 collective-permute-done.14.up_high_ref
  65.8 2.1 %backward.5 = (f32[8,128]{1,0:T(8,128)S(1)}, f32[8,128]{1,0:T(8,128)S(1)}, f32[8,128]{1,0:T(8,128)S(1)}, f32[8,128]{1,0:T(8,128)S(1)}) custom-call(bf16[30,16,128]{2,1,0:T(8,128)(2,1)S(1)} %collective-permute-done.13.up_low_ref, bf16[30,16,128]{2,1,0:T(8,128)(2,1)S(1)} %collective-permute-done.14.up_high_ref, ...), custom_call_target="tpu_custom_call" | custom-call | tf_op jit(solution)/shard_map/backward/pallas_call | solution.py:524
  67.8 0.0 collective-permute-start.15
  67.8 1.3 %collective-permute-start.16 = (f32[8,128]{1,0:T(8,128)S(1)}, f32[8,128]{1,0:T(8,128)S(1)}, u32[]{:S(2)}, u32[]{:S(2)}) collective-permute-start(f32[8,128]{1,0:T(8,128)S(1)} %get-tuple-element.66), channel_id=1, source_target_pairs={{0,2},{1,7},{2,4},{3,1},{4,6},{5,3},{6,0},{7,5},{8,10},{9,15},{10,... | collective-permute-start | bytes 12296 | tf_op jit(solution)/shard_map/ppermute | solution.py:563
  69.1 2.7 %collective-permute-start.17 = (f32[8,128]{1,0:T(8,128)S(1)}, f32[8,128]{1,0:T(8,128)S(1)}, u32[]{:S(2)}, u32[]{:S(2)}) collective-permute-start(f32[8,128]{1,0:T(8,128)S(1)} %get-tuple-element.67), channel_id=1, source_target_pairs={{0,7},{1,2},{2,1},{3,4},{4,3},{5,6},{6,5},{7,0},{8,15},{9,10},{10,... | collective-permute-start | bytes 12296 | tf_op jit(solution)/shard_map/ppermute | solution.py:563
  71.8 0.0 collective-permute-done.15.theirs_ref
  71.8 1.5 %collective-permute-done.16.straight_ref = f32[8,128]{1,0:T(8,128)S(1)} collective-permute-done((f32[8,128]{1,0:T(8,128)S(1)}, f32[8,128]{1,0:T(8,128)S(1)}, u32[]{:S(2)}, u32[]{:S(2)}) %collective-permute-start.16) | collective-permute-done | bytes 4128 | tf_op jit(solution)/shard_map/ppermute | solution.py:563
  73.3 0.6 collective-permute-done.17.cross_ref
  73.9 0.0 collective-permute-start.20
  73.9 0.1 collective-permute-start.19
  74.0 0.9 %collective-permute-start.18 = (f32[16,128]{1,0:T(8,128)S(1)}, f32[16,128]{1,0:T(8,128)S(1)}, u32[]{:S(2)}, u32[]{:S(2)}) collective-permute-start(f32[16,128]{1,0:T(8,128)S(1)} %join.1.refs_0_), channel_id=1, source_target_pairs={{0,8},{1,9},{2,10},{3,11},{4,12},{5,13},{6,14},{7,15},{8,0},{9,1},... | collective-permute-start | bytes 24584 | tf_op jit(solution)/shard_map/ppermute | solution.py:644
  74.9 3.6 %collective-permute-done.20.refs_3_ = f32[16,128]{1,0:T(8,128)S(1)} collective-permute-done((f32[16,128]{1,0:T(8,128)S(1)}, f32[16,128]{1,0:T(8,128)S(1)}, u32[]{:S(2)}, u32[]{:S(2)}) %collective-permute-start.20) | collective-permute-done | bytes 8224 | tf_op jit(solution)/shard_map/ppermute | solution.py:644
  78.5 0.0 collective-permute-done.19.refs_2_
  78.5 0.0 collective-permute-done.18.refs_1_
  78.5 0.7 close.1
  (10 shorter events, 0.0 us)
Async XLA Ops:
  1.9 7.8 %collective-permute-start.1 = (bf16[30,8,128]{2,1,0:T(8,128)(2,1)S(1)}, bf16[30,8,128]{2,1,0:T(8,128)(2,1)S(1)}, u32[]{:S(2)}, u32[]{:S(2)}) collective-permute-start(bf16[30,8,128]{2,1,0:T(8,128)(2,1)S(1)} %get-tuple-element.36.mine_ref), channel_id=1, source_target_pairs={{0,6},{1,3},{2,0},{3,5},{4,2},{5,7},{6,4},{7,1},{8,14},{9,11},{10,... | collective-permute-start | bytes 184328 | tf_op jit(solution)/shard_map/ppermute | solution.py:563
  7.0 5.4 %collective-permute-start.2 = (bf16[30,8,128]{2,1,0:T(8,128)(2,1)S(1)}, bf16[30,8,128]{2,1,0:T(8,128)(2,1)S(1)}, u32[]{:S(2)}, u32[]{:S(2)}) collective-permute-start(bf16[30,8,128]{2,1,0:T(8,128)(2,1)S(1)} %get-tuple-element.37), channel_id=1, source_target_pairs={{0,7},{1,2},{2,1},{3,4},{4,3},{5,6},{6,5},{7,0},{8,15},{9,10},{10,... | collective-permute-start | bytes 184328 | tf_op jit(solution)/shard_map/ppermute | solution.py:563
  7.0 5.4 %collective-permute-start = (bf16[30,8,128]{2,1,0:T(8,128)(2,1)S(1)}, bf16[30,8,128]{2,1,0:T(8,128)(2,1)S(1)}, u32[]{:S(2)}, u32[]{:S(2)}) collective-permute-start(bf16[30,8,128]{2,1,0:T(8,128)(2,1)S(1)} %get-tuple-element.37), channel_id=1, source_target_pairs={{0,1},{1,0},{2,3},{3,2},{4,5},{5,4},{6,7},{7,6},{8,9},{9,8},{10,11... | collective-permute-start | bytes 184328 | tf_op jit(solution)/shard_map/ppermute | solution.py:563
  7.0 5.5 %copy-start = (f32[1,128]{1,0:T(1,128)S(1)}, f32[1,128]{1,0:T(1,128)}, u32[]{:S(2)}) copy-start(f32[1,128]{1,0:T(1,128)} %rate_ref.7) | copy-start | bytes 1540
  14.4 5.9 %collective-permute-start.4 = (bf16[30,16,128]{2,1,0:T(8,128)(2,1)S(1)}, bf16[30,16,128]{2,1,0:T(8,128)(2,1)S(1)}, u32[]{:S(2)}, u32[]{:S(2)}) collective-permute-start(bf16[30,16,128]{2,1,0:T(8,128)(2,1)S(1)} %get-tuple-element.43), channel_id=1, source_target_pairs={{0,10},{1,11},{2,8},{3,9},{4,12},{5,13},{6,14},{7,15},{8,24},{9,25... | collective-permute-start | bytes 368648 | tf_op jit(solution)/shard_map/ppermute | solution.py:577
  14.5 6.2 %collective-permute-start.3 = (bf16[30,16,128]{2,1,0:T(8,128)(2,1)S(1)}, bf16[30,16,128]{2,1,0:T(8,128)(2,1)S(1)}, u32[]{:S(2)}, u32[]{:S(2)}) collective-permute-start(bf16[30,16,128]{2,1,0:T(8,128)(2,1)S(1)} %get-tuple-element.43), channel_id=1, source_target_pairs={{0,8},{1,9},{2,12},{3,13},{4,14},{5,15},{6,10},{7,11},{8,16},{9,17... | collective-permute-start | bytes 368648 | tf_op jit(solution)/shard_map/ppermute | solution.py:577
  20.8 13.9 %copy-start.1 = (f32[128]{0:T(128)S(1)}, f32[128]{0:T(128)}, u32[]{:S(2)}) copy-start(f32[128]{0:T(128)} %param.20) | copy-start | bytes 1540
  20.8 1.3 %collective-permute-start.6 = (bf16[30,16,128]{2,1,0:T(8,128)(2,1)S(1)}, bf16[30,16,128]{2,1,0:T(8,128)(2,1)S(1)}, u32[]{:S(2)}, u32[]{:S(2)}) collective-permute-start(bf16[30,16,128]{2,1,0:T(8,128)(2,1)S(1)} %get-tuple-element.44), channel_id=1, source_target_pairs={{8,16},{9,17},{12,20},{13,21},{14,22},{15,23},{10,18},{11,19},{16,... | collective-permute-start | bytes 368648 | tf_op jit(solution)/shard_map/ppermute | solution.py:577
  20.8 5.7 %collective-permute-start.5 = (bf16[30,16,128]{2,1,0:T(8,128)(2,1)S(1)}, bf16[30,16,128]{2,1,0:T(8,128)(2,1)S(1)}, u32[]{:S(2)}, u32[]{:S(2)}) collective-permute-start(bf16[30,16,128]{2,1,0:T(8,128)(2,1)S(1)} %get-tuple-element.44), channel_id=1, source_target_pairs={{8,20},{9,21},{12,22},{13,23},{14,18},{15,19},{10,16},{11,17},{16,... | collective-permute-start | bytes 368648 | tf_op jit(solution)/shard_map/ppermute | solution.py:577
  26.5 4.5 %collective-permute-start.8 = (bf16[30,16,128]{2,1,0:T(8,128)(2,1)S(1)}, bf16[30,16,128]{2,1,0:T(8,128)(2,1)S(1)}, u32[]{:S(2)}, u32[]{:S(2)}) collective-permute-start(bf16[30,16,128]{2,1,0:T(8,128)(2,1)S(1)} %get-tuple-element.45), channel_id=1, source_target_pairs={{16,26},{17,27},{20,24},{21,25},{22,28},{23,29},{18,30},{19,31},{2... | collective-permute-start | bytes 368648 | tf_op jit(solution)/shard_map/ppermute | solution.py:577
  26.5 8.2 %collective-permute-start.7 = (bf16[30,16,128]{2,1,0:T(8,128)(2,1)S(1)}, bf16[30,16,128]{2,1,0:T(8,128)(2,1)S(1)}, u32[]{:S(2)}, u32[]{:S(2)}) collective-permute-start(bf16[30,16,128]{2,1,0:T(8,128)(2,1)S(1)} %get-tuple-element.45), channel_id=1, source_target_pairs={{16,24},{17,25},{20,28},{21,29},{22,30},{23,31},{18,26},{19,27},{2... | collective-permute-start | bytes 368648 | tf_op jit(solution)/shard_map/ppermute | solution.py:577
  34.7 10.2 %collective-permute-start.9 = (bf16[30,16,128]{2,1,0:T(8,128)(2,1)S(1)}, bf16[30,16,128]{2,1,0:T(8,128)(2,1)S(1)}, u32[]{:S(2)}, u32[]{:S(2)}) collective-permute-start(bf16[30,16,128]{2,1,0:T(8,128)(2,1)S(1)} %get-tuple-element.46), channel_id=1, source_target_pairs={{24,16},{25,17},{28,20},{29,21},{30,22},{31,23},{26,18},{27,19},{1... | collective-permute-start | bytes 368648 | tf_op jit(solution)/shard_map/ppermute | solution.py:577
  42.4 2.4 %collective-permute-start.10 = (bf16[30,16,128]{2,1,0:T(8,128)(2,1)S(1)}, bf16[30,16,128]{2,1,0:T(8,128)(2,1)S(1)}, u32[]{:S(2)}, u32[]{:S(2)}) collective-permute-start(bf16[30,16,128]{2,1,0:T(8,128)(2,1)S(1)} %get-tuple-element.47), channel_id=1, source_target_pairs={{24,20},{25,21},{28,22},{29,23},{30,18},{31,19},{26,16},{27,17},{1... | collective-permute-start | bytes 368648 | tf_op jit(solution)/shard_map/ppermute | solution.py:577
  44.9 8.0 %collective-permute-start.11 = (bf16[30,16,128]{2,1,0:T(8,128)(2,1)S(1)}, bf16[30,16,128]{2,1,0:T(8,128)(2,1)S(1)}, u32[]{:S(2)}, u32[]{:S(2)}) collective-permute-start(bf16[30,16,128]{2,1,0:T(8,128)(2,1)S(1)} %get-tuple-element.52), channel_id=1, source_target_pairs={{16,10},{17,11},{20,8},{21,9},{22,12},{23,13},{18,14},{19,15},{8,0... | collective-permute-start | bytes 368648 | tf_op jit(solution)/shard_map/ppermute | solution.py:577
  50.4 2.4 %collective-permute-start.12 = (bf16[30,16,128]{2,1,0:T(8,128)(2,1)S(1)}, bf16[30,16,128]{2,1,0:T(8,128)(2,1)S(1)}, u32[]{:S(2)}, u32[]{:S(2)}) collective-permute-start(bf16[30,16,128]{2,1,0:T(8,128)(2,1)S(1)} %get-tuple-element.53), channel_id=1, source_target_pairs={{16,8},{17,9},{20,12},{21,13},{22,14},{23,15},{18,10},{19,11},{8,2... | collective-permute-start | bytes 368648 | tf_op jit(solution)/shard_map/ppermute | solution.py:577
  52.9 12.9 %collective-permute-start.13 = (bf16[30,16,128]{2,1,0:T(8,128)(2,1)S(1)}, bf16[30,16,128]{2,1,0:T(8,128)(2,1)S(1)}, u32[]{:S(2)}, u32[]{:S(2)}) collective-permute-start(bf16[30,16,128]{2,1,0:T(8,128)(2,1)S(1)} %get-tuple-element.58), channel_id=1, source_target_pairs={{8,0},{9,1},{12,2},{13,3},{14,4},{15,5},{10,6},{11,7},{0,16},{1,17... | collective-permute-start | bytes 368648 | tf_op jit(solution)/shard_map/ppermute | solution.py:577
  55.5 10.3 %collective-permute-start.14 = (bf16[30,16,128]{2,1,0:T(8,128)(2,1)S(1)}, bf16[30,16,128]{2,1,0:T(8,128)(2,1)S(1)}, u32[]{:S(2)}, u32[]{:S(2)}) collective-permute-start(bf16[30,16,128]{2,1,0:T(8,128)(2,1)S(1)} %get-tuple-element.59), channel_id=1, source_target_pairs={{8,2},{9,3},{12,4},{13,5},{14,6},{15,7},{10,0},{11,1},{0,24},{1,25... | collective-permute-start | bytes 368648 | tf_op jit(solution)/shard_map/ppermute | solution.py:577
  67.8 4.0 %collective-permute-start.15 = (f32[8,128]{1,0:T(8,128)S(1)}, f32[8,128]{1,0:T(8,128)S(1)}, u32[]{:S(2)}, u32[]{:S(2)}) collective-permute-start(f32[8,128]{1,0:T(8,128)S(1)} %get-tuple-element.65), channel_id=1, source_target_pairs={{0,1},{1,0},{2,3},{3,2},{4,5},{5,4},{6,7},{7,6},{8,9},{9,8},{10,11... | collective-permute-start | bytes 12296 | tf_op jit(solution)/shard_map/ppermute | solution.py:563
  67.8 5.5 %collective-permute-start.16 = (f32[8,128]{1,0:T(8,128)S(1)}, f32[8,128]{1,0:T(8,128)S(1)}, u32[]{:S(2)}, u32[]{:S(2)}) collective-permute-start(f32[8,128]{1,0:T(8,128)S(1)} %get-tuple-element.66), channel_id=1, source_target_pairs={{0,2},{1,7},{2,4},{3,1},{4,6},{5,3},{6,0},{7,5},{8,10},{9,15},{10,... | collective-permute-start | bytes 12296 | tf_op jit(solution)/shard_map/ppermute | solution.py:563
  69.1 4.8 %collective-permute-start.17 = (f32[8,128]{1,0:T(8,128)S(1)}, f32[8,128]{1,0:T(8,128)S(1)}, u32[]{:S(2)}, u32[]{:S(2)}) collective-permute-start(f32[8,128]{1,0:T(8,128)S(1)} %get-tuple-element.67), channel_id=1, source_target_pairs={{0,7},{1,2},{2,1},{3,4},{4,3},{5,6},{6,5},{7,0},{8,15},{9,10},{10,... | collective-permute-start | bytes 12296 | tf_op jit(solution)/shard_map/ppermute | solution.py:563
  73.9 4.5 %collective-permute-start.20 = (f32[16,128]{1,0:T(8,128)S(1)}, f32[16,128]{1,0:T(8,128)S(1)}, u32[]{:S(2)}, u32[]{:S(2)}) collective-permute-start(f32[16,128]{1,0:T(8,128)S(1)} %join.1.refs_0_), channel_id=1, source_target_pairs={{0,24},{1,25},{2,26},{3,27},{4,28},{5,29},{6,30},{7,31},{8,9},{9,8... | collective-permute-start | bytes 24584 | tf_op jit(solution)/shard_map/ppermute | solution.py:644
  73.9 4.5 %collective-permute-start.19 = (f32[16,128]{1,0:T(8,128)S(1)}, f32[16,128]{1,0:T(8,128)S(1)}, u32[]{:S(2)}, u32[]{:S(2)}) collective-permute-start(f32[16,128]{1,0:T(8,128)S(1)} %join.1.refs_0_), channel_id=1, source_target_pairs={{0,16},{1,17},{2,18},{3,19},{4,20},{5,21},{6,22},{7,23},{8,9},{9,8... | collective-permute-start | bytes 24584 | tf_op jit(solution)/shard_map/ppermute | solution.py:644
  74.0 4.5 %collective-permute-start.18 = (f32[16,128]{1,0:T(8,128)S(1)}, f32[16,128]{1,0:T(8,128)S(1)}, u32[]{:S(2)}, u32[]{:S(2)}) collective-permute-start(f32[16,128]{1,0:T(8,128)S(1)} %join.1.refs_0_), channel_id=1, source_target_pairs={{0,8},{1,9},{2,10},{3,11},{4,12},{5,13},{6,14},{7,15},{8,0},{9,1},... | collective-permute-start | bytes 24584 | tf_op jit(solution)/shard_map/ppermute | solution.py:644

commit v16 on v15

--- a/solution.py
+++ b/solution.py
@@ -442,15 +442,20 @@
     return numbers[per_slab : per_slab + rows]
 
 
-def stage_kernel(zero_hbm, one_hbm, two_hbm, zero_ref, one_ref, two_ref, sems):
-    pairs = [(zero_hbm, zero_ref)]
-    for source, target in ((one_hbm, one_ref), (two_hbm, two_ref)):
-        pairs += [(source.at[n], target.at[n]) for n in range(2)]
-    copies = [pltpu.make_async_copy(source, target, sems.at[n]) for n, (source, target) in enumerate(pairs)]
-    for copy in copies:
-        copy.start()
-    for copy in copies:
-        copy.wait()
+def stage_kernel(late, zero_hbm, one_hbm, two_hbm, *more):
+    zero_ref, one_ref, two_ref, sems = more[-4:]
+    waits = (lax.axis_index("segment") == 0) & (lax.rem(lax.axis_index("space"), 2) == 0)
+
+    @pl.when(waits == late)
+    def _():
+        pairs = [(zero_hbm, zero_ref)]
+        for source, target in ((one_hbm, one_ref), (two_hbm, two_ref)):
+            pairs += [(source.at[n], target.at[n]) for n in range(2)]
+        copies = [pltpu.make_async_copy(source, target, sems.at[n]) for n, (source, target) in enumerate(pairs)]
+        for copy in copies:
+            copy.start()
+        for copy in copies:
+            copy.wait()
 
 
 def forward_kernel(
@@ -518,7 +523,7 @@
             share(moved, outs)
 
 
-def call(body, operands, shapes, name, spaces=None, scratch=()):
+def call(body, operands, shapes, name, spaces=None, scratch=(), aliases=None):
     spaces = spaces or [pltpu.VMEM] * len(operands)
     operands = [pltpu.with_memory_space_constraint(value, space) for value, space in zip(operands, spaces)]
     return pl.pallas_call(
@@ -527,6 +532,7 @@
         in_specs=[pl.BlockSpec(memory_space=space) for space in spaces],
         out_specs=[pl.BlockSpec(memory_space=pltpu.VMEM) for _ in shapes],
         scratch_shapes=list(scratch),
+        input_output_aliases=aliases or {},
         compiler_params=pltpu.CompilerParams(vmem_limit_bytes=VMEM_LIMIT),
         name=name,
     )(*operands)
@@ -591,9 +597,13 @@
     spaces = [pltpu.HBM] * 3
     on_chip = [pltpu.VMEM(w.shape, w.dtype) for w in stored]
     sems = [pltpu.SemaphoreType.DMA((5,))]
-    weights = call(stage_kernel, stored, on_chip, "stage", spaces, sems)
+    weights = call(functools.partial(stage_kernel, False), stored, on_chip, "stage", spaces, sems)
     whole = shape((coefs + 1, rows, channels), BF16)
     around_all = [call(open_kernel, [mine, partner, straight, cross], [whole, whole], "open")]
+    weights = call(
+        functools.partial(stage_kernel, True), [*stored, *weights, around_all[0][0]], on_chip, "stage",
+        spaces + [pltpu.VMEM] * 4, sems, {3: 0, 4: 1, 5: 2},
+    )
     kept_shapes = [
         shape((2 * rows, edges), BF16), shape((10 * edges, channels), F32), shape((coefs, edges, channels), F32),
     ]

time: 79.3 us -> 78.5 us (0.990)
    ppermute x12, starting transfers between devices: 21.7 us -> 19 us  [hop(): return lax.ppermute(value, axes, ways)]
    ppermute x6, waiting for transfers between devices: 4.9 us -> 6.87 us  [within(): return lax.ppermute(value, axes, ways)]
    ppermute x3, starting transfers between devices: 0.98 us -> 2.92 us  [on_device(): lax.ppermute(both, axes, [(s * slabs + i, t * slabs + j) for s in range(s...]
    ppermute x3, waiting for transfers between devices: 3.56 us -> 1.64 us  [on_device(): lax.ppermute(both, axes, [(s * slabs + i, t * slabs + j) for s in range(s...]
    ppermute x12, waiting for transfers between devices: 29.6 us -> 28.8 us  [hop(): return lax.ppermute(value, axes, ways)]
    pallas_call x12 -> x13, Pallas kernels: 8.66 us -> 8.72 us  [call(): pl.pallas_call(body, out_shape=shapes, in_specs=[pl.BlockSpec(memory_spac...]
  transfers between devices with their start and end apart: 21 -> 21, of which waited for: 12 -> 13; matrix products, arithmetic and copies ran while one was open for 0% -> 0% of each run, Pallas kernels for 3% -> 0%
where the time goes in v16:
time: 78.5 us; the launch traced here: 78.3 us
  waiting for transfers between devices  37.3 us (48%)
  starting transfers between devices  31.6 us (40%)
  Pallas kernels  8.72 us (11%)
    ppermute x12, waiting for transfers between devices, hop(): return lax.ppermute(value, axes, ways)  28.8 us
    ppermute x12, starting transfers between devices, hop(): return lax.ppermute(value, axes, ways)  19 us
    ppermute x6, starting transfers between devices, within(): return lax.ppermute(value, axes, ways)  9.74 us
    pallas_call x13, Pallas kernels, call(): pl.pallas_call(body, out_shape=shapes, in_specs=[pl.BlockSpec(memory_spac...  8.72 us
    ppermute x6, waiting for transfers between devices, within(): return lax.ppermute(value, axes, ways)  6.87 us
    ppermute x3, starting transfers between devices, on_device(): lax.ppermute(both, axes, [(s * slabs + i, t * slabs + j) for s in range(s...  2.92 us
    ppermute x3, waiting for transfers between devices, on_device(): lax.ppermute(both, axes, [(s * slabs + i, t * slabs + j) for s in range(s...  1.64 us
  transfers between devices with their start and end apart: 21, of which 13 were waited for; matrix products, arithmetic and copies ran while one was open for 0% of the time, Pallas kernels for 0%

profile of v16, /device:TPU:0, one launch (start us, length us, event | category | flops | bytes accessed | tf_op | source)
XLA Modules:
  0.0 78.3 jit_solution(76022174672959352)
XLA Ops:
  0.6 1.2 %pack.1 = (bf16[30,8,128]{2,1,0:T(8,128)(2,1)S(1)}, bf16[30,8,128]{2,1,0:T(8,128)(2,1)S(1)}) custom-call(bf16[2,29,8,128]{3,2,1,0:T(8,128)(2,1)} %bitcast.14, f32[3,2,8]{2,1,0:T(2,128)} %bitcast.15, s32[2,8]{1,0:T(2,128)} %species_hbm.1, s32[2,8,8]{2,1,0:T(8,128)} %sources_hbm.1, f32[2,8]{1,0:T(2,128)} %grad_hbm.1, bf16[100,128]{1,0:T(8,128)(2,1)} %table_hbm.1), custom_call_target="tpu_custom_call" | custom-call | tf_op jit(solution)/shard_map/pack/pallas_call | solution.py:529
  1.9 5.1 %collective-permute-start.1 = (bf16[30,8,128]{2,1,0:T(8,128)(2,1)S(1)}, bf16[30,8,128]{2,1,0:T(8,128)(2,1)S(1)}, u32[]{:S(2)}, u32[]{:S(2)}) collective-permute-start(bf16[30,8,128]{2,1,0:T(8,128)(2,1)S(1)} %get-tuple-element.39.mine_ref), channel_id=1, source_target_pairs={{0,6},{1,3},{2,0},{3,5},{4,2},{5,7},{6,4},{7,1},{8,14},{9,11},{10,... | collective-permute-start | bytes 184328 | tf_op jit(solution)/shard_map/ppermute | solution.py:569
  7.0 0.0 collective-permute-start.2
  7.0 0.0 collective-permute-start
  7.0 1.8 %collective-permute-done.1.straight_ref = bf16[30,8,128]{2,1,0:T(8,128)(2,1)S(1)} collective-permute-done((bf16[30,8,128]{2,1,0:T(8,128)(2,1)S(1)}, bf16[30,8,128]{2,1,0:T(8,128)(2,1)S(1)}, u32[]{:S(2)}, u32[]{:S(2)}) %collective-permute-start.1) | collective-permute-done | bytes 61472 | tf_op jit(solution)/shard_map/ppermute | solution.py:569
  8.8 3.6 %collective-permute-done.2.cross_ref = bf16[30,8,128]{2,1,0:T(8,128)(2,1)S(1)} collective-permute-done((bf16[30,8,128]{2,1,0:T(8,128)(2,1)S(1)}, bf16[30,8,128]{2,1,0:T(8,128)(2,1)S(1)}, u32[]{:S(2)}, u32[]{:S(2)}) %collective-permute-start.2) | collective-permute-done | bytes 61472 | tf_op jit(solution)/shard_map/ppermute | solution.py:569
  12.4 0.0 collective-permute-done.partner_ref
  12.4 0.1 open.1
  12.5 0.0 copy-start
  12.5 2.6 %stage.3 = (bf16[896,896]{1,0:T(8,128)(2,1)S(1)}, bf16[2,768,768]{2,1,0:T(8,128)(2,1)S(1)}, bf16[2,640,640]{2,1,0:T(8,128)(2,1)S(1)}) custom-call(bf16[896,896]{1,0:T(8,128)(2,1)} %bitcast.13, bf16[2,768,768]{2,1,0:T(8,128)(2,1)} %bitcast.9, bf16[2,640,640]{2,1,0:T(8,128)(2,1)} %bitcast.11, ...), custom_call_target="tpu_custom_call", output_to_operand_aliasing={{0}: (3, {}), {1}: (4, {}), {2}: (5, {})} | custom-call | tf_op jit(solution)/shard_map/stage/pallas_call | solution.py:529
  15.1 2.0 %forward.3 = (bf16[30,16,128]{2,1,0:T(8,128)(2,1)S(1)}, f32[29,16,128]{2,1,0:T(8,128)S(1)}, bf16[32,128]{1,0:T(8,128)(2,1)S(1)}, f32[1280,128]{1,0:T(8,128)S(1)}, f32[29,128,128]{2,1,0:T(8,128)S(1)}) custom-call(bf16[30,16,128]{2,1,0:T(8,128)(2,1)S(1)} %get-tuple-element.41.more_3_.low_ref, bf16[30,16,128]{2,1,0:T(8,128)(2,1)S(1)} %get-tuple-element.42.high_ref, ...), custom_call_target="tpu_custom_call" | custom-call | tf_op jit(solution)/shard_map/forward/pallas_call | solution.py:529
  17.1 0.1 collective-permute-start.4
  17.2 0.1 collective-permute-start.3
  17.2 5.8 %collective-permute-done.4.high_ref = bf16[30,16,128]{2,1,0:T(8,128)(2,1)S(1)} collective-permute-done((bf16[30,16,128]{2,1,0:T(8,128)(2,1)S(1)}, bf16[30,16,128]{2,1,0:T(8,128)(2,1)S(1)}, u32[]{:S(2)}, u32[]{:S(2)}) %collective-permute-start.4) | collective-permute-done | bytes 122912 | tf_op jit(solution)/shard_map/ppermute | solution.py:583
  23.0 0.4 collective-permute-done.3.low_ref
  23.4 0.0 collective-permute-start.6
  23.4 1.0 %collective-permute-start.5 = (bf16[30,16,128]{2,1,0:T(8,128)(2,1)S(1)}, bf16[30,16,128]{2,1,0:T(8,128)(2,1)S(1)}, u32[]{:S(2)}, u32[]{:S(2)}) collective-permute-start(bf16[30,16,128]{2,1,0:T(8,128)(2,1)S(1)} %get-tuple-element.50), channel_id=1, source_target_pairs={{8,20},{9,21},{12,22},{13,23},{14,18},{15,19},{10,16},{11,17},{16,... | collective-permute-start | bytes 368648 | tf_op jit(solution)/shard_map/ppermute | solution.py:583
  24.5 0.3 collective-permute-done.6.high_ref
  24.8 4.4 %collective-permute-done.5.low_ref = bf16[30,16,128]{2,1,0:T(8,128)(2,1)S(1)} collective-permute-done((bf16[30,16,128]{2,1,0:T(8,128)(2,1)S(1)}, bf16[30,16,128]{2,1,0:T(8,128)(2,1)S(1)}, u32[]{:S(2)}, u32[]{:S(2)}) %collective-permute-start.5) | collective-permute-done | bytes 122912 | tf_op jit(solution)/shard_map/ppermute | solution.py:583
  29.2 0.0 collective-permute-start.8
  29.2 3.1 %collective-permute-start.7 = (bf16[30,16,128]{2,1,0:T(8,128)(2,1)S(1)}, bf16[30,16,128]{2,1,0:T(8,128)(2,1)S(1)}, u32[]{:S(2)}, u32[]{:S(2)}) collective-permute-start(bf16[30,16,128]{2,1,0:T(8,128)(2,1)S(1)} %get-tuple-element.51), channel_id=1, source_target_pairs={{16,24},{17,25},{20,28},{21,29},{22,30},{23,31},{18,26},{19,27},{2... | collective-permute-start | bytes 368648 | tf_op jit(solution)/shard_map/ppermute | solution.py:583
  32.3 0.0 collective-permute-done.8.high_ref
  32.3 3.7 %collective-permute-done.7.low_ref = bf16[30,16,128]{2,1,0:T(8,128)(2,1)S(1)} collective-permute-done((bf16[30,16,128]{2,1,0:T(8,128)(2,1)S(1)}, bf16[30,16,128]{2,1,0:T(8,128)(2,1)S(1)}, u32[]{:S(2)}, u32[]{:S(2)}) %collective-permute-start.7) | collective-permute-done | bytes 122912 | tf_op jit(solution)/shard_map/ppermute | solution.py:583
  36.0 6.4 %collective-permute-start.9 = (bf16[30,16,128]{2,1,0:T(8,128)(2,1)S(1)}, bf16[30,16,128]{2,1,0:T(8,128)(2,1)S(1)}, u32[]{:S(2)}, u32[]{:S(2)}) collective-permute-start(bf16[30,16,128]{2,1,0:T(8,128)(2,1)S(1)} %get-tuple-element.52), channel_id=1, source_target_pairs={{24,16},{25,17},{28,20},{29,21},{30,22},{31,23},{26,18},{27,19},{1... | collective-permute-start | bytes 368648 | tf_op jit(solution)/shard_map/ppermute | solution.py:583
  42.4 0.0 collective-permute-start.10
  42.4 2.4 %collective-permute-done.9.up_low_ref = bf16[30,16,128]{2,1,0:T(8,128)(2,1)S(1)} collective-permute-done((bf16[30,16,128]{2,1,0:T(8,128)(2,1)S(1)}, bf16[30,16,128]{2,1,0:T(8,128)(2,1)S(1)}, u32[]{:S(2)}, u32[]{:S(2)}) %collective-permute-start.9) | collective-permute-done | bytes 122912 | tf_op jit(solution)/shard_map/ppermute | solution.py:583
  44.9 0.0 collective-permute-done.10.up_high_ref
  44.9 5.8 %collective-permute-start.11 = (bf16[30,16,128]{2,1,0:T(8,128)(2,1)S(1)}, bf16[30,16,128]{2,1,0:T(8,128)(2,1)S(1)}, u32[]{:S(2)}, u32[]{:S(2)}) collective-permute-start(bf16[30,16,128]{2,1,0:T(8,128)(2,1)S(1)} %get-tuple-element.58), channel_id=1, source_target_pairs={{16,10},{17,11},{20,8},{21,9},{22,12},{23,13},{18,14},{19,15},{8,0... | collective-permute-start | bytes 368648 | tf_op jit(solution)/shard_map/ppermute | solution.py:583
  50.7 0.0 collective-permute-start.12
  50.7 2.9 %collective-permute-done.11.up_low_ref = bf16[30,16,128]{2,1,0:T(8,128)(2,1)S(1)} collective-permute-done((bf16[30,16,128]{2,1,0:T(8,128)(2,1)S(1)}, bf16[30,16,128]{2,1,0:T(8,128)(2,1)S(1)}, u32[]{:S(2)}, u32[]{:S(2)}) %collective-permute-start.11) | collective-permute-done | bytes 122912 | tf_op jit(solution)/shard_map/ppermute | solution.py:583
  53.6 0.0 collective-permute-done.12.up_high_ref
  53.6 2.5 %collective-permute-start.13 = (bf16[30,16,128]{2,1,0:T(8,128)(2,1)S(1)}, bf16[30,16,128]{2,1,0:T(8,128)(2,1)S(1)}, u32[]{:S(2)}, u32[]{:S(2)}) collective-permute-start(bf16[30,16,128]{2,1,0:T(8,128)(2,1)S(1)} %get-tuple-element.64), channel_id=1, source_target_pairs={{8,0},{9,1},{12,2},{13,3},{14,4},{15,5},{10,6},{11,7},{0,16},{1,17... | collective-permute-start | bytes 368648 | tf_op jit(solution)/shard_map/ppermute | solution.py:583
  56.1 0.0 collective-permute-start.14
  56.1 8.8 %collective-permute-done.13.up_low_ref = bf16[30,16,128]{2,1,0:T(8,128)(2,1)S(1)} collective-permute-done((bf16[30,16,128]{2,1,0:T(8,128)(2,1)S(1)}, bf16[30,16,128]{2,1,0:T(8,128)(2,1)S(1)}, u32[]{:S(2)}, u32[]{:S(2)}) %collective-permute-start.13) | collective-permute-done | bytes 122912 | tf_op jit(solution)/shard_map/ppermute | solution.py:583
  64.9 0.0 collective-permute-done.14.up_high_ref
  64.9 2.1 %backward.5 = (f32[8,128]{1,0:T(8,128)S(1)}, f32[8,128]{1,0:T(8,128)S(1)}, f32[8,128]{1,0:T(8,128)S(1)}, f32[8,128]{1,0:T(8,128)S(1)}) custom-call(bf16[30,16,128]{2,1,0:T(8,128)(2,1)S(1)} %collective-permute-done.13.up_low_ref, bf16[30,16,128]{2,1,0:T(8,128)(2,1)S(1)} %collective-permute-done.14.up_high_ref, ...), custom_call_target="tpu_custom_call" | custom-call | tf_op jit(solution)/shard_map/backward/pallas_call | solution.py:529
  66.9 0.0 collective-permute-start.15
  66.9 1.3 %collective-permute-start.16 = (f32[8,128]{1,0:T(8,128)S(1)}, f32[8,128]{1,0:T(8,128)S(1)}, u32[]{:S(2)}, u32[]{:S(2)}) collective-permute-start(f32[8,128]{1,0:T(8,128)S(1)} %get-tuple-element.72), channel_id=1, source_target_pairs={{0,2},{1,7},{2,4},{3,1},{4,6},{5,3},{6,0},{7,5},{8,10},{9,15},{10,... | collective-permute-start | bytes 12296 | tf_op jit(solution)/shard_map/ppermute | solution.py:569
  68.2 3.4 %collective-permute-start.17 = (f32[8,128]{1,0:T(8,128)S(1)}, f32[8,128]{1,0:T(8,128)S(1)}, u32[]{:S(2)}, u32[]{:S(2)}) collective-permute-start(f32[8,128]{1,0:T(8,128)S(1)} %get-tuple-element.73), channel_id=1, source_target_pairs={{0,7},{1,2},{2,1},{3,4},{4,3},{5,6},{6,5},{7,0},{8,15},{9,10},{10,... | collective-permute-start | bytes 12296 | tf_op jit(solution)/shard_map/ppermute | solution.py:569
  71.6 1.1 %collective-permute-done.16.straight_ref = f32[8,128]{1,0:T(8,128)S(1)} collective-permute-done((f32[8,128]{1,0:T(8,128)S(1)}, f32[8,128]{1,0:T(8,128)S(1)}, u32[]{:S(2)}, u32[]{:S(2)}) %collective-permute-start.16) | collective-permute-done | bytes 4128 | tf_op jit(solution)/shard_map/ppermute | solution.py:569
  72.7 0.3 collective-permute-done.17.cross_ref
  73.1 0.2 collective-permute-start.20
  73.3 0.0 collective-permute-start.19
  73.3 2.7 %collective-permute-start.18 = (f32[16,128]{1,0:T(8,128)S(1)}, f32[16,128]{1,0:T(8,128)S(1)}, u32[]{:S(2)}, u32[]{:S(2)}) collective-permute-start(f32[16,128]{1,0:T(8,128)S(1)} %join.1.refs_0_), channel_id=1, source_target_pairs={{0,8},{1,9},{2,10},{3,11},{4,12},{5,13},{6,14},{7,15},{8,0},{9,1},... | collective-permute-start | bytes 24584 | tf_op jit(solution)/shard_map/ppermute | solution.py:654
  76.0 1.6 %collective-permute-done.20.refs_3_ = f32[16,128]{1,0:T(8,128)S(1)} collective-permute-done((f32[16,128]{1,0:T(8,128)S(1)}, f32[16,128]{1,0:T(8,128)S(1)}, u32[]{:S(2)}, u32[]{:S(2)}) %collective-permute-start.20) | collective-permute-done | bytes 8224 | tf_op jit(solution)/shard_map/ppermute | solution.py:654
  77.6 0.0 collective-permute-done.19.refs_2_
  77.6 0.0 collective-permute-done.18.refs_1_
  77.6 0.7 close.1
  (11 shorter events, 0.1 us)
Async XLA Ops:
  1.9 7.0 %collective-permute-start.1 = (bf16[30,8,128]{2,1,0:T(8,128)(2,1)S(1)}, bf16[30,8,128]{2,1,0:T(8,128)(2,1)S(1)}, u32[]{:S(2)}, u32[]{:S(2)}) collective-permute-start(bf16[30,8,128]{2,1,0:T(8,128)(2,1)S(1)} %get-tuple-element.39.mine_ref), channel_id=1, source_target_pairs={{0,6},{1,3},{2,0},{3,5},{4,2},{5,7},{6,4},{7,1},{8,14},{9,11},{10,... | collective-permute-start | bytes 184328 | tf_op jit(solution)/shard_map/ppermute | solution.py:569
  7.0 5.4 %collective-permute-start.2 = (bf16[30,8,128]{2,1,0:T(8,128)(2,1)S(1)}, bf16[30,8,128]{2,1,0:T(8,128)(2,1)S(1)}, u32[]{:S(2)}, u32[]{:S(2)}) collective-permute-start(bf16[30,8,128]{2,1,0:T(8,128)(2,1)S(1)} %get-tuple-element.40), channel_id=1, source_target_pairs={{0,7},{1,2},{2,1},{3,4},{4,3},{5,6},{6,5},{7,0},{8,15},{9,10},{10,... | collective-permute-start | bytes 184328 | tf_op jit(solution)/shard_map/ppermute | solution.py:569
  7.0 5.4 %collective-permute-start = (bf16[30,8,128]{2,1,0:T(8,128)(2,1)S(1)}, bf16[30,8,128]{2,1,0:T(8,128)(2,1)S(1)}, u32[]{:S(2)}, u32[]{:S(2)}) collective-permute-start(bf16[30,8,128]{2,1,0:T(8,128)(2,1)S(1)} %get-tuple-element.40), channel_id=1, source_target_pairs={{0,1},{1,0},{2,3},{3,2},{4,5},{5,4},{6,7},{7,6},{8,9},{9,8},{10,11... | collective-permute-start | bytes 184328 | tf_op jit(solution)/shard_map/ppermute | solution.py:569
  12.5 2.7 %copy-start = (f32[1,128]{1,0:T(1,128)S(1)}, f32[1,128]{1,0:T(1,128)}, u32[]{:S(2)}) copy-start(f32[1,128]{1,0:T(1,128)} %rate_ref.7) | copy-start | bytes 1540
  17.1 5.9 %collective-permute-start.4 = (bf16[30,16,128]{2,1,0:T(8,128)(2,1)S(1)}, bf16[30,16,128]{2,1,0:T(8,128)(2,1)S(1)}, u32[]{:S(2)}, u32[]{:S(2)}) collective-permute-start(bf16[30,16,128]{2,1,0:T(8,128)(2,1)S(1)} %get-tuple-element.49), channel_id=1, source_target_pairs={{0,10},{1,11},{2,8},{3,9},{4,12},{5,13},{6,14},{7,15},{8,24},{9,25... | collective-permute-start | bytes 368648 | tf_op jit(solution)/shard_map/ppermute | solution.py:583
  17.2 6.2 %collective-permute-start.3 = (bf16[30,16,128]{2,1,0:T(8,128)(2,1)S(1)}, bf16[30,16,128]{2,1,0:T(8,128)(2,1)S(1)}, u32[]{:S(2)}, u32[]{:S(2)}) collective-permute-start(bf16[30,16,128]{2,1,0:T(8,128)(2,1)S(1)} %get-tuple-element.49), channel_id=1, source_target_pairs={{0,8},{1,9},{2,12},{3,13},{4,14},{5,15},{6,10},{7,11},{8,16},{9,17... | collective-permute-start | bytes 368648 | tf_op jit(solution)/shard_map/ppermute | solution.py:583
  23.4 12.6 %copy-start.1 = (f32[128]{0:T(128)S(1)}, f32[128]{0:T(128)}, u32[]{:S(2)}) copy-start(f32[128]{0:T(128)} %param.20) | copy-start | bytes 1540
  23.4 1.3 %collective-permute-start.6 = (bf16[30,16,128]{2,1,0:T(8,128)(2,1)S(1)}, bf16[30,16,128]{2,1,0:T(8,128)(2,1)S(1)}, u32[]{:S(2)}, u32[]{:S(2)}) collective-permute-start(bf16[30,16,128]{2,1,0:T(8,128)(2,1)S(1)} %get-tuple-element.50), channel_id=1, source_target_pairs={{8,16},{9,17},{12,20},{13,21},{14,22},{15,23},{10,18},{11,19},{16,... | collective-permute-start | bytes 368648 | tf_op jit(solution)/shard_map/ppermute | solution.py:583
  23.4 5.7 %collective-permute-start.5 = (bf16[30,16,128]{2,1,0:T(8,128)(2,1)S(1)}, bf16[30,16,128]{2,1,0:T(8,128)(2,1)S(1)}, u32[]{:S(2)}, u32[]{:S(2)}) collective-permute-start(bf16[30,16,128]{2,1,0:T(8,128)(2,1)S(1)} %get-tuple-element.50), channel_id=1, source_target_pairs={{8,20},{9,21},{12,22},{13,23},{14,18},{15,19},{10,16},{11,17},{16,... | collective-permute-start | bytes 368648 | tf_op jit(solution)/shard_map/ppermute | solution.py:583
  29.2 3.1 %collective-permute-start.8 = (bf16[30,16,128]{2,1,0:T(8,128)(2,1)S(1)}, bf16[30,16,128]{2,1,0:T(8,128)(2,1)S(1)}, u32[]{:S(2)}, u32[]{:S(2)}) collective-permute-start(bf16[30,16,128]{2,1,0:T(8,128)(2,1)S(1)} %get-tuple-element.51), channel_id=1, source_target_pairs={{16,26},{17,27},{20,24},{21,25},{22,28},{23,29},{18,30},{19,31},{2... | collective-permute-start | bytes 368648 | tf_op jit(solution)/shard_map/ppermute | solution.py:583
  29.2 6.9 %collective-permute-start.7 = (bf16[30,16,128]{2,1,0:T(8,128)(2,1)S(1)}, bf16[30,16,128]{2,1,0:T(8,128)(2,1)S(1)}, u32[]{:S(2)}, u32[]{:S(2)}) collective-permute-start(bf16[30,16,128]{2,1,0:T(8,128)(2,1)S(1)} %get-tuple-element.51), channel_id=1, source_target_pairs={{16,24},{17,25},{20,28},{21,29},{22,30},{23,31},{18,26},{19,27},{2... | collective-permute-start | bytes 368648 | tf_op jit(solution)/shard_map/ppermute | solution.py:583
  36.0 8.8 %collective-permute-start.9 = (bf16[30,16,128]{2,1,0:T(8,128)(2,1)S(1)}, bf16[30,16,128]{2,1,0:T(8,128)(2,1)S(1)}, u32[]{:S(2)}, u32[]{:S(2)}) collective-permute-start(bf16[30,16,128]{2,1,0:T(8,128)(2,1)S(1)} %get-tuple-element.52), channel_id=1, source_target_pairs={{24,16},{25,17},{28,20},{29,21},{30,22},{31,23},{26,18},{27,19},{1... | collective-permute-start | bytes 368648 | tf_op jit(solution)/shard_map/ppermute | solution.py:583
  42.4 2.4 %collective-permute-start.10 = (bf16[30,16,128]{2,1,0:T(8,128)(2,1)S(1)}, bf16[30,16,128]{2,1,0:T(8,128)(2,1)S(1)}, u32[]{:S(2)}, u32[]{:S(2)}) collective-permute-start(bf16[30,16,128]{2,1,0:T(8,128)(2,1)S(1)} %get-tuple-element.53), channel_id=1, source_target_pairs={{24,20},{25,21},{28,22},{29,23},{30,18},{31,19},{26,16},{27,17},{1... | collective-permute-start | bytes 368648 | tf_op jit(solution)/shard_map/ppermute | solution.py:583
  44.9 8.7 %collective-permute-start.11 = (bf16[30,16,128]{2,1,0:T(8,128)(2,1)S(1)}, bf16[30,16,128]{2,1,0:T(8,128)(2,1)S(1)}, u32[]{:S(2)}, u32[]{:S(2)}) collective-permute-start(bf16[30,16,128]{2,1,0:T(8,128)(2,1)S(1)} %get-tuple-element.58), channel_id=1, source_target_pairs={{16,10},{17,11},{20,8},{21,9},{22,12},{23,13},{18,14},{19,15},{8,0... | collective-permute-start | bytes 368648 | tf_op jit(solution)/shard_map/ppermute | solution.py:583
  50.7 2.9 %collective-permute-start.12 = (bf16[30,16,128]{2,1,0:T(8,128)(2,1)S(1)}, bf16[30,16,128]{2,1,0:T(8,128)(2,1)S(1)}, u32[]{:S(2)}, u32[]{:S(2)}) collective-permute-start(bf16[30,16,128]{2,1,0:T(8,128)(2,1)S(1)} %get-tuple-element.59), channel_id=1, source_target_pairs={{16,8},{17,9},{20,12},{21,13},{22,14},{23,15},{18,10},{19,11},{8,2... | collective-permute-start | bytes 368648 | tf_op jit(solution)/shard_map/ppermute | solution.py:583
  53.6 11.3 %collective-permute-start.13 = (bf16[30,16,128]{2,1,0:T(8,128)(2,1)S(1)}, bf16[30,16,128]{2,1,0:T(8,128)(2,1)S(1)}, u32[]{:S(2)}, u32[]{:S(2)}) collective-permute-start(bf16[30,16,128]{2,1,0:T(8,128)(2,1)S(1)} %get-tuple-element.64), channel_id=1, source_target_pairs={{8,0},{9,1},{12,2},{13,3},{14,4},{15,5},{10,6},{11,7},{0,16},{1,17... | collective-permute-start | bytes 368648 | tf_op jit(solution)/shard_map/ppermute | solution.py:583
  56.1 8.8 %collective-permute-start.14 = (bf16[30,16,128]{2,1,0:T(8,128)(2,1)S(1)}, bf16[30,16,128]{2,1,0:T(8,128)(2,1)S(1)}, u32[]{:S(2)}, u32[]{:S(2)}) collective-permute-start(bf16[30,16,128]{2,1,0:T(8,128)(2,1)S(1)} %get-tuple-element.65), channel_id=1, source_target_pairs={{8,2},{9,3},{12,4},{13,5},{14,6},{15,7},{10,0},{11,1},{0,24},{1,25... | collective-permute-start | bytes 368648 | tf_op jit(solution)/shard_map/ppermute | solution.py:583
  66.9 4.6 %collective-permute-start.15 = (f32[8,128]{1,0:T(8,128)S(1)}, f32[8,128]{1,0:T(8,128)S(1)}, u32[]{:S(2)}, u32[]{:S(2)}) collective-permute-start(f32[8,128]{1,0:T(8,128)S(1)} %get-tuple-element.71), channel_id=1, source_target_pairs={{0,1},{1,0},{2,3},{3,2},{4,5},{5,4},{6,7},{7,6},{8,9},{9,8},{10,11... | collective-permute-start | bytes 12296 | tf_op jit(solution)/shard_map/ppermute | solution.py:569
  66.9 5.8 %collective-permute-start.16 = (f32[8,128]{1,0:T(8,128)S(1)}, f32[8,128]{1,0:T(8,128)S(1)}, u32[]{:S(2)}, u32[]{:S(2)}) collective-permute-start(f32[8,128]{1,0:T(8,128)S(1)} %get-tuple-element.72), channel_id=1, source_target_pairs={{0,2},{1,7},{2,4},{3,1},{4,6},{5,3},{6,0},{7,5},{8,10},{9,15},{10,... | collective-permute-start | bytes 12296 | tf_op jit(solution)/shard_map/ppermute | solution.py:569
  68.2 4.8 %collective-permute-start.17 = (f32[8,128]{1,0:T(8,128)S(1)}, f32[8,128]{1,0:T(8,128)S(1)}, u32[]{:S(2)}, u32[]{:S(2)}) collective-permute-start(f32[8,128]{1,0:T(8,128)S(1)} %get-tuple-element.73), channel_id=1, source_target_pairs={{0,7},{1,2},{2,1},{3,4},{4,3},{5,6},{6,5},{7,0},{8,15},{9,10},{10,... | collective-permute-start | bytes 12296 | tf_op jit(solution)/shard_map/ppermute | solution.py:569
  73.1 4.5 %collective-permute-start.20 = (f32[16,128]{1,0:T(8,128)S(1)}, f32[16,128]{1,0:T(8,128)S(1)}, u32[]{:S(2)}, u32[]{:S(2)}) collective-permute-start(f32[16,128]{1,0:T(8,128)S(1)} %join.1.refs_0_), channel_id=1, source_target_pairs={{0,24},{1,25},{2,26},{3,27},{4,28},{5,29},{6,30},{7,31},{8,9},{9,8... | collective-permute-start | bytes 24584 | tf_op jit(solution)/shard_map/ppermute | solution.py:654
  73.3 4.3 %collective-permute-start.19 = (f32[16,128]{1,0:T(8,128)S(1)}, f32[16,128]{1,0:T(8,128)S(1)}, u32[]{:S(2)}, u32[]{:S(2)}) collective-permute-start(f32[16,128]{1,0:T(8,128)S(1)} %join.1.refs_0_), channel_id=1, source_target_pairs={{0,16},{1,17},{2,18},{3,19},{4,20},{5,21},{6,22},{7,23},{8,9},{9,8... | collective-permute-start | bytes 24584 | tf_op jit(solution)/shard_map/ppermute | solution.py:654
  73.3 4.3 %collective-permute-start.18 = (f32[16,128]{1,0:T(8,128)S(1)}, f32[16,128]{1,0:T(8,128)S(1)}, u32[]{:S(2)}, u32[]{:S(2)}) collective-permute-start(f32[16,128]{1,0:T(8,128)S(1)} %join.1.refs_0_), channel_id=1, source_target_pairs={{0,8},{1,9},{2,10},{3,11},{4,12},{5,13},{6,14},{7,15},{8,0},{9,1},... | collective-permute-start | bytes 24584 | tf_op jit(solution)/shard_map/ppermute | solution.py:654

commit v17 on v16

--- a/solution.py
+++ b/solution.py
@@ -45,16 +45,12 @@
     return lax.dot_general(a, b, (((1,), (0,)), ((), ())), preferred_element_type=F32)
 
 
-def dot_t(a, b):
-    return lax.dot_general(a, b, (((1,), (1,)), ((), ())), preferred_element_type=F32)
-
-
-def fine_dot(value, weights, product):
+def fine_dot(value, weights):
     rows = value.shape[0]
     stacked = jnp.concatenate(split(value), axis=0)
     outs = []
     for weight in weights:
-        out = product(stacked, weight)
+        out = dot(stacked, weight)
         outs.append(out[:rows] + out[rows:])
     return outs
 
@@ -117,7 +113,7 @@
         [pool(scaled(group[:, sz.cols(k)], k), rows) for k in range(sz.zero)], axis=1
     )
     kept = 1 if last else sz.zero
-    (zout,) = fine_dot(zin, [zero_ref[:, sz.cols(0, kept)]], dot)
+    (zout,) = fine_dot(zin, [zero_ref[:, sz.cols(0, kept)]])
     for k in range(kept):
         pooled[k] = zout[:, sz.cols(k)] * factor
     for order in range(2):
@@ -135,7 +131,7 @@
         both = jnp.concatenate(
             [jnp.concatenate(res, axis=1), jnp.concatenate(ims, axis=1)], axis=0
         )
-        a, b = fine_dot(both, [weight_ref[0], weight_ref[1]], dot)
+        a, b = fine_dot(both, [weight_ref[0], weight_ref[1]])
         out_re = (a[:rows] - b[rows:]) * factor
         out_im = (b[:rows] + a[rows:]) * factor
         for k in range(count):
@@ -179,7 +175,7 @@
 
     radial = geo_at(geo_ref, 0, edges)
     kept = 1 if last else sz.zero
-    (dz,) = fine_dot(jnp.concatenate(d_pooled[:kept], axis=1), [zero_ref[:, sz.cols(0, kept)]], dot_t)
+    (dz,) = fine_dot(jnp.concatenate(d_pooled[:kept], axis=1), [zero_ref[sz.cols(0, kept), :]])
 
     def spread(block):
         return jnp.concatenate([block] * (edges // rows), axis=0)
@@ -217,7 +213,7 @@
             ],
             axis=0,
         )
-        a, b = fine_dot(both, [weight_ref[0], weight_ref[1]], dot_t)
+        a, b = fine_dot(both, [weight_ref[0], weight_ref[1]])
         d_re = a[:rows] + b[rows:]
         d_im = a[rows:] - b[:rows]
         q_cos = jnp.zeros((edges, sz.c), F32)
@@ -442,20 +438,33 @@
     return numbers[per_slab : per_slab + rows]
 
 
+def bring(pairs, sems):
+    copies = [pltpu.make_async_copy(source, target, sems.at[n]) for n, (source, target) in enumerate(pairs)]
+    for copy in copies:
+        copy.start()
+    for copy in copies:
+        copy.wait()
+
+
 def stage_kernel(late, zero_hbm, one_hbm, two_hbm, *more):
-    zero_ref, one_ref, two_ref, sems = more[-4:]
+    zero_ref, one_ref, two_ref, *vectors, sems = more[4:] if late else more[2:]
     waits = (lax.axis_index("segment") == 0) & (lax.rem(lax.axis_index("space"), 2) == 0)
+    if not late:
+        bring(list(zip(more[:2], vectors)), sems)
 
     @pl.when(waits == late)
     def _():
         pairs = [(zero_hbm, zero_ref)]
         for source, target in ((one_hbm, one_ref), (two_hbm, two_ref)):
             pairs += [(source.at[n], target.at[n]) for n in range(2)]
-        copies = [pltpu.make_async_copy(source, target, sems.at[n]) for n, (source, target) in enumerate(pairs)]
-        for copy in copies:
-            copy.start()
-        for copy in copies:
-            copy.wait()
+        bring(pairs, sems)
+
+
+def flip_kernel(zero_ref, one_ref, two_ref, _, zero_t_ref, one_t_ref, two_t_ref):
+    zero_t_ref[...] = jnp.transpose(zero_ref[...])
+    for n in range(2):
+        one_t_ref[n] = jnp.transpose(one_ref[n])
+        two_t_ref[n] = jnp.transpose(two_ref[n])
 
 
 def forward_kernel(
@@ -478,7 +487,8 @@
 
 
 def turn_kernel(
-    tick, sz, slabs, neighbours, low_ref, high_ref, rate_ref, zero_ref, one_ref, two_ref, read_ref,
+    tick, sz, slabs, neighbours, low_ref, high_ref, rate_ref, zero_ref, one_ref, two_ref,
+    zero_t_ref, one_t_ref, two_t_ref, read_ref,
     back_low_ref, back_high_ref, hot_ref, hot_t_ref, geo_ref, faded_ref
 ):
     @pl.when(lax.axis_index("segment") == tick)
@@ -498,7 +508,7 @@
         energy = around(jnp.where(lane == 3, energy, 0.0), rows // 2)
         upstream = [own[:, 3:4] * read * (gate + updated * gate * (1.0 - gate))]
         moved = backward(
-            upstream, pooled, hot_t_ref, geo_ref, faded_ref, zero_ref, one_ref, two_ref, sz, rows, True, outs
+            upstream, pooled, hot_t_ref, geo_ref, faded_ref, zero_t_ref, one_t_ref, two_t_ref, sz, rows, True, outs
         )
         send_back(moved + energy, outs, sz)
 
@@ -597,7 +607,11 @@
     spaces = [pltpu.HBM] * 3
     on_chip = [pltpu.VMEM(w.shape, w.dtype) for w in stored]
     sems = [pltpu.SemaphoreType.DMA((5,))]
-    weights = call(functools.partial(stage_kernel, False), stored, on_chip, "stage", spaces, sems)
+    vectors = [radial_rate, read_weight.reshape(1, channels)]
+    *weights, rate, read = call(
+        functools.partial(stage_kernel, False), stored + vectors,
+        on_chip + [pltpu.VMEM(v.shape, v.dtype) for v in vectors], "stage", [pltpu.HBM] * 5, sems,
+    )
     whole = shape((coefs + 1, rows, channels), BF16)
     around_all = [call(open_kernel, [mine, partner, straight, cross], [whole, whole], "open")]
     weights = call(
@@ -612,19 +626,21 @@
     for tick in range(segments - 1):
         out, *residuals = call(
             functools.partial(forward_kernel, tick, sz, slabs, neighbours),
-            [*around_all[tick], radial_rate, *weights],
+            [*around_all[tick], rate, *weights],
             [whole, shape((coefs, rows, channels), F32), *kept_shapes],
             "forward",
             scratch=hot,
         )
         kept.append(residuals)
+        if tick == 0:
+            flipped = call(flip_kernel, [*weights, out], on_chip, "flip")
         ways = (1, 0) if tick % 2 else (0, -1)
         around_all.append([hop(out, tick, tick + 1, by, way) for way, by in enumerate(ways)])
     final = segments - 1
     slab_sums = shape((per_slab, channels), F32)
     parts = call(
         functools.partial(turn_kernel, final, sz, slabs, neighbours),
-        [*around_all[final], radial_rate, *weights, read_weight.reshape(1, channels)],
+        [*around_all[final], rate, *weights, *flipped, read],
         [whole, whole],
         "turn",
         scratch=hot + [pltpu.VMEM(v.shape, v.dtype) for v in kept_shapes],
@@ -635,7 +651,7 @@
         pooled, *residuals = kept[tick]
         parts = call(
             functools.partial(backward_kernel, tick, sz),
-            [*up, pooled, *residuals, *weights],
+            [*up, pooled, *residuals, *flipped],
             [whole, whole] if tick else [slab_sums] * 4,
             "backward",
         )

time: 78.5 us -> 75.7 us (0.964)
  starting transfers between devices: 31.6 us -> 29.1 us
  waiting for transfers between devices: 37.3 us -> 35.4 us
  Pallas kernels: 8.72 us -> 10.2 us
    ppermute x12, waiting for transfers between devices: 28.8 us -> 26.3 us  [hop(): return lax.ppermute(value, axes, ways)]
    ppermute x12, starting transfers between devices: 19 us -> 17.3 us  [hop(): return lax.ppermute(value, axes, ways)]
    pallas_call x13 -> x14, Pallas kernels: 8.72 us -> 10.2 us  [call(): pl.pallas_call(body, out_shape=shapes, in_specs=[pl.BlockSpec(memory_spac...]
  transfers between devices with their start and end apart: 21 -> 21, of which waited for: 13 -> 13; matrix products, arithmetic and copies ran while one was open for 0% -> 0% of each run, Pallas kernels for 0% -> 3%
where the time goes in v17:
time: 75.7 us; the launch traced here: 75.5 us
  waiting for transfers between devices  35.4 us (47%)
  starting transfers between devices  29.1 us (38%)
  Pallas kernels  10.2 us (13%)
    ppermute x12, waiting for transfers between devices, hop(): return lax.ppermute(value, axes, ways)  26.3 us
    ppermute x12, starting transfers between devices, hop(): return lax.ppermute(value, axes, ways)  17.3 us
    pallas_call x14, Pallas kernels, call(): pl.pallas_call(body, out_shape=shapes, in_specs=[pl.BlockSpec(memory_spac...  10.2 us
    ppermute x6, starting transfers between devices, within(): return lax.ppermute(value, axes, ways)  9.55 us
    ppermute x6, waiting for transfers between devices, within(): return lax.ppermute(value, axes, ways)  6.92 us
    ppermute x3, starting transfers between devices, on_device(): lax.ppermute(both, axes, [(s * slabs + i, t * slabs + j) for s in range(s...  2.31 us
    ppermute x3, waiting for transfers between devices, on_device(): lax.ppermute(both, axes, [(s * slabs + i, t * slabs + j) for s in range(s...  2.23 us
  transfers between devices with their start and end apart: 21, of which 13 were waited for; matrix products, arithmetic and copies ran while one was open for 0% of the time, Pallas kernels for 3%

profile of v17, /device:TPU:0, one launch (start us, length us, event | category | flops | bytes accessed | tf_op | source)
XLA Modules:
  0.0 75.5 jit_solution(16973376775274628288)
XLA Ops:
  0.6 1.2 %pack.1 = (bf16[30,8,128]{2,1,0:T(8,128)(2,1)S(1)}, bf16[30,8,128]{2,1,0:T(8,128)(2,1)S(1)}) custom-call(bf16[2,29,8,128]{3,2,1,0:T(8,128)(2,1)} %bitcast.13, f32[3,2,8]{2,1,0:T(2,128)} %bitcast.14, s32[2,8]{1,0:T(2,128)} %species_hbm.1, s32[2,8,8]{2,1,0:T(8,128)} %sources_hbm.1, f32[2,8]{1,0:T(2,128)} %grad_hbm.1, bf16[100,128]{1,0:T(8,128)(2,1)} %table_hbm.1), custom_call_target="tpu_custom_call" | custom-call | tf_op jit(solution)/shard_map/pack/pallas_call | solution.py:539
  1.9 5.1 %collective-permute-start.1 = (bf16[30,8,128]{2,1,0:T(8,128)(2,1)S(1)}, bf16[30,8,128]{2,1,0:T(8,128)(2,1)S(1)}, u32[]{:S(2)}, u32[]{:S(2)}) collective-permute-start(bf16[30,8,128]{2,1,0:T(8,128)(2,1)S(1)} %get-tuple-element.44.mine_ref), channel_id=1, source_target_pairs={{0,6},{1,3},{2,0},{3,5},{4,2},{5,7},{6,4},{7,1},{8,14},{9,11},{10,... | collective-permute-start | bytes 184328 | tf_op jit(solution)/shard_map/ppermute | solution.py:579
  7.0 0.0 collective-permute-start.2
  7.0 0.0 collective-permute-start
  7.0 0.7 stage.2
  7.7 1.1 %collective-permute-done.1.straight_ref = bf16[30,8,128]{2,1,0:T(8,128)(2,1)S(1)} collective-permute-done((bf16[30,8,128]{2,1,0:T(8,128)(2,1)S(1)}, bf16[30,8,128]{2,1,0:T(8,128)(2,1)S(1)}, u32[]{:S(2)}, u32[]{:S(2)}) %collective-permute-start.1) | collective-permute-done | bytes 61472 | tf_op jit(solution)/shard_map/ppermute | solution.py:579
  8.8 3.6 %collective-permute-done.2.cross_ref = bf16[30,8,128]{2,1,0:T(8,128)(2,1)S(1)} collective-permute-done((bf16[30,8,128]{2,1,0:T(8,128)(2,1)S(1)}, bf16[30,8,128]{2,1,0:T(8,128)(2,1)S(1)}, u32[]{:S(2)}, u32[]{:S(2)}) %collective-permute-start.2) | collective-permute-done | bytes 61472 | tf_op jit(solution)/shard_map/ppermute | solution.py:579
  12.4 0.0 collective-permute-done.partner_ref
  12.4 0.1 open.1
  12.5 2.6 %stage.3 = (bf16[896,896]{1,0:T(8,128)(2,1)S(1)}, bf16[2,768,768]{2,1,0:T(8,128)(2,1)S(1)}, bf16[2,640,640]{2,1,0:T(8,128)(2,1)S(1)}) custom-call(bf16[896,896]{1,0:T(8,128)(2,1)} %bitcast.12, bf16[2,768,768]{2,1,0:T(8,128)(2,1)} %bitcast.8, bf16[2,640,640]{2,1,0:T(8,128)(2,1)} %bitcast.10, ...), custom_call_target="tpu_custom_call", output_to_operand_aliasing={{0}: (3, {}), {1}: (4, {}), {2}: (5, {})} | custom-call | tf_op jit(solution)/shard_map/stage/pallas_call | solution.py:539
  15.1 2.0 %forward.3 = (bf16[30,16,128]{2,1,0:T(8,128)(2,1)S(1)}, f32[29,16,128]{2,1,0:T(8,128)S(1)}, bf16[32,128]{1,0:T(8,128)(2,1)S(1)}, f32[1280,128]{1,0:T(8,128)S(1)}, f32[29,128,128]{2,1,0:T(8,128)S(1)}) custom-call(bf16[30,16,128]{2,1,0:T(8,128)(2,1)S(1)} %get-tuple-element.46.more_3_.low_ref, bf16[30,16,128]{2,1,0:T(8,128)(2,1)S(1)} %get-tuple-element.47.high_ref, ...), custom_call_target="tpu_custom_call" | custom-call | tf_op jit(solution)/shard_map/forward/pallas_call | solution.py:539
  17.1 0.1 collective-permute-start.4
  17.1 0.1 collective-permute-start.3
  17.2 5.8 %collective-permute-done.4.high_ref = bf16[30,16,128]{2,1,0:T(8,128)(2,1)S(1)} collective-permute-done((bf16[30,16,128]{2,1,0:T(8,128)(2,1)S(1)}, bf16[30,16,128]{2,1,0:T(8,128)(2,1)S(1)}, u32[]{:S(2)}, u32[]{:S(2)}) %collective-permute-start.4) | collective-permute-done | bytes 122912 | tf_op jit(solution)/shard_map/ppermute | solution.py:593
  23.0 0.4 collective-permute-done.3.low_ref
  23.4 0.0 collective-permute-start.6
  23.4 1.0 %collective-permute-start.5 = (bf16[30,16,128]{2,1,0:T(8,128)(2,1)S(1)}, bf16[30,16,128]{2,1,0:T(8,128)(2,1)S(1)}, u32[]{:S(2)}, u32[]{:S(2)}) collective-permute-start(bf16[30,16,128]{2,1,0:T(8,128)(2,1)S(1)} %get-tuple-element.56), channel_id=1, source_target_pairs={{8,20},{9,21},{12,22},{13,23},{14,18},{15,19},{10,16},{11,17},{16,... | collective-permute-start | bytes 368648 | tf_op jit(solution)/shard_map/ppermute | solution.py:593
  24.4 0.3 collective-permute-done.6.high_ref
  24.7 4.4 %collective-permute-done.5.low_ref = bf16[30,16,128]{2,1,0:T(8,128)(2,1)S(1)} collective-permute-done((bf16[30,16,128]{2,1,0:T(8,128)(2,1)S(1)}, bf16[30,16,128]{2,1,0:T(8,128)(2,1)S(1)}, u32[]{:S(2)}, u32[]{:S(2)}) %collective-permute-start.5) | collective-permute-done | bytes 122912 | tf_op jit(solution)/shard_map/ppermute | solution.py:593
  29.1 0.0 collective-permute-start.8
  29.1 3.1 %collective-permute-start.7 = (bf16[30,16,128]{2,1,0:T(8,128)(2,1)S(1)}, bf16[30,16,128]{2,1,0:T(8,128)(2,1)S(1)}, u32[]{:S(2)}, u32[]{:S(2)}) collective-permute-start(bf16[30,16,128]{2,1,0:T(8,128)(2,1)S(1)} %get-tuple-element.57), channel_id=1, source_target_pairs={{16,24},{17,25},{20,28},{21,29},{22,30},{23,31},{18,26},{19,27},{2... | collective-permute-start | bytes 368648 | tf_op jit(solution)/shard_map/ppermute | solution.py:593
  32.2 1.5 %flip.1 = (bf16[896,896]{1,0:T(8,128)(2,1)S(1)}, bf16[2,768,768]{2,1,0:T(8,128)(2,1)S(1)}, bf16[2,640,640]{2,1,0:T(8,128)(2,1)S(1)}) custom-call(bf16[896,896]{1,0:T(8,128)(2,1)S(1)} %get-tuple-element.52.zero_ref, bf16[2,768,768]{2,1,0:T(8,128)(2,1)S(1)} %get-tuple-element.53.one_ref, bf16[2,640,640]{2,1,0:T(8,128)(2,1)S(1)} %get-tuple-element.54.two_ref, ...), custom_call_target="tpu_custom_call" | custom-call | tf_op jit(solution)/shard_map/flip/pallas_call | solution.py:539
  33.7 0.0 collective-permute-done.8.high_ref
  33.7 2.2 %collective-permute-done.7.low_ref = bf16[30,16,128]{2,1,0:T(8,128)(2,1)S(1)} collective-permute-done((bf16[30,16,128]{2,1,0:T(8,128)(2,1)S(1)}, bf16[30,16,128]{2,1,0:T(8,128)(2,1)S(1)}, u32[]{:S(2)}, u32[]{:S(2)}) %collective-permute-start.7) | collective-permute-done | bytes 122912 | tf_op jit(solution)/shard_map/ppermute | solution.py:593
  36.0 5.8 %collective-permute-start.9 = (bf16[30,16,128]{2,1,0:T(8,128)(2,1)S(1)}, bf16[30,16,128]{2,1,0:T(8,128)(2,1)S(1)}, u32[]{:S(2)}, u32[]{:S(2)}) collective-permute-start(bf16[30,16,128]{2,1,0:T(8,128)(2,1)S(1)} %get-tuple-element.62), channel_id=1, source_target_pairs={{24,16},{25,17},{28,20},{29,21},{30,22},{31,23},{26,18},{27,19},{1... | collective-permute-start | bytes 368648 | tf_op jit(solution)/shard_map/ppermute | solution.py:593
  41.8 0.0 collective-permute-start.10
  41.8 2.4 %collective-permute-done.9.up_low_ref = bf16[30,16,128]{2,1,0:T(8,128)(2,1)S(1)} collective-permute-done((bf16[30,16,128]{2,1,0:T(8,128)(2,1)S(1)}, bf16[30,16,128]{2,1,0:T(8,128)(2,1)S(1)}, u32[]{:S(2)}, u32[]{:S(2)}) %collective-permute-start.9) | collective-permute-done | bytes 122912 | tf_op jit(solution)/shard_map/ppermute | solution.py:593
  44.2 0.0 collective-permute-done.10.up_high_ref
  44.2 4.7 %collective-permute-start.11 = (bf16[30,16,128]{2,1,0:T(8,128)(2,1)S(1)}, bf16[30,16,128]{2,1,0:T(8,128)(2,1)S(1)}, u32[]{:S(2)}, u32[]{:S(2)}) collective-permute-start(bf16[30,16,128]{2,1,0:T(8,128)(2,1)S(1)} %get-tuple-element.68), channel_id=1, source_target_pairs={{16,10},{17,11},{20,8},{21,9},{22,12},{23,13},{18,14},{19,15},{8,0... | collective-permute-start | bytes 368648 | tf_op jit(solution)/shard_map/ppermute | solution.py:593
  48.9 0.0 collective-permute-start.12
  48.9 2.4 %collective-permute-done.11.up_low_ref = bf16[30,16,128]{2,1,0:T(8,128)(2,1)S(1)} collective-permute-done((bf16[30,16,128]{2,1,0:T(8,128)(2,1)S(1)}, bf16[30,16,128]{2,1,0:T(8,128)(2,1)S(1)}, u32[]{:S(2)}, u32[]{:S(2)}) %collective-permute-start.11) | collective-permute-done | bytes 122912 | tf_op jit(solution)/shard_map/ppermute | solution.py:593
  51.4 0.0 collective-permute-done.12.up_high_ref
  51.4 2.5 %collective-permute-start.13 = (bf16[30,16,128]{2,1,0:T(8,128)(2,1)S(1)}, bf16[30,16,128]{2,1,0:T(8,128)(2,1)S(1)}, u32[]{:S(2)}, u32[]{:S(2)}) collective-permute-start(bf16[30,16,128]{2,1,0:T(8,128)(2,1)S(1)} %get-tuple-element.74), channel_id=1, source_target_pairs={{8,0},{9,1},{12,2},{13,3},{14,4},{15,5},{10,6},{11,7},{0,16},{1,17... | collective-permute-start | bytes 368648 | tf_op jit(solution)/shard_map/ppermute | solution.py:593
  53.9 0.0 collective-permute-start.14
  53.9 8.3 %collective-permute-done.13.up_low_ref = bf16[30,16,128]{2,1,0:T(8,128)(2,1)S(1)} collective-permute-done((bf16[30,16,128]{2,1,0:T(8,128)(2,1)S(1)}, bf16[30,16,128]{2,1,0:T(8,128)(2,1)S(1)}, u32[]{:S(2)}, u32[]{:S(2)}) %collective-permute-start.13) | collective-permute-done | bytes 122912 | tf_op jit(solution)/shard_map/ppermute | solution.py:593
  62.2 0.0 collective-permute-done.14.up_high_ref
  62.2 1.4 %backward.5 = (f32[8,128]{1,0:T(8,128)S(1)}, f32[8,128]{1,0:T(8,128)S(1)}, f32[8,128]{1,0:T(8,128)S(1)}, f32[8,128]{1,0:T(8,128)S(1)}) custom-call(bf16[30,16,128]{2,1,0:T(8,128)(2,1)S(1)} %collective-permute-done.13.up_low_ref, bf16[30,16,128]{2,1,0:T(8,128)(2,1)S(1)} %collective-permute-done.14.up_high_ref, ...), custom_call_target="tpu_custom_call" | custom-call | tf_op jit(solution)/shard_map/backward/pallas_call | solution.py:539
  63.6 0.0 collective-permute-start.15
  63.6 1.8 %collective-permute-start.16 = (f32[8,128]{1,0:T(8,128)S(1)}, f32[8,128]{1,0:T(8,128)S(1)}, u32[]{:S(2)}, u32[]{:S(2)}) collective-permute-start(f32[8,128]{1,0:T(8,128)S(1)} %get-tuple-element.82), channel_id=1, source_target_pairs={{0,2},{1,7},{2,4},{3,1},{4,6},{5,3},{6,0},{7,5},{8,10},{9,15},{10,... | collective-permute-start | bytes 12296 | tf_op jit(solution)/shard_map/ppermute | solution.py:579
  65.4 2.6 %collective-permute-start.17 = (f32[8,128]{1,0:T(8,128)S(1)}, f32[8,128]{1,0:T(8,128)S(1)}, u32[]{:S(2)}, u32[]{:S(2)}) collective-permute-start(f32[8,128]{1,0:T(8,128)S(1)} %get-tuple-element.83), channel_id=1, source_target_pairs={{0,7},{1,2},{2,1},{3,4},{4,3},{5,6},{6,5},{7,0},{8,15},{9,10},{10,... | collective-permute-start | bytes 12296 | tf_op jit(solution)/shard_map/ppermute | solution.py:579
  68.0 0.0 collective-permute-done.15.theirs_ref
  68.0 1.4 %collective-permute-done.16.straight_ref = f32[8,128]{1,0:T(8,128)S(1)} collective-permute-done((f32[8,128]{1,0:T(8,128)S(1)}, f32[8,128]{1,0:T(8,128)S(1)}, u32[]{:S(2)}, u32[]{:S(2)}) %collective-permute-start.16) | collective-permute-done | bytes 4128 | tf_op jit(solution)/shard_map/ppermute | solution.py:579
  69.5 0.8 %collective-permute-done.17.cross_ref = f32[8,128]{1,0:T(8,128)S(1)} collective-permute-done((f32[8,128]{1,0:T(8,128)S(1)}, f32[8,128]{1,0:T(8,128)S(1)}, u32[]{:S(2)}, u32[]{:S(2)}) %collective-permute-start.17) | collective-permute-done | bytes 4128 | tf_op jit(solution)/shard_map/ppermute | solution.py:579
  70.2 0.0 collective-permute-start.20
  70.2 0.1 collective-permute-start.19
  70.3 2.2 %collective-permute-start.18 = (f32[16,128]{1,0:T(8,128)S(1)}, f32[16,128]{1,0:T(8,128)S(1)}, u32[]{:S(2)}, u32[]{:S(2)}) collective-permute-start(f32[16,128]{1,0:T(8,128)S(1)} %join.1.refs_0_), channel_id=1, source_target_pairs={{0,8},{1,9},{2,10},{3,11},{4,12},{5,13},{6,14},{7,15},{8,0},{9,1},... | collective-permute-start | bytes 24584 | tf_op jit(solution)/shard_map/ppermute | solution.py:670
  72.6 2.2 %collective-permute-done.20.refs_3_ = f32[16,128]{1,0:T(8,128)S(1)} collective-permute-done((f32[16,128]{1,0:T(8,128)S(1)}, f32[16,128]{1,0:T(8,128)S(1)}, u32[]{:S(2)}, u32[]{:S(2)}) %collective-permute-start.20) | collective-permute-done | bytes 8224 | tf_op jit(solution)/shard_map/ppermute | solution.py:670
  74.8 0.7 close.1
  (8 shorter events, 0.0 us)
Async XLA Ops:
  1.9 7.0 %collective-permute-start.1 = (bf16[30,8,128]{2,1,0:T(8,128)(2,1)S(1)}, bf16[30,8,128]{2,1,0:T(8,128)(2,1)S(1)}, u32[]{:S(2)}, u32[]{:S(2)}) collective-permute-start(bf16[30,8,128]{2,1,0:T(8,128)(2,1)S(1)} %get-tuple-element.44.mine_ref), channel_id=1, source_target_pairs={{0,6},{1,3},{2,0},{3,5},{4,2},{5,7},{6,4},{7,1},{8,14},{9,11},{10,... | collective-permute-start | bytes 184328 | tf_op jit(solution)/shard_map/ppermute | solution.py:579
  7.0 5.4 %collective-permute-start.2 = (bf16[30,8,128]{2,1,0:T(8,128)(2,1)S(1)}, bf16[30,8,128]{2,1,0:T(8,128)(2,1)S(1)}, u32[]{:S(2)}, u32[]{:S(2)}) collective-permute-start(bf16[30,8,128]{2,1,0:T(8,128)(2,1)S(1)} %get-tuple-element.45), channel_id=1, source_target_pairs={{0,7},{1,2},{2,1},{3,4},{4,3},{5,6},{6,5},{7,0},{8,15},{9,10},{10,... | collective-permute-start | bytes 184328 | tf_op jit(solution)/shard_map/ppermute | solution.py:579
  7.0 5.4 %collective-permute-start = (bf16[30,8,128]{2,1,0:T(8,128)(2,1)S(1)}, bf16[30,8,128]{2,1,0:T(8,128)(2,1)S(1)}, u32[]{:S(2)}, u32[]{:S(2)}) collective-permute-start(bf16[30,8,128]{2,1,0:T(8,128)(2,1)S(1)} %get-tuple-element.45), channel_id=1, source_target_pairs={{0,1},{1,0},{2,3},{3,2},{4,5},{5,4},{6,7},{7,6},{8,9},{9,8},{10,11... | collective-permute-start | bytes 184328 | tf_op jit(solution)/shard_map/ppermute | solution.py:579
  17.1 5.9 %collective-permute-start.4 = (bf16[30,16,128]{2,1,0:T(8,128)(2,1)S(1)}, bf16[30,16,128]{2,1,0:T(8,128)(2,1)S(1)}, u32[]{:S(2)}, u32[]{:S(2)}) collective-permute-start(bf16[30,16,128]{2,1,0:T(8,128)(2,1)S(1)} %get-tuple-element.55._), channel_id=1, source_target_pairs={{0,10},{1,11},{2,8},{3,9},{4,12},{5,13},{6,14},{7,15},{8,24},{9,25... | collective-permute-start | bytes 368648 | tf_op jit(solution)/shard_map/ppermute | solution.py:593
  17.1 6.2 %collective-permute-start.3 = (bf16[30,16,128]{2,1,0:T(8,128)(2,1)S(1)}, bf16[30,16,128]{2,1,0:T(8,128)(2,1)S(1)}, u32[]{:S(2)}, u32[]{:S(2)}) collective-permute-start(bf16[30,16,128]{2,1,0:T(8,128)(2,1)S(1)} %get-tuple-element.55._), channel_id=1, source_target_pairs={{0,8},{1,9},{2,12},{3,13},{4,14},{5,15},{6,10},{7,11},{8,16},{9,17... | collective-permute-start | bytes 368648 | tf_op jit(solution)/shard_map/ppermute | solution.py:593
  23.4 1.3 %collective-permute-start.6 = (bf16[30,16,128]{2,1,0:T(8,128)(2,1)S(1)}, bf16[30,16,128]{2,1,0:T(8,128)(2,1)S(1)}, u32[]{:S(2)}, u32[]{:S(2)}) collective-permute-start(bf16[30,16,128]{2,1,0:T(8,128)(2,1)S(1)} %get-tuple-element.56), channel_id=1, source_target_pairs={{8,16},{9,17},{12,20},{13,21},{14,22},{15,23},{10,18},{11,19},{16,... | collective-permute-start | bytes 368648 | tf_op jit(solution)/shard_map/ppermute | solution.py:593
  23.4 5.7 %collective-permute-start.5 = (bf16[30,16,128]{2,1,0:T(8,128)(2,1)S(1)}, bf16[30,16,128]{2,1,0:T(8,128)(2,1)S(1)}, u32[]{:S(2)}, u32[]{:S(2)}) collective-permute-start(bf16[30,16,128]{2,1,0:T(8,128)(2,1)S(1)} %get-tuple-element.56), channel_id=1, source_target_pairs={{8,20},{9,21},{12,22},{13,23},{14,18},{15,19},{10,16},{11,17},{16,... | collective-permute-start | bytes 368648 | tf_op jit(solution)/shard_map/ppermute | solution.py:593
  29.1 4.6 %collective-permute-start.8 = (bf16[30,16,128]{2,1,0:T(8,128)(2,1)S(1)}, bf16[30,16,128]{2,1,0:T(8,128)(2,1)S(1)}, u32[]{:S(2)}, u32[]{:S(2)}) collective-permute-start(bf16[30,16,128]{2,1,0:T(8,128)(2,1)S(1)} %get-tuple-element.57), channel_id=1, source_target_pairs={{16,26},{17,27},{20,24},{21,25},{22,28},{23,29},{18,30},{19,31},{2... | collective-permute-start | bytes 368648 | tf_op jit(solution)/shard_map/ppermute | solution.py:593
  29.1 6.8 %collective-permute-start.7 = (bf16[30,16,128]{2,1,0:T(8,128)(2,1)S(1)}, bf16[30,16,128]{2,1,0:T(8,128)(2,1)S(1)}, u32[]{:S(2)}, u32[]{:S(2)}) collective-permute-start(bf16[30,16,128]{2,1,0:T(8,128)(2,1)S(1)} %get-tuple-element.57), channel_id=1, source_target_pairs={{16,24},{17,25},{20,28},{21,29},{22,30},{23,31},{18,26},{19,27},{2... | collective-permute-start | bytes 368648 | tf_op jit(solution)/shard_map/ppermute | solution.py:593
  36.0 8.2 %collective-permute-start.9 = (bf16[30,16,128]{2,1,0:T(8,128)(2,1)S(1)}, bf16[30,16,128]{2,1,0:T(8,128)(2,1)S(1)}, u32[]{:S(2)}, u32[]{:S(2)}) collective-permute-start(bf16[30,16,128]{2,1,0:T(8,128)(2,1)S(1)} %get-tuple-element.62), channel_id=1, source_target_pairs={{24,16},{25,17},{28,20},{29,21},{30,22},{31,23},{26,18},{27,19},{1... | collective-permute-start | bytes 368648 | tf_op jit(solution)/shard_map/ppermute | solution.py:593
  41.8 2.4 %collective-permute-start.10 = (bf16[30,16,128]{2,1,0:T(8,128)(2,1)S(1)}, bf16[30,16,128]{2,1,0:T(8,128)(2,1)S(1)}, u32[]{:S(2)}, u32[]{:S(2)}) collective-permute-start(bf16[30,16,128]{2,1,0:T(8,128)(2,1)S(1)} %get-tuple-element.63), channel_id=1, source_target_pairs={{24,20},{25,21},{28,22},{29,23},{30,18},{31,19},{26,16},{27,17},{1... | collective-permute-start | bytes 368648 | tf_op jit(solution)/shard_map/ppermute | solution.py:593
  44.2 7.1 %collective-permute-start.11 = (bf16[30,16,128]{2,1,0:T(8,128)(2,1)S(1)}, bf16[30,16,128]{2,1,0:T(8,128)(2,1)S(1)}, u32[]{:S(2)}, u32[]{:S(2)}) collective-permute-start(bf16[30,16,128]{2,1,0:T(8,128)(2,1)S(1)} %get-tuple-element.68), channel_id=1, source_target_pairs={{16,10},{17,11},{20,8},{21,9},{22,12},{23,13},{18,14},{19,15},{8,0... | collective-permute-start | bytes 368648 | tf_op jit(solution)/shard_map/ppermute | solution.py:593
  48.9 2.4 %collective-permute-start.12 = (bf16[30,16,128]{2,1,0:T(8,128)(2,1)S(1)}, bf16[30,16,128]{2,1,0:T(8,128)(2,1)S(1)}, u32[]{:S(2)}, u32[]{:S(2)}) collective-permute-start(bf16[30,16,128]{2,1,0:T(8,128)(2,1)S(1)} %get-tuple-element.69), channel_id=1, source_target_pairs={{16,8},{17,9},{20,12},{21,13},{22,14},{23,15},{18,10},{19,11},{8,2... | collective-permute-start | bytes 368648 | tf_op jit(solution)/shard_map/ppermute | solution.py:593
  51.4 10.8 %collective-permute-start.13 = (bf16[30,16,128]{2,1,0:T(8,128)(2,1)S(1)}, bf16[30,16,128]{2,1,0:T(8,128)(2,1)S(1)}, u32[]{:S(2)}, u32[]{:S(2)}) collective-permute-start(bf16[30,16,128]{2,1,0:T(8,128)(2,1)S(1)} %get-tuple-element.74), channel_id=1, source_target_pairs={{8,0},{9,1},{12,2},{13,3},{14,4},{15,5},{10,6},{11,7},{0,16},{1,17... | collective-permute-start | bytes 368648 | tf_op jit(solution)/shard_map/ppermute | solution.py:593
  53.9 8.3 %collective-permute-start.14 = (bf16[30,16,128]{2,1,0:T(8,128)(2,1)S(1)}, bf16[30,16,128]{2,1,0:T(8,128)(2,1)S(1)}, u32[]{:S(2)}, u32[]{:S(2)}) collective-permute-start(bf16[30,16,128]{2,1,0:T(8,128)(2,1)S(1)} %get-tuple-element.75), channel_id=1, source_target_pairs={{8,2},{9,3},{12,4},{13,5},{14,6},{15,7},{10,0},{11,1},{0,24},{1,25... | collective-permute-start | bytes 368648 | tf_op jit(solution)/shard_map/ppermute | solution.py:593
  63.6 4.4 %collective-permute-start.15 = (f32[8,128]{1,0:T(8,128)S(1)}, f32[8,128]{1,0:T(8,128)S(1)}, u32[]{:S(2)}, u32[]{:S(2)}) collective-permute-start(f32[8,128]{1,0:T(8,128)S(1)} %get-tuple-element.81), channel_id=1, source_target_pairs={{0,1},{1,0},{2,3},{3,2},{4,5},{5,4},{6,7},{7,6},{8,9},{9,8},{10,11... | collective-permute-start | bytes 12296 | tf_op jit(solution)/shard_map/ppermute | solution.py:579
  63.6 5.9 %collective-permute-start.16 = (f32[8,128]{1,0:T(8,128)S(1)}, f32[8,128]{1,0:T(8,128)S(1)}, u32[]{:S(2)}, u32[]{:S(2)}) collective-permute-start(f32[8,128]{1,0:T(8,128)S(1)} %get-tuple-element.82), channel_id=1, source_target_pairs={{0,2},{1,7},{2,4},{3,1},{4,6},{5,3},{6,0},{7,5},{8,10},{9,15},{10,... | collective-permute-start | bytes 12296 | tf_op jit(solution)/shard_map/ppermute | solution.py:579
  65.4 4.8 %collective-permute-start.17 = (f32[8,128]{1,0:T(8,128)S(1)}, f32[8,128]{1,0:T(8,128)S(1)}, u32[]{:S(2)}, u32[]{:S(2)}) collective-permute-start(f32[8,128]{1,0:T(8,128)S(1)} %get-tuple-element.83), channel_id=1, source_target_pairs={{0,7},{1,2},{2,1},{3,4},{4,3},{5,6},{6,5},{7,0},{8,15},{9,10},{10,... | collective-permute-start | bytes 12296 | tf_op jit(solution)/shard_map/ppermute | solution.py:579
  70.2 4.5 %collective-permute-start.20 = (f32[16,128]{1,0:T(8,128)S(1)}, f32[16,128]{1,0:T(8,128)S(1)}, u32[]{:S(2)}, u32[]{:S(2)}) collective-permute-start(f32[16,128]{1,0:T(8,128)S(1)} %join.1.refs_0_), channel_id=1, source_target_pairs={{0,24},{1,25},{2,26},{3,27},{4,28},{5,29},{6,30},{7,31},{8,9},{9,8... | collective-permute-start | bytes 24584 | tf_op jit(solution)/shard_map/ppermute | solution.py:670
  70.2 4.5 %collective-permute-start.19 = (f32[16,128]{1,0:T(8,128)S(1)}, f32[16,128]{1,0:T(8,128)S(1)}, u32[]{:S(2)}, u32[]{:S(2)}) collective-permute-start(f32[16,128]{1,0:T(8,128)S(1)} %join.1.refs_0_), channel_id=1, source_target_pairs={{0,16},{1,17},{2,18},{3,19},{4,20},{5,21},{6,22},{7,23},{8,9},{9,8... | collective-permute-start | bytes 24584 | tf_op jit(solution)/shard_map/ppermute | solution.py:670
  70.3 4.5 %collective-permute-start.18 = (f32[16,128]{1,0:T(8,128)S(1)}, f32[16,128]{1,0:T(8,128)S(1)}, u32[]{:S(2)}, u32[]{:S(2)}) collective-permute-start(f32[16,128]{1,0:T(8,128)S(1)} %join.1.refs_0_), channel_id=1, source_target_pairs={{0,8},{1,9},{2,10},{3,11},{4,12},{5,13},{6,14},{7,15},{8,0},{9,1},... | collective-permute-start | bytes 24584 | tf_op jit(solution)/shard_map/ppermute | solution.py:670

commit v18 on v17

--- a/solution.py
+++ b/solution.py
@@ -454,9 +454,13 @@
 
     @pl.when(waits == late)
     def _():
-        pairs = [(zero_hbm, zero_ref)]
+        whole = [(zero_hbm, zero_ref)]
         for source, target in ((one_hbm, one_ref), (two_hbm, two_ref)):
-            pairs += [(source.at[n], target.at[n]) for n in range(2)]
+            whole += [(source.at[n], target.at[n]) for n in range(2)]
+        pairs = []
+        for source, target in whole:
+            half = source.shape[0] // 2
+            pairs += [(source.at[pl.ds(n * half, half)], target.at[pl.ds(n * half, half)]) for n in range(2)]
         bring(pairs, sems)
 
 
@@ -574,8 +578,12 @@
 
     pairs = slabs // 2
 
+    def swapped(i):
+        return i + 1 - 2 * (i % 2)
+
     def within(value, target):
-        ways = [(s * slabs + i, s * slabs + target(i) % slabs) for s in range(segments) for i in range(slabs)]
+        ways = [(i, target(i) % slabs) for i in range(slabs)]
+        ways += [(s * slabs + i, s * slabs + swapped(i)) for s in range(1, segments) for i in range(slabs)]
         return lax.ppermute(value, axes, ways)
 
     def hop(value, start, stop, by, way):
@@ -589,7 +597,7 @@
         else:
             ways += [(b, a) for a, b in ways]
         moving = {a for a, _ in ways}
-        ways += [(i, i + 1 - 2 * (i % 2)) for i in range(segments * slabs) if i not in moving]
+        ways += [(i, swapped(i)) for i in range(segments * slabs) if i not in moving]
         return lax.ppermute(value, axes, ways)
 
     raw = [
@@ -600,13 +608,13 @@
         pack_kernel, raw, [packed, packed], "pack", [pltpu.HBM] * len(raw),
         [pltpu.VMEM(v.shape, v.dtype) for v in raw] + [pltpu.SemaphoreType.DMA((len(raw),))],
     )
-    partner = within(other, lambda i: i + 1 - 2 * (i % 2))
+    partner = within(other, swapped)
     straight = within(mine, lambda i: i + 2 if i % 2 else i - 2)
     cross = within(other, lambda i: i + 1 if i % 2 else i - 1)
     stored = [zero_weight[0], one_weight[0], two_weight[0]]
     spaces = [pltpu.HBM] * 3
     on_chip = [pltpu.VMEM(w.shape, w.dtype) for w in stored]
-    sems = [pltpu.SemaphoreType.DMA((5,))]
+    sems = [pltpu.SemaphoreType.DMA((10,))]
     vectors = [radial_rate, read_weight.reshape(1, channels)]
     *weights, rate, read = call(
         functools.partial(stage_kernel, False), stored + vectors,
@@ -656,7 +664,7 @@
             "backward",
         )
     here, theirs, straight, cross = parts
-    theirs = within(theirs, lambda i: i + 1 - 2 * (i % 2))
+    theirs = within(theirs, swapped)
     straight = within(straight, lambda i: i - 2 if i % 2 else i + 2)
     cross = within(cross, lambda i: i + 1 if i % 2 else i - 1)
     (both,) = call(join_kernel, [here, theirs, straight, cross], [shape((rows, channels), F32)], "join")
@@ -664,7 +672,7 @@
     def across(section, i, stop):
         if section in (0, stop):
             return stop - section, i
-        return section, i + 1 - 2 * (i % 2)
+        return section, swapped(i)
 
     copies = [both] + [
         lax.ppermute(

time: 75.7 us -> 75 us (level)
  starting transfers between devices: 29.1 us -> 27.2 us
  waiting for transfers between devices: 35.4 us -> 36.6 us
    ppermute x3, starting transfers between devices: 2.31 us -> 0.14 us  [on_device(): lax.ppermute(both, axes, [(s * slabs + i, t * slabs + j) for s in range(s...]
    ppermute x3, waiting for transfers between devices: 2.23 us -> 4.39 us  [on_device(): lax.ppermute(both, axes, [(s * slabs + i, t * slabs + j) for s in range(s...]
    ppermute x12, waiting for transfers between devices: 26.3 us -> 24.9 us  [hop(): return lax.ppermute(value, axes, ways)]
where the time goes in v18:
time: 75 us; the launch traced here: 74.9 us
  waiting for transfers between devices  36.6 us (49%)
  starting transfers between devices  27.2 us (36%)
  Pallas kernels  10.3 us (14%)
  between operations  0.75 us (1%)
    ppermute x12, waiting for transfers between devices, hop(): return lax.ppermute(value, axes, ways)  24.9 us
    ppermute x12, starting transfers between devices, hop(): return lax.ppermute(value, axes, ways)  17.2 us
    pallas_call x14, Pallas kernels, call(): pl.pallas_call(body, out_shape=shapes, in_specs=[pl.BlockSpec(memory_spac...  10.3 us
    ppermute x6, starting transfers between devices, within(): return lax.ppermute(value, axes, ways)  9.9 us
    ppermute x6, waiting for transfers between devices, within(): return lax.ppermute(value, axes, ways)  7.33 us
    ppermute x3, waiting for transfers between devices, on_device(): lax.ppermute(both, axes, [(s * slabs + i, t * slabs + j) for s in range(s...  4.39 us
  transfers between devices with their start and end apart: 21, of which 13 were waited for; matrix products, arithmetic and copies ran while one was open for 0% of the time, Pallas kernels for 3%

profile of v18, /device:TPU:0, one launch (start us, length us, event | category | flops | bytes accessed | tf_op | source)
XLA Modules:
  0.0 74.9 jit_solution(6759548461057077871)
XLA Ops:
  0.6 1.2 %pack.1 = (bf16[30,8,128]{2,1,0:T(8,128)(2,1)S(1)}, bf16[30,8,128]{2,1,0:T(8,128)(2,1)S(1)}) custom-call(bf16[2,29,8,128]{3,2,1,0:T(8,128)(2,1)} %bitcast.13, f32[3,2,8]{2,1,0:T(2,128)} %bitcast.14, s32[2,8]{1,0:T(2,128)} %species_hbm.1, s32[2,8,8]{2,1,0:T(8,128)} %sources_hbm.1, f32[2,8]{1,0:T(2,128)} %grad_hbm.1, bf16[100,128]{1,0:T(8,128)(2,1)} %table_hbm.1), custom_call_target="tpu_custom_call" | custom-call | tf_op jit(solution)/shard_map/pack/pallas_call | solution.py:543
  1.9 5.1 %collective-permute-start.1 = (bf16[30,8,128]{2,1,0:T(8,128)(2,1)S(1)}, bf16[30,8,128]{2,1,0:T(8,128)(2,1)S(1)}, u32[]{:S(2)}, u32[]{:S(2)}) collective-permute-start(bf16[30,8,128]{2,1,0:T(8,128)(2,1)S(1)} %get-tuple-element.44.mine_ref), channel_id=1, source_target_pairs={{0,6},{1,3},{2,0},{3,5},{4,2},{5,7},{6,4},{7,1},{8,9},{9,8},{10,11... | collective-permute-start | bytes 184328 | tf_op jit(solution)/shard_map/ppermute | solution.py:587
  7.0 0.0 collective-permute-start.2
  7.0 0.0 collective-permute-start
  7.0 0.8 %stage.2 = (bf16[896,896]{1,0:T(8,128)(2,1)S(1)}, bf16[2,768,768]{2,1,0:T(8,128)(2,1)S(1)}, bf16[2,640,640]{2,1,0:T(8,128)(2,1)S(1)}, f32[1,128]{1,0:T(1,128)S(1)}, f32[1,128]{1,0:T(1,128)S(1)}) custom-call(bf16[896,896]{1,0:T(8,128)(2,1)} %bitcast.11, bf16[2,768,768]{2,1,0:T(8,128)(2,1)} %bitcast.7, bf16[2,640,640]{2,1,0:T(8,128)(2,1)} %bitcast.9, ...), custom_call_target="tpu_custom_call" | custom-call | tf_op jit(solution)/shard_map/stage/pallas_call | solution.py:543
  7.7 1.1 %collective-permute-done.1.straight_ref = bf16[30,8,128]{2,1,0:T(8,128)(2,1)S(1)} collective-permute-done((bf16[30,8,128]{2,1,0:T(8,128)(2,1)S(1)}, bf16[30,8,128]{2,1,0:T(8,128)(2,1)S(1)}, u32[]{:S(2)}, u32[]{:S(2)}) %collective-permute-start.1) | collective-permute-done | bytes 61472 | tf_op jit(solution)/shard_map/ppermute | solution.py:587
  8.8 3.6 %collective-permute-done.2.cross_ref = bf16[30,8,128]{2,1,0:T(8,128)(2,1)S(1)} collective-permute-done((bf16[30,8,128]{2,1,0:T(8,128)(2,1)S(1)}, bf16[30,8,128]{2,1,0:T(8,128)(2,1)S(1)}, u32[]{:S(2)}, u32[]{:S(2)}) %collective-permute-start.2) | collective-permute-done | bytes 61472 | tf_op jit(solution)/shard_map/ppermute | solution.py:587
  12.4 0.0 collective-permute-done.partner_ref
  12.4 0.1 open.1
  12.5 2.7 %stage.3 = (bf16[896,896]{1,0:T(8,128)(2,1)S(1)}, bf16[2,768,768]{2,1,0:T(8,128)(2,1)S(1)}, bf16[2,640,640]{2,1,0:T(8,128)(2,1)S(1)}) custom-call(bf16[896,896]{1,0:T(8,128)(2,1)} %bitcast.12, bf16[2,768,768]{2,1,0:T(8,128)(2,1)} %bitcast.8, bf16[2,640,640]{2,1,0:T(8,128)(2,1)} %bitcast.10, ...), custom_call_target="tpu_custom_call", output_to_operand_aliasing={{0}: (3, {}), {1}: (4, {}), {2}: (5, {})} | custom-call | tf_op jit(solution)/shard_map/stage/pallas_call | solution.py:543
  15.1 2.0 %forward.3 = (bf16[30,16,128]{2,1,0:T(8,128)(2,1)S(1)}, f32[29,16,128]{2,1,0:T(8,128)S(1)}, bf16[32,128]{1,0:T(8,128)(2,1)S(1)}, f32[1280,128]{1,0:T(8,128)S(1)}, f32[29,128,128]{2,1,0:T(8,128)S(1)}) custom-call(bf16[30,16,128]{2,1,0:T(8,128)(2,1)S(1)} %get-tuple-element.46.more_3_.low_ref, bf16[30,16,128]{2,1,0:T(8,128)(2,1)S(1)} %get-tuple-element.47.high_ref, ...), custom_call_target="tpu_custom_call" | custom-call | tf_op jit(solution)/shard_map/forward/pallas_call | solution.py:543
  17.1 0.1 collective-permute-start.4
  17.2 0.1 collective-permute-start.3
  17.2 5.8 %collective-permute-done.4.high_ref = bf16[30,16,128]{2,1,0:T(8,128)(2,1)S(1)} collective-permute-done((bf16[30,16,128]{2,1,0:T(8,128)(2,1)S(1)}, bf16[30,16,128]{2,1,0:T(8,128)(2,1)S(1)}, u32[]{:S(2)}, u32[]{:S(2)}) %collective-permute-start.4) | collective-permute-done | bytes 122912 | tf_op jit(solution)/shard_map/ppermute | solution.py:601
  23.0 0.4 collective-permute-done.3.low_ref
  23.4 1.0 %collective-permute-start.5 = (bf16[30,16,128]{2,1,0:T(8,128)(2,1)S(1)}, bf16[30,16,128]{2,1,0:T(8,128)(2,1)S(1)}, u32[]{:S(2)}, u32[]{:S(2)}) collective-permute-start(bf16[30,16,128]{2,1,0:T(8,128)(2,1)S(1)} %get-tuple-element.56), channel_id=1, source_target_pairs={{8,20},{9,21},{12,22},{13,23},{14,18},{15,19},{10,16},{11,17},{16,... | collective-permute-start | bytes 368648 | tf_op jit(solution)/shard_map/ppermute | solution.py:601
  24.5 0.3 collective-permute-done.6.high_ref
  24.7 4.4 %collective-permute-done.5.low_ref = bf16[30,16,128]{2,1,0:T(8,128)(2,1)S(1)} collective-permute-done((bf16[30,16,128]{2,1,0:T(8,128)(2,1)S(1)}, bf16[30,16,128]{2,1,0:T(8,128)(2,1)S(1)}, u32[]{:S(2)}, u32[]{:S(2)}) %collective-permute-start.5) | collective-permute-done | bytes 122912 | tf_op jit(solution)/shard_map/ppermute | solution.py:601
  29.1 0.0 collective-permute-start.8
  29.2 3.1 %collective-permute-start.7 = (bf16[30,16,128]{2,1,0:T(8,128)(2,1)S(1)}, bf16[30,16,128]{2,1,0:T(8,128)(2,1)S(1)}, u32[]{:S(2)}, u32[]{:S(2)}) collective-permute-start(bf16[30,16,128]{2,1,0:T(8,128)(2,1)S(1)} %get-tuple-element.57), channel_id=1, source_target_pairs={{16,24},{17,25},{20,28},{21,29},{22,30},{23,31},{18,26},{19,27},{2... | collective-permute-start | bytes 368648 | tf_op jit(solution)/shard_map/ppermute | solution.py:601
  32.2 1.5 %flip.1 = (bf16[896,896]{1,0:T(8,128)(2,1)S(1)}, bf16[2,768,768]{2,1,0:T(8,128)(2,1)S(1)}, bf16[2,640,640]{2,1,0:T(8,128)(2,1)S(1)}) custom-call(bf16[896,896]{1,0:T(8,128)(2,1)S(1)} %get-tuple-element.52.zero_ref, bf16[2,768,768]{2,1,0:T(8,128)(2,1)S(1)} %get-tuple-element.53.one_ref, bf16[2,640,640]{2,1,0:T(8,128)(2,1)S(1)} %get-tuple-element.54.two_ref, ...), custom_call_target="tpu_custom_call" | custom-call | tf_op jit(solution)/shard_map/flip/pallas_call | solution.py:543
  33.8 0.0 collective-permute-done.8.high_ref
  33.8 2.2 %collective-permute-done.7.low_ref = bf16[30,16,128]{2,1,0:T(8,128)(2,1)S(1)} collective-permute-done((bf16[30,16,128]{2,1,0:T(8,128)(2,1)S(1)}, bf16[30,16,128]{2,1,0:T(8,128)(2,1)S(1)}, u32[]{:S(2)}, u32[]{:S(2)}) %collective-permute-start.7) | collective-permute-done | bytes 122912 | tf_op jit(solution)/shard_map/ppermute | solution.py:601
  36.0 5.8 %collective-permute-start.9 = (bf16[30,16,128]{2,1,0:T(8,128)(2,1)S(1)}, bf16[30,16,128]{2,1,0:T(8,128)(2,1)S(1)}, u32[]{:S(2)}, u32[]{:S(2)}) collective-permute-start(bf16[30,16,128]{2,1,0:T(8,128)(2,1)S(1)} %get-tuple-element.62), channel_id=1, source_target_pairs={{24,16},{25,17},{28,20},{29,21},{30,22},{31,23},{26,18},{27,19},{1... | collective-permute-start | bytes 368648 | tf_op jit(solution)/shard_map/ppermute | solution.py:601
  41.8 2.4 %collective-permute-done.9.up_low_ref = bf16[30,16,128]{2,1,0:T(8,128)(2,1)S(1)} collective-permute-done((bf16[30,16,128]{2,1,0:T(8,128)(2,1)S(1)}, bf16[30,16,128]{2,1,0:T(8,128)(2,1)S(1)}, u32[]{:S(2)}, u32[]{:S(2)}) %collective-permute-start.9) | collective-permute-done | bytes 122912 | tf_op jit(solution)/shard_map/ppermute | solution.py:601
  44.3 0.0 collective-permute-done.10.up_high_ref
  44.3 4.4 %collective-permute-start.11 = (bf16[30,16,128]{2,1,0:T(8,128)(2,1)S(1)}, bf16[30,16,128]{2,1,0:T(8,128)(2,1)S(1)}, u32[]{:S(2)}, u32[]{:S(2)}) collective-permute-start(bf16[30,16,128]{2,1,0:T(8,128)(2,1)S(1)} %get-tuple-element.68), channel_id=1, source_target_pairs={{16,10},{17,11},{20,8},{21,9},{22,12},{23,13},{18,14},{19,15},{8,0... | collective-permute-start | bytes 368648 | tf_op jit(solution)/shard_map/ppermute | solution.py:601
  48.6 0.0 collective-permute-start.12
  48.6 2.4 %collective-permute-done.11.up_low_ref = bf16[30,16,128]{2,1,0:T(8,128)(2,1)S(1)} collective-permute-done((bf16[30,16,128]{2,1,0:T(8,128)(2,1)S(1)}, bf16[30,16,128]{2,1,0:T(8,128)(2,1)S(1)}, u32[]{:S(2)}, u32[]{:S(2)}) %collective-permute-start.11) | collective-permute-done | bytes 122912 | tf_op jit(solution)/shard_map/ppermute | solution.py:601
  51.1 0.0 collective-permute-done.12.up_high_ref
  51.1 2.5 %collective-permute-start.13 = (bf16[30,16,128]{2,1,0:T(8,128)(2,1)S(1)}, bf16[30,16,128]{2,1,0:T(8,128)(2,1)S(1)}, u32[]{:S(2)}, u32[]{:S(2)}) collective-permute-start(bf16[30,16,128]{2,1,0:T(8,128)(2,1)S(1)} %get-tuple-element.74), channel_id=1, source_target_pairs={{8,0},{9,1},{12,2},{13,3},{14,4},{15,5},{10,6},{11,7},{0,16},{1,17... | collective-permute-start | bytes 368648 | tf_op jit(solution)/shard_map/ppermute | solution.py:601
  53.6 0.2 collective-permute-start.14
  53.8 6.9 %collective-permute-done.13.up_low_ref = bf16[30,16,128]{2,1,0:T(8,128)(2,1)S(1)} collective-permute-done((bf16[30,16,128]{2,1,0:T(8,128)(2,1)S(1)}, bf16[30,16,128]{2,1,0:T(8,128)(2,1)S(1)}, u32[]{:S(2)}, u32[]{:S(2)}) %collective-permute-start.13) | collective-permute-done | bytes 122912 | tf_op jit(solution)/shard_map/ppermute | solution.py:601
  60.7 0.0 collective-permute-done.14.up_high_ref
  60.7 1.4 %backward.5 = (f32[8,128]{1,0:T(8,128)S(1)}, f32[8,128]{1,0:T(8,128)S(1)}, f32[8,128]{1,0:T(8,128)S(1)}, f32[8,128]{1,0:T(8,128)S(1)}) custom-call(bf16[30,16,128]{2,1,0:T(8,128)(2,1)S(1)} %collective-permute-done.13.up_low_ref, bf16[30,16,128]{2,1,0:T(8,128)(2,1)S(1)} %collective-permute-done.14.up_high_ref, ...), custom_call_target="tpu_custom_call" | custom-call | tf_op jit(solution)/shard_map/backward/pallas_call | solution.py:543
  62.1 0.0 collective-permute-start.15
  62.1 2.6 %collective-permute-start.16 = (f32[8,128]{1,0:T(8,128)S(1)}, f32[8,128]{1,0:T(8,128)S(1)}, u32[]{:S(2)}, u32[]{:S(2)}) collective-permute-start(f32[8,128]{1,0:T(8,128)S(1)} %get-tuple-element.82), channel_id=1, source_target_pairs={{0,2},{1,7},{2,4},{3,1},{4,6},{5,3},{6,0},{7,5},{8,9},{9,8},{10,11... | collective-permute-start | bytes 12296 | tf_op jit(solution)/shard_map/ppermute | solution.py:587
  64.7 2.2 %collective-permute-start.17 = (f32[8,128]{1,0:T(8,128)S(1)}, f32[8,128]{1,0:T(8,128)S(1)}, u32[]{:S(2)}, u32[]{:S(2)}) collective-permute-start(f32[8,128]{1,0:T(8,128)S(1)} %get-tuple-element.83), channel_id=1, source_target_pairs={{0,7},{1,2},{2,1},{3,4},{4,3},{5,6},{6,5},{7,0},{8,9},{9,8},{10,11... | collective-permute-start | bytes 12296 | tf_op jit(solution)/shard_map/ppermute | solution.py:587
  66.9 0.0 collective-permute-done.15.theirs_ref
  66.9 0.7 collective-permute-done.16.straight_ref
  67.6 2.0 %collective-permute-done.17.cross_ref = f32[8,128]{1,0:T(8,128)S(1)} collective-permute-done((f32[8,128]{1,0:T(8,128)S(1)}, f32[8,128]{1,0:T(8,128)S(1)}, u32[]{:S(2)}, u32[]{:S(2)}) %collective-permute-start.17) | collective-permute-done | bytes 4128 | tf_op jit(solution)/shard_map/ppermute | solution.py:587
  69.6 0.0 collective-permute-start.20
  69.6 0.1 collective-permute-start.19
  69.7 0.1 collective-permute-start.18
  69.8 4.4 %collective-permute-done.20.refs_3_ = f32[16,128]{1,0:T(8,128)S(1)} collective-permute-done((f32[16,128]{1,0:T(8,128)S(1)}, f32[16,128]{1,0:T(8,128)S(1)}, u32[]{:S(2)}, u32[]{:S(2)}) %collective-permute-start.20) | collective-permute-done | bytes 8224 | tf_op jit(solution)/shard_map/ppermute | solution.py:678
  74.1 0.0 collective-permute-done.19.refs_2_
  74.1 0.0 collective-permute-done.18.refs_1_
  74.1 0.7 close.1
  (8 shorter events, 0.0 us)
Async XLA Ops:
  1.9 7.0 %collective-permute-start.1 = (bf16[30,8,128]{2,1,0:T(8,128)(2,1)S(1)}, bf16[30,8,128]{2,1,0:T(8,128)(2,1)S(1)}, u32[]{:S(2)}, u32[]{:S(2)}) collective-permute-start(bf16[30,8,128]{2,1,0:T(8,128)(2,1)S(1)} %get-tuple-element.44.mine_ref), channel_id=1, source_target_pairs={{0,6},{1,3},{2,0},{3,5},{4,2},{5,7},{6,4},{7,1},{8,9},{9,8},{10,11... | collective-permute-start | bytes 184328 | tf_op jit(solution)/shard_map/ppermute | solution.py:587
  7.0 5.4 %collective-permute-start.2 = (bf16[30,8,128]{2,1,0:T(8,128)(2,1)S(1)}, bf16[30,8,128]{2,1,0:T(8,128)(2,1)S(1)}, u32[]{:S(2)}, u32[]{:S(2)}) collective-permute-start(bf16[30,8,128]{2,1,0:T(8,128)(2,1)S(1)} %get-tuple-element.45), channel_id=1, source_target_pairs={{0,7},{1,2},{2,1},{3,4},{4,3},{5,6},{6,5},{7,0},{8,9},{9,8},{10,11... | collective-permute-start | bytes 184328 | tf_op jit(solution)/shard_map/ppermute | solution.py:587
  7.0 5.4 %collective-permute-start = (bf16[30,8,128]{2,1,0:T(8,128)(2,1)S(1)}, bf16[30,8,128]{2,1,0:T(8,128)(2,1)S(1)}, u32[]{:S(2)}, u32[]{:S(2)}) collective-permute-start(bf16[30,8,128]{2,1,0:T(8,128)(2,1)S(1)} %get-tuple-element.45), channel_id=1, source_target_pairs={{0,1},{1,0},{2,3},{3,2},{4,5},{5,4},{6,7},{7,6},{8,9},{9,8},{10,11... | collective-permute-start | bytes 184328 | tf_op jit(solution)/shard_map/ppermute | solution.py:587
  17.1 5.9 %collective-permute-start.4 = (bf16[30,16,128]{2,1,0:T(8,128)(2,1)S(1)}, bf16[30,16,128]{2,1,0:T(8,128)(2,1)S(1)}, u32[]{:S(2)}, u32[]{:S(2)}) collective-permute-start(bf16[30,16,128]{2,1,0:T(8,128)(2,1)S(1)} %get-tuple-element.55._), channel_id=1, source_target_pairs={{0,10},{1,11},{2,8},{3,9},{4,12},{5,13},{6,14},{7,15},{8,24},{9,25... | collective-permute-start | bytes 368648 | tf_op jit(solution)/shard_map/ppermute | solution.py:601
  17.2 6.2 %collective-permute-start.3 = (bf16[30,16,128]{2,1,0:T(8,128)(2,1)S(1)}, bf16[30,16,128]{2,1,0:T(8,128)(2,1)S(1)}, u32[]{:S(2)}, u32[]{:S(2)}) collective-permute-start(bf16[30,16,128]{2,1,0:T(8,128)(2,1)S(1)} %get-tuple-element.55._), channel_id=1, source_target_pairs={{0,8},{1,9},{2,12},{3,13},{4,14},{5,15},{6,10},{7,11},{8,16},{9,17... | collective-permute-start | bytes 368648 | tf_op jit(solution)/shard_map/ppermute | solution.py:601
  23.4 1.3 %collective-permute-start.6 = (bf16[30,16,128]{2,1,0:T(8,128)(2,1)S(1)}, bf16[30,16,128]{2,1,0:T(8,128)(2,1)S(1)}, u32[]{:S(2)}, u32[]{:S(2)}) collective-permute-start(bf16[30,16,128]{2,1,0:T(8,128)(2,1)S(1)} %get-tuple-element.56), channel_id=1, source_target_pairs={{8,16},{9,17},{12,20},{13,21},{14,22},{15,23},{10,18},{11,19},{16,... | collective-permute-start | bytes 368648 | tf_op jit(solution)/shard_map/ppermute | solution.py:601
  23.4 5.7 %collective-permute-start.5 = (bf16[30,16,128]{2,1,0:T(8,128)(2,1)S(1)}, bf16[30,16,128]{2,1,0:T(8,128)(2,1)S(1)}, u32[]{:S(2)}, u32[]{:S(2)}) collective-permute-start(bf16[30,16,128]{2,1,0:T(8,128)(2,1)S(1)} %get-tuple-element.56), channel_id=1, source_target_pairs={{8,20},{9,21},{12,22},{13,23},{14,18},{15,19},{10,16},{11,17},{16,... | collective-permute-start | bytes 368648 | tf_op jit(solution)/shard_map/ppermute | solution.py:601
  29.1 4.6 %collective-permute-start.8 = (bf16[30,16,128]{2,1,0:T(8,128)(2,1)S(1)}, bf16[30,16,128]{2,1,0:T(8,128)(2,1)S(1)}, u32[]{:S(2)}, u32[]{:S(2)}) collective-permute-start(bf16[30,16,128]{2,1,0:T(8,128)(2,1)S(1)} %get-tuple-element.57), channel_id=1, source_target_pairs={{16,26},{17,27},{20,24},{21,25},{22,28},{23,29},{18,30},{19,31},{2... | collective-permute-start | bytes 368648 | tf_op jit(solution)/shard_map/ppermute | solution.py:601
  29.2 6.8 %collective-permute-start.7 = (bf16[30,16,128]{2,1,0:T(8,128)(2,1)S(1)}, bf16[30,16,128]{2,1,0:T(8,128)(2,1)S(1)}, u32[]{:S(2)}, u32[]{:S(2)}) collective-permute-start(bf16[30,16,128]{2,1,0:T(8,128)(2,1)S(1)} %get-tuple-element.57), channel_id=1, source_target_pairs={{16,24},{17,25},{20,28},{21,29},{22,30},{23,31},{18,26},{19,27},{2... | collective-permute-start | bytes 368648 | tf_op jit(solution)/shard_map/ppermute | solution.py:601
  36.0 8.3 %collective-permute-start.9 = (bf16[30,16,128]{2,1,0:T(8,128)(2,1)S(1)}, bf16[30,16,128]{2,1,0:T(8,128)(2,1)S(1)}, u32[]{:S(2)}, u32[]{:S(2)}) collective-permute-start(bf16[30,16,128]{2,1,0:T(8,128)(2,1)S(1)} %get-tuple-element.62), channel_id=1, source_target_pairs={{24,16},{25,17},{28,20},{29,21},{30,22},{31,23},{26,18},{27,19},{1... | collective-permute-start | bytes 368648 | tf_op jit(solution)/shard_map/ppermute | solution.py:601
  41.8 2.4 %collective-permute-start.10 = (bf16[30,16,128]{2,1,0:T(8,128)(2,1)S(1)}, bf16[30,16,128]{2,1,0:T(8,128)(2,1)S(1)}, u32[]{:S(2)}, u32[]{:S(2)}) collective-permute-start(bf16[30,16,128]{2,1,0:T(8,128)(2,1)S(1)} %get-tuple-element.63), channel_id=1, source_target_pairs={{24,20},{25,21},{28,22},{29,23},{30,18},{31,19},{26,16},{27,17},{1... | collective-permute-start | bytes 368648 | tf_op jit(solution)/shard_map/ppermute | solution.py:601
  44.3 6.8 %collective-permute-start.11 = (bf16[30,16,128]{2,1,0:T(8,128)(2,1)S(1)}, bf16[30,16,128]{2,1,0:T(8,128)(2,1)S(1)}, u32[]{:S(2)}, u32[]{:S(2)}) collective-permute-start(bf16[30,16,128]{2,1,0:T(8,128)(2,1)S(1)} %get-tuple-element.68), channel_id=1, source_target_pairs={{16,10},{17,11},{20,8},{21,9},{22,12},{23,13},{18,14},{19,15},{8,0... | collective-permute-start | bytes 368648 | tf_op jit(solution)/shard_map/ppermute | solution.py:601
  48.6 2.4 %collective-permute-start.12 = (bf16[30,16,128]{2,1,0:T(8,128)(2,1)S(1)}, bf16[30,16,128]{2,1,0:T(8,128)(2,1)S(1)}, u32[]{:S(2)}, u32[]{:S(2)}) collective-permute-start(bf16[30,16,128]{2,1,0:T(8,128)(2,1)S(1)} %get-tuple-element.69), channel_id=1, source_target_pairs={{16,8},{17,9},{20,12},{21,13},{22,14},{23,15},{18,10},{19,11},{8,2... | collective-permute-start | bytes 368648 | tf_op jit(solution)/shard_map/ppermute | solution.py:601
  51.1 9.6 %collective-permute-start.13 = (bf16[30,16,128]{2,1,0:T(8,128)(2,1)S(1)}, bf16[30,16,128]{2,1,0:T(8,128)(2,1)S(1)}, u32[]{:S(2)}, u32[]{:S(2)}) collective-permute-start(bf16[30,16,128]{2,1,0:T(8,128)(2,1)S(1)} %get-tuple-element.74), channel_id=1, source_target_pairs={{8,0},{9,1},{12,2},{13,3},{14,4},{15,5},{10,6},{11,7},{0,16},{1,17... | collective-permute-start | bytes 368648 | tf_op jit(solution)/shard_map/ppermute | solution.py:601
  53.6 7.2 %collective-permute-start.14 = (bf16[30,16,128]{2,1,0:T(8,128)(2,1)S(1)}, bf16[30,16,128]{2,1,0:T(8,128)(2,1)S(1)}, u32[]{:S(2)}, u32[]{:S(2)}) collective-permute-start(bf16[30,16,128]{2,1,0:T(8,128)(2,1)S(1)} %get-tuple-element.75), channel_id=1, source_target_pairs={{8,2},{9,3},{12,4},{13,5},{14,6},{15,7},{10,0},{11,1},{0,24},{1,25... | collective-permute-start | bytes 368648 | tf_op jit(solution)/shard_map/ppermute | solution.py:601
  62.1 4.8 %collective-permute-start.15 = (f32[8,128]{1,0:T(8,128)S(1)}, f32[8,128]{1,0:T(8,128)S(1)}, u32[]{:S(2)}, u32[]{:S(2)}) collective-permute-start(f32[8,128]{1,0:T(8,128)S(1)} %get-tuple-element.81), channel_id=1, source_target_pairs={{0,1},{1,0},{2,3},{3,2},{4,5},{5,4},{6,7},{7,6},{8,9},{9,8},{10,11... | collective-permute-start | bytes 12296 | tf_op jit(solution)/shard_map/ppermute | solution.py:587
  62.1 5.5 %collective-permute-start.16 = (f32[8,128]{1,0:T(8,128)S(1)}, f32[8,128]{1,0:T(8,128)S(1)}, u32[]{:S(2)}, u32[]{:S(2)}) collective-permute-start(f32[8,128]{1,0:T(8,128)S(1)} %get-tuple-element.82), channel_id=1, source_target_pairs={{0,2},{1,7},{2,4},{3,1},{4,6},{5,3},{6,0},{7,5},{8,9},{9,8},{10,11... | collective-permute-start | bytes 12296 | tf_op jit(solution)/shard_map/ppermute | solution.py:587
  64.7 4.8 %collective-permute-start.17 = (f32[8,128]{1,0:T(8,128)S(1)}, f32[8,128]{1,0:T(8,128)S(1)}, u32[]{:S(2)}, u32[]{:S(2)}) collective-permute-start(f32[8,128]{1,0:T(8,128)S(1)} %get-tuple-element.83), channel_id=1, source_target_pairs={{0,7},{1,2},{2,1},{3,4},{4,3},{5,6},{6,5},{7,0},{8,9},{9,8},{10,11... | collective-permute-start | bytes 12296 | tf_op jit(solution)/shard_map/ppermute | solution.py:587
  69.6 4.5 %collective-permute-start.20 = (f32[16,128]{1,0:T(8,128)S(1)}, f32[16,128]{1,0:T(8,128)S(1)}, u32[]{:S(2)}, u32[]{:S(2)}) collective-permute-start(f32[16,128]{1,0:T(8,128)S(1)} %join.1.refs_0_), channel_id=1, source_target_pairs={{0,24},{1,25},{2,26},{3,27},{4,28},{5,29},{6,30},{7,31},{8,9},{9,8... | collective-permute-start | bytes 24584 | tf_op jit(solution)/shard_map/ppermute | solution.py:678
  69.6 4.5 %collective-permute-start.19 = (f32[16,128]{1,0:T(8,128)S(1)}, f32[16,128]{1,0:T(8,128)S(1)}, u32[]{:S(2)}, u32[]{:S(2)}) collective-permute-start(f32[16,128]{1,0:T(8,128)S(1)} %join.1.refs_0_), channel_id=1, source_target_pairs={{0,16},{1,17},{2,18},{3,19},{4,20},{5,21},{6,22},{7,23},{8,9},{9,8... | collective-permute-start | bytes 24584 | tf_op jit(solution)/shard_map/ppermute | solution.py:678
  69.7 4.5 %collective-permute-start.18 = (f32[16,128]{1,0:T(8,128)S(1)}, f32[16,128]{1,0:T(8,128)S(1)}, u32[]{:S(2)}, u32[]{:S(2)}) collective-permute-start(f32[16,128]{1,0:T(8,128)S(1)} %join.1.refs_0_), channel_id=1, source_target_pairs={{0,8},{1,9},{2,10},{3,11},{4,12},{5,13},{6,14},{7,15},{8,0},{9,1},... | collective-permute-start | bytes 24584 | tf_op jit(solution)/shard_map/ppermute | solution.py:678

commit v19 on v18

--- a/solution.py
+++ b/solution.py
@@ -449,19 +449,22 @@
 def stage_kernel(late, zero_hbm, one_hbm, two_hbm, *more):
     zero_ref, one_ref, two_ref, *vectors, sems = more[4:] if late else more[2:]
     waits = (lax.axis_index("segment") == 0) & (lax.rem(lax.axis_index("space"), 2) == 0)
-    if not late:
-        bring(list(zip(more[:2], vectors)), sems)
-
-    @pl.when(waits == late)
-    def _():
-        whole = [(zero_hbm, zero_ref)]
-        for source, target in ((one_hbm, one_ref), (two_hbm, two_ref)):
-            whole += [(source.at[n], target.at[n]) for n in range(2)]
+
+    def halves(whole):
         pairs = []
         for source, target in whole:
             half = source.shape[0] // 2
             pairs += [(source.at[pl.ds(n * half, half)], target.at[pl.ds(n * half, half)]) for n in range(2)]
-        bring(pairs, sems)
+        return pairs
+
+    ones = halves([(one_hbm.at[n], one_ref.at[n]) for n in range(2)])
+    if late:
+        pl.when(waits)(lambda: bring(ones, sems))
+        return
+    rest = halves([(zero_hbm, zero_ref)] + [(two_hbm.at[n], two_ref.at[n]) for n in range(2)])
+    rest += list(zip(more[:2], vectors))
+    pl.when(waits)(lambda: bring(rest, sems))
+    pl.when(jnp.logical_not(waits))(lambda: bring(rest + ones, sems))
 
 
 def flip_kernel(zero_ref, one_ref, two_ref, _, zero_t_ref, one_t_ref, two_t_ref):
@@ -614,7 +617,7 @@
     stored = [zero_weight[0], one_weight[0], two_weight[0]]
     spaces = [pltpu.HBM] * 3
     on_chip = [pltpu.VMEM(w.shape, w.dtype) for w in stored]
-    sems = [pltpu.SemaphoreType.DMA((10,))]
+    sems = [pltpu.SemaphoreType.DMA((12,))]
     vectors = [radial_rate, read_weight.reshape(1, channels)]
     *weights, rate, read = call(
         functools.partial(stage_kernel, False), stored + vectors,
@@ -670,7 +673,11 @@
     (both,) = call(join_kernel, [here, theirs, straight, cross], [shape((rows, channels), F32)], "join")
 
     def across(section, i, stop):
-        if section in (0, stop):
+        if stop == segments - 1 and stop > 1:
+            ring = {0: stop, stop: stop - 1, stop - 1: 0}
+            if section in ring:
+                return ring[section], i
+        elif section in (0, stop):
             return stop - section, i
         return section, swapped(i)
 

time: 75 us -> 75.3 us (level)
  starting transfers between devices: 27.2 us -> 29.3 us
  waiting for transfers between devices: 36.6 us -> 34.6 us
    ppermute x6, waiting for transfers between devices: 7.33 us -> 4.94 us  [within(): return lax.ppermute(value, axes, ways)]
    ppermute x3, starting transfers between devices: 0.14 us -> 2.02 us  [on_device(): lax.ppermute(both, axes, [(s * slabs + i, t * slabs + j) for s in range(s...]
    ppermute x12, waiting for transfers between devices: 24.9 us -> 26 us  [hop(): return lax.ppermute(value, axes, ways)]
  transfers between devices with their start and end apart: 21 -> 21, of which waited for: 13 -> 14; matrix products, arithmetic and copies ran while one was open for 0% -> 0% of each run, Pallas kernels for 3% -> 5%
where the time goes in v19:
time: 75.3 us; the launch traced here: 75.1 us
  waiting for transfers between devices  34.6 us (46%)
  starting transfers between devices  29.3 us (39%)
  Pallas kernels  10.5 us (14%)
    ppermute x12, waiting for transfers between devices, hop(): return lax.ppermute(value, axes, ways)  26 us
    ppermute x12, starting transfers between devices, hop(): return lax.ppermute(value, axes, ways)  17.2 us
    pallas_call x14, Pallas kernels, call(): pl.pallas_call(body, out_shape=shapes, in_specs=[pl.BlockSpec(memory_spac...  10.5 us
    ppermute x6, starting transfers between devices, within(): return lax.ppermute(value, axes, ways)  10.1 us
    ppermute x6, waiting for transfers between devices, within(): return lax.ppermute(value, axes, ways)  4.94 us
    ppermute x3, waiting for transfers between devices, on_device(): lax.ppermute(both, axes, [(s * slabs + i, t * slabs + j) for s in range(s...  3.65 us
    ppermute x3, starting transfers between devices, on_device(): lax.ppermute(both, axes, [(s * slabs + i, t * slabs + j) for s in range(s...  2.02 us
  transfers between devices with their start and end apart: 21, of which 14 were waited for; matrix products, arithmetic and copies ran while one was open for 0% of the time, Pallas kernels for 5%

profile of v19, /device:TPU:0, one launch (start us, length us, event | category | flops | bytes accessed | tf_op | source)
XLA Modules:
  0.0 75.1 jit_solution(7271441864029459216)
XLA Ops:
  0.6 1.2 %pack.1 = (bf16[30,8,128]{2,1,0:T(8,128)(2,1)S(1)}, bf16[30,8,128]{2,1,0:T(8,128)(2,1)S(1)}) custom-call(bf16[2,29,8,128]{3,2,1,0:T(8,128)(2,1)} %bitcast.13, f32[3,2,8]{2,1,0:T(2,128)} %bitcast.14, s32[2,8]{1,0:T(2,128)} %species_hbm.1, s32[2,8,8]{2,1,0:T(8,128)} %sources_hbm.1, f32[2,8]{1,0:T(2,128)} %grad_hbm.1, bf16[100,128]{1,0:T(8,128)(2,1)} %table_hbm.1), custom_call_target="tpu_custom_call" | custom-call | tf_op jit(solution)/shard_map/pack/pallas_call | solution.py:546
  1.9 5.1 %collective-permute-start.1 = (bf16[30,8,128]{2,1,0:T(8,128)(2,1)S(1)}, bf16[30,8,128]{2,1,0:T(8,128)(2,1)S(1)}, u32[]{:S(2)}, u32[]{:S(2)}) collective-permute-start(bf16[30,8,128]{2,1,0:T(8,128)(2,1)S(1)} %get-tuple-element.44.mine_ref), channel_id=1, source_target_pairs={{0,6},{1,3},{2,0},{3,5},{4,2},{5,7},{6,4},{7,1},{8,9},{9,8},{10,11... | collective-permute-start | bytes 184328 | tf_op jit(solution)/shard_map/ppermute | solution.py:590
  7.0 0.0 collective-permute-start.2
  7.0 0.0 collective-permute-start
  7.0 2.0 %stage.2 = (bf16[896,896]{1,0:T(8,128)(2,1)S(1)}, bf16[2,768,768]{2,1,0:T(8,128)(2,1)S(1)}, bf16[2,640,640]{2,1,0:T(8,128)(2,1)S(1)}, f32[1,128]{1,0:T(1,128)S(1)}, f32[1,128]{1,0:T(1,128)S(1)}) custom-call(bf16[896,896]{1,0:T(8,128)(2,1)} %bitcast.11, bf16[2,768,768]{2,1,0:T(8,128)(2,1)} %bitcast.7, bf16[2,640,640]{2,1,0:T(8,128)(2,1)} %bitcast.9, ...), custom_call_target="tpu_custom_call" | custom-call | tf_op jit(solution)/shard_map/stage/pallas_call | solution.py:546
  8.9 0.0 collective-permute-done.1.straight_ref
  8.9 3.5 %collective-permute-done.2.cross_ref = bf16[30,8,128]{2,1,0:T(8,128)(2,1)S(1)} collective-permute-done((bf16[30,8,128]{2,1,0:T(8,128)(2,1)S(1)}, bf16[30,8,128]{2,1,0:T(8,128)(2,1)S(1)}, u32[]{:S(2)}, u32[]{:S(2)}) %collective-permute-start.2) | collective-permute-done | bytes 61472 | tf_op jit(solution)/shard_map/ppermute | solution.py:590
  12.4 0.0 collective-permute-done.partner_ref
  12.4 0.1 open.1
  12.5 1.7 %stage.3 = (bf16[896,896]{1,0:T(8,128)(2,1)S(1)}, bf16[2,768,768]{2,1,0:T(8,128)(2,1)S(1)}, bf16[2,640,640]{2,1,0:T(8,128)(2,1)S(1)}) custom-call(bf16[896,896]{1,0:T(8,128)(2,1)} %bitcast.12, bf16[2,768,768]{2,1,0:T(8,128)(2,1)} %bitcast.8, bf16[2,640,640]{2,1,0:T(8,128)(2,1)} %bitcast.10, ...), custom_call_target="tpu_custom_call", output_to_operand_aliasing={{0}: (3, {}), {1}: (4, {}), {2}: (5, {})} | custom-call | tf_op jit(solution)/shard_map/stage/pallas_call | solution.py:546
  14.2 2.0 %forward.3 = (bf16[30,16,128]{2,1,0:T(8,128)(2,1)S(1)}, f32[29,16,128]{2,1,0:T(8,128)S(1)}, bf16[32,128]{1,0:T(8,128)(2,1)S(1)}, f32[1280,128]{1,0:T(8,128)S(1)}, f32[29,128,128]{2,1,0:T(8,128)S(1)}) custom-call(bf16[30,16,128]{2,1,0:T(8,128)(2,1)S(1)} %get-tuple-element.46.more_3_.low_ref, bf16[30,16,128]{2,1,0:T(8,128)(2,1)S(1)} %get-tuple-element.47.high_ref, ...), custom_call_target="tpu_custom_call" | custom-call | tf_op jit(solution)/shard_map/forward/pallas_call | solution.py:546
  16.1 0.1 collective-permute-start.4
  16.2 0.1 collective-permute-start.3
  16.3 5.8 %collective-permute-done.4.high_ref = bf16[30,16,128]{2,1,0:T(8,128)(2,1)S(1)} collective-permute-done((bf16[30,16,128]{2,1,0:T(8,128)(2,1)S(1)}, bf16[30,16,128]{2,1,0:T(8,128)(2,1)S(1)}, u32[]{:S(2)}, u32[]{:S(2)}) %collective-permute-start.4) | collective-permute-done | bytes 122912 | tf_op jit(solution)/shard_map/ppermute | solution.py:604
  22.1 0.4 collective-permute-done.3.low_ref
  22.5 0.0 collective-permute-start.6
  22.5 1.0 %collective-permute-start.5 = (bf16[30,16,128]{2,1,0:T(8,128)(2,1)S(1)}, bf16[30,16,128]{2,1,0:T(8,128)(2,1)S(1)}, u32[]{:S(2)}, u32[]{:S(2)}) collective-permute-start(bf16[30,16,128]{2,1,0:T(8,128)(2,1)S(1)} %get-tuple-element.56), channel_id=1, source_target_pairs={{8,20},{9,21},{12,22},{13,23},{14,18},{15,19},{10,16},{11,17},{16,... | collective-permute-start | bytes 368648 | tf_op jit(solution)/shard_map/ppermute | solution.py:604
  23.5 0.3 collective-permute-done.6.high_ref
  23.8 4.4 %collective-permute-done.5.low_ref = bf16[30,16,128]{2,1,0:T(8,128)(2,1)S(1)} collective-permute-done((bf16[30,16,128]{2,1,0:T(8,128)(2,1)S(1)}, bf16[30,16,128]{2,1,0:T(8,128)(2,1)S(1)}, u32[]{:S(2)}, u32[]{:S(2)}) %collective-permute-start.5) | collective-permute-done | bytes 122912 | tf_op jit(solution)/shard_map/ppermute | solution.py:604
  28.2 0.0 collective-permute-start.8
  28.2 3.1 %collective-permute-start.7 = (bf16[30,16,128]{2,1,0:T(8,128)(2,1)S(1)}, bf16[30,16,128]{2,1,0:T(8,128)(2,1)S(1)}, u32[]{:S(2)}, u32[]{:S(2)}) collective-permute-start(bf16[30,16,128]{2,1,0:T(8,128)(2,1)S(1)} %get-tuple-element.57), channel_id=1, source_target_pairs={{16,24},{17,25},{20,28},{21,29},{22,30},{23,31},{18,26},{19,27},{2... | collective-permute-start | bytes 368648 | tf_op jit(solution)/shard_map/ppermute | solution.py:604
  31.3 1.5 %flip.1 = (bf16[896,896]{1,0:T(8,128)(2,1)S(1)}, bf16[2,768,768]{2,1,0:T(8,128)(2,1)S(1)}, bf16[2,640,640]{2,1,0:T(8,128)(2,1)S(1)}) custom-call(bf16[896,896]{1,0:T(8,128)(2,1)S(1)} %get-tuple-element.52.zero_ref, bf16[2,768,768]{2,1,0:T(8,128)(2,1)S(1)} %get-tuple-element.53.one_ref, bf16[2,640,640]{2,1,0:T(8,128)(2,1)S(1)} %get-tuple-element.54.two_ref, ...), custom_call_target="tpu_custom_call" | custom-call | tf_op jit(solution)/shard_map/flip/pallas_call | solution.py:546
  32.8 0.0 collective-permute-done.8.high_ref
  32.8 2.2 %collective-permute-done.7.low_ref = bf16[30,16,128]{2,1,0:T(8,128)(2,1)S(1)} collective-permute-done((bf16[30,16,128]{2,1,0:T(8,128)(2,1)S(1)}, bf16[30,16,128]{2,1,0:T(8,128)(2,1)S(1)}, u32[]{:S(2)}, u32[]{:S(2)}) %collective-permute-start.7) | collective-permute-done | bytes 122912 | tf_op jit(solution)/shard_map/ppermute | solution.py:604
  35.1 5.8 %collective-permute-start.9 = (bf16[30,16,128]{2,1,0:T(8,128)(2,1)S(1)}, bf16[30,16,128]{2,1,0:T(8,128)(2,1)S(1)}, u32[]{:S(2)}, u32[]{:S(2)}) collective-permute-start(bf16[30,16,128]{2,1,0:T(8,128)(2,1)S(1)} %get-tuple-element.62), channel_id=1, source_target_pairs={{24,16},{25,17},{28,20},{29,21},{30,22},{31,23},{26,18},{27,19},{1... | collective-permute-start | bytes 368648 | tf_op jit(solution)/shard_map/ppermute | solution.py:604
  40.9 0.0 collective-permute-start.10
  40.9 2.4 %collective-permute-done.9.up_low_ref = bf16[30,16,128]{2,1,0:T(8,128)(2,1)S(1)} collective-permute-done((bf16[30,16,128]{2,1,0:T(8,128)(2,1)S(1)}, bf16[30,16,128]{2,1,0:T(8,128)(2,1)S(1)}, u32[]{:S(2)}, u32[]{:S(2)}) %collective-permute-start.9) | collective-permute-done | bytes 122912 | tf_op jit(solution)/shard_map/ppermute | solution.py:604
  43.3 0.0 collective-permute-done.10.up_high_ref
  43.3 4.4 %collective-permute-start.11 = (bf16[30,16,128]{2,1,0:T(8,128)(2,1)S(1)}, bf16[30,16,128]{2,1,0:T(8,128)(2,1)S(1)}, u32[]{:S(2)}, u32[]{:S(2)}) collective-permute-start(bf16[30,16,128]{2,1,0:T(8,128)(2,1)S(1)} %get-tuple-element.68), channel_id=1, source_target_pairs={{16,10},{17,11},{20,8},{21,9},{22,12},{23,13},{18,14},{19,15},{8,0... | collective-permute-start | bytes 368648 | tf_op jit(solution)/shard_map/ppermute | solution.py:604
  47.7 0.0 collective-permute-start.12
  47.7 2.4 %collective-permute-done.11.up_low_ref = bf16[30,16,128]{2,1,0:T(8,128)(2,1)S(1)} collective-permute-done((bf16[30,16,128]{2,1,0:T(8,128)(2,1)S(1)}, bf16[30,16,128]{2,1,0:T(8,128)(2,1)S(1)}, u32[]{:S(2)}, u32[]{:S(2)}) %collective-permute-start.11) | collective-permute-done | bytes 122912 | tf_op jit(solution)/shard_map/ppermute | solution.py:604
  50.1 0.0 collective-permute-done.12.up_high_ref
  50.1 2.5 %collective-permute-start.13 = (bf16[30,16,128]{2,1,0:T(8,128)(2,1)S(1)}, bf16[30,16,128]{2,1,0:T(8,128)(2,1)S(1)}, u32[]{:S(2)}, u32[]{:S(2)}) collective-permute-start(bf16[30,16,128]{2,1,0:T(8,128)(2,1)S(1)} %get-tuple-element.74), channel_id=1, source_target_pairs={{8,0},{9,1},{12,2},{13,3},{14,4},{15,5},{10,6},{11,7},{0,16},{1,17... | collective-permute-start | bytes 368648 | tf_op jit(solution)/shard_map/ppermute | solution.py:604
  52.6 0.2 collective-permute-start.14
  52.9 8.0 %collective-permute-done.13.up_low_ref = bf16[30,16,128]{2,1,0:T(8,128)(2,1)S(1)} collective-permute-done((bf16[30,16,128]{2,1,0:T(8,128)(2,1)S(1)}, bf16[30,16,128]{2,1,0:T(8,128)(2,1)S(1)}, u32[]{:S(2)}, u32[]{:S(2)}) %collective-permute-start.13) | collective-permute-done | bytes 122912 | tf_op jit(solution)/shard_map/ppermute | solution.py:604
  60.8 0.0 collective-permute-done.14.up_high_ref
  60.8 1.4 %backward.5 = (f32[8,128]{1,0:T(8,128)S(1)}, f32[8,128]{1,0:T(8,128)S(1)}, f32[8,128]{1,0:T(8,128)S(1)}, f32[8,128]{1,0:T(8,128)S(1)}) custom-call(bf16[30,16,128]{2,1,0:T(8,128)(2,1)S(1)} %collective-permute-done.13.up_low_ref, bf16[30,16,128]{2,1,0:T(8,128)(2,1)S(1)} %collective-permute-done.14.up_high_ref, ...), custom_call_target="tpu_custom_call" | custom-call | tf_op jit(solution)/shard_map/backward/pallas_call | solution.py:546
  62.2 1.6 %collective-permute-start.16 = (f32[8,128]{1,0:T(8,128)S(1)}, f32[8,128]{1,0:T(8,128)S(1)}, u32[]{:S(2)}, u32[]{:S(2)}) collective-permute-start(f32[8,128]{1,0:T(8,128)S(1)} %get-tuple-element.82), channel_id=1, source_target_pairs={{0,2},{1,7},{2,4},{3,1},{4,6},{5,3},{6,0},{7,5},{8,9},{9,8},{10,11... | collective-permute-start | bytes 12296 | tf_op jit(solution)/shard_map/ppermute | solution.py:590
  63.9 3.3 %collective-permute-start.17 = (f32[8,128]{1,0:T(8,128)S(1)}, f32[8,128]{1,0:T(8,128)S(1)}, u32[]{:S(2)}, u32[]{:S(2)}) collective-permute-start(f32[8,128]{1,0:T(8,128)S(1)} %get-tuple-element.83), channel_id=1, source_target_pairs={{0,7},{1,2},{2,1},{3,4},{4,3},{5,6},{6,5},{7,0},{8,9},{9,8},{10,11... | collective-permute-start | bytes 12296 | tf_op jit(solution)/shard_map/ppermute | solution.py:590
  67.2 0.0 collective-permute-done.15.theirs_ref
  67.2 0.5 collective-permute-done.16.straight_ref
  67.7 1.0 %collective-permute-done.17.cross_ref = f32[8,128]{1,0:T(8,128)S(1)} collective-permute-done((f32[8,128]{1,0:T(8,128)S(1)}, f32[8,128]{1,0:T(8,128)S(1)}, u32[]{:S(2)}, u32[]{:S(2)}) %collective-permute-start.17) | collective-permute-done | bytes 4128 | tf_op jit(solution)/shard_map/ppermute | solution.py:590
  68.7 2.0 %collective-permute-start.19 = (f32[16,128]{1,0:T(8,128)S(1)}, f32[16,128]{1,0:T(8,128)S(1)}, u32[]{:S(2)}, u32[]{:S(2)}) collective-permute-start(f32[16,128]{1,0:T(8,128)S(1)} %join.1.refs_0_), channel_id=1, source_target_pairs={{0,16},{1,17},{2,18},{3,19},{4,20},{5,21},{6,22},{7,23},{8,9},{9,8... | collective-permute-start | bytes 24584 | tf_op jit(solution)/shard_map/ppermute | solution.py:685
  70.7 0.0 collective-permute-start.18
  70.7 1.6 %collective-permute-done.20.refs_3_ = f32[16,128]{1,0:T(8,128)S(1)} collective-permute-done((f32[16,128]{1,0:T(8,128)S(1)}, f32[16,128]{1,0:T(8,128)S(1)}, u32[]{:S(2)}, u32[]{:S(2)}) %collective-permute-start.20) | collective-permute-done | bytes 8224 | tf_op jit(solution)/shard_map/ppermute | solution.py:685
  72.4 0.1 collective-permute-done.19.refs_2_
  72.4 1.9 %collective-permute-done.18.refs_1_ = f32[16,128]{1,0:T(8,128)S(1)} collective-permute-done((f32[16,128]{1,0:T(8,128)S(1)}, f32[16,128]{1,0:T(8,128)S(1)}, u32[]{:S(2)}, u32[]{:S(2)}) %collective-permute-start.18) | collective-permute-done | bytes 8224 | tf_op jit(solution)/shard_map/ppermute | solution.py:685
  74.4 0.7 close.1
  (8 shorter events, 0.0 us)
Async XLA Ops:
  1.9 7.1 %collective-permute-start.1 = (bf16[30,8,128]{2,1,0:T(8,128)(2,1)S(1)}, bf16[30,8,128]{2,1,0:T(8,128)(2,1)S(1)}, u32[]{:S(2)}, u32[]{:S(2)}) collective-permute-start(bf16[30,8,128]{2,1,0:T(8,128)(2,1)S(1)} %get-tuple-element.44.mine_ref), channel_id=1, source_target_pairs={{0,6},{1,3},{2,0},{3,5},{4,2},{5,7},{6,4},{7,1},{8,9},{9,8},{10,11... | collective-permute-start | bytes 184328 | tf_op jit(solution)/shard_map/ppermute | solution.py:590
  7.0 5.4 %collective-permute-start.2 = (bf16[30,8,128]{2,1,0:T(8,128)(2,1)S(1)}, bf16[30,8,128]{2,1,0:T(8,128)(2,1)S(1)}, u32[]{:S(2)}, u32[]{:S(2)}) collective-permute-start(bf16[30,8,128]{2,1,0:T(8,128)(2,1)S(1)} %get-tuple-element.45), channel_id=1, source_target_pairs={{0,7},{1,2},{2,1},{3,4},{4,3},{5,6},{6,5},{7,0},{8,9},{9,8},{10,11... | collective-permute-start | bytes 184328 | tf_op jit(solution)/shard_map/ppermute | solution.py:590
  7.0 5.4 %collective-permute-start = (bf16[30,8,128]{2,1,0:T(8,128)(2,1)S(1)}, bf16[30,8,128]{2,1,0:T(8,128)(2,1)S(1)}, u32[]{:S(2)}, u32[]{:S(2)}) collective-permute-start(bf16[30,8,128]{2,1,0:T(8,128)(2,1)S(1)} %get-tuple-element.45), channel_id=1, source_target_pairs={{0,1},{1,0},{2,3},{3,2},{4,5},{5,4},{6,7},{7,6},{8,9},{9,8},{10,11... | collective-permute-start | bytes 184328 | tf_op jit(solution)/shard_map/ppermute | solution.py:590
  16.1 5.9 %collective-permute-start.4 = (bf16[30,16,128]{2,1,0:T(8,128)(2,1)S(1)}, bf16[30,16,128]{2,1,0:T(8,128)(2,1)S(1)}, u32[]{:S(2)}, u32[]{:S(2)}) collective-permute-start(bf16[30,16,128]{2,1,0:T(8,128)(2,1)S(1)} %get-tuple-element.55._), channel_id=1, source_target_pairs={{0,10},{1,11},{2,8},{3,9},{4,12},{5,13},{6,14},{7,15},{8,24},{9,25... | collective-permute-start | bytes 368648 | tf_op jit(solution)/shard_map/ppermute | solution.py:604
  16.2 6.2 %collective-permute-start.3 = (bf16[30,16,128]{2,1,0:T(8,128)(2,1)S(1)}, bf16[30,16,128]{2,1,0:T(8,128)(2,1)S(1)}, u32[]{:S(2)}, u32[]{:S(2)}) collective-permute-start(bf16[30,16,128]{2,1,0:T(8,128)(2,1)S(1)} %get-tuple-element.55._), channel_id=1, source_target_pairs={{0,8},{1,9},{2,12},{3,13},{4,14},{5,15},{6,10},{7,11},{8,16},{9,17... | collective-permute-start | bytes 368648 | tf_op jit(solution)/shard_map/ppermute | solution.py:604
  22.5 1.3 %collective-permute-start.6 = (bf16[30,16,128]{2,1,0:T(8,128)(2,1)S(1)}, bf16[30,16,128]{2,1,0:T(8,128)(2,1)S(1)}, u32[]{:S(2)}, u32[]{:S(2)}) collective-permute-start(bf16[30,16,128]{2,1,0:T(8,128)(2,1)S(1)} %get-tuple-element.56), channel_id=1, source_target_pairs={{8,16},{9,17},{12,20},{13,21},{14,22},{15,23},{10,18},{11,19},{16,... | collective-permute-start | bytes 368648 | tf_op jit(solution)/shard_map/ppermute | solution.py:604
  22.5 5.7 %collective-permute-start.5 = (bf16[30,16,128]{2,1,0:T(8,128)(2,1)S(1)}, bf16[30,16,128]{2,1,0:T(8,128)(2,1)S(1)}, u32[]{:S(2)}, u32[]{:S(2)}) collective-permute-start(bf16[30,16,128]{2,1,0:T(8,128)(2,1)S(1)} %get-tuple-element.56), channel_id=1, source_target_pairs={{8,20},{9,21},{12,22},{13,23},{14,18},{15,19},{10,16},{11,17},{16,... | collective-permute-start | bytes 368648 | tf_op jit(solution)/shard_map/ppermute | solution.py:604
  28.2 4.6 %collective-permute-start.8 = (bf16[30,16,128]{2,1,0:T(8,128)(2,1)S(1)}, bf16[30,16,128]{2,1,0:T(8,128)(2,1)S(1)}, u32[]{:S(2)}, u32[]{:S(2)}) collective-permute-start(bf16[30,16,128]{2,1,0:T(8,128)(2,1)S(1)} %get-tuple-element.57), channel_id=1, source_target_pairs={{16,26},{17,27},{20,24},{21,25},{22,28},{23,29},{18,30},{19,31},{2... | collective-permute-start | bytes 368648 | tf_op jit(solution)/shard_map/ppermute | solution.py:604
  28.2 6.8 %collective-permute-start.7 = (bf16[30,16,128]{2,1,0:T(8,128)(2,1)S(1)}, bf16[30,16,128]{2,1,0:T(8,128)(2,1)S(1)}, u32[]{:S(2)}, u32[]{:S(2)}) collective-permute-start(bf16[30,16,128]{2,1,0:T(8,128)(2,1)S(1)} %get-tuple-element.57), channel_id=1, source_target_pairs={{16,24},{17,25},{20,28},{21,29},{22,30},{23,31},{18,26},{19,27},{2... | collective-permute-start | bytes 368648 | tf_op jit(solution)/shard_map/ppermute | solution.py:604
  35.1 8.2 %collective-permute-start.9 = (bf16[30,16,128]{2,1,0:T(8,128)(2,1)S(1)}, bf16[30,16,128]{2,1,0:T(8,128)(2,1)S(1)}, u32[]{:S(2)}, u32[]{:S(2)}) collective-permute-start(bf16[30,16,128]{2,1,0:T(8,128)(2,1)S(1)} %get-tuple-element.62), channel_id=1, source_target_pairs={{24,16},{25,17},{28,20},{29,21},{30,22},{31,23},{26,18},{27,19},{1... | collective-permute-start | bytes 368648 | tf_op jit(solution)/shard_map/ppermute | solution.py:604
  40.9 2.4 %collective-permute-start.10 = (bf16[30,16,128]{2,1,0:T(8,128)(2,1)S(1)}, bf16[30,16,128]{2,1,0:T(8,128)(2,1)S(1)}, u32[]{:S(2)}, u32[]{:S(2)}) collective-permute-start(bf16[30,16,128]{2,1,0:T(8,128)(2,1)S(1)} %get-tuple-element.63), channel_id=1, source_target_pairs={{24,20},{25,21},{28,22},{29,23},{30,18},{31,19},{26,16},{27,17},{1... | collective-permute-start | bytes 368648 | tf_op jit(solution)/shard_map/ppermute | solution.py:604
  43.3 6.8 %collective-permute-start.11 = (bf16[30,16,128]{2,1,0:T(8,128)(2,1)S(1)}, bf16[30,16,128]{2,1,0:T(8,128)(2,1)S(1)}, u32[]{:S(2)}, u32[]{:S(2)}) collective-permute-start(bf16[30,16,128]{2,1,0:T(8,128)(2,1)S(1)} %get-tuple-element.68), channel_id=1, source_target_pairs={{16,10},{17,11},{20,8},{21,9},{22,12},{23,13},{18,14},{19,15},{8,0... | collective-permute-start | bytes 368648 | tf_op jit(solution)/shard_map/ppermute | solution.py:604
  47.7 2.4 %collective-permute-start.12 = (bf16[30,16,128]{2,1,0:T(8,128)(2,1)S(1)}, bf16[30,16,128]{2,1,0:T(8,128)(2,1)S(1)}, u32[]{:S(2)}, u32[]{:S(2)}) collective-permute-start(bf16[30,16,128]{2,1,0:T(8,128)(2,1)S(1)} %get-tuple-element.69), channel_id=1, source_target_pairs={{16,8},{17,9},{20,12},{21,13},{22,14},{23,15},{18,10},{19,11},{8,2... | collective-permute-start | bytes 368648 | tf_op jit(solution)/shard_map/ppermute | solution.py:604
  50.1 10.7 %collective-permute-start.13 = (bf16[30,16,128]{2,1,0:T(8,128)(2,1)S(1)}, bf16[30,16,128]{2,1,0:T(8,128)(2,1)S(1)}, u32[]{:S(2)}, u32[]{:S(2)}) collective-permute-start(bf16[30,16,128]{2,1,0:T(8,128)(2,1)S(1)} %get-tuple-element.74), channel_id=1, source_target_pairs={{8,0},{9,1},{12,2},{13,3},{14,4},{15,5},{10,6},{11,7},{0,16},{1,17... | collective-permute-start | bytes 368648 | tf_op jit(solution)/shard_map/ppermute | solution.py:604
  52.6 8.2 %collective-permute-start.14 = (bf16[30,16,128]{2,1,0:T(8,128)(2,1)S(1)}, bf16[30,16,128]{2,1,0:T(8,128)(2,1)S(1)}, u32[]{:S(2)}, u32[]{:S(2)}) collective-permute-start(bf16[30,16,128]{2,1,0:T(8,128)(2,1)S(1)} %get-tuple-element.75), channel_id=1, source_target_pairs={{8,2},{9,3},{12,4},{13,5},{14,6},{15,7},{10,0},{11,1},{0,24},{1,25... | collective-permute-start | bytes 368648 | tf_op jit(solution)/shard_map/ppermute | solution.py:604
  62.2 5.0 %collective-permute-start.15 = (f32[8,128]{1,0:T(8,128)S(1)}, f32[8,128]{1,0:T(8,128)S(1)}, u32[]{:S(2)}, u32[]{:S(2)}) collective-permute-start(f32[8,128]{1,0:T(8,128)S(1)} %get-tuple-element.81), channel_id=1, source_target_pairs={{0,1},{1,0},{2,3},{3,2},{4,5},{5,4},{6,7},{7,6},{8,9},{9,8},{10,11... | collective-permute-start | bytes 12296 | tf_op jit(solution)/shard_map/ppermute | solution.py:590
  62.2 5.5 %collective-permute-start.16 = (f32[8,128]{1,0:T(8,128)S(1)}, f32[8,128]{1,0:T(8,128)S(1)}, u32[]{:S(2)}, u32[]{:S(2)}) collective-permute-start(f32[8,128]{1,0:T(8,128)S(1)} %get-tuple-element.82), channel_id=1, source_target_pairs={{0,2},{1,7},{2,4},{3,1},{4,6},{5,3},{6,0},{7,5},{8,9},{9,8},{10,11... | collective-permute-start | bytes 12296 | tf_op jit(solution)/shard_map/ppermute | solution.py:590
  63.9 4.8 %collective-permute-start.17 = (f32[8,128]{1,0:T(8,128)S(1)}, f32[8,128]{1,0:T(8,128)S(1)}, u32[]{:S(2)}, u32[]{:S(2)}) collective-permute-start(f32[8,128]{1,0:T(8,128)S(1)} %get-tuple-element.83), channel_id=1, source_target_pairs={{0,7},{1,2},{2,1},{3,4},{4,3},{5,6},{6,5},{7,0},{8,9},{9,8},{10,11... | collective-permute-start | bytes 12296 | tf_op jit(solution)/shard_map/ppermute | solution.py:590
  68.7 3.7 %collective-permute-start.20 = (f32[16,128]{1,0:T(8,128)S(1)}, f32[16,128]{1,0:T(8,128)S(1)}, u32[]{:S(2)}, u32[]{:S(2)}) collective-permute-start(f32[16,128]{1,0:T(8,128)S(1)} %join.1.refs_0_), channel_id=1, source_target_pairs={{0,24},{1,25},{2,26},{3,27},{4,28},{5,29},{6,30},{7,31},{8,9},{9,8... | collective-permute-start | bytes 24584 | tf_op jit(solution)/shard_map/ppermute | solution.py:685
  68.7 3.7 %collective-permute-start.19 = (f32[16,128]{1,0:T(8,128)S(1)}, f32[16,128]{1,0:T(8,128)S(1)}, u32[]{:S(2)}, u32[]{:S(2)}) collective-permute-start(f32[16,128]{1,0:T(8,128)S(1)} %join.1.refs_0_), channel_id=1, source_target_pairs={{0,16},{1,17},{2,18},{3,19},{4,20},{5,21},{6,22},{7,23},{8,9},{9,8... | collective-permute-start | bytes 24584 | tf_op jit(solution)/shard_map/ppermute | solution.py:685
  70.7 3.7 %collective-permute-start.18 = (f32[16,128]{1,0:T(8,128)S(1)}, f32[16,128]{1,0:T(8,128)S(1)}, u32[]{:S(2)}, u32[]{:S(2)}) collective-permute-start(f32[16,128]{1,0:T(8,128)S(1)} %join.1.refs_0_), channel_id=1, source_target_pairs={{0,8},{1,9},{2,10},{3,11},{4,12},{5,13},{6,14},{7,15},{8,0},{9,1},... | collective-permute-start | bytes 24584 | tf_op jit(solution)/shard_map/ppermute | solution.py:685

commit v20 on v18

--- a/solution.py
+++ b/solution.py
@@ -472,13 +472,13 @@
 
 
 def forward_kernel(
-    tick, sz, slabs, neighbours, low_ref, high_ref, rate_ref, zero_ref, one_ref, two_ref,
+    tick, swap, sz, slabs, neighbours, low_ref, high_ref, rate_ref, zero_ref, one_ref, two_ref,
     out_ref, pooled_ref, hot_t_ref, geo_ref, faded_ref, hot_ref
 ):
     @pl.when(lax.axis_index("segment") == tick)
     def _():
         rows = low_ref.shape[1]
-        refs = (low_ref, high_ref)
+        refs = (high_ref, low_ref) if swap else (low_ref, high_ref)
         edges_of(refs, sz.coefs, slabs, neighbours, rate_ref, hot_ref, hot_t_ref, geo_ref)
         pooled = forward(refs, hot_ref, geo_ref, faded_ref, zero_ref, one_ref, two_ref, sz, rows, False)
         signal = signal_of(pooled, sz)
@@ -491,14 +491,14 @@
 
 
 def turn_kernel(
-    tick, sz, slabs, neighbours, low_ref, high_ref, rate_ref, zero_ref, one_ref, two_ref,
+    tick, swap, sz, slabs, neighbours, low_ref, high_ref, rate_ref, zero_ref, one_ref, two_ref,
     zero_t_ref, one_t_ref, two_t_ref, read_ref,
     back_low_ref, back_high_ref, hot_ref, hot_t_ref, geo_ref, faded_ref
 ):
     @pl.when(lax.axis_index("segment") == tick)
     def _():
         rows = low_ref.shape[1]
-        refs = (low_ref, high_ref)
+        refs = (high_ref, low_ref) if swap else (low_ref, high_ref)
         outs = (back_low_ref, back_high_ref)
         own = edges_of(refs, sz.coefs, slabs, neighbours, rate_ref, hot_ref, hot_t_ref, geo_ref)
         pooled = forward(refs, hot_ref, geo_ref, faded_ref, zero_ref, one_ref, two_ref, sz, rows, True)
@@ -630,10 +630,10 @@
         shape((2 * rows, edges), BF16), shape((10 * edges, channels), F32), shape((coefs, edges, channels), F32),
     ]
     hot = [pltpu.VMEM((edges, 2 * rows), BF16)]
-    kept = []
+    kept, swaps = [], [False]
     for tick in range(segments - 1):
         out, *residuals = call(
-            functools.partial(forward_kernel, tick, sz, slabs, neighbours),
+            functools.partial(forward_kernel, tick, swaps[tick], sz, slabs, neighbours),
             [*around_all[tick], rate, *weights],
             [whole, shape((coefs, rows, channels), F32), *kept_shapes],
             "forward",
@@ -643,11 +643,13 @@
         if tick == 0:
             flipped = call(flip_kernel, [*weights, out], on_chip, "flip")
         ways = (1, 0) if tick % 2 else (0, -1)
-        around_all.append([hop(out, tick, tick + 1, by, way) for way, by in enumerate(ways)])
+        sent = [hop(out, tick, tick + 1, by, way) for way, by in enumerate(ways)]
+        swaps.append(ways[0] == 0)
+        around_all.append(sent[::-1] if swaps[-1] else sent)
     final = segments - 1
     slab_sums = shape((per_slab, channels), F32)
     parts = call(
-        functools.partial(turn_kernel, final, sz, slabs, neighbours),
+        functools.partial(turn_kernel, final, swaps[final], sz, slabs, neighbours),
         [*around_all[final], rate, *weights, *flipped, read],
         [whole, whole],
         "turn",
@@ -659,7 +661,7 @@
         pooled, *residuals = kept[tick]
         parts = call(
             functools.partial(backward_kernel, tick, sz),
-            [*up, pooled, *residuals, *flipped],
+            [*(up if ways[0] == 0 else up[::-1]), pooled, *residuals, *flipped],
             [whole, whole] if tick else [slab_sums] * 4,
             "backward",
         )

time: 75 us -> 75.6 us (level)
  waiting for transfers between devices: 36.6 us -> 39.5 us
  starting transfers between devices: 27.2 us -> 24.9 us
    ppermute x6, starting transfers between devices: 9.9 us -> 7.9 us  [within(): return lax.ppermute(value, axes, ways)]
    ppermute x12, waiting for transfers between devices: 24.9 us -> 26.8 us  [hop(): return lax.ppermute(value, axes, ways)]
    ppermute x6, waiting for transfers between devices: 7.33 us -> 8.25 us  [within(): return lax.ppermute(value, axes, ways)]
  transfers between devices with their start and end apart: 21 -> 21, of which waited for: 13 -> 12; matrix products, arithmetic and copies ran while one was open for 0% -> 0% of each run, Pallas kernels for 3% -> 3%
where the time goes in v20:
time: 75.6 us; the launch traced here: 75.5 us
  waiting for transfers between devices  39.5 us (52%)
  starting transfers between devices  24.9 us (33%)
  Pallas kernels  10.3 us (14%)
    ppermute x12, waiting for transfers between devices, hop(): return lax.ppermute(value, axes, ways)  26.8 us
    ppermute x12, starting transfers between devices, hop(): return lax.ppermute(value, axes, ways)  16.9 us
    pallas_call x14, Pallas kernels, call(): pl.pallas_call(body, out_shape=shapes, in_specs=[pl.BlockSpec(memory_spac...  10.3 us
    ppermute x6, waiting for transfers between devices, within(): return lax.ppermute(value, axes, ways)  8.25 us
    ppermute x6, starting transfers between devices, within(): return lax.ppermute(value, axes, ways)  7.9 us
    ppermute x3, waiting for transfers between devices, on_device(): lax.ppermute(both, axes, [(s * slabs + i, t * slabs + j) for s in range(s...  4.39 us
  transfers between devices with their start and end apart: 21, of which 12 were waited for; matrix products, arithmetic and copies ran while one was open for 0% of the time, Pallas kernels for 3%

profile of v20, /device:TPU:0, one launch (start us, length us, event | category | flops | bytes accessed | tf_op | source)
XLA Modules:
  0.0 75.5 jit_solution(8900531305817691829)
XLA Ops:
  0.6 1.2 %pack.1 = (bf16[30,8,128]{2,1,0:T(8,128)(2,1)S(1)}, bf16[30,8,128]{2,1,0:T(8,128)(2,1)S(1)}) custom-call(bf16[2,29,8,128]{3,2,1,0:T(8,128)(2,1)} %bitcast.13, f32[3,2,8]{2,1,0:T(2,128)} %bitcast.14, s32[2,8]{1,0:T(2,128)} %species_hbm.1, s32[2,8,8]{2,1,0:T(8,128)} %sources_hbm.1, f32[2,8]{1,0:T(2,128)} %grad_hbm.1, bf16[100,128]{1,0:T(8,128)(2,1)} %table_hbm.1), custom_call_target="tpu_custom_call" | custom-call | tf_op jit(solution)/shard_map/pack/pallas_call | solution.py:543
  1.9 5.1 %collective-permute-start.1 = (bf16[30,8,128]{2,1,0:T(8,128)(2,1)S(1)}, bf16[30,8,128]{2,1,0:T(8,128)(2,1)S(1)}, u32[]{:S(2)}, u32[]{:S(2)}) collective-permute-start(bf16[30,8,128]{2,1,0:T(8,128)(2,1)S(1)} %get-tuple-element.44.mine_ref), channel_id=1, source_target_pairs={{0,6},{1,3},{2,0},{3,5},{4,2},{5,7},{6,4},{7,1},{8,9},{9,8},{10,11... | collective-permute-start | bytes 184328 | tf_op jit(solution)/shard_map/ppermute | solution.py:587
  7.0 0.0 collective-permute-start.2
  7.0 0.0 collective-permute-start
  7.0 0.8 %stage.2 = (bf16[896,896]{1,0:T(8,128)(2,1)S(1)}, bf16[2,768,768]{2,1,0:T(8,128)(2,1)S(1)}, bf16[2,640,640]{2,1,0:T(8,128)(2,1)S(1)}, f32[1,128]{1,0:T(1,128)S(1)}, f32[1,128]{1,0:T(1,128)S(1)}) custom-call(bf16[896,896]{1,0:T(8,128)(2,1)} %bitcast.11, bf16[2,768,768]{2,1,0:T(8,128)(2,1)} %bitcast.7, bf16[2,640,640]{2,1,0:T(8,128)(2,1)} %bitcast.9, ...), custom_call_target="tpu_custom_call" | custom-call | tf_op jit(solution)/shard_map/stage/pallas_call | solution.py:543
  7.7 1.1 %collective-permute-done.1.straight_ref = bf16[30,8,128]{2,1,0:T(8,128)(2,1)S(1)} collective-permute-done((bf16[30,8,128]{2,1,0:T(8,128)(2,1)S(1)}, bf16[30,8,128]{2,1,0:T(8,128)(2,1)S(1)}, u32[]{:S(2)}, u32[]{:S(2)}) %collective-permute-start.1) | collective-permute-done | bytes 61472 | tf_op jit(solution)/shard_map/ppermute | solution.py:587
  8.8 3.6 %collective-permute-done.2.cross_ref = bf16[30,8,128]{2,1,0:T(8,128)(2,1)S(1)} collective-permute-done((bf16[30,8,128]{2,1,0:T(8,128)(2,1)S(1)}, bf16[30,8,128]{2,1,0:T(8,128)(2,1)S(1)}, u32[]{:S(2)}, u32[]{:S(2)}) %collective-permute-start.2) | collective-permute-done | bytes 61472 | tf_op jit(solution)/shard_map/ppermute | solution.py:587
  12.4 0.0 collective-permute-done.partner_ref
  12.4 0.1 open.1
  12.5 2.7 %stage.3 = (bf16[896,896]{1,0:T(8,128)(2,1)S(1)}, bf16[2,768,768]{2,1,0:T(8,128)(2,1)S(1)}, bf16[2,640,640]{2,1,0:T(8,128)(2,1)S(1)}) custom-call(bf16[896,896]{1,0:T(8,128)(2,1)} %bitcast.12, bf16[2,768,768]{2,1,0:T(8,128)(2,1)} %bitcast.8, bf16[2,640,640]{2,1,0:T(8,128)(2,1)} %bitcast.10, ...), custom_call_target="tpu_custom_call", output_to_operand_aliasing={{0}: (3, {}), {1}: (4, {}), {2}: (5, {})} | custom-call | tf_op jit(solution)/shard_map/stage/pallas_call | solution.py:543
  15.1 2.0 %forward.3 = (bf16[30,16,128]{2,1,0:T(8,128)(2,1)S(1)}, f32[29,16,128]{2,1,0:T(8,128)S(1)}, bf16[32,128]{1,0:T(8,128)(2,1)S(1)}, f32[1280,128]{1,0:T(8,128)S(1)}, f32[29,128,128]{2,1,0:T(8,128)S(1)}) custom-call(bf16[30,16,128]{2,1,0:T(8,128)(2,1)S(1)} %get-tuple-element.46.more_3_.low_ref, bf16[30,16,128]{2,1,0:T(8,128)(2,1)S(1)} %get-tuple-element.47.high_ref, ...), custom_call_target="tpu_custom_call" | custom-call | tf_op jit(solution)/shard_map/forward/pallas_call | solution.py:543
  17.1 0.1 collective-permute-start.4
  17.2 0.1 collective-permute-start.3
  17.2 6.1 %collective-permute-done.4.high_ref = bf16[30,16,128]{2,1,0:T(8,128)(2,1)S(1)} collective-permute-done((bf16[30,16,128]{2,1,0:T(8,128)(2,1)S(1)}, bf16[30,16,128]{2,1,0:T(8,128)(2,1)S(1)}, u32[]{:S(2)}, u32[]{:S(2)}) %collective-permute-start.4) | collective-permute-done | bytes 122912 | tf_op jit(solution)/shard_map/ppermute | solution.py:601
  23.3 0.0 collective-permute-done.3.low_ref
  23.3 0.0 collective-permute-start.6
  23.4 1.0 %collective-permute-start.5 = (bf16[30,16,128]{2,1,0:T(8,128)(2,1)S(1)}, bf16[30,16,128]{2,1,0:T(8,128)(2,1)S(1)}, u32[]{:S(2)}, u32[]{:S(2)}) collective-permute-start(bf16[30,16,128]{2,1,0:T(8,128)(2,1)S(1)} %get-tuple-element.56), channel_id=1, source_target_pairs={{8,20},{9,21},{12,22},{13,23},{14,18},{15,19},{10,16},{11,17},{16,... | collective-permute-start | bytes 368648 | tf_op jit(solution)/shard_map/ppermute | solution.py:601
  24.4 0.3 collective-permute-done.6.high_ref
  24.7 4.4 %collective-permute-done.5.low_ref = bf16[30,16,128]{2,1,0:T(8,128)(2,1)S(1)} collective-permute-done((bf16[30,16,128]{2,1,0:T(8,128)(2,1)S(1)}, bf16[30,16,128]{2,1,0:T(8,128)(2,1)S(1)}, u32[]{:S(2)}, u32[]{:S(2)}) %collective-permute-start.5) | collective-permute-done | bytes 122912 | tf_op jit(solution)/shard_map/ppermute | solution.py:601
  29.1 2.9 %collective-permute-start.8 = (bf16[30,16,128]{2,1,0:T(8,128)(2,1)S(1)}, bf16[30,16,128]{2,1,0:T(8,128)(2,1)S(1)}, u32[]{:S(2)}, u32[]{:S(2)}) collective-permute-start(bf16[30,16,128]{2,1,0:T(8,128)(2,1)S(1)} %get-tuple-element.57), channel_id=1, source_target_pairs={{16,24},{17,25},{20,28},{21,29},{22,30},{23,31},{18,26},{19,27},{2... | collective-permute-start | bytes 368648 | tf_op jit(solution)/shard_map/ppermute | solution.py:601
  32.0 0.0 collective-permute-start.7
  32.0 1.5 %flip.1 = (bf16[896,896]{1,0:T(8,128)(2,1)S(1)}, bf16[2,768,768]{2,1,0:T(8,128)(2,1)S(1)}, bf16[2,640,640]{2,1,0:T(8,128)(2,1)S(1)}) custom-call(bf16[896,896]{1,0:T(8,128)(2,1)S(1)} %get-tuple-element.52.zero_ref, bf16[2,768,768]{2,1,0:T(8,128)(2,1)S(1)} %get-tuple-element.53.one_ref, bf16[2,640,640]{2,1,0:T(8,128)(2,1)S(1)} %get-tuple-element.54.two_ref, ...), custom_call_target="tpu_custom_call" | custom-call | tf_op jit(solution)/shard_map/flip/pallas_call | solution.py:543
  33.5 2.2 %collective-permute-done.8.high_ref = bf16[30,16,128]{2,1,0:T(8,128)(2,1)S(1)} collective-permute-done((bf16[30,16,128]{2,1,0:T(8,128)(2,1)S(1)}, bf16[30,16,128]{2,1,0:T(8,128)(2,1)S(1)}, u32[]{:S(2)}, u32[]{:S(2)}) %collective-permute-start.8) | collective-permute-done | bytes 122912 | tf_op jit(solution)/shard_map/ppermute | solution.py:601
  35.8 0.0 collective-permute-done.7.low_ref
  35.8 7.0 %collective-permute-start.9 = (bf16[30,16,128]{2,1,0:T(8,128)(2,1)S(1)}, bf16[30,16,128]{2,1,0:T(8,128)(2,1)S(1)}, u32[]{:S(2)}, u32[]{:S(2)}) collective-permute-start(bf16[30,16,128]{2,1,0:T(8,128)(2,1)S(1)} %get-tuple-element.62), channel_id=1, source_target_pairs={{24,16},{25,17},{28,20},{29,21},{30,22},{31,23},{26,18},{27,19},{1... | collective-permute-start | bytes 368648 | tf_op jit(solution)/shard_map/ppermute | solution.py:601
  42.7 0.0 collective-permute-start.10
  42.7 2.4 %collective-permute-done.9.up_low_ref = bf16[30,16,128]{2,1,0:T(8,128)(2,1)S(1)} collective-permute-done((bf16[30,16,128]{2,1,0:T(8,128)(2,1)S(1)}, bf16[30,16,128]{2,1,0:T(8,128)(2,1)S(1)}, u32[]{:S(2)}, u32[]{:S(2)}) %collective-permute-start.9) | collective-permute-done | bytes 122912 | tf_op jit(solution)/shard_map/ppermute | solution.py:601
  45.2 0.0 collective-permute-done.10.up_high_ref
  45.2 0.0 collective-permute-start.11
  45.2 3.6 %collective-permute-start.12 = (bf16[30,16,128]{2,1,0:T(8,128)(2,1)S(1)}, bf16[30,16,128]{2,1,0:T(8,128)(2,1)S(1)}, u32[]{:S(2)}, u32[]{:S(2)}) collective-permute-start(bf16[30,16,128]{2,1,0:T(8,128)(2,1)S(1)} %get-tuple-element.69), channel_id=1, source_target_pairs={{16,10},{17,11},{20,8},{21,9},{22,12},{23,13},{18,14},{19,15},{8,0... | collective-permute-start | bytes 368648 | tf_op jit(solution)/shard_map/ppermute | solution.py:601
  48.8 0.0 collective-permute-done.11.up_low_ref
  48.8 3.9 %collective-permute-done.12.up_high_ref = bf16[30,16,128]{2,1,0:T(8,128)(2,1)S(1)} collective-permute-done((bf16[30,16,128]{2,1,0:T(8,128)(2,1)S(1)}, bf16[30,16,128]{2,1,0:T(8,128)(2,1)S(1)}, u32[]{:S(2)}, u32[]{:S(2)}) %collective-permute-start.12) | collective-permute-done | bytes 122912 | tf_op jit(solution)/shard_map/ppermute | solution.py:601
  52.7 2.2 %collective-permute-start.13 = (bf16[30,16,128]{2,1,0:T(8,128)(2,1)S(1)}, bf16[30,16,128]{2,1,0:T(8,128)(2,1)S(1)}, u32[]{:S(2)}, u32[]{:S(2)}) collective-permute-start(bf16[30,16,128]{2,1,0:T(8,128)(2,1)S(1)} %get-tuple-element.74), channel_id=1, source_target_pairs={{8,0},{9,1},{12,2},{13,3},{14,4},{15,5},{10,6},{11,7},{0,16},{1,17... | collective-permute-start | bytes 368648 | tf_op jit(solution)/shard_map/ppermute | solution.py:601
  54.9 0.0 collective-permute-start.14
  54.9 7.4 %collective-permute-done.13.up_low_ref = bf16[30,16,128]{2,1,0:T(8,128)(2,1)S(1)} collective-permute-done((bf16[30,16,128]{2,1,0:T(8,128)(2,1)S(1)}, bf16[30,16,128]{2,1,0:T(8,128)(2,1)S(1)}, u32[]{:S(2)}, u32[]{:S(2)}) %collective-permute-start.13) | collective-permute-done | bytes 122912 | tf_op jit(solution)/shard_map/ppermute | solution.py:601
  62.4 0.0 collective-permute-done.14.up_high_ref
  62.4 1.4 %backward.5 = (f32[8,128]{1,0:T(8,128)S(1)}, f32[8,128]{1,0:T(8,128)S(1)}, f32[8,128]{1,0:T(8,128)S(1)}, f32[8,128]{1,0:T(8,128)S(1)}) custom-call(bf16[30,16,128]{2,1,0:T(8,128)(2,1)S(1)} %collective-permute-done.13.up_low_ref, bf16[30,16,128]{2,1,0:T(8,128)(2,1)S(1)} %collective-permute-done.14.up_high_ref, ...), custom_call_target="tpu_custom_call" | custom-call | tf_op jit(solution)/shard_map/backward/pallas_call | solution.py:543
  63.8 0.0 collective-permute-start.15
  63.8 1.5 %collective-permute-start.16 = (f32[8,128]{1,0:T(8,128)S(1)}, f32[8,128]{1,0:T(8,128)S(1)}, u32[]{:S(2)}, u32[]{:S(2)}) collective-permute-start(f32[8,128]{1,0:T(8,128)S(1)} %get-tuple-element.82), channel_id=1, source_target_pairs={{0,2},{1,7},{2,4},{3,1},{4,6},{5,3},{6,0},{7,5},{8,9},{9,8},{10,11... | collective-permute-start | bytes 12296 | tf_op jit(solution)/shard_map/ppermute | solution.py:587
  65.3 1.2 %collective-permute-start.17 = (f32[8,128]{1,0:T(8,128)S(1)}, f32[8,128]{1,0:T(8,128)S(1)}, u32[]{:S(2)}, u32[]{:S(2)}) collective-permute-start(f32[8,128]{1,0:T(8,128)S(1)} %get-tuple-element.83), channel_id=1, source_target_pairs={{0,7},{1,2},{2,1},{3,4},{4,3},{5,6},{6,5},{7,0},{8,9},{9,8},{10,11... | collective-permute-start | bytes 12296 | tf_op jit(solution)/shard_map/ppermute | solution.py:587
  66.6 0.0 collective-permute-done.15.theirs_ref
  66.6 2.7 %collective-permute-done.16.straight_ref = f32[8,128]{1,0:T(8,128)S(1)} collective-permute-done((f32[8,128]{1,0:T(8,128)S(1)}, f32[8,128]{1,0:T(8,128)S(1)}, u32[]{:S(2)}, u32[]{:S(2)}) %collective-permute-start.16) | collective-permute-done | bytes 4128 | tf_op jit(solution)/shard_map/ppermute | solution.py:587
  69.2 0.9 %collective-permute-done.17.cross_ref = f32[8,128]{1,0:T(8,128)S(1)} collective-permute-done((f32[8,128]{1,0:T(8,128)S(1)}, f32[8,128]{1,0:T(8,128)S(1)}, u32[]{:S(2)}, u32[]{:S(2)}) %collective-permute-start.17) | collective-permute-done | bytes 4128 | tf_op jit(solution)/shard_map/ppermute | solution.py:587
  70.2 0.0 collective-permute-start.20
  70.2 0.1 collective-permute-start.19
  70.3 0.1 collective-permute-start.18
  70.3 4.4 %collective-permute-done.20.refs_3_ = f32[16,128]{1,0:T(8,128)S(1)} collective-permute-done((f32[16,128]{1,0:T(8,128)S(1)}, f32[16,128]{1,0:T(8,128)S(1)}, u32[]{:S(2)}, u32[]{:S(2)}) %collective-permute-start.20) | collective-permute-done | bytes 8224 | tf_op jit(solution)/shard_map/ppermute | solution.py:680
  74.7 0.7 close.1
  (8 shorter events, 0.0 us)
Async XLA Ops:
  1.9 7.0 %collective-permute-start.1 = (bf16[30,8,128]{2,1,0:T(8,128)(2,1)S(1)}, bf16[30,8,128]{2,1,0:T(8,128)(2,1)S(1)}, u32[]{:S(2)}, u32[]{:S(2)}) collective-permute-start(bf16[30,8,128]{2,1,0:T(8,128)(2,1)S(1)} %get-tuple-element.44.mine_ref), channel_id=1, source_target_pairs={{0,6},{1,3},{2,0},{3,5},{4,2},{5,7},{6,4},{7,1},{8,9},{9,8},{10,11... | collective-permute-start | bytes 184328 | tf_op jit(solution)/shard_map/ppermute | solution.py:587
  7.0 5.4 %collective-permute-start.2 = (bf16[30,8,128]{2,1,0:T(8,128)(2,1)S(1)}, bf16[30,8,128]{2,1,0:T(8,128)(2,1)S(1)}, u32[]{:S(2)}, u32[]{:S(2)}) collective-permute-start(bf16[30,8,128]{2,1,0:T(8,128)(2,1)S(1)} %get-tuple-element.45), channel_id=1, source_target_pairs={{0,7},{1,2},{2,1},{3,4},{4,3},{5,6},{6,5},{7,0},{8,9},{9,8},{10,11... | collective-permute-start | bytes 184328 | tf_op jit(solution)/shard_map/ppermute | solution.py:587
  7.0 5.4 %collective-permute-start = (bf16[30,8,128]{2,1,0:T(8,128)(2,1)S(1)}, bf16[30,8,128]{2,1,0:T(8,128)(2,1)S(1)}, u32[]{:S(2)}, u32[]{:S(2)}) collective-permute-start(bf16[30,8,128]{2,1,0:T(8,128)(2,1)S(1)} %get-tuple-element.45), channel_id=1, source_target_pairs={{0,1},{1,0},{2,3},{3,2},{4,5},{5,4},{6,7},{7,6},{8,9},{9,8},{10,11... | collective-permute-start | bytes 184328 | tf_op jit(solution)/shard_map/ppermute | solution.py:587
  17.1 6.2 %collective-permute-start.4 = (bf16[30,16,128]{2,1,0:T(8,128)(2,1)S(1)}, bf16[30,16,128]{2,1,0:T(8,128)(2,1)S(1)}, u32[]{:S(2)}, u32[]{:S(2)}) collective-permute-start(bf16[30,16,128]{2,1,0:T(8,128)(2,1)S(1)} %get-tuple-element.55._), channel_id=1, source_target_pairs={{0,8},{1,9},{2,12},{3,13},{4,14},{5,15},{6,10},{7,11},{8,16},{9,17... | collective-permute-start | bytes 368648 | tf_op jit(solution)/shard_map/ppermute | solution.py:601
  17.2 6.2 %collective-permute-start.3 = (bf16[30,16,128]{2,1,0:T(8,128)(2,1)S(1)}, bf16[30,16,128]{2,1,0:T(8,128)(2,1)S(1)}, u32[]{:S(2)}, u32[]{:S(2)}) collective-permute-start(bf16[30,16,128]{2,1,0:T(8,128)(2,1)S(1)} %get-tuple-element.55._), channel_id=1, source_target_pairs={{0,10},{1,11},{2,8},{3,9},{4,12},{5,13},{6,14},{7,15},{8,24},{9,25... | collective-permute-start | bytes 368648 | tf_op jit(solution)/shard_map/ppermute | solution.py:601
  23.3 1.3 %collective-permute-start.6 = (bf16[30,16,128]{2,1,0:T(8,128)(2,1)S(1)}, bf16[30,16,128]{2,1,0:T(8,128)(2,1)S(1)}, u32[]{:S(2)}, u32[]{:S(2)}) collective-permute-start(bf16[30,16,128]{2,1,0:T(8,128)(2,1)S(1)} %get-tuple-element.56), channel_id=1, source_target_pairs={{8,16},{9,17},{12,20},{13,21},{14,22},{15,23},{10,18},{11,19},{16,... | collective-permute-start | bytes 368648 | tf_op jit(solution)/shard_map/ppermute | solution.py:601
  23.4 5.7 %collective-permute-start.5 = (bf16[30,16,128]{2,1,0:T(8,128)(2,1)S(1)}, bf16[30,16,128]{2,1,0:T(8,128)(2,1)S(1)}, u32[]{:S(2)}, u32[]{:S(2)}) collective-permute-start(bf16[30,16,128]{2,1,0:T(8,128)(2,1)S(1)} %get-tuple-element.56), channel_id=1, source_target_pairs={{8,20},{9,21},{12,22},{13,23},{14,18},{15,19},{10,16},{11,17},{16,... | collective-permute-start | bytes 368648 | tf_op jit(solution)/shard_map/ppermute | solution.py:601
  29.1 6.7 %collective-permute-start.8 = (bf16[30,16,128]{2,1,0:T(8,128)(2,1)S(1)}, bf16[30,16,128]{2,1,0:T(8,128)(2,1)S(1)}, u32[]{:S(2)}, u32[]{:S(2)}) collective-permute-start(bf16[30,16,128]{2,1,0:T(8,128)(2,1)S(1)} %get-tuple-element.57), channel_id=1, source_target_pairs={{16,24},{17,25},{20,28},{21,29},{22,30},{23,31},{18,26},{19,27},{2... | collective-permute-start | bytes 368648 | tf_op jit(solution)/shard_map/ppermute | solution.py:601
  32.0 3.8 %collective-permute-start.7 = (bf16[30,16,128]{2,1,0:T(8,128)(2,1)S(1)}, bf16[30,16,128]{2,1,0:T(8,128)(2,1)S(1)}, u32[]{:S(2)}, u32[]{:S(2)}) collective-permute-start(bf16[30,16,128]{2,1,0:T(8,128)(2,1)S(1)} %get-tuple-element.57), channel_id=1, source_target_pairs={{16,26},{17,27},{20,24},{21,25},{22,28},{23,29},{18,30},{19,31},{2... | collective-permute-start | bytes 368648 | tf_op jit(solution)/shard_map/ppermute | solution.py:601
  35.8 9.4 %collective-permute-start.9 = (bf16[30,16,128]{2,1,0:T(8,128)(2,1)S(1)}, bf16[30,16,128]{2,1,0:T(8,128)(2,1)S(1)}, u32[]{:S(2)}, u32[]{:S(2)}) collective-permute-start(bf16[30,16,128]{2,1,0:T(8,128)(2,1)S(1)} %get-tuple-element.62), channel_id=1, source_target_pairs={{24,16},{25,17},{28,20},{29,21},{30,22},{31,23},{26,18},{27,19},{1... | collective-permute-start | bytes 368648 | tf_op jit(solution)/shard_map/ppermute | solution.py:601
  42.7 2.4 %collective-permute-start.10 = (bf16[30,16,128]{2,1,0:T(8,128)(2,1)S(1)}, bf16[30,16,128]{2,1,0:T(8,128)(2,1)S(1)}, u32[]{:S(2)}, u32[]{:S(2)}) collective-permute-start(bf16[30,16,128]{2,1,0:T(8,128)(2,1)S(1)} %get-tuple-element.63), channel_id=1, source_target_pairs={{24,20},{25,21},{28,22},{29,23},{30,18},{31,19},{26,16},{27,17},{1... | collective-permute-start | bytes 368648 | tf_op jit(solution)/shard_map/ppermute | solution.py:601
  45.2 3.6 %collective-permute-start.11 = (bf16[30,16,128]{2,1,0:T(8,128)(2,1)S(1)}, bf16[30,16,128]{2,1,0:T(8,128)(2,1)S(1)}, u32[]{:S(2)}, u32[]{:S(2)}) collective-permute-start(bf16[30,16,128]{2,1,0:T(8,128)(2,1)S(1)} %get-tuple-element.68), channel_id=1, source_target_pairs={{16,8},{17,9},{20,12},{21,13},{22,14},{23,15},{18,10},{19,11},{8,2... | collective-permute-start | bytes 368648 | tf_op jit(solution)/shard_map/ppermute | solution.py:601
  45.2 7.5 %collective-permute-start.12 = (bf16[30,16,128]{2,1,0:T(8,128)(2,1)S(1)}, bf16[30,16,128]{2,1,0:T(8,128)(2,1)S(1)}, u32[]{:S(2)}, u32[]{:S(2)}) collective-permute-start(bf16[30,16,128]{2,1,0:T(8,128)(2,1)S(1)} %get-tuple-element.69), channel_id=1, source_target_pairs={{16,10},{17,11},{20,8},{21,9},{22,12},{23,13},{18,14},{19,15},{8,0... | collective-permute-start | bytes 368648 | tf_op jit(solution)/shard_map/ppermute | solution.py:601
  52.7 9.7 %collective-permute-start.13 = (bf16[30,16,128]{2,1,0:T(8,128)(2,1)S(1)}, bf16[30,16,128]{2,1,0:T(8,128)(2,1)S(1)}, u32[]{:S(2)}, u32[]{:S(2)}) collective-permute-start(bf16[30,16,128]{2,1,0:T(8,128)(2,1)S(1)} %get-tuple-element.74), channel_id=1, source_target_pairs={{8,0},{9,1},{12,2},{13,3},{14,4},{15,5},{10,6},{11,7},{0,16},{1,17... | collective-permute-start | bytes 368648 | tf_op jit(solution)/shard_map/ppermute | solution.py:601
  54.9 7.4 %collective-permute-start.14 = (bf16[30,16,128]{2,1,0:T(8,128)(2,1)S(1)}, bf16[30,16,128]{2,1,0:T(8,128)(2,1)S(1)}, u32[]{:S(2)}, u32[]{:S(2)}) collective-permute-start(bf16[30,16,128]{2,1,0:T(8,128)(2,1)S(1)} %get-tuple-element.75), channel_id=1, source_target_pairs={{8,2},{9,3},{12,4},{13,5},{14,6},{15,7},{10,0},{11,1},{0,24},{1,25... | collective-permute-start | bytes 368648 | tf_op jit(solution)/shard_map/ppermute | solution.py:601
  63.8 2.8 %collective-permute-start.15 = (f32[8,128]{1,0:T(8,128)S(1)}, f32[8,128]{1,0:T(8,128)S(1)}, u32[]{:S(2)}, u32[]{:S(2)}) collective-permute-start(f32[8,128]{1,0:T(8,128)S(1)} %get-tuple-element.81), channel_id=1, source_target_pairs={{0,1},{1,0},{2,3},{3,2},{4,5},{5,4},{6,7},{7,6},{8,9},{9,8},{10,11... | collective-permute-start | bytes 12296 | tf_op jit(solution)/shard_map/ppermute | solution.py:587
  63.8 5.5 %collective-permute-start.16 = (f32[8,128]{1,0:T(8,128)S(1)}, f32[8,128]{1,0:T(8,128)S(1)}, u32[]{:S(2)}, u32[]{:S(2)}) collective-permute-start(f32[8,128]{1,0:T(8,128)S(1)} %get-tuple-element.82), channel_id=1, source_target_pairs={{0,2},{1,7},{2,4},{3,1},{4,6},{5,3},{6,0},{7,5},{8,9},{9,8},{10,11... | collective-permute-start | bytes 12296 | tf_op jit(solution)/shard_map/ppermute | solution.py:587
  65.3 4.8 %collective-permute-start.17 = (f32[8,128]{1,0:T(8,128)S(1)}, f32[8,128]{1,0:T(8,128)S(1)}, u32[]{:S(2)}, u32[]{:S(2)}) collective-permute-start(f32[8,128]{1,0:T(8,128)S(1)} %get-tuple-element.83), channel_id=1, source_target_pairs={{0,7},{1,2},{2,1},{3,4},{4,3},{5,6},{6,5},{7,0},{8,9},{9,8},{10,11... | collective-permute-start | bytes 12296 | tf_op jit(solution)/shard_map/ppermute | solution.py:587
  70.2 4.5 %collective-permute-start.20 = (f32[16,128]{1,0:T(8,128)S(1)}, f32[16,128]{1,0:T(8,128)S(1)}, u32[]{:S(2)}, u32[]{:S(2)}) collective-permute-start(f32[16,128]{1,0:T(8,128)S(1)} %join.1.refs_0_), channel_id=1, source_target_pairs={{0,24},{1,25},{2,26},{3,27},{4,28},{5,29},{6,30},{7,31},{8,9},{9,8... | collective-permute-start | bytes 24584 | tf_op jit(solution)/shard_map/ppermute | solution.py:680
  70.2 4.5 %collective-permute-start.19 = (f32[16,128]{1,0:T(8,128)S(1)}, f32[16,128]{1,0:T(8,128)S(1)}, u32[]{:S(2)}, u32[]{:S(2)}) collective-permute-start(f32[16,128]{1,0:T(8,128)S(1)} %join.1.refs_0_), channel_id=1, source_target_pairs={{0,16},{1,17},{2,18},{3,19},{4,20},{5,21},{6,22},{7,23},{8,9},{9,8... | collective-permute-start | bytes 24584 | tf_op jit(solution)/shard_map/ppermute | solution.py:680
  70.3 4.5 %collective-permute-start.18 = (f32[16,128]{1,0:T(8,128)S(1)}, f32[16,128]{1,0:T(8,128)S(1)}, u32[]{:S(2)}, u32[]{:S(2)}) collective-permute-start(f32[16,128]{1,0:T(8,128)S(1)} %join.1.refs_0_), channel_id=1, source_target_pairs={{0,8},{1,9},{2,10},{3,11},{4,12},{5,13},{6,14},{7,15},{8,0},{9,1},... | collective-permute-start | bytes 24584 | tf_op jit(solution)/shard_map/ppermute | solution.py:680
